TPU v7x, 32 devices: a whole 2x2x4 slice. The times are simulated.
32 devices in a mesh: grp: 2 (over y), ctx: 4 (over z), tp: 4 (over x, core).
Axes of the slice: x: 2, y: 2, z: 4, core: 2. Of those that a mesh axis runs over, the one named last changes fastest.
Arguments:
- queries: bfloat16 [16, 128, 4096], P(('grp', 'ctx'), None, 'tp'), parts along dimension 0, may hold values from -31 to 31
- cont_keys: bfloat16 [16, 128, 256], P(('grp', 'ctx')), parts along dimension 0, may hold values from -10 to 10
- cont_values: bfloat16 [16, 128, 256], P(('grp', 'ctx')), parts along dimension 0, may hold values from -6 to 6
- prompt_keys: bfloat16 [8192, 256], P(('grp', 'ctx')), parts along dimension 0, may hold values from -9.5625 to 9.5625
- prompt_values: bfloat16 [8192, 256], P(('grp', 'ctx')), parts along dimension 0, may hold values from -6 to 6
- block_lists: int32 [32, 16, 4, 8], P('tp', ('grp', 'ctx')), parts along dimension 1, may hold values from 0 to 15, as said below
- tile_counts: int32 [32, 16, 4], P('tp', ('grp', 'ctx')), parts along dimension 1, may hold values from 0 to 8, as said below
- out_weight: bfloat16 [4096, 4096], P('tp'), may hold values from -0.09375 to 0.09375
- residual: bfloat16 [16, 128, 4096], P(('grp', 'ctx')), parts along dimension 0, may hold values from -5 to 5
- norm_gain: bfloat16 [4096], P('tp'), may hold values from 0.5 to 1.5
Outputs:
- stream: bfloat16 [16, 128, 4096], P(('grp', 'ctx'), None, 'tp'), parts along dimension 0
- normed: bfloat16 [16, 128, 4096], P(('grp', 'ctx'), None, 'tp'), parts along dimension 0
There are 2 independent parts, one for each index of `grp`. A program takes and returns all parts, laid end to end along the dimension named above; an argument that names none is the same for every part. Nothing has to cross between parts.
Inputs may be any that keep to these rules, and one draw needn't show every extreme that they name: `block_lists`: block numbers within one source shard of 1024 rows; the 8 entries of one list are distinct, and entries past the list's count are valid numbers that are not used. `tile_counts`: for every head and continuation some source has all 8 entries used; a count may be 0.
All inputs are finite; a program needn't handle non-finite values.
Results may differ from a plain program's by a relative error of at most 0.013.
Values may be sent and summed in bfloat16 or wider, within the bound.
No kernel may reach another device: no remote copies, remote signals or barrier semaphores. Data moves between devices by JAX's collectives and lax.ppermute only.
A program may use at most 64 MiB of HBM per device.

v0:
```python
import math

import jax
import jax.numpy as jnp
from jax import lax
from jax.sharding import PartitionSpec as P

HEADS = 32
KVH = 2
HD = 128
BLK = 64
TILES = 8


very_low = -1e30


def start_state(head_count, cont_count, length):
    shape = (head_count, cont_count, length)
    return (
        jnp.full(shape, very_low, jnp.float32),
        jnp.zeros(shape, jnp.float32),
        jnp.zeros(shape + (HD,), jnp.float32),
    )


def absorb(carried, scores, usable, values, pattern):
    running, totals, weighted = carried
    masked = jnp.where(usable, scores, very_low)
    new_top = jnp.maximum(running, jnp.max(masked, axis=-1))
    weights = jnp.where(usable, jnp.exp(scores - new_top[..., None]), 0.0)
    factor = jnp.exp(running - new_top)
    totals = totals * factor + jnp.sum(weights, axis=-1)
    weighted = weighted * factor[..., None] + jnp.einsum(
        pattern, weights.astype(jnp.bfloat16), values, preferred_element_type=jnp.float32
    )
    return (new_top, totals, weighted)


def shard_term(carried, query_block, key_rows, value_rows, tile_lists, tile_used):
    head_count, cont_count, length, depth = query_block.shape
    block_count = key_rows.shape[0] // BLK
    key_tiles = key_rows.reshape(block_count, BLK, HD)[tile_lists].reshape(
        head_count, cont_count, TILES * BLK, HD
    )
    value_tiles = value_rows.reshape(block_count, BLK, HD)[tile_lists].reshape(
        head_count, cont_count, TILES * BLK, HD
    )
    scores = jnp.einsum(
        "hcqd,hckd->hcqk", query_block, key_tiles, preferred_element_type=jnp.float32
    ) * (1.0 / math.sqrt(HD))
    usable = jnp.repeat(jnp.arange(TILES)[None, None, :] < tile_used[:, :, None], BLK, axis=2)[
        :, :, None, :
    ]
    return absorb(carried, scores, usable, value_tiles, "hcqk,hckd->hcqd")


def shards(
    queries,
    cont_keys,
    cont_values,
    prompt_keys,
    prompt_values,
    block_lists,
    tile_counts,
    out_weight,
    residual,
    norm_gain,
):
    cont_dev, length, query_width = queries.shape
    heads_dev = query_width // HD
    rows_dev = prompt_keys.shape[0]
    model_width = residual.shape[2]
    share_width = norm_gain.shape[0]
    scaling = 1.0 / math.sqrt(HD)
    kv_group = lax.axis_index("tp") * heads_dev // (HEADS // KVH)
    head_keys = lax.dynamic_slice_in_dim(prompt_keys, kv_group * HD, HD, 1)
    head_values = lax.dynamic_slice_in_dim(prompt_values, kv_group * HD, HD, 1)
    own_keys = lax.dynamic_slice_in_dim(cont_keys, kv_group * HD, HD, 2)
    own_values = lax.dynamic_slice_in_dim(cont_values, kv_group * HD, HD, 2)
    query_heads = queries.reshape(cont_dev, length, heads_dev, HD).transpose(2, 0, 1, 3)
    key_piece = lax.all_gather(head_keys, "ctx", axis=0, tiled=True)
    value_piece = lax.all_gather(head_values, "ctx", axis=0, tiled=True)
    source_count = key_piece.shape[0] // rows_dev

    def one_source(offset, carried_in):
        key_rows = lax.dynamic_slice_in_dim(key_piece, offset * rows_dev, rows_dev, 0)
        value_rows = lax.dynamic_slice_in_dim(value_piece, offset * rows_dev, rows_dev, 0)
        tile_lists = lax.dynamic_index_in_dim(block_lists, offset, 2, keepdims=False)
        tile_used = lax.dynamic_index_in_dim(tile_counts, offset, 2, keepdims=False)
        return shard_term(carried_in, query_heads, key_rows, value_rows, tile_lists, tile_used)

    carried = lax.fori_loop(0, source_count, one_source, start_state(heads_dev, cont_dev, length))
    positions = jnp.arange(length)
    causal = (positions[:, None] >= positions[None, :])[None, None]
    own_scores = (
        jnp.einsum("hcqd,ckd->hcqk", query_heads, own_keys, preferred_element_type=jnp.float32)
        * scaling
    )
    carried = absorb(carried, own_scores, causal, own_values, "hcqk,ckd->hcqd")
    running, totals, weighted = carried
    attended = (weighted / totals[..., None]).astype(jnp.bfloat16)
    attended = attended.transpose(1, 2, 0, 3).reshape(cont_dev * length, query_width)
    head_terms = jnp.dot(attended, out_weight, preferred_element_type=jnp.float32)
    flat_residual = residual.reshape(cont_dev * length, model_width)
    first_column = lax.axis_index("tp") * share_width
    summed = lax.psum(head_terms.astype(jnp.bfloat16), "tp").astype(jnp.float32)
    stream_full = flat_residual.astype(jnp.float32) + summed
    mean_square = jnp.mean(stream_full * stream_full, axis=-1, keepdims=True)
    stream_sum = lax.dynamic_slice_in_dim(stream_full, first_column, share_width, 1)
    normed = stream_sum * lax.rsqrt(mean_square + 1e-05) * norm_gain.astype(jnp.float32)
    return (
        stream_sum.astype(jnp.bfloat16).reshape(cont_dev, length, share_width),
        normed.astype(jnp.bfloat16).reshape(cont_dev, length, share_width),
    )


def solution(mesh):
    placed = (
        P(("grp", "ctx"), None, "tp"),
        P(("grp", "ctx"), None, None),
        P(("grp", "ctx"), None, None),
        P(("grp", "ctx"), None),
        P(("grp", "ctx"), None),
        P("tp", ("grp", "ctx"), None, None),
        P("tp", ("grp", "ctx"), None),
        P("tp", None),
        P(("grp", "ctx"), None, None),
        P("tp"),
    )
    return jax.shard_map(
        shards,
        mesh=mesh,
        in_specs=placed,
        out_specs=(P(("grp", "ctx"), None, "tp"), P(("grp", "ctx"), None, "tp")),
        check_vma=False,
    )
```

profile of v0, /device:TPU:0, one launch (start us, length us, event | category | flops | bytes accessed | tf_op | source)
XLA Modules:
  0.0 219.7 jit_solution(6090512216553213584)
XLA Ops:
  9.0 1.7 constant_dynamic-slice_fusion.4
  10.8 1.3 copy.42
  13.1 2.1 select_reduce_fusion.1
  15.2 25.6 %all-gather.3.cloned.1.call-done = bf16[4096,128]{1,0:T(8,128)(2,1)} async-done(((bf16[1024,128]{1,0:T(8,128)(2,1)}), bf16[4096,128]{1,0:T(8,128)(2,1)}) %all-gather.3.cloned.1.call-update) | async-done | bytes 1048592 | tf_op jit(solution)/shard_map/all_gather | solution.py:82
  40.8 29.0 %all-gather.5.cloned.1.call-done = bf16[4096,128]{1,0:T(8,128)(2,1)} async-done(((bf16[1024,128]{1,0:T(8,128)(2,1)}), bf16[4096,128]{1,0:T(8,128)(2,1)}) %all-gather.5.cloned.1.call-update) | async-done | bytes 1048592 | tf_op jit(solution)/shard_map/all_gather | solution.py:83
  69.8 75.9 %while.18 = (s32[]{:T(128)}, f32[8,2,128]{2,1,0:T(2,128)S(1)}, f32[8,2,128]{2,1,0:T(2,128)S(1)}, f32[8,2,128,128]{3,2,1,0:T(8,128)}, s32[8,2,4]{0,2,1:T(4,128)},...) while((s32[]{:T(128)}, f32[8,2,128]{2,1,0:T(2,128)S(1)}, ...), condition=%wide.region_3.4_spmd.clone, body=%wide.region_0.3_spmd.clone.sunk | while | flops 549203456 | bytes 29042816 | solution.py:93
  73.8 4.6 %select_reduce_fusion.3 = (f32[8,2,128]{2,1,0:T(2,128)S(1)}, f32[8,2,512,128]{3,2,1,0:T(8,128)}) fusion(pred[8,2,512]{2,1,0:T(4,128)(4,1)S(1)} %copy.82, bf16[8,2,512,128]{3,2,1,0:T(8,128)(2,1)S(1)} %bitcast.94, bf16[8,2,128,128]{3,2,1,0:T(8,128)(2,1)} %get-tuple-element.348), kind=kOutput, calls=%fused_computation.5.clone.1 | convolution fusion | flops 271579136 | bytes 6832128 | tf_op jit(solution)/shard_map/while/body/eval_jaxpr/hcqd,hckd->hcqk/dot_general | solution.py:49
  78.5 3.6 %bitcast_reduce_fusion.2 = f32[8,2,128]{2,1,0:T(2,128)S(1)} fusion(f32[8,2,512,128]{3,2,1,0:T(8,128)} %get-tuple-element.311, f32[8,2,128]{2,1,0:T(2,128)S(1)} %fusion.45, pred[8,2,512]{2,1,0:T(4,128)(4,1)S(1)} %copy.82), kind=kLoop, calls=%fused_computation.3.clone.1 | loop fusion | flops 4192256 | bytes 4218880 | tf_op jit(solution)/shard_map/while/body/eval_jaxpr/reduce_sum | solution.py:33
  83.0 5.7 %fusion.47 = f32[8,2,128,128]{3,2,1,0:T(8,128)} fusion(bf16[8,2,512,128]{3,2,1,0:T(8,128)(2,1)S(1)} %bitcast.95, f32[8,2,512,128]{3,2,1,0:T(8,128)} %get-tuple-element.311, f32[8,2,128]{2,1,0:T(2,128)S(1)} %fusion.45, pred[8,2,512]{2,1,0:T(4,128)(4,1)S(1)} %copy.82, f32[8,2,128,128]{3,2,1,0:T(8,128)} %get-tuple-element.331, ...), kind=kOutput, calls=%fused_computation.11.clone.1 | convolution fusion | flops 273416192 | bytes 8413185 | tf_op jit(solution)/shard_map/while/body/eval_jaxpr/hcqk,hckd->hcqd/dot_general | solution.py:34
  92.7 4.6 %select_reduce_fusion.3 = (f32[8,2,128]{2,1,0:T(2,128)S(1)}, f32[8,2,512,128]{3,2,1,0:T(8,128)}) fusion(pred[8,2,512]{2,1,0:T(4,128)(4,1)S(1)} %copy.82, bf16[8,2,512,128]{3,2,1,0:T(8,128)(2,1)S(1)} %bitcast.94, bf16[8,2,128,128]{3,2,1,0:T(8,128)(2,1)} %get-tuple-element.348), kind=kOutput, calls=%fused_computation.5.clone.1 | convolution fusion | flops 271579136 | bytes 6832128 | tf_op jit(solution)/shard_map/while/body/eval_jaxpr/hcqd,hckd->hcqk/dot_general | solution.py:49
  97.3 3.6 %bitcast_reduce_fusion.2 = f32[8,2,128]{2,1,0:T(2,128)S(1)} fusion(f32[8,2,512,128]{3,2,1,0:T(8,128)} %get-tuple-element.311, f32[8,2,128]{2,1,0:T(2,128)S(1)} %fusion.45, pred[8,2,512]{2,1,0:T(4,128)(4,1)S(1)} %copy.82), kind=kLoop, calls=%fused_computation.3.clone.1 | loop fusion | flops 4192256 | bytes 4218880 | tf_op jit(solution)/shard_map/while/body/eval_jaxpr/reduce_sum | solution.py:33
  101.9 5.8 %fusion.47 = f32[8,2,128,128]{3,2,1,0:T(8,128)} fusion(bf16[8,2,512,128]{3,2,1,0:T(8,128)(2,1)S(1)} %bitcast.95, f32[8,2,512,128]{3,2,1,0:T(8,128)} %get-tuple-element.311, f32[8,2,128]{2,1,0:T(2,128)S(1)} %fusion.45, pred[8,2,512]{2,1,0:T(4,128)(4,1)S(1)} %copy.82, f32[8,2,128,128]{3,2,1,0:T(8,128)} %get-tuple-element.331, ...), kind=kOutput, calls=%fused_computation.11.clone.1 | convolution fusion | flops 273416192 | bytes 8413185 | tf_op jit(solution)/shard_map/while/body/eval_jaxpr/hcqk,hckd->hcqd/dot_general | solution.py:34
  111.7 4.6 %select_reduce_fusion.3 = (f32[8,2,128]{2,1,0:T(2,128)S(1)}, f32[8,2,512,128]{3,2,1,0:T(8,128)}) fusion(pred[8,2,512]{2,1,0:T(4,128)(4,1)S(1)} %copy.82, bf16[8,2,512,128]{3,2,1,0:T(8,128)(2,1)S(1)} %bitcast.94, bf16[8,2,128,128]{3,2,1,0:T(8,128)(2,1)} %get-tuple-element.348), kind=kOutput, calls=%fused_computation.5.clone.1 | convolution fusion | flops 271579136 | bytes 6832128 | tf_op jit(solution)/shard_map/while/body/eval_jaxpr/hcqd,hckd->hcqk/dot_general | solution.py:49
  116.3 3.6 %bitcast_reduce_fusion.2 = f32[8,2,128]{2,1,0:T(2,128)S(1)} fusion(f32[8,2,512,128]{3,2,1,0:T(8,128)} %get-tuple-element.311, f32[8,2,128]{2,1,0:T(2,128)S(1)} %fusion.45, pred[8,2,512]{2,1,0:T(4,128)(4,1)S(1)} %copy.82), kind=kLoop, calls=%fused_computation.3.clone.1 | loop fusion | flops 4192256 | bytes 4218880 | tf_op jit(solution)/shard_map/while/body/eval_jaxpr/reduce_sum | solution.py:33
  120.9 5.8 %fusion.47 = f32[8,2,128,128]{3,2,1,0:T(8,128)} fusion(bf16[8,2,512,128]{3,2,1,0:T(8,128)(2,1)S(1)} %bitcast.95, f32[8,2,512,128]{3,2,1,0:T(8,128)} %get-tuple-element.311, f32[8,2,128]{2,1,0:T(2,128)S(1)} %fusion.45, pred[8,2,512]{2,1,0:T(4,128)(4,1)S(1)} %copy.82, f32[8,2,128,128]{3,2,1,0:T(8,128)} %get-tuple-element.331, ...), kind=kOutput, calls=%fused_computation.11.clone.1 | convolution fusion | flops 273416192 | bytes 8413185 | tf_op jit(solution)/shard_map/while/body/eval_jaxpr/hcqk,hckd->hcqd/dot_general | solution.py:34
  130.7 4.6 %select_reduce_fusion.3 = (f32[8,2,128]{2,1,0:T(2,128)S(1)}, f32[8,2,512,128]{3,2,1,0:T(8,128)}) fusion(pred[8,2,512]{2,1,0:T(4,128)(4,1)S(1)} %copy.82, bf16[8,2,512,128]{3,2,1,0:T(8,128)(2,1)S(1)} %bitcast.94, bf16[8,2,128,128]{3,2,1,0:T(8,128)(2,1)} %get-tuple-element.348), kind=kOutput, calls=%fused_computation.5.clone.1 | convolution fusion | flops 271579136 | bytes 6832128 | tf_op jit(solution)/shard_map/while/body/eval_jaxpr/hcqd,hckd->hcqk/dot_general | solution.py:49
  135.3 3.6 %bitcast_reduce_fusion.2 = f32[8,2,128]{2,1,0:T(2,128)S(1)} fusion(f32[8,2,512,128]{3,2,1,0:T(8,128)} %get-tuple-element.311, f32[8,2,128]{2,1,0:T(2,128)S(1)} %fusion.45, pred[8,2,512]{2,1,0:T(4,128)(4,1)S(1)} %copy.82), kind=kLoop, calls=%fused_computation.3.clone.1 | loop fusion | flops 4192256 | bytes 4218880 | tf_op jit(solution)/shard_map/while/body/eval_jaxpr/reduce_sum | solution.py:33
  139.9 5.8 %fusion.47 = f32[8,2,128,128]{3,2,1,0:T(8,128)} fusion(bf16[8,2,512,128]{3,2,1,0:T(8,128)(2,1)S(1)} %bitcast.95, f32[8,2,512,128]{3,2,1,0:T(8,128)} %get-tuple-element.311, f32[8,2,128]{2,1,0:T(2,128)S(1)} %fusion.45, pred[8,2,512]{2,1,0:T(4,128)(4,1)S(1)} %copy.82, f32[8,2,128,128]{3,2,1,0:T(8,128)} %get-tuple-element.331, ...), kind=kOutput, calls=%fused_computation.11.clone.1 | convolution fusion | flops 273416192 | bytes 8413185 | tf_op jit(solution)/shard_map/while/body/eval_jaxpr/hcqk,hckd->hcqd/dot_general | solution.py:34
  145.8 1.6 copy.49
  147.3 1.4 fusion.15
  148.8 1.6 fusion.14
  150.7 7.2 %convolution_convert_fusion = bf16[256,4096]{1,0:T(8,128)(2,1)} fusion(bf16[1024,4096]{1,0:T(8,128)(2,1)} %param.19, bf16[32,8,8,128]{3,2,1,0:T(8,128)(2,1)S(1)} %bitcast.99), kind=kOutput, calls=%fused_computation.28 | convolution fusion | flops 2148532224 | bytes 11010048 | tf_op jit(solution)/shard_map/dot_general | solution.py:104
  158.0 51.0 %all-reduce.2.cloned.1.call-done = bf16[256,4096]{1,0:T(8,128)(2,1)} async-done(((bf16[256,4096]{1,0:T(8,128)(2,1)}), bf16[256,4096]{1,0:T(8,128)(2,1)}) %all-reduce.2.cloned.1.call-update) | async-done | bytes 2097168 | tf_op jit(solution)/shard_map/psum | solution.py:107
  209.0 2.4 %multiply_reduce_fusion = (f32[256]{0:T(256)S(1)}, f32[256,4096]{1,0:T(8,128)S(1)}) fusion(bf16[256,4096]{1,0:T(8,128)(2,1)} %all-reduce.2.cloned.1.call-done, bf16[2,128,4096]{2,1,0:T(8,128)(2,1)S(1)} %copy-done.1), kind=kLoop, calls=%fused_computation.30 | loop fusion | flops 5242624 | bytes 8389632 | tf_op jit(solution)/shard_map/reduce_sum | solution.py:109
  (91 shorter events, 24.6 us)
Async XLA Ops:
  7.2 1.0 copy-start
  7.2 33.6 %all-gather.3.cloned.1.call-start = ((), (), s32[]{:S(2)}) async-start(), calls=%async_computation | async-start | bytes 1310720 | tf_op jit(solution)/shard_map/all_gather | solution.py:82
  9.0 60.9 %all-gather.5.cloned.1.call-start = ((), (), s32[]{:S(2)}) async-start(), calls=%async_computation.1 | async-start | bytes 1310720 | tf_op jit(solution)/shard_map/all_gather | solution.py:83
  10.7 198.3 %all-reduce.2.cloned.1.call-start = ((), (), s32[]{:S(2)}) async-start(), calls=%async_computation.2 | async-start | bytes 4194304 | tf_op jit(solution)/shard_map/psum | solution.py:107
  69.8 78.9 %copy-start.3 = (bf16[2,128,256]{2,1,0:T(8,128)(2,1)S(1)}, bf16[2,128,256]{2,1,0:T(8,128)(2,1)}, u32[]{:S(2)}) copy-start(bf16[2,128,256]{2,1,0:T(8,128)(2,1)} %param.14) | copy-start | bytes 393220
  150.7 7.2 %copy-start.2 = (bf16[1024]{0:T(1024)(128)(2,1)S(1)}, bf16[1024]{0:T(1024)(128)(2,1)}, u32[]{:S(2)}) copy-start(bf16[1024]{0:T(1024)(128)(2,1)} %param.21) | copy-start | bytes 6148
  150.7 58.2 %copy-start.1 = (bf16[2,128,4096]{2,1,0:T(8,128)(2,1)S(1)}, bf16[2,128,4096]{2,1,0:T(8,128)(2,1)}, u32[]{:S(2)}) copy-start(bf16[2,128,4096]{2,1,0:T(8,128)(2,1)} %param.20) | copy-start | bytes 6291460
Sparse Core Ops, SparseCore 0:
  10.2 30.6 all-gather.2
  42.4 27.4 all-gather.4
  158.1 50.8 all-reduce.1
where the time goes:
time: 221 us; the launch traced here: 220 us
  waiting for transfers between devices  106 us (48%)
  matrix products  52.7 us (24%)
  local copies, waits for them, and re-layouts  27.5 us (12%)
  other arithmetic  19.6 us (9%)
  between operations  13.9 us (6%)
    psum x1, waiting for transfers between devices, shards(): summed = lax.psum(head_terms.astype(jnp.bfloat16), 'tp').astype(jnp.float32)  51 us
    all_gather x1, waiting for transfers between devices, shards(): value_piece = lax.all_gather(head_values, 'ctx', axis=0, tiled=True)  29 us
    all_gather x1, waiting for transfers between devices, shards(): key_piece = lax.all_gather(head_keys, 'ctx', axis=0, tiled=True)  25.6 us
    dot_general x5, matrix products, absorb(): jnp.einsum(pattern, weights.astype(jnp.bfloat16), values, preferred_eleme...  24.9 us
    dot_general x4, matrix products, shard_term(): jnp.einsum('hcqd,hckd->hcqk', query_block, key_tiles, preferred_element_t...  18.5 us
    reduce_sum x5, other arithmetic, absorb(): totals = totals * factor + jnp.sum(weights, axis=-1)  15.8 us
    dot_general x1, matrix products, shards(): jnp.dot(attended, out_weight, preferred_element_type=jnp.float32)  7.18 us
  transfers between devices with their start and end apart: 3, of which 3 were waited for; matrix products, arithmetic and copies ran while one was open for 3% of the time, Pallas kernels for 0%

commit v1 on v0

v1 whole, which is shorter than its diff:
```python
import functools
import math

import jax
import jax.numpy as jnp
from jax import lax
from jax.experimental import pallas as pl
from jax.experimental.pallas import tpu as pltpu
from jax.sharding import PartitionSpec as P

HEADS = 32
KVH = 2
HD = 128
BLK = 64
TILES = 8
CORES = 2

VERY_LOW = -1e30
TO_LOG2 = math.log2(math.e) / math.sqrt(HD)

VMEM_LIMIT = 40 * 1024 * 1024
NT = (((1,), (1,)), ((), ()))


def absorb(state, scores, values):
    top, total, acc = state
    new_top = jnp.maximum(top, jnp.max(scores, axis=1, keepdims=True))
    weights = jnp.exp2((scores - new_top) * TO_LOG2)
    factor = jnp.exp2((top - new_top) * TO_LOG2)
    total = total * factor + jnp.sum(weights, axis=1, keepdims=True)
    acc = acc * factor + jnp.dot(
        weights.astype(jnp.bfloat16), values, preferred_element_type=jnp.float32
    )
    return new_top, total, acc


def load_state(acc_ref, stat_ref, index):
    return stat_ref[index, :, 0:1], stat_ref[index, :, 64:65], acc_ref[index]


def store_state(acc_ref, stat_ref, index, state):
    top, total, acc = state
    lane = lax.broadcasted_iota(jnp.int32, stat_ref.shape[1:], 1)
    stat_ref[index] = jnp.where(lane < 64, top, total)
    acc_ref[index] = acc


def shard_scores(lists_ref, counts_ref, q_ref, kv_ref, source, sources, head, cont):
    conts = q_ref.shape[0]
    place = (head * conts + cont) * sources + source
    count = counts_ref[place]
    starts = [
        pl.multiple_of(lists_ref[place * TILES + t] * BLK, BLK) for t in range(TILES)
    ]
    query = q_ref[cont, :, pl.ds(pl.multiple_of(head * HD, HD), HD)]
    keys = jnp.concatenate([kv_ref[pl.ds(s, BLK), 0:HD] for s in starts], axis=0)
    values = jnp.concatenate([kv_ref[pl.ds(s, BLK), HD : 2 * HD] for s in starts], axis=0)
    scores = lax.dot_general(query, keys, NT, preferred_element_type=jnp.float32)
    column = lax.broadcasted_iota(jnp.int32, scores.shape, 1)
    return jnp.where(column < count * BLK, scores, VERY_LOW), values


def first_kernel(
    sources, lists_ref, counts_ref, q_ref, kv_ref, ck_ref, cv_ref, acc_ref, stat_ref
):
    conts, length, width = q_ref.shape
    heads = width // HD
    group = lax.axis_index("tp") * heads // (HEADS // KVH)
    lanes = pl.ds(pl.multiple_of(group * HD, HD), HD)
    own = lax.axis_index("ctx")

    def one_head(head, carry):
        made = []
        for cont in range(conts):
            query = q_ref[cont, :, pl.ds(pl.multiple_of(head * HD, HD), HD)]
            scores = lax.dot_general(
                query, ck_ref[cont, :, lanes], NT, preferred_element_type=jnp.float32
            )
            row = lax.broadcasted_iota(jnp.int32, scores.shape, 0)
            column = lax.broadcasted_iota(jnp.int32, scores.shape, 1)
            scores = jnp.where(column <= row, scores, VERY_LOW)
            more, values = shard_scores(
                lists_ref, counts_ref, q_ref, kv_ref, own, sources, head, cont
            )
            made.append((jnp.concatenate([scores, more], axis=1), values))
        states = []
        for cont in range(conts):
            scores, values = made[cont]
            values = jnp.concatenate([cv_ref[cont, :, lanes], values], axis=0)
            start = (
                jnp.full((length, 1), VERY_LOW, jnp.float32),
                jnp.zeros((length, 1), jnp.float32),
                jnp.zeros((length, HD), jnp.float32),
            )
            states.append(absorb(start, scores, values))
        for cont in range(conts):
            store_state(acc_ref, stat_ref, head * conts + cont, states[cont])
        return carry

    lax.fori_loop(0, heads, one_head, 0)


def step_sources(step, sources):
    spot = lax.axis_index("ctx")
    core = lax.axis_index("tp") % CORES
    mine = jnp.where(core == 0, spot - step, spot + step)
    theirs = jnp.where(core == 0, spot + step, spot - step)
    return mine, theirs


def absorb_arrivals(step, sources, lists_ref, counts_ref, q_ref, kv_refs, before, after):
    conts, _, width = q_ref.shape
    heads = width // HD
    for part, source in enumerate(step_sources(step, sources)):
        valid = (source >= 0) & (source < sources)
        held = before if part == 0 else after

        @pl.when(valid)
        def _():
            def one_head(head, carry):
                pairs = [head * conts + cont for cont in range(conts)]
                states = [load_state(*held, pair) for pair in pairs]
                made = [
                    shard_scores(
                        lists_ref, counts_ref, q_ref, kv_refs[part], source, sources, head, cont
                    )
                    for cont in range(conts)
                ]
                states = [absorb(state, *got) for state, got in zip(states, made)]
                for pair, state in zip(pairs, states):
                    store_state(*after, pair, state)
                return carry

            lax.fori_loop(0, heads, one_head, 0)

        if part == 0:

            @pl.when(jnp.logical_not(valid))
            def _():
                for source_ref, target_ref in zip(before, after):
                    target_ref[...] = source_ref[...]


def middle_kernel(
    step,
    sources,
    lists_ref,
    counts_ref,
    q_ref,
    mine_ref,
    theirs_ref,
    acc_in,
    stat_in,
    acc_ref,
    stat_ref,
):
    absorb_arrivals(
        step,
        sources,
        lists_ref,
        counts_ref,
        q_ref,
        (mine_ref, theirs_ref),
        (acc_in, stat_in),
        (acc_ref, stat_ref),
    )


def last_kernel(
    step,
    sources,
    lists_ref,
    counts_ref,
    q_ref,
    mine_ref,
    theirs_ref,
    acc_in,
    stat_in,
    weight_ref,
    attended_ref,
    give_ref,
    acc_ref,
    stat_ref,
    weight_buf,
    sems,
):
    conts, length, width = q_ref.shape
    heads = width // HD
    chips, rows, share = give_ref.shape
    place = lax.axis_index("tp")
    chip, core = place // CORES, place % CORES
    copies = []
    for k in range(chips):
        start = (lax.rem(chip + k, chips) * CORES + 1 - core) * share
        copies.append(
            pltpu.make_async_copy(
                weight_ref.at[:, pl.ds(pl.multiple_of(start, HD), share)],
                weight_buf.at[k],
                sems.at[k],
            )
        )
    for copy in copies:
        copy.start()
    absorb_arrivals(
        step,
        sources,
        lists_ref,
        counts_ref,
        q_ref,
        (mine_ref, theirs_ref),
        (acc_in, stat_in),
        (acc_ref, stat_ref),
    )

    def finish(head, carry):
        for cont in range(conts):
            _, total, acc = load_state(acc_ref, stat_ref, head * conts + cont)
            attended_ref[
                cont * length : (cont + 1) * length,
                pl.ds(pl.multiple_of(head * HD, HD), HD),
            ] = (acc / total).astype(jnp.bfloat16)
        return carry

    lax.fori_loop(0, heads, finish, 0)
    for k in range(chips):
        copies[k].wait()

        def columns(j, carry):
            lanes = pl.ds(pl.multiple_of(j * 256, 256), 256)
            give_ref[k, :, lanes] = jnp.dot(
                attended_ref[...], weight_buf[k, :, lanes], preferred_element_type=jnp.float32
            ).astype(jnp.bfloat16)
            return carry

        lax.fori_loop(0, share // 256, columns, 0)


def keep_kernel(_, attended_ref, weight_ref, keep_ref):
    keep_ref[0] = jnp.dot(
        attended_ref[...], weight_ref[...], preferred_element_type=jnp.float32
    )


def whole(space):
    return pl.BlockSpec(memory_space=space)


def shards(
    queries,
    cont_keys,
    cont_values,
    prompt_keys,
    prompt_values,
    block_lists,
    tile_counts,
    out_weight,
    residual,
    norm_gain,
    *,
    sources,
    members,
):
    conts, length, width = queries.shape
    heads = width // HD
    model_width = residual.shape[2]
    share = norm_gain.shape[0]
    rows = conts * length
    chips = members // CORES
    place = lax.axis_index("tp")
    chip, core = place // CORES, place % CORES
    group = place * heads // (HEADS // KVH)

    payload = jnp.concatenate(
        [
            lax.dynamic_slice_in_dim(prompt_keys, group * HD, HD, 1),
            lax.dynamic_slice_in_dim(prompt_values, group * HD, HD, 1),
        ],
        axis=1,
    )
    along = [
        (z * members + t, (z + (1 if t % CORES == 0 else -1)) * members + t)
        for z in range(sources)
        for t in range(members)
        if 0 <= z + (1 if t % CORES == 0 else -1) < sources
    ]
    sibling = [(t, t ^ 1) for t in range(members)]

    lists = block_lists.reshape(-1)
    counts = tile_counts.reshape(-1)
    pairs = heads * conts
    state_shape = (
        jax.ShapeDtypeStruct((pairs, length, HD), jnp.float32),
        jax.ShapeDtypeStruct((pairs, length, HD), jnp.float32),
    )
    params = pltpu.CompilerParams(vmem_limit_bytes=VMEM_LIMIT)

    def cost(keys):
        return pl.CostEstimate(
            flops=4 * pairs * length * keys * HD,
            bytes_accessed=4 * 2**20,
            transcendentals=pairs * length * keys,
        )

    smem, vmem = whole(pltpu.SMEM), whole(pltpu.VMEM)
    state = pl.pallas_call(
        functools.partial(first_kernel, sources),
        out_shape=state_shape,
        in_specs=[smem, smem] + [vmem] * 4,
        out_specs=(vmem, vmem),
        compiler_params=params,
        cost_estimate=cost(TILES * BLK + length),
        name="attend_own",
    )(lists, counts, queries, payload, cont_keys, cont_values)

    moving = payload
    for step in range(1, sources):
        moving = lax.ppermute(moving, ("ctx", "tp"), along)
        swapped = lax.ppermute(moving, "tp", sibling)
        if step < sources - 1:
            state = pl.pallas_call(
                functools.partial(middle_kernel, step, sources),
                out_shape=state_shape,
                in_specs=[smem, smem] + [vmem] * 5,
                out_specs=(vmem, vmem),
                input_output_aliases={5: 0, 6: 1},
                compiler_params=params,
                cost_estimate=cost(TILES * BLK),
                name="attend_step",
            )(lists, counts, queries, moving, swapped, *state)

    attended, give = pl.pallas_call(
        functools.partial(last_kernel, sources - 1, sources),
        out_shape=(
            jax.ShapeDtypeStruct((rows, width), jnp.bfloat16),
            jax.ShapeDtypeStruct((chips, rows, share), jnp.bfloat16),
        ),
        in_specs=[smem, smem] + [vmem] * 5 + [whole(pl.ANY)],
        out_specs=(vmem, vmem),
        scratch_shapes=[
            pltpu.VMEM((pairs, length, HD), jnp.float32),
            pltpu.VMEM((pairs, length, HD), jnp.float32),
            pltpu.VMEM((chips, width, share), jnp.bfloat16),
            pltpu.SemaphoreType.DMA((chips,)),
        ],
        compiler_params=params,
        cost_estimate=cost(TILES * BLK),
        name="attend_last",
    )(lists, counts, queries, moving, swapped, *state, out_weight)

    got = lax.ppermute(give, "tp", sibling)
    tile = 512
    tiles = share // tile
    order = ((chip + jnp.arange(chips)) % chips * CORES + core).astype(jnp.int32)
    keep = pl.pallas_call(
        keep_kernel,
        out_shape=jax.ShapeDtypeStruct((chips, rows, share), jnp.float32),
        grid_spec=pltpu.PrefetchScalarGridSpec(
            num_scalar_prefetch=1,
            grid=(chips * tiles,),
            in_specs=[
                pl.BlockSpec((rows, width), lambda i, order: (0, 0)),
                pl.BlockSpec(
                    (width, tile), lambda i, order: (0, order[i // tiles] * tiles + i % tiles)
                ),
            ],
            out_specs=pl.BlockSpec((1, rows, tile), lambda i, order: (i // tiles, 0, i % tiles)),
        ),
        compiler_params=params,
        cost_estimate=pl.CostEstimate(
            flops=2 * rows * width * share * chips,
            bytes_accessed=2 * width * share * chips,
            transcendentals=0,
        ),
        name="project_keep",
    )(order, attended, out_weight)

    total = jnp.zeros((rows, share), jnp.float32)
    for k in range(1, chips):
        onward = (keep[k] + got[k].astype(jnp.float32)).astype(jnp.bfloat16)
        to_chip = [
            (t, (t // CORES + k) % chips * CORES + t % CORES) for t in range(members)
        ]
        total = total + lax.ppermute(onward, "tp", to_chip).astype(jnp.float32)
    flat_residual = residual.reshape(rows, model_width)
    own_residual = lax.dynamic_slice_in_dim(flat_residual, place * share, share, 1)
    near = own_residual.astype(jnp.float32) + (keep[0] + got[0].astype(jnp.float32))
    stream_sum = near + total
    squares = jnp.sum(stream_sum * stream_sum, axis=-1)
    all_squares = squares
    for k in range(1, members):
        shift = [(t, (t + k) % members) for t in range(members)]
        all_squares = all_squares + lax.ppermute(squares, "tp", shift)
    scale = lax.rsqrt(all_squares / model_width + 1e-05)[:, None]
    normed = stream_sum * scale * norm_gain.astype(jnp.float32)
    shape = (conts, length, share)
    return (
        stream_sum.astype(jnp.bfloat16).reshape(shape),
        normed.astype(jnp.bfloat16).reshape(shape),
    )


def solution(mesh):
    placed = (
        P(("grp", "ctx"), None, "tp"),
        P(("grp", "ctx"), None, None),
        P(("grp", "ctx"), None, None),
        P(("grp", "ctx"), None),
        P(("grp", "ctx"), None),
        P("tp", ("grp", "ctx"), None, None),
        P("tp", ("grp", "ctx"), None),
        P("tp", None),
        P(("grp", "ctx"), None, None),
        P("tp"),
    )
    return jax.shard_map(
        functools.partial(
            shards, sources=mesh.shape["ctx"], members=mesh.shape["tp"]
        ),
        mesh=mesh,
        in_specs=placed,
        out_specs=(P(("grp", "ctx"), None, "tp"), P(("grp", "ctx"), None, "tp")),
        check_vma=False,
    )
```

time: 221 us -> 94.7 us (0.43)
  waiting for transfers between devices: 106 us -> 33.8 us
  matrix products: 52.7 us -> 0 us
  Pallas kernels: 0 us -> 31 us
  local copies, waits for them, and re-layouts: 27.5 us -> 6.65 us
  starting transfers between devices: 0.12 us -> 18 us
  other arithmetic: 19.6 us -> 3.96 us
  between operations: 13.9 us -> 0.93 us
    all_gather x2 -> x0, waiting for transfers between devices: 54.6 us -> none  [the longest x1 29 us: shards(): value_piece = lax.all_gather(head_values, 'ctx', axis=0, tiled=True)]
    dot_general x11 -> x0, matrix products: 52.7 us -> none  [the longest x5 24.9 us: absorb(): jnp.einsum(pattern, weights.astype(jnp.bfloat16), values, preferred_eleme...]
    psum x1 -> x0, waiting for transfers between devices: 51 us -> none  [shards(): summed = lax.psum(head_terms.astype(jnp.bfloat16), 'tp').astype(jnp.float32)]
    ppermute x0 -> x11, waiting for transfers between devices: none -> 33.8 us  [the longest x3 18.6 us: shards(): moving = lax.ppermute(moving, ('ctx', 'tp'), along)]
    pallas_call x0 -> x5, Pallas kernels: none -> 31 us  [the longest x2 12.4 us: shards(): pl.pallas_call(functools.partial(middle_kernel, step, sources), out_shape...]
    ppermute x0 -> x11, starting transfers between devices: none -> 18 us  [the longest x3 13.8 us: shards(): moving = lax.ppermute(moving, ('ctx', 'tp'), along)]
    reduce_sum x6 -> x1, other arithmetic: 18.1 us -> 1.55 us  [shards(): squares = jnp.sum(stream_sum * stream_sum, axis=-1)]
    dynamic_slice x14 -> x1, local copies, waits for them, and re-layouts: 12.6 us -> 1.14 us  [shards(): lax.dynamic_slice_in_dim(prompt_values, group * HD, HD, 1)]
  transfers between devices with their start and end apart: 3 -> 11, of which waited for: 3 -> 7; matrix products, arithmetic and copies ran while one was open for 3% -> 0% of each run, Pallas kernels for 0% -> 21%
where the time goes in v1:
time: 94.7 us; the launch traced here: 94.3 us
  waiting for transfers between devices  33.8 us (36%)
  Pallas kernels  31 us (33%)
  starting transfers between devices  18 us (19%)
  local copies, waits for them, and re-layouts  6.65 us (7%)
  other arithmetic  3.96 us (4%)
    ppermute x3, waiting for transfers between devices, shards(): moving = lax.ppermute(moving, ('ctx', 'tp'), along)  18.6 us
    ppermute x3, starting transfers between devices, shards(): moving = lax.ppermute(moving, ('ctx', 'tp'), along)  13.8 us
    ppermute x1, waiting for transfers between devices, shards(): total = total + lax.ppermute(onward, 'tp', to_chip).astype(jnp.float32)  12.8 us
    pallas_call x2, Pallas kernels, shards(): pl.pallas_call(functools.partial(middle_kernel, step, sources), out_shape...  12.4 us
    pallas_call x1, Pallas kernels, shards(): pl.pallas_call(functools.partial(last_kernel, sources - 1, sources), out_...  10.8 us
    unnamed x21, local copies, waits for them, and re-layouts  5.32 us
    pallas_call x1, Pallas kernels, shards(): pl.pallas_call(functools.partial(first_kernel, sources), out_shape=state_...  4.84 us
    pallas_call x1, Pallas kernels, shards(): pl.pallas_call(keep_kernel, out_shape=jax.ShapeDtypeStruct((chips, rows,...  2.91 us
  transfers between devices with their start and end apart: 11, of which 7 were waited for; matrix products, arithmetic and copies ran while one was open for 0% of the time, Pallas kernels for 21%

profile of v1, /device:TPU:0, one launch (start us, length us, event | category | flops | bytes accessed | tf_op | source)
XLA Modules:
  0.0 94.3 jit_solution(14553456271819215805)
XLA Ops:
  0.7 1.1 %constant_dynamic-slice_fusion = (bf16[1024,128]{1,0:T(8,128)(2,1)S(1)}, bf16[1024,128]{1,0:T(8,128)(2,1)S(1)}) fusion(bf16[1024,256]{1,0:T(8,128)(2,1)} %param.14, s32[]{:T(128)S(6)} %select_n.32, bf16[1024,256]{1,0:T(8,128)(2,1)} %param.13), kind=kLoop, calls=%fused_computation.14 | loop fusion | bytes 1048580 | tf_op jit(solution)/shard_map/dynamic_slice | solution.py:276
  1.9 5.0 %collective-permute-start = (bf16[1024,256]{1,0:T(8,128)(2,1)S(1)}, bf16[1024,256]{1,0:T(8,128)(2,1)S(1)}, u32[]{:S(2)}, u32[]{:S(2)}) collective-permute-start(bf16[1024,256]{1,0:T(8,128)(2,1)S(1)} %pad_maximum_fusion.kv_ref), channel_id=1, source_target_pairs={{0,4},{2,6},{4,8},{5,1},{6,10},{7,3},{8,12},{9,5},{10,14},{11,7},{... | collective-permute-start | bytes 1572872 | tf_op jit(solution)/shard_map/ppermute | solution.py:317
  6.9 0.8 copy-done.3
  7.7 5.9 %collective-permute-done.mine_ref = bf16[1024,256]{1,0:T(8,128)(2,1)S(1)} collective-permute-done((bf16[1024,256]{1,0:T(8,128)(2,1)S(1)}, bf16[1024,256]{1,0:T(8,128)(2,1)S(1)}, u32[]{:S(2)}, u32[]{:S(2)}) %collective-permute-start) | collective-permute-done | bytes 524320 | tf_op jit(solution)/shard_map/ppermute | solution.py:317
  13.5 4.4 %collective-permute-start.1 = (bf16[1024,256]{1,0:T(8,128)(2,1)S(1)}, bf16[1024,256]{1,0:T(8,128)(2,1)S(1)}, u32[]{:S(2)}, u32[]{:S(2)}) collective-permute-start(bf16[1024,256]{1,0:T(8,128)(2,1)S(1)} %collective-permute-done.mine_ref), channel_id=1, source_target_pairs={{0,4},{2,6},{4,8},{5,1},{6,10},{7,3},{8,12},{9,5},{10,14},{11,7},{... | collective-permute-start | bytes 1572872 | tf_op jit(solution)/shard_map/ppermute | solution.py:317
  17.9 6.6 %collective-permute-done.1.mine_ref = bf16[1024,256]{1,0:T(8,128)(2,1)S(1)} collective-permute-done((bf16[1024,256]{1,0:T(8,128)(2,1)S(1)}, bf16[1024,256]{1,0:T(8,128)(2,1)S(1)}, u32[]{:S(2)}, u32[]{:S(2)}) %collective-permute-start.1) | collective-permute-done | bytes 524320 | tf_op jit(solution)/shard_map/ppermute | solution.py:317
  24.6 4.4 %collective-permute-start.2 = (bf16[1024,256]{1,0:T(8,128)(2,1)S(1)}, bf16[1024,256]{1,0:T(8,128)(2,1)S(1)}, u32[]{:S(2)}, u32[]{:S(2)}) collective-permute-start(bf16[1024,256]{1,0:T(8,128)(2,1)S(1)} %collective-permute-done.1.mine_ref), channel_id=1, source_target_pairs={{0,4},{2,6},{4,8},{5,1},{6,10},{7,3},{8,12},{9,5},{10,14},{11,7},{... | collective-permute-start | bytes 1572872 | tf_op jit(solution)/shard_map/ppermute | solution.py:317
  29.6 6.1 %collective-permute-done.2.mine_ref = bf16[1024,256]{1,0:T(8,128)(2,1)S(1)} collective-permute-done((bf16[1024,256]{1,0:T(8,128)(2,1)S(1)}, bf16[1024,256]{1,0:T(8,128)(2,1)S(1)}, u32[]{:S(2)}, u32[]{:S(2)}) %collective-permute-start.2) | collective-permute-done | bytes 524320 | tf_op jit(solution)/shard_map/ppermute | solution.py:317
  36.0 1.0 %copy-done.4 = bf16[1024,256]{1,0:T(8,128)(2,1)S(1)} copy-done((bf16[1024,256]{1,0:T(8,128)(2,1)S(1)}, bf16[1024,256]{1,0:T(8,128)(2,1)}, u32[]{:S(2)}) %copy-start.4) | copy-done | bytes 524312
  37.0 4.8 %attend_own.1 = (f32[16,128,128]{2,1,0:T(8,128)S(1)}, f32[16,128,128]{2,1,0:T(8,128)S(1)}) custom-call(s32[512]{0:T(512)S(1)} %reshape.27.lists_ref, s32[64]{0:T(128)S(1)} %reshape.28.counts_ref, bf16[2,128,1024]{2,1,0:T(8,128)(2,1)S(1)} %copy-done.2, bf16[1024,256]{1,0:T(8,128)(2,1)S(1)} %copy-done.4, bf16[2,128,256]{2,1,0:T(8,128)(2,1)S(1)} %copy-done.5, ...), custom_call_target="tpu_custom_call" | custom-call | flops 671088640 | bytes 4194304 | tf_op jit(solution)/shard_map/attend_own/pallas_call | solution.py:305
  41.9 6.4 %attend_step.2 = (f32[16,128,128]{2,1,0:T(8,128)S(1)}, f32[16,128,128]{2,1,0:T(8,128)S(1)}) custom-call(s32[512]{0:T(512)S(1)} %reshape.27.lists_ref, s32[64]{0:T(128)S(1)} %reshape.28.counts_ref, bf16[2,128,1024]{2,1,0:T(8,128)(2,1)S(1)} %copy-done.2, ...), custom_call_target="tpu_custom_call", output_to_operand_aliasing={{0}: (5, {}), {1}: (6, {})} | custom-call | flops 536870912 | bytes 4194304 | tf_op jit(solution)/shard_map/attend_step/pallas_call | solution.py:320
  48.3 6.0 %attend_step.3 = (f32[16,128,128]{2,1,0:T(8,128)S(1)}, f32[16,128,128]{2,1,0:T(8,128)S(1)}) custom-call(s32[512]{0:T(512)S(1)} %reshape.27.lists_ref, s32[64]{0:T(128)S(1)} %reshape.28.counts_ref, bf16[2,128,1024]{2,1,0:T(8,128)(2,1)S(1)} %copy-done.2, ...), custom_call_target="tpu_custom_call", output_to_operand_aliasing={{0}: (5, {}), {1}: (6, {})} | custom-call | flops 536870912 | bytes 4194304 | tf_op jit(solution)/shard_map/attend_step/pallas_call | solution.py:320
  54.3 10.8 %attend_last.1 = (bf16[256,1024]{1,0:T(8,128)(2,1)S(1)}, bf16[2,256,1024]{2,1,0:T(8,128)(2,1)}) custom-call(s32[512]{0:T(512)S(1)} %reshape.27.lists_ref, s32[64]{0:T(128)S(1)} %reshape.28.counts_ref, bf16[2,128,1024]{2,1,0:T(8,128)(2,1)S(1)} %copy-done.2, bf16[1024,256]{1,0:T(8,128)(2,1)S(1)} %collective-permute-done.2.mine_ref, ...), custom_call_target="tpu_custom_call" | custom-call | flops 536870912 | bytes 4194304 | tf_op jit(solution)/shard_map/attend_last/pallas_call | solution.py:331
  65.3 3.4 %copy-done.1 = bf16[1024,4096]{1,0:T(8,128)(2,1)S(1)} copy-done((bf16[1024,4096]{1,0:T(8,128)(2,1)S(1)}, bf16[1024,4096]{1,0:T(8,128)(2,1)}, u32[]{:S(2)}) %copy-start.1) | copy-done | bytes 8388632
  68.7 2.9 %project_keep.1 = f32[2,256,1024]{2,1,0:T(8,128)S(1)} custom-call(s32[2]{0:T(128)S(1)} %fusion.6._, bf16[256,1024]{1,0:T(8,128)(2,1)S(1)} %get-tuple-element.16.attended_ref, bf16[1024,4096]{1,0:T(8,128)(2,1)S(1)} %copy-done.1), custom_call_target="tpu_custom_call" | custom-call | flops 1073741824 | bytes 4194304 | tf_op jit(solution)/shard_map/project_keep/pallas_call | solution.py:354
  71.6 1.2 %fusion.4 = bf16[256,1024]{1,0:T(8,128)(2,1)S(1)} fusion(f32[2,256,1024]{2,1,0:T(8,128)S(1)} %project_keep.1, bf16[2,256,1024]{2,1,0:T(8,128)(2,1)} %collective-permute-done.6), kind=kLoop, calls=%fused_computation.8 | loop fusion | flops 786432 | bytes 2097152 | tf_op jit(solution)/shard_map/convert_element_type | solution.py:379
  72.8 1.5 %collective-permute-start.7 = (bf16[256,1024]{1,0:T(8,128)(2,1)S(1)}, bf16[256,1024]{1,0:T(8,128)(2,1)S(1)}, u32[]{:S(2)}, u32[]{:S(2)}) collective-permute-start(bf16[256,1024]{1,0:T(8,128)(2,1)S(1)} %fusion.4), channel_id=1, source_target_pairs={{0,2},{1,3},{2,0},{3,1},{4,6},{5,7},{6,4},{7,5},{8,10},{9,11},{10,... | collective-permute-start | bytes 1572872 | tf_op jit(solution)/shard_map/ppermute | solution.py:383
  74.3 12.8 %collective-permute-done.7 = bf16[256,1024]{1,0:T(8,128)(2,1)S(1)} collective-permute-done((bf16[256,1024]{1,0:T(8,128)(2,1)S(1)}, bf16[256,1024]{1,0:T(8,128)(2,1)S(1)}, u32[]{:S(2)}, u32[]{:S(2)}) %collective-permute-start.7) | collective-permute-done | bytes 524320 | tf_op jit(solution)/shard_map/ppermute | solution.py:383
  87.2 1.5 %multiply_reduce_fusion = (f32[256]{0:T(256)S(1)}, f32[256,1024]{1,0:T(8,128)S(1)}) fusion(bf16[256,1024]{1,0:T(8,128)(2,1)S(1)} %collective-permute-done.7, bf16[2,256,1024]{2,1,0:T(8,128)(2,1)} %collective-permute-done.6, f32[2,256,1024]{2,1,0:T(8,128)S(1)} %project_keep.1, bf16[256,4096]{1,0:T(8,128)(2,1)} %bitcast.14, s32[]{:T(128)S(6)} %select_n.27), kind=kLoop, calls=%fused_computation.7 | loop fusion | flops 2096896 | bytes 3671044 | tf_op jit(solution)/shard_map/reduce_sum | solution.py:388
  88.7 0.8 collective-permute-start.10
  89.5 1.2 %collective-permute-start.9 = (f32[256]{0:T(256)S(1)}, f32[256]{0:T(256)S(1)}, u32[]{:S(2)}, u32[]{:S(2)}) collective-permute-start(f32[256]{0:T(256)S(1)} %get-tuple-element.18), channel_id=1, source_target_pairs={{0,2},{1,3},{2,0},{3,1},{4,6},{5,7},{6,4},{7,5},{8,10},{9,11},{10,... | collective-permute-start | bytes 3080 | tf_op jit(solution)/shard_map/ppermute | solution.py:392
  90.8 1.7 %collective-permute-done.8 = f32[256]{0:T(256)S(1)} collective-permute-done((f32[256]{0:T(256)S(1)}, f32[256]{0:T(256)S(1)}, u32[]{:S(2)}, u32[]{:S(2)}) %collective-permute-start.8) | collective-permute-done | bytes 1056 | tf_op jit(solution)/shard_map/ppermute | solution.py:392
  92.5 0.6 collective-permute-done.9
  93.2 1.1 %multiply_convert_fusion = (bf16[256,1024]{1,0:T(8,128)(2,1)}, bf16[256,1024]{1,0:T(8,128)(2,1)}) fusion(f32[256,1024]{1,0:T(8,128)S(1)} %get-tuple-element.19, f32[1024]{0:T(1024)S(1)} %convert_element_type.36, f32[256]{0:T(256)S(1)} %add_rsqrt_fusion), kind=kLoop, calls=%fused_computation.6 | loop fusion | flops 1048576 | bytes 2102272 | tf_op jit(solution)/shard_map/convert_element_type | solution.py:398
  (34 shorter events, 1.1 us)
Async XLA Ops:
  0.6 35.0 %copy-start.8 = (s32[8,2,4]{0,2,1:T(4,128)S(1)}, s32[8,2,4]{0,2,1:T(4,128)}, u32[]{:S(2)}) copy-start(s32[8,2,4]{0,2,1:T(4,128)} %param.16) | copy-start | bytes 772
  0.6 35.2 %copy-start.7 = (s32[8,2,4,8]{3,2,1,0:T(4,128)S(1)}, s32[8,2,4,8]{3,2,1,0:T(4,128)}, u32[]{:S(2)}) copy-start(s32[8,2,4,8]{3,2,1,0:T(4,128)} %param.15) | copy-start | bytes 6148
  0.7 35.3 %copy-start.2 = (bf16[2,128,1024]{2,1,0:T(8,128)(2,1)S(1)}, bf16[2,128,1024]{2,1,0:T(8,128)(2,1)}, u32[]{:S(2)}) copy-start(bf16[2,128,1024]{2,1,0:T(8,128)(2,1)} %q_ref.7) | copy-start | bytes 1572868
  0.7 35.3 %copy-start.5 = (bf16[2,128,256]{2,1,0:T(8,128)(2,1)S(1)}, bf16[2,128,256]{2,1,0:T(8,128)(2,1)}, u32[]{:S(2)}) copy-start(bf16[2,128,256]{2,1,0:T(8,128)(2,1)} %ck_ref.1) | copy-start | bytes 393220
  0.7 35.3 %copy-start.6 = (bf16[2,128,256]{2,1,0:T(8,128)(2,1)S(1)}, bf16[2,128,256]{2,1,0:T(8,128)(2,1)}, u32[]{:S(2)}) copy-start(bf16[2,128,256]{2,1,0:T(8,128)(2,1)} %cv_ref.1) | copy-start | bytes 393220
  1.9 11.6 %collective-permute-start = (bf16[1024,256]{1,0:T(8,128)(2,1)S(1)}, bf16[1024,256]{1,0:T(8,128)(2,1)S(1)}, u32[]{:S(2)}, u32[]{:S(2)}) collective-permute-start(bf16[1024,256]{1,0:T(8,128)(2,1)S(1)} %pad_maximum_fusion.kv_ref), channel_id=1, source_target_pairs={{0,4},{2,6},{4,8},{5,1},{6,10},{7,3},{8,12},{9,5},{10,14},{11,7},{... | collective-permute-start | bytes 1572872 | tf_op jit(solution)/shard_map/ppermute | solution.py:317
  6.9 0.8 copy-start.3
  13.5 11.1 %collective-permute-start.1 = (bf16[1024,256]{1,0:T(8,128)(2,1)S(1)}, bf16[1024,256]{1,0:T(8,128)(2,1)S(1)}, u32[]{:S(2)}, u32[]{:S(2)}) collective-permute-start(bf16[1024,256]{1,0:T(8,128)(2,1)S(1)} %collective-permute-done.mine_ref), channel_id=1, source_target_pairs={{0,4},{2,6},{4,8},{5,1},{6,10},{7,3},{8,12},{9,5},{10,14},{11,7},{... | collective-permute-start | bytes 1572872 | tf_op jit(solution)/shard_map/ppermute | solution.py:317
  24.6 11.1 %collective-permute-start.2 = (bf16[1024,256]{1,0:T(8,128)(2,1)S(1)}, bf16[1024,256]{1,0:T(8,128)(2,1)S(1)}, u32[]{:S(2)}, u32[]{:S(2)}) collective-permute-start(bf16[1024,256]{1,0:T(8,128)(2,1)S(1)} %collective-permute-done.1.mine_ref), channel_id=1, source_target_pairs={{0,4},{2,6},{4,8},{5,1},{6,10},{7,3},{8,12},{9,5},{10,14},{11,7},{... | collective-permute-start | bytes 1572872 | tf_op jit(solution)/shard_map/ppermute | solution.py:317
  29.0 12.9 %collective-permute-start.5 = (bf16[1024,256]{1,0:T(8,128)(2,1)S(1)}, bf16[1024,256]{1,0:T(8,128)(2,1)}, u32[]{:S(2)}, u32[]{:S(2)}) collective-permute-start(bf16[1024,256]{1,0:T(8,128)(2,1)S(1)} %collective-permute-done.mine_ref), channel_id=1, source_target_pairs={{0,1},{1,0},{2,3},{3,2},{4,5},{5,4},{6,7},{7,6},{8,9},{9,8},{10,11... | collective-permute-start | bytes 1572872 | tf_op jit(solution)/shard_map/ppermute | solution.py:318
  29.1 19.3 %collective-permute-start.4 = (bf16[1024,256]{1,0:T(8,128)(2,1)S(1)}, bf16[1024,256]{1,0:T(8,128)(2,1)S(1)}, u32[]{:S(2)}, u32[]{:S(2)}) collective-permute-start(bf16[1024,256]{1,0:T(8,128)(2,1)S(1)} %collective-permute-done.1.mine_ref), channel_id=1, source_target_pairs={{0,1},{1,0},{2,3},{3,2},{4,5},{5,4},{6,7},{7,6},{8,9},{9,8},{10,11... | collective-permute-start | bytes 1572872 | tf_op jit(solution)/shard_map/ppermute | solution.py:318
  35.7 18.7 %collective-permute-start.3 = (bf16[1024,256]{1,0:T(8,128)(2,1)S(1)}, bf16[1024,256]{1,0:T(8,128)(2,1)S(1)}, u32[]{:S(2)}, u32[]{:S(2)}) collective-permute-start(bf16[1024,256]{1,0:T(8,128)(2,1)S(1)} %collective-permute-done.2.mine_ref), channel_id=1, source_target_pairs={{0,1},{1,0},{2,3},{3,2},{4,5},{5,4},{6,7},{7,6},{8,9},{9,8},{10,11... | collective-permute-start | bytes 1572872 | tf_op jit(solution)/shard_map/ppermute | solution.py:318
  36.0 1.0 %copy-start.4 = (bf16[1024,256]{1,0:T(8,128)(2,1)S(1)}, bf16[1024,256]{1,0:T(8,128)(2,1)}, u32[]{:S(2)}) copy-start(bf16[1024,256]{1,0:T(8,128)(2,1)} %copy-done.3) | copy-start | bytes 1572868
  37.0 17.3 %copy-start = (bf16[1024,4096]{1,0:T(8,128)(2,1)S(1)}, bf16[1024,4096]{1,0:T(8,128)(2,1)}, u32[]{:S(2)}) copy-start(bf16[1024,4096]{1,0:T(8,128)(2,1)} %weight_ref.3) | copy-start | bytes 25165828
  65.2 6.4 %collective-permute-start.6 = (bf16[2,256,1024]{2,1,0:T(8,128)(2,1)}, bf16[2,256,1024]{2,1,0:T(8,128)(2,1)}, u32[]{:S(2)}, u32[]{:S(2)}) collective-permute-start(bf16[2,256,1024]{2,1,0:T(8,128)(2,1)} %get-tuple-element.17), channel_id=1, source_target_pairs={{0,1},{1,0},{2,3},{3,2},{4,5},{5,4},{6,7},{7,6},{8,9},{9,8},{10,11... | collective-permute-start | bytes 3145736 | tf_op jit(solution)/shard_map/ppermute | solution.py:350
  65.3 3.4 %copy-start.1 = (bf16[1024,4096]{1,0:T(8,128)(2,1)S(1)}, bf16[1024,4096]{1,0:T(8,128)(2,1)}, u32[]{:S(2)}) copy-start(bf16[1024,4096]{1,0:T(8,128)(2,1)} %weight_ref.3) | copy-start | bytes 25165828
  72.8 18.0 %copy-start.9 = (bf16[1024]{0:T(1024)(128)(2,1)S(1)}, bf16[1024]{0:T(1024)(128)(2,1)}, u32[]{:S(2)}) copy-start(bf16[1024]{0:T(1024)(128)(2,1)} %param.19) | copy-start | bytes 6148
  72.8 14.4 %collective-permute-start.7 = (bf16[256,1024]{1,0:T(8,128)(2,1)S(1)}, bf16[256,1024]{1,0:T(8,128)(2,1)S(1)}, u32[]{:S(2)}, u32[]{:S(2)}) collective-permute-start(bf16[256,1024]{1,0:T(8,128)(2,1)S(1)} %fusion.4), channel_id=1, source_target_pairs={{0,2},{1,3},{2,0},{3,1},{4,6},{5,7},{6,4},{7,5},{8,10},{9,11},{10,... | collective-permute-start | bytes 1572872 | tf_op jit(solution)/shard_map/ppermute | solution.py:383
  88.7 2.1 %collective-permute-start.10 = (f32[256]{0:T(256)S(1)}, f32[256]{0:T(256)S(1)}, u32[]{:S(2)}, u32[]{:S(2)}) collective-permute-start(f32[256]{0:T(256)S(1)} %get-tuple-element.18), channel_id=1, source_target_pairs={{0,3},{1,0},{2,1},{3,2},{4,7},{5,4},{6,5},{7,6},{8,11},{9,8},{10,9... | collective-permute-start | bytes 3080 | tf_op jit(solution)/shard_map/ppermute | solution.py:392
  89.5 3.0 %collective-permute-start.8 = (f32[256]{0:T(256)S(1)}, f32[256]{0:T(256)S(1)}, u32[]{:S(2)}, u32[]{:S(2)}) collective-permute-start(f32[256]{0:T(256)S(1)} %get-tuple-element.18), channel_id=1, source_target_pairs={{0,1},{1,2},{2,3},{3,0},{4,5},{5,6},{6,7},{7,4},{8,9},{9,10},{10,1... | collective-permute-start | bytes 3080 | tf_op jit(solution)/shard_map/ppermute | solution.py:392
  89.5 3.6 %collective-permute-start.9 = (f32[256]{0:T(256)S(1)}, f32[256]{0:T(256)S(1)}, u32[]{:S(2)}, u32[]{:S(2)}) collective-permute-start(f32[256]{0:T(256)S(1)} %get-tuple-element.18), channel_id=1, source_target_pairs={{0,2},{1,3},{2,0},{3,1},{4,6},{5,7},{6,4},{7,5},{8,10},{9,11},{10,... | collective-permute-start | bytes 3080 | tf_op jit(solution)/shard_map/ppermute | solution.py:392

commit v2 on v0

v2 whole, which is shorter than its diff:
```python
import functools
import math

import jax
import jax.numpy as jnp
from jax import lax
from jax.experimental import pallas as pl
from jax.experimental.pallas import tpu as pltpu
from jax.sharding import PartitionSpec as P

HEADS = 32
KVH = 2
HD = 128
BLK = 64
TILES = 8
CORES = 2
TOKENS = TILES * BLK

VERY_LOW = -1e30
TO_LOG2 = math.log2(math.e) / math.sqrt(HD)

VMEM_LIMIT = 24 * 1024 * 1024
NT = (((1,), (1,)), ((), ()))


def key_group(heads):
    return lax.axis_index("tp") * heads // (HEADS // KVH)


def group_lanes(heads):
    return pl.ds(pl.multiple_of(key_group(heads) * HD, HD), HD)


def pack_kernel(heads, keys_ref, values_ref, packed_ref, values_buf, sems):
    rows = keys_ref.shape[0]
    lanes = group_lanes(heads)
    keys_copy = pltpu.make_async_copy(
        keys_ref.at[:, lanes], packed_ref.at[pl.ds(0, rows)], sems.at[0]
    )
    values_copy = pltpu.make_async_copy(values_ref.at[:, lanes], values_buf, sems.at[1])
    values_copy.start()
    keys_copy.start()
    values_copy.wait()
    for p in range(rows // HD):
        packed_ref[rows + p * HD : rows + (p + 1) * HD, :] = values_buf[
            p * HD : (p + 1) * HD, :
        ].T
    keys_copy.wait()


def both_ways(kv_ref, flipped_ref):
    rows = kv_ref.shape[0] // 2
    for p in range(rows // HD):
        pair = kv_ref[rows + p * HD : rows + (p + 1) * HD, :]
        flipped_ref[p * HD : (p + 1) * HD, :] = pair
        flipped_ref[rows + p * HD : rows + (p + 1) * HD, :] = jnp.concatenate(
            [pair[:, BLK:], pair[:, :BLK]], axis=1
        )


def shard_scores(lists_ref, counts_ref, q_ref, kv_ref, flipped_ref, source, sources, head, cont):
    conts = q_ref.shape[0]
    pairs = kv_ref.shape[0] // 2 // HD
    place = (head * conts + cont) * sources + source
    count = counts_ref[place]
    blocks = [lists_ref[place * TILES + t] for t in range(TILES)]
    query = q_ref[cont, :, pl.ds(pl.multiple_of(head * HD, HD), HD)]
    keys = jnp.concatenate(
        [kv_ref[pl.ds(pl.multiple_of(b * BLK, BLK), BLK), :] for b in blocks], axis=0
    )
    scores = lax.dot_general(keys, query, NT, preferred_element_type=jnp.float32)
    lane = lax.broadcasted_iota(jnp.int32, (HD, HD), 1)
    halves = []
    for t, b in enumerate(blocks):
        spot = ((b + t) % 2 * pairs + b // 2) * HD
        halves.append(flipped_ref[pl.ds(pl.multiple_of(spot, HD), HD), :])
    values = jnp.concatenate(
        [jnp.where(lane < BLK, a, b) for a, b in zip(halves[::2], halves[1::2])], axis=1
    )
    tiles = [
        (scores[t * BLK : (t + 1) * BLK], t < count) for t in range(TILES)
    ]
    return tiles, values


def fold(op, tile):
    return functools.reduce(op, [tile[i : i + 8] for i in range(0, tile.shape[0], 8)])


def absorb(state, tiles, values):
    top, total, acc = state
    tops = [
        jnp.where(live, fold(jnp.maximum, tile), VERY_LOW) for tile, live in tiles
    ]
    best = jnp.max(functools.reduce(jnp.maximum, tops), axis=0, keepdims=True)
    new_top = jnp.maximum(top, best)
    weights = [
        jnp.exp2((tile - jnp.where(live, new_top, -VERY_LOW)) * TO_LOG2) for tile, live in tiles
    ]
    factor = jnp.exp2((top - new_top) * TO_LOG2)
    sums = functools.reduce(jnp.add, [fold(jnp.add, w) for w in weights])
    total = total * factor + jnp.sum(sums, axis=0, keepdims=True)
    rounded = jnp.concatenate([w.astype(jnp.bfloat16) for w in weights], axis=0)
    acc = acc * factor + jnp.dot(values, rounded, preferred_element_type=jnp.float32)
    return new_top, total, acc


def load_state(acc_ref, stat_ref, index):
    both = stat_ref[index]
    return both[0:1], both[1:2], acc_ref[index]


def store_state(acc_ref, stat_ref, index, state):
    top, total, acc = state
    stat_ref[index] = jnp.concatenate([top, total] + [total] * 6, axis=0)
    acc_ref[index] = acc


def first_kernel(
    sources,
    lists_ref,
    counts_ref,
    q_ref,
    kv_ref,
    ck_ref,
    cv_ref,
    weight_ref,
    acc_ref,
    stat_ref,
    give_ref,
    keep_ref,
    flipped_ref,
    own_ref,
    sems,
):
    conts, length, width = q_ref.shape
    heads = width // HD
    chips, _, share = give_ref.shape
    place = lax.axis_index("tp")
    chip, core = place // CORES, place % CORES
    copies = []
    for which, target in enumerate((give_ref, keep_ref)):
        held = core if which else 1 - core
        for k in range(chips):
            start = (lax.rem(chip + k, chips) * CORES + held) * share
            copies.append(
                pltpu.make_async_copy(
                    weight_ref.at[:, pl.ds(pl.multiple_of(start, HD), share)],
                    target.at[k],
                    sems.at[which, k],
                )
            )
    for copy in copies:
        copy.start()
    lanes = group_lanes(heads)
    own = lax.axis_index("ctx")
    both_ways(kv_ref, flipped_ref)
    for cont in range(conts):
        own_ref[cont] = cv_ref[cont, :, lanes].T

    def one_head(head, carry):
        made = []
        for cont in range(conts):
            query = q_ref[cont, :, pl.ds(pl.multiple_of(head * HD, HD), HD)]
            scores = lax.dot_general(
                ck_ref[cont, :, lanes], query, NT, preferred_element_type=jnp.float32
            )
            key = lax.broadcasted_iota(jnp.int32, scores.shape, 0)
            row = lax.broadcasted_iota(jnp.int32, scores.shape, 1)
            scores = jnp.where(key <= row, scores, VERY_LOW)
            tiles, values = shard_scores(
                lists_ref, counts_ref, q_ref, kv_ref, flipped_ref, own, sources, head, cont
            )
            made.append(
                ([(scores, True)] + tiles, jnp.concatenate([own_ref[cont], values], axis=1))
            )
        states = []
        for cont in range(conts):
            start = (
                jnp.full((1, length), VERY_LOW, jnp.float32),
                jnp.zeros((1, length), jnp.float32),
                jnp.zeros((HD, length), jnp.float32),
            )
            states.append(absorb(start, *made[cont]))
        for cont in range(conts):
            store_state(acc_ref, stat_ref, head * conts + cont, states[cont])
        return carry

    lax.fori_loop(0, heads, one_head, 0)
    for copy in copies:
        copy.wait()


def arrivals(step, sources):
    spot = lax.axis_index("ctx")
    core = lax.axis_index("tp") % CORES
    if sources == 4:
        if step == 1:
            mine = jnp.bitwise_xor(spot, 1 + core)
            return ((mine, True), (jnp.bitwise_xor(mine, 3), True))
        far = jnp.bitwise_xor(spot, 3)
        return ((far, core == 1), (far, core == 0))
    mine = jnp.where(core == 0, spot - step, spot + step)
    theirs = jnp.where(core == 0, spot + step, spot - step)
    return tuple((s, (s >= 0) & (s < sources)) for s in (mine, theirs))


def steps_of(sources):
    return 2 if sources == 4 else sources - 1


def absorb_arrivals(
    step, sources, chosen, lists_ref, counts_ref, q_ref, kv_refs, flipped_ref, before, after
):
    conts, _, width = q_ref.shape
    heads = width // HD
    together = 2 // len(chosen)
    one_of_two = sources == 4 and step == 2
    for part, (source, valid) in enumerate(arrivals(step, sources)):
        held = before if part == 0 or one_of_two else after

        def absorb_part():
            both_ways(kv_refs[part], flipped_ref)

            def some_heads(index, carry):
                work = [
                    (index * together + j, cont) for j in range(together) for cont in chosen
                ]
                pairs = [head * conts + cont for head, cont in work]
                states = [load_state(*held, pair) for pair in pairs]
                made = [
                    shard_scores(
                        lists_ref,
                        counts_ref,
                        q_ref,
                        kv_refs[part],
                        flipped_ref,
                        source,
                        sources,
                        head,
                        cont,
                    )
                    for head, cont in work
                ]
                states = [absorb(state, *got) for state, got in zip(states, made)]
                for pair, state in zip(pairs, states):
                    store_state(*after, pair, state)
                return carry

            lax.fori_loop(0, heads // together, some_heads, 0)

        if valid is True:
            absorb_part()
            continue
        pl.when(valid)(absorb_part)
        if part == 0 and not one_of_two:

            @pl.when(jnp.logical_not(valid))
            def _():
                for source_ref, target_ref in zip(before, after):
                    target_ref[...] = source_ref[...]


def middle_kernel(
    step,
    sources,
    lists_ref,
    counts_ref,
    q_ref,
    mine_ref,
    theirs_ref,
    acc_in,
    stat_in,
    acc_ref,
    stat_ref,
    flipped_ref,
):
    absorb_arrivals(
        step,
        sources,
        tuple(range(q_ref.shape[0])),
        lists_ref,
        counts_ref,
        q_ref,
        (mine_ref, theirs_ref),
        flipped_ref,
        (acc_in, stat_in),
        (acc_ref, stat_ref),
    )


def last_kernel(
    step,
    sources,
    cont,
    lists_ref,
    counts_ref,
    q_ref,
    mine_ref,
    theirs_ref,
    acc_in,
    stat_in,
    weight_ref,
    attended_ref,
    give_ref,
    acc_ref,
    stat_ref,
    flipped_ref,
):
    conts, length, width = q_ref.shape
    heads = width // HD
    absorb_arrivals(
        step,
        sources,
        (cont,),
        lists_ref,
        counts_ref,
        q_ref,
        (mine_ref, theirs_ref),
        flipped_ref,
        (acc_in, stat_in),
        (acc_ref, stat_ref),
    )
    for head in range(heads):
        _, total, acc = load_state(acc_ref, stat_ref, head * conts + cont)
        attended_ref[:, head * HD : (head + 1) * HD] = (acc / total).T.astype(jnp.bfloat16)
    project(attended_ref, weight_ref, give_ref)


def project(attended_ref, weight_ref, out_ref):
    chips, _, share = weight_ref.shape
    for k in range(chips):
        out_ref[k] = jnp.dot(
            attended_ref[...], weight_ref[k], preferred_element_type=jnp.float32
        ).astype(out_ref.dtype)


def onward_kernel(attended_ref, weight_ref, got_ref, *onward_refs):
    for k, onward_ref in enumerate(onward_refs, 1):
        onward_ref[...] = (
            jnp.dot(attended_ref[...], weight_ref[k], preferred_element_type=jnp.float32)
            + got_ref[k].astype(jnp.float32)
        ).astype(jnp.bfloat16)


def near_kernel(attended_ref, weight_ref, got_ref, residual_ref, near_ref):
    near_ref[...] = (
        residual_ref[...].astype(jnp.float32)
        + jnp.dot(attended_ref[...], weight_ref[0], preferred_element_type=jnp.float32)
        + got_ref[0].astype(jnp.float32)
    )


def shards(
    queries,
    cont_keys,
    cont_values,
    prompt_keys,
    prompt_values,
    block_lists,
    tile_counts,
    out_weight,
    residual,
    norm_gain,
    *,
    sources,
    members,
):
    conts, length, width = queries.shape
    heads = width // HD
    rows_dev = prompt_keys.shape[0]
    model_width = residual.shape[2]
    share = norm_gain.shape[0]
    chips = members // CORES
    place = lax.axis_index("tp")
    pairs = heads * conts
    params = pltpu.CompilerParams(vmem_limit_bytes=VMEM_LIMIT)
    smem = pl.BlockSpec(memory_space=pltpu.SMEM)
    vmem = pl.BlockSpec(memory_space=pltpu.VMEM)
    anywhere = pl.BlockSpec(memory_space=pltpu.HBM)

    def array(shape, dtype):
        return jax.ShapeDtypeStruct(shape, dtype)

    def cost(keys=0, flops=0, pairs=pairs):
        return pl.CostEstimate(flops=1024, bytes_accessed=1024, transcendentals=0)

    packed = pl.pallas_call(
        functools.partial(pack_kernel, heads),
        out_shape=array((2 * rows_dev, HD), jnp.bfloat16),
        in_specs=[anywhere] * 2,
        out_specs=vmem,
        scratch_shapes=[
            pltpu.VMEM((rows_dev, HD), jnp.bfloat16),
            pltpu.SemaphoreType.DMA((2,)),
        ],
        compiler_params=params,
        cost_estimate=cost(flops=2**20),
        name="pack",
    )(prompt_keys, prompt_values)

    def across(step):
        def target(z, t):
            if sources == 4 and step == 1:
                return z ^ (1 + t % CORES)
            if sources == 4:
                return z ^ 1 if t % CORES == 1 else None
            to = z + step if t % CORES == 0 else z - step
            return to if 0 <= to < sources else None

        return [
            (z * members + t, target(z, t) * members + t)
            for z in range(sources)
            for t in range(members)
            if target(z, t) is not None
        ]

    sibling = [(t, t ^ 1) for t in range(members)]
    steps = steps_of(sources)
    lists = block_lists.reshape(-1)
    counts = tile_counts.reshape(-1)
    state_shape = (
        array((pairs, HD, length), jnp.float32),
        array((pairs, 8, length), jnp.float32),
    )
    state_scratch = [pltpu.VMEM(s.shape, s.dtype) for s in state_shape]
    flipped = pltpu.VMEM((2 * rows_dev, HD), jnp.bfloat16)
    weight_shape = array((chips, width, share), jnp.bfloat16)

    *state, give_weight, keep_weight = pl.pallas_call(
        functools.partial(first_kernel, sources),
        out_shape=state_shape + (weight_shape, weight_shape),
        in_specs=[smem, smem] + [vmem] * 4 + [anywhere],
        out_specs=(vmem,) * 4,
        scratch_shapes=[
            flipped,
            pltpu.VMEM((conts, HD, length), jnp.bfloat16),
            pltpu.SemaphoreType.DMA((2, chips)),
        ],
        compiler_params=params,
        cost_estimate=cost(TOKENS + length),
        name="attend_own",
    )(lists, counts, queries, packed, cont_keys, cont_values, out_weight)

    mine = None
    for step in range(1, steps + 1):
        sent = mine if sources == 4 and step == 2 else packed
        mine = lax.ppermute(sent, ("ctx", "tp"), across(step))
        mine, state = lax.optimization_barrier((mine, tuple(state)))
        theirs = lax.ppermute(mine, "tp", sibling)
        if step < steps:
            state = pl.pallas_call(
                functools.partial(middle_kernel, step, sources),
                out_shape=state_shape,
                in_specs=[smem, smem] + [vmem] * 5,
                out_specs=(vmem, vmem),
                scratch_shapes=[flipped],
                compiler_params=params,
                cost_estimate=cost(TOKENS),
                name="attend_step",
            )(lists, counts, queries, mine, theirs, *state)

    attended, given, got = [], [], []
    for cont in range(conts):
        if cont > 0:
            state, given[-1] = lax.optimization_barrier((state, given[-1]))
        made, give = pl.pallas_call(
            functools.partial(last_kernel, steps, sources, cont),
            out_shape=(
                array((length, width), jnp.bfloat16),
                array((chips, length, share), jnp.bfloat16),
            ),
            in_specs=[smem, smem] + [vmem] * 6,
            out_specs=(vmem, vmem),
            scratch_shapes=state_scratch + [flipped],
            compiler_params=params,
            cost_estimate=cost(TOKENS, 2 * length * width * share * chips, heads),
            name="attend_last",
        )(lists, counts, queries, mine, theirs, *state, give_weight)
        attended.append(made)
        given.append(give)
    got = [lax.ppermute(give, "tp", sibling) for give in given]

    far = [[] for _ in range(conts)]
    for cont in range(conts):
        onward = pl.pallas_call(
            onward_kernel,
            out_shape=(array((length, share), jnp.bfloat16),) * (chips - 1),
            in_specs=[vmem] * 3,
            out_specs=(vmem,) * (chips - 1),
            compiler_params=params,
            cost_estimate=cost(flops=2 * length * width * share * (chips - 1)),
            name="project_onward",
        )(attended[cont], keep_weight, got[cont])
        for k in range(1, chips):
            to_chip = [
                (t, (t // CORES + k) % chips * CORES + t % CORES) for t in range(members)
            ]
            far[cont].append(lax.ppermute(onward[k - 1], "tp", to_chip))

    streams, norms = [], []
    gain = norm_gain.astype(jnp.float32)
    for cont in range(conts):
        own_residual = lax.dynamic_slice_in_dim(residual[cont], place * share, share, 1)
        near = pl.pallas_call(
            near_kernel,
            out_shape=array((length, share), jnp.float32),
            in_specs=[vmem] * 4,
            out_specs=vmem,
            compiler_params=params,
            cost_estimate=cost(flops=2 * length * width * share),
            name="project_near",
        )(attended[cont], keep_weight, got[cont], own_residual)
        stream_sum = near
        for part in far[cont]:
            stream_sum = stream_sum + part.astype(jnp.float32)
        squares = jnp.sum(stream_sum * stream_sum, axis=-1)
        all_squares = squares
        for k in range(1, members):
            shift = [(t, (t + k) % members) for t in range(members)]
            all_squares = all_squares + lax.ppermute(squares, "tp", shift)
        scale = lax.rsqrt(all_squares / model_width + 1e-05)[:, None]
        streams.append(stream_sum.astype(jnp.bfloat16))
        norms.append((stream_sum * scale * gain).astype(jnp.bfloat16))
    return jnp.stack(streams), jnp.stack(norms)


def solution(mesh):
    placed = (
        P(("grp", "ctx"), None, "tp"),
        P(("grp", "ctx"), None, None),
        P(("grp", "ctx"), None, None),
        P(("grp", "ctx"), None),
        P(("grp", "ctx"), None),
        P("tp", ("grp", "ctx"), None, None),
        P("tp", ("grp", "ctx"), None),
        P("tp", None),
        P(("grp", "ctx"), None, None),
        P("tp"),
    )
    return jax.shard_map(
        functools.partial(
            shards, sources=mesh.shape["ctx"], members=mesh.shape["tp"]
        ),
        mesh=mesh,
        in_specs=placed,
        out_specs=(P(("grp", "ctx"), None, "tp"), P(("grp", "ctx"), None, "tp")),
        check_vma=False,
    )
```

time: 221 us -> 67.9 us (0.31)
  waiting for transfers between devices: 106 us -> 8.58 us
  matrix products: 52.7 us -> 0 us
  Pallas kernels: 0 us -> 26.2 us
  other arithmetic: 19.6 us -> 3.47 us
  starting transfers between devices: 0.12 us -> 13.9 us
  local copies, waits for them, and re-layouts: 27.5 us -> 14.4 us
  between operations: 13.9 us -> 0.83 us
    all_gather x2 -> x0, waiting for transfers between devices: 54.6 us -> none  [the longest x1 29 us: shards(): value_piece = lax.all_gather(head_values, 'ctx', axis=0, tiled=True)]
    dot_general x11 -> x0, matrix products: 52.7 us -> none  [the longest x5 24.9 us: absorb(): jnp.einsum(pattern, weights.astype(jnp.bfloat16), values, preferred_eleme...]
    psum x1 -> x0, waiting for transfers between devices: 51 us -> none  [shards(): summed = lax.psum(head_terms.astype(jnp.bfloat16), 'tp').astype(jnp.float32)]
    pallas_call x0 -> x9, Pallas kernels: none -> 26.2 us  [the longest x1 9.7 us: shards(): pl.pallas_call(functools.partial(middle_kernel, step, sources), out_shape...]
    reduce_sum x6 -> x2, other arithmetic: 18.1 us -> 1.25 us  [shards(): squares = jnp.sum(stream_sum * stream_sum, axis=-1)]
    ppermute x0 -> x14, starting transfers between devices: none -> 13.9 us  [the longest x6 4.98 us: shards(): all_squares = all_squares + lax.ppermute(squares, 'tp', shift)]
    dynamic_slice x14 -> x2, local copies, waits for them, and re-layouts: 12.6 us -> 1 us  [shards(): lax.dynamic_slice_in_dim(residual[cont], place * share, share, 1)]
    ppermute x0 -> x14, waiting for transfers between devices: none -> 8.58 us  [the longest x6 2.53 us: shards(): all_squares = all_squares + lax.ppermute(squares, 'tp', shift)]
  transfers between devices with their start and end apart: 3 -> 14, of which waited for: 3 -> 8; matrix products, arithmetic and copies ran while one was open for 3% -> 8% of each run, Pallas kernels for 0% -> 27%
where the time goes in v2:
time: 67.9 us; the launch traced here: 67.3 us
  Pallas kernels  26.2 us (39%)
  local copies, waits for them, and re-layouts  14.4 us (21%)
  starting transfers between devices  13.9 us (20%)
  waiting for transfers between devices  8.58 us (13%)
  other arithmetic  3.47 us (5%)
  between operations  0.83 us (1%)
    unnamed x23, local copies, waits for them, and re-layouts  11.3 us
    pallas_call x1, Pallas kernels, shards(): pl.pallas_call(functools.partial(middle_kernel, step, sources), out_shape...  9.7 us
    pallas_call x2, Pallas kernels, shards(): pl.pallas_call(functools.partial(last_kernel, steps, sources, cont), out_...  7.49 us
    pallas_call x1, Pallas kernels, shards(): pl.pallas_call(functools.partial(first_kernel, sources), out_shape=state_...  6.91 us
    ppermute x6, starting transfers between devices, shards(): all_squares = all_squares + lax.ppermute(squares, 'tp', shift)  4.98 us
    ppermute x2, starting transfers between devices, shards(): mine = lax.ppermute(sent, ('ctx', 'tp'), across(step))  3.77 us
    ppermute x6, waiting for transfers between devices, shards(): all_squares = all_squares + lax.ppermute(squares, 'tp', shift)  2.53 us
    ppermute x2, starting transfers between devices, shards(): theirs = lax.ppermute(mine, 'tp', sibling)  2.4 us
  transfers between devices with their start and end apart: 14, of which 8 were waited for; matrix products, arithmetic and copies ran while one was open for 8% of the time, Pallas kernels for 27%

profile of v2, /device:TPU:0, one launch (start us, length us, event | category | flops | bytes accessed | tf_op | source)
XLA Modules:
  0.0 67.3 jit_solution(5900697536737261518)
XLA Ops:
  0.6 1.0 %copy-done.5 = bf16[1024,256]{1,0:T(8,128)(2,1)S(1)} copy-done((bf16[1024,256]{1,0:T(8,128)(2,1)S(1)}, bf16[1024,256]{1,0:T(8,128)(2,1)}, u32[]{:S(2)}) %copy-start.5) | copy-done | bytes 524312
  1.7 1.0 %copy-done.6 = bf16[1024,256]{1,0:T(8,128)(2,1)S(1)} copy-done((bf16[1024,256]{1,0:T(8,128)(2,1)S(1)}, bf16[1024,256]{1,0:T(8,128)(2,1)}, u32[]{:S(2)}) %copy-start.6) | copy-done | bytes 524312
  3.0 3.1 %collective-permute-start = (bf16[2048,128]{1,0:T(8,128)(2,1)S(1)}, bf16[2048,128]{1,0:T(8,128)(2,1)S(1)}, u32[]{:S(2)}, u32[]{:S(2)}) collective-permute-start(bf16[2048,128]{1,0:T(8,128)(2,1)S(1)} %pack.1.kv_ref), channel_id=1, source_target_pairs={{0,4},{1,9},{2,6},{3,11},{4,0},{5,13},{6,2},{7,15},{8,12},{9,1},{1... | collective-permute-start | bytes 1572872 | tf_op jit(solution)/shard_map/ppermute | solution.py:448
  7.8 1.0 %copy-done.2 = bf16[2,128,1024]{2,1,0:T(8,128)(2,1)S(1)} copy-done((bf16[2,128,1024]{2,1,0:T(8,128)(2,1)S(1)}, bf16[2,128,1024]{2,1,0:T(8,128)(2,1)}, u32[]{:S(2)}) %copy-start.2) | copy-done | bytes 524312
  8.8 3.4 %copy-done.4 = bf16[1024,4096]{1,0:T(8,128)(2,1)S(1)} copy-done((bf16[1024,4096]{1,0:T(8,128)(2,1)S(1)}, bf16[1024,4096]{1,0:T(8,128)(2,1)}, u32[]{:S(2)}) %copy-start.4) | copy-done | bytes 8388632
  14.0 6.9 %attend_own.1 = (f32[16,128,128]{2,1,0:T(8,128)S(1)}, f32[16,8,128]{2,1,0:T(8,128)S(1)}, bf16[2,1024,1024]{2,1,0:T(8,128)(2,1)S(1)}, bf16[2,1024,1024]{2,1,0:T(8,128)(2,1)S(1)}) custom-call(s32[512]{0:T(512)S(1)} %reshape.15.lists_ref, s32[64]{0:T(128)S(1)} %reshape.16.counts_ref, bf16[2,128,1024]{2,1,0:T(8,128)(2,1)S(1)} %copy-done.2, ...), custom_call_target="tpu_custom_call" | custom-call | flops 1024 | bytes 1024 | tf_op jit(solution)/shard_map/attend_own/pallas_call | solution.py:430
  23.1 9.7 %attend_step.1 = (f32[16,128,128]{2,1,0:T(8,128)S(1)}, f32[16,8,128]{2,1,0:T(8,128)S(1)}) custom-call(s32[512]{0:T(512)S(1)} %reshape.15.lists_ref, s32[64]{0:T(128)S(1)} %reshape.16.counts_ref, bf16[2,128,1024]{2,1,0:T(8,128)(2,1)S(1)} %copy-done.3, bf16[2048,128]{1,0:T(8,128)(2,1)S(1)} %collective-permute-done.mine_ref, ...), custom_call_target="tpu_custom_call" | custom-call | flops 1024 | bytes 1024 | tf_op jit(solution)/shard_map/attend_step/pallas_call | solution.py:452
  32.8 1.8 %collective-permute-start.3 = (bf16[2048,128]{1,0:T(8,128)(2,1)S(1)}, bf16[2048,128]{1,0:T(8,128)(2,1)S(1)}, u32[]{:S(2)}, u32[]{:S(2)}) collective-permute-start(bf16[2048,128]{1,0:T(8,128)(2,1)S(1)} %collective-permute-done.1.mine_ref), channel_id=1, source_target_pairs={{0,1},{1,0},{2,3},{3,2},{4,5},{5,4},{6,7},{7,6},{8,9},{9,8},{10,11... | collective-permute-start | bytes 1572872 | tf_op jit(solution)/shard_map/ppermute | solution.py:450
  34.6 1.5 %collective-permute-done.3.theirs_ref = bf16[2048,128]{1,0:T(8,128)(2,1)S(1)} collective-permute-done((bf16[2048,128]{1,0:T(8,128)(2,1)S(1)}, bf16[2048,128]{1,0:T(8,128)(2,1)S(1)}, u32[]{:S(2)}, u32[]{:S(2)}) %collective-permute-start.3) | collective-permute-done | bytes 524320 | tf_op jit(solution)/shard_map/ppermute | solution.py:450
  36.1 3.7 %attend_last.2 = (bf16[128,1024]{1,0:T(8,128)(2,1)S(1)}, bf16[2,128,1024]{2,1,0:T(8,128)(2,1)S(1)}) custom-call(s32[512]{0:T(512)S(1)} %reshape.15.lists_ref, s32[64]{0:T(128)S(1)} %reshape.16.counts_ref, bf16[2,128,1024]{2,1,0:T(8,128)(2,1)S(1)} %copy-done.3, bf16[2048,128]{1,0:T(8,128)(2,1)S(1)} %collective-permute-done.1.mine_ref, ...), custom_call_target="tpu_custom_call" | custom-call | flops 1024 | bytes 1024 | tf_op jit(solution)/shard_map/attend_last/pallas_call | solution.py:467
  39.9 3.8 %attend_last.3 = (bf16[128,1024]{1,0:T(8,128)(2,1)S(1)}, bf16[2,128,1024]{2,1,0:T(8,128)(2,1)S(1)}) custom-call(s32[512]{0:T(512)S(1)} %reshape.15.lists_ref, s32[64]{0:T(128)S(1)} %reshape.16.counts_ref, bf16[2,128,1024]{2,1,0:T(8,128)(2,1)S(1)} %copy-done.3, bf16[2048,128]{1,0:T(8,128)(2,1)S(1)} %collective-permute-done.1.mine_ref, ...), custom_call_target="tpu_custom_call" | custom-call | flops 1024 | bytes 1024 | tf_op jit(solution)/shard_map/attend_last/pallas_call | solution.py:467
  44.2 1.4 %collective-permute-done.6.got_ref = bf16[2,128,1024]{2,1,0:T(8,128)(2,1)S(1)} collective-permute-done((bf16[2,128,1024]{2,1,0:T(8,128)(2,1)S(1)}, bf16[2,128,1024]{2,1,0:T(8,128)(2,1)S(1)}, u32[]{:S(2)}, u32[]{:S(2)}) %collective-permute-start.6) | collective-permute-done | bytes 524320 | tf_op jit(solution)/shard_map/ppermute | solution.py:482
  46.1 1.6 %collective-permute-start.7 = (bf16[128,1024]{1,0:T(8,128)(2,1)S(1)}, bf16[128,1024]{1,0:T(8,128)(2,1)}, u32[]{:S(2)}, u32[]{:S(2)}) collective-permute-start(bf16[128,1024]{1,0:T(8,128)(2,1)S(1)} %project_onward.3), channel_id=1, source_target_pairs={{0,2},{1,3},{2,0},{3,1},{4,6},{5,7},{6,4},{7,5},{8,10},{9,11},{10,... | collective-permute-start | bytes 786440 | tf_op jit(solution)/shard_map/ppermute | solution.py:499
  47.7 1.2 %fusion.2 = (bf16[1,128,4096]{2,1,0:T(8,128)(2,1)S(1)}, bf16[1,128,4096]{2,1,0:T(8,128)(2,1)}) fusion(bf16[2,128,4096]{2,1,0:T(8,128)(2,1)S(1)} %copy-done.9), kind=kLoop, calls=%fused_computation.16 | loop fusion | bytes 4194304 | tf_op jit(solution)/shard_map/slice | solution.py:504
  48.9 1.0 %dynamic-slice_bitcast_fusion.residual_ref = bf16[128,1024]{1,0:T(8,128)(2,1)S(1)} fusion(bf16[1,128,4096]{2,1,0:T(8,128)(2,1)} %get-tuple-element.41, s32[]{:T(128)S(6)} %select_n.4), kind=kLoop, calls=%fused_computation.11 | loop fusion | bytes 524292 | tf_op jit(solution)/shard_map/dynamic_slice | solution.py:504
  49.9 2.2 %copy-done.1 = bf16[2,1024,1024]{2,1,0:T(8,128)(2,1)S(1)} copy-done((bf16[2,1024,1024]{2,1,0:T(8,128)(2,1)S(1)}, bf16[2,1024,1024]{2,1,0:T(8,128)(2,1)}, u32[]{:S(2)}) %copy-start.1) | copy-done | bytes 4194328
  54.8 1.1 %multiply_reduce_fusion = f32[128]{0:T(128)S(1)} fusion(f32[128,1024]{1,0:T(8,128)S(1)} %project_near.3, bf16[128,1024]{1,0:T(8,128)(2,1)} %collective-permute-done.7), kind=kLoop, calls=%fused_computation.3 | loop fusion | flops 524160 | bytes 786944 | tf_op jit(solution)/shard_map/reduce_sum | solution.py:517
  56.0 2.0 %collective-permute-start.12 = (f32[128]{0:T(128)S(1)}, f32[128]{0:T(128)S(1)}, u32[]{:S(2)}, u32[]{:S(2)}) collective-permute-start(f32[128]{0:T(128)S(1)} %multiply_reduce_fusion), channel_id=1, source_target_pairs={{0,2},{1,3},{2,0},{3,1},{4,6},{5,7},{6,4},{7,5},{8,10},{9,11},{10,... | collective-permute-start | bytes 1544 | tf_op jit(solution)/shard_map/ppermute | solution.py:521
  58.0 1.4 %collective-permute-start.13 = (f32[128]{0:T(128)S(1)}, f32[128]{0:T(128)S(1)}, u32[]{:S(2)}, u32[]{:S(2)}) collective-permute-start(f32[128]{0:T(128)S(1)} %multiply_reduce_fusion), channel_id=1, source_target_pairs={{0,3},{1,0},{2,1},{3,2},{4,7},{5,4},{6,5},{7,6},{8,11},{9,8},{10,9... | collective-permute-start | bytes 1544 | tf_op jit(solution)/shard_map/ppermute | solution.py:521
  59.4 1.5 %collective-permute-done.5 = bf16[128,1024]{1,0:T(8,128)(2,1)S(1)} collective-permute-done((bf16[128,1024]{1,0:T(8,128)(2,1)S(1)}, bf16[128,1024]{1,0:T(8,128)(2,1)S(1)}, u32[]{:S(2)}, u32[]{:S(2)}) %collective-permute-start.5) | collective-permute-done | bytes 262176 | tf_op jit(solution)/shard_map/ppermute | solution.py:499
  61.6 1.0 %collective-permute-start.9 = (f32[128]{0:T(128)S(1)}, f32[128]{0:T(128)S(1)}, u32[]{:S(2)}, u32[]{:S(2)}) collective-permute-start(f32[128]{0:T(128)S(1)} %multiply_reduce_fusion.1), channel_id=1, source_target_pairs={{0,2},{1,3},{2,0},{3,1},{4,6},{5,7},{6,4},{7,5},{8,10},{9,11},{10,... | collective-permute-start | bytes 1544 | tf_op jit(solution)/shard_map/ppermute | solution.py:521
  62.7 1.7 %collective-permute-done.8 = f32[128]{0:T(128)S(1)} collective-permute-done((f32[128]{0:T(128)S(1)}, f32[128]{0:T(128)S(1)}, u32[]{:S(2)}, u32[]{:S(2)}) %collective-permute-start.8) | collective-permute-done | bytes 544 | tf_op jit(solution)/shard_map/ppermute | solution.py:521
  65.1 1.1 %fusion = (bf16[1,128,1024]{2,1,0:T(8,128)(2,1)S(1)}, bf16[1,128,1024]{2,1,0:T(8,128)(2,1)S(1)}, bf16[1,128,1024]{2,1,0:T(8,128)(2,1)S(1)}, bf16[1,128,1024]{2,1,0:T(8,128)(2,1)S(1)}) fusion(f32[1024]{0:T(1024)S(1)} %convert_element_type.25, f32[128]{0:T(128)S(1)} %add_rsqrt_fusion.1, f32[128,1024]{1,0:T(8,128)S(1)} %project_near.2, ...), kind=kLoop, calls=%fused_computation.8 | loop fusion | flops 1572864 | bytes 2626560 | tf_op jit(solution)/shard_map/stack | solution.py:525
  66.3 1.1 %pad_maximum_fusion = (bf16[2,128,1024]{2,1,0:T(8,128)(2,1)}, bf16[2,128,1024]{2,1,0:T(8,128)(2,1)}) fusion(bf16[1,128,1024]{2,1,0:T(8,128)(2,1)S(1)} %get-tuple-element.46, bf16[1,128,1024]{2,1,0:T(8,128)(2,1)S(1)} %get-tuple-element.43, bf16[1,128,1024]{2,1,0:T(8,128)(2,1)S(1)} %get-tuple-element.47, bf16[1,128,1024]{2,1,0:T(8,128)(2,1)S(1)} %get-tuple-element.42), kind=kLoop, calls=%fused_computation | loop fusion | flops 524288 | bytes 2097152 | tf_op jit(solution)/shard_map/stack | solution.py:525
  (48 shorter events, 11.4 us)
Async XLA Ops:
  0.6 1.0 %copy-start.5 = (bf16[1024,256]{1,0:T(8,128)(2,1)S(1)}, bf16[1024,256]{1,0:T(8,128)(2,1)}, u32[]{:S(2)}) copy-start(bf16[1024,256]{1,0:T(8,128)(2,1)} %keys_ref.1) | copy-start | bytes 1572868
  1.7 1.0 %copy-start.6 = (bf16[1024,256]{1,0:T(8,128)(2,1)S(1)}, bf16[1024,256]{1,0:T(8,128)(2,1)}, u32[]{:S(2)}) copy-start(bf16[1024,256]{1,0:T(8,128)(2,1)} %values_ref.1) | copy-start | bytes 1572868
  3.0 18.0 %collective-permute-start = (bf16[2048,128]{1,0:T(8,128)(2,1)S(1)}, bf16[2048,128]{1,0:T(8,128)(2,1)S(1)}, u32[]{:S(2)}, u32[]{:S(2)}) collective-permute-start(bf16[2048,128]{1,0:T(8,128)(2,1)S(1)} %pack.1.kv_ref), channel_id=1, source_target_pairs={{0,4},{1,9},{2,6},{3,11},{4,0},{5,13},{6,2},{7,15},{8,12},{9,1},{1... | collective-permute-start | bytes 1572872 | tf_op jit(solution)/shard_map/ppermute | solution.py:448
  7.8 1.0 %copy-start.2 = (bf16[2,128,1024]{2,1,0:T(8,128)(2,1)S(1)}, bf16[2,128,1024]{2,1,0:T(8,128)(2,1)}, u32[]{:S(2)}) copy-start(bf16[2,128,1024]{2,1,0:T(8,128)(2,1)} %q_ref.7) | copy-start | bytes 1572868
  8.8 3.4 %copy-start.4 = (bf16[1024,4096]{1,0:T(8,128)(2,1)S(1)}, bf16[1024,4096]{1,0:T(8,128)(2,1)}, u32[]{:S(2)}) copy-start(bf16[1024,4096]{1,0:T(8,128)(2,1)} %weight_ref.1) | copy-start | bytes 25165828
  12.2 0.9 %copy-start.7 = (bf16[2,128,256]{2,1,0:T(8,128)(2,1)S(1)}, bf16[2,128,256]{2,1,0:T(8,128)(2,1)}, u32[]{:S(2)}) copy-start(bf16[2,128,256]{2,1,0:T(8,128)(2,1)} %ck_ref.1) | copy-start | bytes 393220
  14.0 9.1 %copy-start.3 = (bf16[2,128,1024]{2,1,0:T(8,128)(2,1)S(1)}, bf16[2,128,1024]{2,1,0:T(8,128)(2,1)}, u32[]{:S(2)}) copy-start(bf16[2,128,1024]{2,1,0:T(8,128)(2,1)} %q_ref.7) | copy-start | bytes 1572868
  20.9 24.7 %copy-start = (bf16[2,1024,1024]{2,1,0:T(8,128)(2,1)}, bf16[2,1024,1024]{2,1,0:T(8,128)(2,1)S(1)}, u32[]{:S(2)}) copy-start(bf16[2,1024,1024]{2,1,0:T(8,128)(2,1)S(1)} %get-tuple-element.33.weight_ref) | copy-start | bytes 12582916
  20.9 2.2 %collective-permute-start.2 = (bf16[2048,128]{1,0:T(8,128)(2,1)S(1)}, bf16[2048,128]{1,0:T(8,128)(2,1)S(1)}, u32[]{:S(2)}, u32[]{:S(2)}) collective-permute-start(bf16[2048,128]{1,0:T(8,128)(2,1)S(1)} %collective-permute-done.mine_ref), channel_id=1, source_target_pairs={{0,1},{1,0},{2,3},{3,2},{4,5},{5,4},{6,7},{7,6},{8,9},{9,8},{10,11... | collective-permute-start | bytes 1572872 | tf_op jit(solution)/shard_map/ppermute | solution.py:450
  21.6 11.2 %collective-permute-start.1 = (bf16[2048,128]{1,0:T(8,128)(2,1)S(1)}, bf16[2048,128]{1,0:T(8,128)(2,1)S(1)}, u32[]{:S(2)}, u32[]{:S(2)}) collective-permute-start(bf16[2048,128]{1,0:T(8,128)(2,1)S(1)} %collective-permute-done.mine_ref), channel_id=1, source_target_pairs={{1,5},{3,7},{5,1},{7,3},{9,13},{11,15},{13,9},{15,11},{17,21},{19,... | collective-permute-start | bytes 1572872 | tf_op jit(solution)/shard_map/ppermute | solution.py:448
  32.8 3.3 %collective-permute-start.3 = (bf16[2048,128]{1,0:T(8,128)(2,1)S(1)}, bf16[2048,128]{1,0:T(8,128)(2,1)S(1)}, u32[]{:S(2)}, u32[]{:S(2)}) collective-permute-start(bf16[2048,128]{1,0:T(8,128)(2,1)S(1)} %collective-permute-done.1.mine_ref), channel_id=1, source_target_pairs={{0,1},{1,0},{2,3},{3,2},{4,5},{5,4},{6,7},{7,6},{8,9},{9,8},{10,11... | collective-permute-start | bytes 1572872 | tf_op jit(solution)/shard_map/ppermute | solution.py:450
  43.6 4.0 %copy-start.9 = (bf16[2,128,4096]{2,1,0:T(8,128)(2,1)S(1)}, bf16[2,128,4096]{2,1,0:T(8,128)(2,1)}, u32[]{:S(2)}) copy-start(bf16[2,128,4096]{2,1,0:T(8,128)(2,1)} %param.18) | copy-start | bytes 6291460
  43.7 2.0 %collective-permute-start.6 = (bf16[2,128,1024]{2,1,0:T(8,128)(2,1)S(1)}, bf16[2,128,1024]{2,1,0:T(8,128)(2,1)S(1)}, u32[]{:S(2)}, u32[]{:S(2)}) collective-permute-start(bf16[2,128,1024]{2,1,0:T(8,128)(2,1)S(1)} %get-tuple-element.39), channel_id=1, source_target_pairs={{0,1},{1,0},{2,3},{3,2},{4,5},{5,4},{6,7},{7,6},{8,9},{9,8},{10,11... | collective-permute-start | bytes 1572872 | tf_op jit(solution)/shard_map/ppermute | solution.py:482
  44.1 5.8 %collective-permute-start.4 = (bf16[2,128,1024]{2,1,0:T(8,128)(2,1)S(1)}, bf16[2,128,1024]{2,1,0:T(8,128)(2,1)S(1)}, u32[]{:S(2)}, u32[]{:S(2)}) collective-permute-start(bf16[2,128,1024]{2,1,0:T(8,128)(2,1)S(1)} %get-tuple-element.35), channel_id=1, source_target_pairs={{0,1},{1,0},{2,3},{3,2},{4,5},{5,4},{6,7},{7,6},{8,9},{9,8},{10,11... | collective-permute-start | bytes 1572872 | tf_op jit(solution)/shard_map/ppermute | solution.py:482
  46.1 8.7 %collective-permute-start.7 = (bf16[128,1024]{1,0:T(8,128)(2,1)S(1)}, bf16[128,1024]{1,0:T(8,128)(2,1)}, u32[]{:S(2)}, u32[]{:S(2)}) collective-permute-start(bf16[128,1024]{1,0:T(8,128)(2,1)S(1)} %project_onward.3), channel_id=1, source_target_pairs={{0,2},{1,3},{2,0},{3,1},{4,6},{5,7},{6,4},{7,5},{8,10},{9,11},{10,... | collective-permute-start | bytes 786440 | tf_op jit(solution)/shard_map/ppermute | solution.py:499
  48.9 4.2 %copy-start.10 = (bf16[1024]{0:T(1024)(128)(2,1)S(1)}, bf16[1024]{0:T(1024)(128)(2,1)}, u32[]{:S(2)}) copy-start(bf16[1024]{0:T(1024)(128)(2,1)} %param.19) | copy-start | bytes 6148
  49.9 2.2 %copy-start.1 = (bf16[2,1024,1024]{2,1,0:T(8,128)(2,1)S(1)}, bf16[2,1024,1024]{2,1,0:T(8,128)(2,1)}, u32[]{:S(2)}) copy-start(bf16[2,1024,1024]{2,1,0:T(8,128)(2,1)} %copy-done) | copy-start | bytes 12582916
  52.5 8.4 %collective-permute-start.5 = (bf16[128,1024]{1,0:T(8,128)(2,1)S(1)}, bf16[128,1024]{1,0:T(8,128)(2,1)S(1)}, u32[]{:S(2)}, u32[]{:S(2)}) collective-permute-start(bf16[128,1024]{1,0:T(8,128)(2,1)S(1)} %project_onward.2), channel_id=1, source_target_pairs={{0,2},{1,3},{2,0},{3,1},{4,6},{5,7},{6,4},{7,5},{8,10},{9,11},{10,... | collective-permute-start | bytes 786440 | tf_op jit(solution)/shard_map/ppermute | solution.py:499
  55.9 5.6 %collective-permute-start.11 = (f32[128]{0:T(128)S(1)}, f32[128]{0:T(128)S(1)}, u32[]{:S(2)}, u32[]{:S(2)}) collective-permute-start(f32[128]{0:T(128)S(1)} %multiply_reduce_fusion), channel_id=1, source_target_pairs={{0,1},{1,2},{2,3},{3,0},{4,5},{5,6},{6,7},{7,4},{8,9},{9,10},{10,1... | collective-permute-start | bytes 1544 | tf_op jit(solution)/shard_map/ppermute | solution.py:521
  56.0 6.6 %collective-permute-start.12 = (f32[128]{0:T(128)S(1)}, f32[128]{0:T(128)S(1)}, u32[]{:S(2)}, u32[]{:S(2)}) collective-permute-start(f32[128]{0:T(128)S(1)} %multiply_reduce_fusion), channel_id=1, source_target_pairs={{0,2},{1,3},{2,0},{3,1},{4,6},{5,7},{6,4},{7,5},{8,10},{9,11},{10,... | collective-permute-start | bytes 1544 | tf_op jit(solution)/shard_map/ppermute | solution.py:521
  58.0 4.6 %collective-permute-start.13 = (f32[128]{0:T(128)S(1)}, f32[128]{0:T(128)S(1)}, u32[]{:S(2)}, u32[]{:S(2)}) collective-permute-start(f32[128]{0:T(128)S(1)} %multiply_reduce_fusion), channel_id=1, source_target_pairs={{0,3},{1,0},{2,1},{3,2},{4,7},{5,4},{6,5},{7,6},{8,11},{9,8},{10,9... | collective-permute-start | bytes 1544 | tf_op jit(solution)/shard_map/ppermute | solution.py:521
  61.0 1.6 %collective-permute-start.10 = (f32[128]{0:T(128)S(1)}, f32[128]{0:T(128)S(1)}, u32[]{:S(2)}, u32[]{:S(2)}) collective-permute-start(f32[128]{0:T(128)S(1)} %multiply_reduce_fusion.1), channel_id=1, source_target_pairs={{0,3},{1,0},{2,1},{3,2},{4,7},{5,4},{6,5},{7,6},{8,11},{9,8},{10,9... | collective-permute-start | bytes 1544 | tf_op jit(solution)/shard_map/ppermute | solution.py:521
  61.4 3.0 %collective-permute-start.8 = (f32[128]{0:T(128)S(1)}, f32[128]{0:T(128)S(1)}, u32[]{:S(2)}, u32[]{:S(2)}) collective-permute-start(f32[128]{0:T(128)S(1)} %multiply_reduce_fusion.1), channel_id=1, source_target_pairs={{0,1},{1,2},{2,3},{3,0},{4,5},{5,6},{6,7},{7,4},{8,9},{9,10},{10,1... | collective-permute-start | bytes 1544 | tf_op jit(solution)/shard_map/ppermute | solution.py:521
  61.6 3.5 %collective-permute-start.9 = (f32[128]{0:T(128)S(1)}, f32[128]{0:T(128)S(1)}, u32[]{:S(2)}, u32[]{:S(2)}) collective-permute-start(f32[128]{0:T(128)S(1)} %multiply_reduce_fusion.1), channel_id=1, source_target_pairs={{0,2},{1,3},{2,0},{3,1},{4,6},{5,7},{6,4},{7,5},{8,10},{9,11},{10,... | collective-permute-start | bytes 1544 | tf_op jit(solution)/shard_map/ppermute | solution.py:521
  (1 other events, 0.9 us)

commit v3 on v2

--- a/solution.py
+++ b/solution.py
@@ -116,54 +116,71 @@
     acc_ref[index] = acc
 
 
+def start_all(copies):
+    for copy in copies:
+        copy.start()
+    return copies
+
+
+def weight_copies(weight_ref, target, sems, sibling):
+    chips, _, share = target.shape
+    place = lax.axis_index("tp")
+    chip, core = place // CORES, place % CORES
+    held = 1 - core if sibling else core
+    copies = []
+    for k in range(chips):
+        start = (lax.rem(chip + k, chips) * CORES + held) * share
+        copies.append(
+            pltpu.make_async_copy(
+                weight_ref.at[:, pl.ds(pl.multiple_of(start, HD), share)],
+                target.at[k],
+                sems.at[k],
+            )
+        )
+    return copies
+
+
 def first_kernel(
     sources,
     lists_ref,
     counts_ref,
+    kv_ref,
+    queries_ref,
+    cont_keys_ref,
+    cont_values_ref,
+    acc_ref,
+    stat_ref,
     q_ref,
-    kv_ref,
+    flipped_ref,
     ck_ref,
     cv_ref,
-    weight_ref,
-    acc_ref,
-    stat_ref,
-    give_ref,
-    keep_ref,
-    flipped_ref,
     own_ref,
     sems,
 ):
     conts, length, width = q_ref.shape
     heads = width // HD
-    chips, _, share = give_ref.shape
-    place = lax.axis_index("tp")
-    chip, core = place // CORES, place % CORES
-    copies = []
-    for which, target in enumerate((give_ref, keep_ref)):
-        held = core if which else 1 - core
-        for k in range(chips):
-            start = (lax.rem(chip + k, chips) * CORES + held) * share
-            copies.append(
-                pltpu.make_async_copy(
-                    weight_ref.at[:, pl.ds(pl.multiple_of(start, HD), share)],
-                    target.at[k],
-                    sems.at[which, k],
-                )
-            )
-    for copy in copies:
-        copy.start()
     lanes = group_lanes(heads)
+    copies = start_all(
+        [
+            pltpu.make_async_copy(cont_values_ref.at[:, :, lanes], cv_ref, sems.at[0]),
+            pltpu.make_async_copy(cont_keys_ref.at[:, :, lanes], ck_ref, sems.at[1]),
+            pltpu.make_async_copy(queries_ref, q_ref, sems.at[2]),
+        ]
+    )
     own = lax.axis_index("ctx")
     both_ways(kv_ref, flipped_ref)
+    copies[0].wait()
     for cont in range(conts):
-        own_ref[cont] = cv_ref[cont, :, lanes].T
+        own_ref[cont] = cv_ref[cont].T
+    copies[1].wait()
+    copies[2].wait()
 
     def one_head(head, carry):
         made = []
         for cont in range(conts):
             query = q_ref[cont, :, pl.ds(pl.multiple_of(head * HD, HD), HD)]
             scores = lax.dot_general(
-                ck_ref[cont, :, lanes], query, NT, preferred_element_type=jnp.float32
+                ck_ref[cont], query, NT, preferred_element_type=jnp.float32
             )
             key = lax.broadcasted_iota(jnp.int32, scores.shape, 0)
             row = lax.broadcasted_iota(jnp.int32, scores.shape, 1)
@@ -187,8 +204,6 @@
         return carry
 
     lax.fori_loop(0, heads, one_head, 0)
-    for copy in copies:
-        copy.wait()
 
 
 def arrivals(step, sources):
@@ -264,6 +279,8 @@
 def middle_kernel(
     step,
     sources,
+    chosen,
+    with_weight,
     lists_ref,
     counts_ref,
     q_ref,
@@ -271,14 +288,17 @@
     theirs_ref,
     acc_in,
     stat_in,
-    acc_ref,
-    stat_ref,
-    flipped_ref,
+    *refs,
 ):
+    if with_weight:
+        weight_ref, acc_ref, stat_ref, give_ref, flipped_ref, sems = refs
+        copies = start_all(weight_copies(weight_ref, give_ref, sems, True))
+    else:
+        acc_ref, stat_ref, flipped_ref = refs
     absorb_arrivals(
         step,
         sources,
-        tuple(range(q_ref.shape[0])),
+        chosen,
         lists_ref,
         counts_ref,
         q_ref,
@@ -287,6 +307,19 @@
         (acc_in, stat_in),
         (acc_ref, stat_ref),
     )
+    if with_weight:
+        for copy in copies:
+            copy.wait()
+
+
+def finish_and_give(cont, conts, acc_ref, stat_ref, weight_ref, attended_ref, give_ref):
+    for head in range(attended_ref.shape[1] // HD):
+        _, total, acc = load_state(acc_ref, stat_ref, head * conts + cont)
+        attended_ref[:, head * HD : (head + 1) * HD] = (acc / total).T.astype(jnp.bfloat16)
+    for k in range(weight_ref.shape[0]):
+        give_ref[k] = jnp.dot(
+            attended_ref[...], weight_ref[k], preferred_element_type=jnp.float32
+        ).astype(give_ref.dtype)
 
 
 def last_kernel(
@@ -300,15 +333,17 @@
     theirs_ref,
     acc_in,
     stat_in,
+    give_weight_ref,
     weight_ref,
     attended_ref,
     give_ref,
+    keep_weight_ref,
     acc_ref,
     stat_ref,
     flipped_ref,
+    sems,
 ):
-    conts, length, width = q_ref.shape
-    heads = width // HD
+    copies = start_all(weight_copies(weight_ref, keep_weight_ref, sems, False))
     absorb_arrivals(
         step,
         sources,
@@ -321,18 +356,15 @@
         (acc_in, stat_in),
         (acc_ref, stat_ref),
     )
-    for head in range(heads):
-        _, total, acc = load_state(acc_ref, stat_ref, head * conts + cont)
-        attended_ref[:, head * HD : (head + 1) * HD] = (acc / total).T.astype(jnp.bfloat16)
-    project(attended_ref, weight_ref, give_ref)
-
-
-def project(attended_ref, weight_ref, out_ref):
-    chips, _, share = weight_ref.shape
-    for k in range(chips):
-        out_ref[k] = jnp.dot(
-            attended_ref[...], weight_ref[k], preferred_element_type=jnp.float32
-        ).astype(out_ref.dtype)
+    finish_and_give(
+        cont, q_ref.shape[0], acc_ref, stat_ref, give_weight_ref, attended_ref, give_ref
+    )
+    for copy in copies:
+        copy.wait()
+
+
+def finish_kernel(cont, conts, acc_ref, stat_ref, weight_ref, attended_ref, give_ref):
+    finish_and_give(cont, conts, acc_ref, stat_ref, weight_ref, attended_ref, give_ref)
 
 
 def onward_kernel(attended_ref, weight_ref, got_ref, *onward_refs):
@@ -343,12 +375,41 @@
         ).astype(jnp.bfloat16)
 
 
-def near_kernel(attended_ref, weight_ref, got_ref, residual_ref, near_ref):
-    near_ref[...] = (
-        residual_ref[...].astype(jnp.float32)
-        + jnp.dot(attended_ref[...], weight_ref[0], preferred_element_type=jnp.float32)
-        + got_ref[0].astype(jnp.float32)
-    )
+def near_kernel(cont, attended_ref, weight_ref, got_ref, residual_ref, near_ref, own_ref, sem):
+    share = near_ref.shape[1]
+    start = pl.multiple_of(lax.axis_index("tp") * share, HD)
+    copy = pltpu.make_async_copy(
+        residual_ref.at[cont, :, pl.ds(start, share)], own_ref, sem.at[0]
+    )
+    copy.start()
+    near_ref[...] = jnp.dot(
+        attended_ref[...], weight_ref[0], preferred_element_type=jnp.float32
+    ) + got_ref[0].astype(jnp.float32)
+    copy.wait()
+    near_ref[...] += own_ref[...].astype(jnp.float32)
+
+
+def sum_kernel(count, *refs):
+    near_ref, fars, (total_ref, squares_ref) = refs[0], refs[1 : 1 + count], refs[1 + count :]
+    total = near_ref[...]
+    for far_ref in fars:
+        total = total + far_ref[...].astype(jnp.float32)
+    total_ref[...] = total
+    sums = jnp.sum(total * total, axis=1, keepdims=True)
+    squares_ref[...] = jnp.broadcast_to(sums, (sums.shape[0], HD)).T[:8]
+
+
+def norm_kernel(conts, members, model_width, *refs):
+    totals, squares = refs[:conts], refs[conts : conts + members]
+    gain_ref, stream_ref, normed_ref = refs[conts + members :]
+    gain = gain_ref[...].astype(jnp.float32)
+    for cont in range(conts):
+        row = functools.reduce(jnp.add, [ref[cont * 8 : cont * 8 + 1, :] for ref in squares])
+        scale = lax.rsqrt(row / model_width + 1e-05)
+        scale = jnp.broadcast_to(scale, (HD, scale.shape[1])).T[:, 0:1]
+        total = totals[cont][...]
+        stream_ref[cont] = total.astype(jnp.bfloat16)
+        normed_ref[cont] = (total * scale * gain).astype(jnp.bfloat16)
 
 
 def shards(
@@ -377,27 +438,30 @@
     params = pltpu.CompilerParams(vmem_limit_bytes=VMEM_LIMIT)
     smem = pl.BlockSpec(memory_space=pltpu.SMEM)
     vmem = pl.BlockSpec(memory_space=pltpu.VMEM)
-    anywhere = pl.BlockSpec(memory_space=pltpu.HBM)
+    hbm = pl.BlockSpec(memory_space=pltpu.HBM)
 
     def array(shape, dtype):
         return jax.ShapeDtypeStruct(shape, dtype)
 
-    def cost(keys=0, flops=0, pairs=pairs):
-        return pl.CostEstimate(flops=1024, bytes_accessed=1024, transcendentals=0)
+    def cost(flops=1024):
+        return pl.CostEstimate(flops=flops, bytes_accessed=1024, transcendentals=0)
+
+    def in_hbm(x):
+        return pltpu.with_memory_space_constraint(x, pltpu.HBM)
 
     packed = pl.pallas_call(
         functools.partial(pack_kernel, heads),
         out_shape=array((2 * rows_dev, HD), jnp.bfloat16),
-        in_specs=[anywhere] * 2,
+        in_specs=[hbm] * 2,
         out_specs=vmem,
         scratch_shapes=[
             pltpu.VMEM((rows_dev, HD), jnp.bfloat16),
             pltpu.SemaphoreType.DMA((2,)),
         ],
         compiler_params=params,
-        cost_estimate=cost(flops=2**20),
+        cost_estimate=cost(),
         name="pack",
-    )(prompt_keys, prompt_values)
+    )(in_hbm(prompt_keys), in_hbm(prompt_values))
 
     def across(step):
         def target(z, t):
@@ -427,20 +491,34 @@
     flipped = pltpu.VMEM((2 * rows_dev, HD), jnp.bfloat16)
     weight_shape = array((chips, width, share), jnp.bfloat16)
 
-    *state, give_weight, keep_weight = pl.pallas_call(
+    *state, q = pl.pallas_call(
         functools.partial(first_kernel, sources),
-        out_shape=state_shape + (weight_shape, weight_shape),
-        in_specs=[smem, smem] + [vmem] * 4 + [anywhere],
-        out_specs=(vmem,) * 4,
+        out_shape=state_shape + (array(queries.shape, jnp.bfloat16),),
+        in_specs=[smem, smem, vmem] + [hbm] * 3,
+        out_specs=(vmem,) * 3,
         scratch_shapes=[
             flipped,
+            pltpu.VMEM((conts, length, HD), jnp.bfloat16),
+            pltpu.VMEM((conts, length, HD), jnp.bfloat16),
             pltpu.VMEM((conts, HD, length), jnp.bfloat16),
-            pltpu.SemaphoreType.DMA((2, chips)),
+            pltpu.SemaphoreType.DMA((3,)),
         ],
         compiler_params=params,
-        cost_estimate=cost(TOKENS + length),
+        cost_estimate=cost(),
         name="attend_own",
-    )(lists, counts, queries, packed, cont_keys, cont_values, out_weight)
+    )(lists, counts, packed, in_hbm(queries), in_hbm(cont_keys), in_hbm(cont_values))
+
+    def attend_step(step, chosen, with_weight, state):
+        return pl.pallas_call(
+            functools.partial(middle_kernel, step, sources, chosen, with_weight),
+            out_shape=state_shape + ((weight_shape,) if with_weight else ()),
+            in_specs=[smem, smem] + [vmem] * 5 + [hbm] * with_weight,
+            out_specs=(vmem,) * (2 + with_weight),
+            scratch_shapes=[flipped] + [pltpu.SemaphoreType.DMA((chips,))] * with_weight,
+            compiler_params=params,
+            cost_estimate=cost(),
+            name="attend_step",
+        )(lists, counts, q, mine, theirs, *state, *([in_hbm(out_weight)] * with_weight))
 
     mine = None
     for step in range(1, steps + 1):
@@ -449,80 +527,109 @@
         mine, state = lax.optimization_barrier((mine, tuple(state)))
         theirs = lax.ppermute(mine, "tp", sibling)
         if step < steps:
-            state = pl.pallas_call(
-                functools.partial(middle_kernel, step, sources),
-                out_shape=state_shape,
-                in_specs=[smem, smem] + [vmem] * 5,
-                out_specs=(vmem, vmem),
-                scratch_shapes=[flipped],
-                compiler_params=params,
-                cost_estimate=cost(TOKENS),
-                name="attend_step",
-            )(lists, counts, queries, mine, theirs, *state)
-
-    attended, given, got = [], [], []
-    for cont in range(conts):
-        if cont > 0:
-            state, given[-1] = lax.optimization_barrier((state, given[-1]))
-        made, give = pl.pallas_call(
-            functools.partial(last_kernel, steps, sources, cont),
-            out_shape=(
-                array((length, width), jnp.bfloat16),
-                array((chips, length, share), jnp.bfloat16),
-            ),
-            in_specs=[smem, smem] + [vmem] * 6,
-            out_specs=(vmem, vmem),
-            scratch_shapes=state_scratch + [flipped],
-            compiler_params=params,
-            cost_estimate=cost(TOKENS, 2 * length * width * share * chips, heads),
-            name="attend_last",
-        )(lists, counts, queries, mine, theirs, *state, give_weight)
-        attended.append(made)
-        given.append(give)
-    got = [lax.ppermute(give, "tp", sibling) for give in given]
-
-    far = [[] for _ in range(conts)]
-    for cont in range(conts):
-        onward = pl.pallas_call(
+            *state, give_weight = attend_step(step, tuple(range(conts)), True, state)
+
+    attended, give, keep_weight = pl.pallas_call(
+        functools.partial(last_kernel, steps, sources, 0),
+        out_shape=(
+            array((length, width), jnp.bfloat16),
+            array((chips, length, share), jnp.bfloat16),
+            weight_shape,
+        ),
+        in_specs=[smem, smem] + [vmem] * 6 + [hbm],
+        out_specs=(vmem,) * 3,
+        scratch_shapes=[pltpu.VMEM(a.shape, a.dtype) for a in state_shape]
+        + [flipped, pltpu.SemaphoreType.DMA((chips,))],
+        compiler_params=params,
+        cost_estimate=cost(),
+        name="attend_last",
+    )(lists, counts, q, mine, theirs, *state, give_weight, in_hbm(out_weight))
+
+    def onward(attended, got):
+        parts = pl.pallas_call(
             onward_kernel,
             out_shape=(array((length, share), jnp.bfloat16),) * (chips - 1),
             in_specs=[vmem] * 3,
             out_specs=(vmem,) * (chips - 1),
             compiler_params=params,
-            cost_estimate=cost(flops=2 * length * width * share * (chips - 1)),
+            cost_estimate=cost(),
             name="project_onward",
-        )(attended[cont], keep_weight, got[cont])
+        )(attended, keep_weight, got)
+        far = []
         for k in range(1, chips):
             to_chip = [
                 (t, (t // CORES + k) % chips * CORES + t % CORES) for t in range(members)
             ]
-            far[cont].append(lax.ppermute(onward[k - 1], "tp", to_chip))
-
-    streams, norms = [], []
-    gain = norm_gain.astype(jnp.float32)
+            far.append(lax.ppermute(parts[k - 1], "tp", to_chip))
+        return parts, far
+
+    def near(cont, attended, got):
+        return pl.pallas_call(
+            functools.partial(near_kernel, cont),
+            out_shape=array((length, share), jnp.float32),
+            in_specs=[vmem] * 3 + [hbm],
+            out_specs=vmem,
+            scratch_shapes=[
+                pltpu.VMEM((length, share), jnp.bfloat16),
+                pltpu.SemaphoreType.DMA((1,)),
+            ],
+            compiler_params=params,
+            cost_estimate=cost(),
+            name="project_near",
+        )(attended, keep_weight, got, in_hbm(residual))
+
+    got = lax.ppermute(give, "tp", sibling)
+    rest = state
+    nears, fars = [], []
     for cont in range(conts):
-        own_residual = lax.dynamic_slice_in_dim(residual[cont], place * share, share, 1)
-        near = pl.pallas_call(
-            near_kernel,
-            out_shape=array((length, share), jnp.float32),
-            in_specs=[vmem] * 4,
-            out_specs=vmem,
+        if cont > 0:
+            rest = attend_step(steps, (cont,), False, state)
+            rest, got, parts = lax.optimization_barrier((rest, got, parts))
+            attended, give = pl.pallas_call(
+                functools.partial(finish_kernel, cont, conts),
+                out_shape=(
+                    array((length, width), jnp.bfloat16),
+                    array((chips, length, share), jnp.bfloat16),
+                ),
+                in_specs=[vmem] * 3,
+                out_specs=(vmem,) * 2,
+                compiler_params=params,
+                cost_estimate=cost(),
+                name="finish",
+            )(*rest, give_weight)
+            got = lax.ppermute(give, "tp", sibling)
+        parts, far = onward(attended, got)
+        fars.append(far)
+        nears.append(near(cont, attended, got))
+
+    totals, squares = [], []
+    for cont in range(conts):
+        total, square = pl.pallas_call(
+            functools.partial(sum_kernel, chips - 1),
+            out_shape=(array((length, share), jnp.float32), array((8, length), jnp.float32)),
+            in_specs=[vmem] * chips,
+            out_specs=(vmem,) * 2,
             compiler_params=params,
-            cost_estimate=cost(flops=2 * length * width * share),
-            name="project_near",
-        )(attended[cont], keep_weight, got[cont], own_residual)
-        stream_sum = near
-        for part in far[cont]:
-            stream_sum = stream_sum + part.astype(jnp.float32)
-        squares = jnp.sum(stream_sum * stream_sum, axis=-1)
-        all_squares = squares
-        for k in range(1, members):
-            shift = [(t, (t + k) % members) for t in range(members)]
-            all_squares = all_squares + lax.ppermute(squares, "tp", shift)
-        scale = lax.rsqrt(all_squares / model_width + 1e-05)[:, None]
-        streams.append(stream_sum.astype(jnp.bfloat16))
-        norms.append((stream_sum * scale * gain).astype(jnp.bfloat16))
-    return jnp.stack(streams), jnp.stack(norms)
+            cost_estimate=cost(),
+            name="add_up",
+        )(nears[cont], *fars[cont])
+        totals.append(total)
+        squares.append(square)
+    squares = jnp.concatenate(squares, axis=0)
+    all_squares = [squares] + [
+        lax.ppermute(squares, "tp", [(t, (t + k) % members) for t in range(members)])
+        for k in range(1, members)
+    ]
+    out = array((conts, length, share), jnp.bfloat16)
+    return pl.pallas_call(
+        functools.partial(norm_kernel, conts, members, model_width),
+        out_shape=(out, out),
+        in_specs=[vmem] * (conts + members + 1),
+        out_specs=(vmem, vmem),
+        compiler_params=params,
+        cost_estimate=cost(),
+        name="norm",
+    )(*totals, *all_squares, norm_gain.reshape(1, share))
 
 
 def solution(mesh):

time: 67.9 us -> 62 us (0.913)
  local copies, waits for them, and re-layouts: 14.4 us -> 1.74 us
  waiting for transfers between devices: 8.58 us -> 16.9 us
  Pallas kernels: 26.2 us -> 29.8 us
  other arithmetic: 3.47 us -> 0 us
  starting transfers between devices: 13.9 us -> 12.4 us
    unnamed x23 -> x4, local copies, waits for them, and re-layouts: 11.3 us -> 0.78 us
    ppermute x2, waiting for transfers between devices: 0.01 us -> 4.37 us  [shards(): mine = lax.ppermute(sent, ('ctx', 'tp'), across(step))]
    ppermute x10 -> x7, waiting for transfers between devices: 6.19 us -> 10.2 us  [the longest x2 7.55 us: onward(): far.append(lax.ppermute(parts[k - 1], 'tp', to_chip))]
    pallas_call x7 -> x11, Pallas kernels: 19 us -> 22.4 us  [the longest x2 12.7 us: attend_step(): pl.pallas_call(functools.partial(middle_kernel, step, sources, chosen, wi...]
    another operation x2 -> x0, other arithmetic: 2.2 us -> none  [shards(): return (jnp.stack(streams), jnp.stack(norms))]
    ppermute x10 -> x7, starting transfers between devices: 7.72 us -> 5.71 us  [the longest x2 3.06 us: onward(): far.append(lax.ppermute(parts[k - 1], 'tp', to_chip))]
    reduce_sum x2 -> x0, other arithmetic: 1.25 us -> none  [shards(): squares = jnp.sum(stream_sum * stream_sum, axis=-1)]
    slice x1 -> x0, local copies, waits for them, and re-layouts: 1.19 us -> none  [shards(): residual[cont]]
  transfers between devices with their start and end apart: 14 -> 11, of which waited for: 8 -> 8; matrix products, arithmetic and copies ran while one was open for 8% -> 3% of each run, Pallas kernels for 27% -> 36%
where the time goes in v3:
time: 62 us; the launch traced here: 61.7 us
  Pallas kernels  29.8 us (48%)
  waiting for transfers between devices  16.9 us (27%)
  starting transfers between devices  12.4 us (20%)
  local copies, waits for them, and re-layouts  1.74 us (3%)
  between operations  0.75 us (1%)
    pallas_call x2, Pallas kernels, attend_step(): pl.pallas_call(functools.partial(middle_kernel, step, sources, chosen, wi...  12.7 us
    ppermute x2, waiting for transfers between devices, onward(): far.append(lax.ppermute(parts[k - 1], 'tp', to_chip))  7.55 us
    pallas_call x1, Pallas kernels, shards(): pl.pallas_call(functools.partial(first_kernel, sources), out_shape=state_...  6.3 us
    ppermute x2, waiting for transfers between devices, shards(): mine = lax.ppermute(sent, ('ctx', 'tp'), across(step))  4.37 us
    pallas_call x1, Pallas kernels, shards(): pl.pallas_call(functools.partial(last_kernel, steps, sources, 0), out_sha...  3.8 us
    ppermute x2, starting transfers between devices, shards(): mine = lax.ppermute(sent, ('ctx', 'tp'), across(step))  3.77 us
    ppermute x2, starting transfers between devices, onward(): far.append(lax.ppermute(parts[k - 1], 'tp', to_chip))  3.06 us
    ppermute x2, starting transfers between devices, shards(): theirs = lax.ppermute(mine, 'tp', sibling)  2.96 us
  transfers between devices with their start and end apart: 11, of which 8 were waited for; matrix products, arithmetic and copies ran while one was open for 3% of the time, Pallas kernels for 36%

profile of v3, /device:TPU:0, one launch (start us, length us, event | category | flops | bytes accessed | tf_op | source)
XLA Modules:
  0.0 61.7 jit_solution(1279543261195423268)
XLA Ops:
  0.6 1.1 %pack.1.kv_ref = bf16[2048,128]{1,0:T(8,128)(2,1)S(1)} custom-call(bf16[1024,256]{1,0:T(8,128)(2,1)} %keys_ref.1, bf16[1024,256]{1,0:T(8,128)(2,1)} %values_ref.1), custom_call_target="tpu_custom_call" | custom-call | flops 1024 | bytes 1024 | tf_op jit(solution)/shard_map/pack/pallas_call | solution.py:452
  1.7 3.1 %collective-permute-start = (bf16[2048,128]{1,0:T(8,128)(2,1)S(1)}, bf16[2048,128]{1,0:T(8,128)(2,1)S(1)}, u32[]{:S(2)}, u32[]{:S(2)}) collective-permute-start(bf16[2048,128]{1,0:T(8,128)(2,1)S(1)} %pack.1.kv_ref), channel_id=1, source_target_pairs={{0,4},{1,9},{2,6},{3,11},{4,0},{5,13},{6,2},{7,15},{8,12},{9,1},{1... | collective-permute-start | bytes 1572872 | tf_op jit(solution)/shard_map/ppermute | solution.py:526
  4.8 0.8 %copy.13 = s32[8,2,4]{2,1,0:T(2,128)S(1)} copy(s32[8,2,4]{0,2,1:T(4,128)} %param.16) | data formatting | bytes 512 | tf_op args[6]
  5.7 0.9 %reshape.13.lists_ref = s32[512]{0:T(512)S(1)} reshape(s32[8,2,4,8]{3,2,1,0:T(4,128)} %param.15) | data formatting | bytes 4096 | tf_op jit(solution)/shard_map/reshape | solution.py:484
  6.6 6.3 %attend_own.1 = (f32[16,128,128]{2,1,0:T(8,128)S(1)}, f32[16,8,128]{2,1,0:T(8,128)S(1)}, bf16[2,128,1024]{2,1,0:T(8,128)(2,1)S(1)}) custom-call(s32[512]{0:T(512)S(1)} %reshape.13.lists_ref, s32[64]{0:T(128)S(1)} %reshape.14.counts_ref, bf16[2048,128]{1,0:T(8,128)(2,1)S(1)} %pack.1.kv_ref, bf16[2,128,1024]{2,1,0:T(8,128)(2,1)} %queries_ref.1, ...), custom_call_target="tpu_custom_call" | custom-call | flops 1024 | bytes 1024 | tf_op jit(solution)/shard_map/attend_own/pallas_call | solution.py:494
  12.9 4.4 %collective-permute-done.mine_ref = bf16[2048,128]{1,0:T(8,128)(2,1)S(1)} collective-permute-done((bf16[2048,128]{1,0:T(8,128)(2,1)S(1)}, bf16[2048,128]{1,0:T(8,128)(2,1)S(1)}, u32[]{:S(2)}, u32[]{:S(2)}) %collective-permute-start) | collective-permute-done | bytes 524320 | tf_op jit(solution)/shard_map/ppermute | solution.py:526
  17.6 0.7 %collective-permute-start.1 = (bf16[2048,128]{1,0:T(8,128)(2,1)S(1)}, bf16[2048,128]{1,0:T(8,128)(2,1)S(1)}, u32[]{:S(2)}, u32[]{:S(2)}) collective-permute-start(bf16[2048,128]{1,0:T(8,128)(2,1)S(1)} %collective-permute-done.mine_ref), channel_id=1, source_target_pairs={{1,5},{3,7},{5,1},{7,3},{9,13},{11,15},{13,9},{15,11},{17,21},{19,... | collective-permute-start | bytes 1572872 | tf_op jit(solution)/shard_map/ppermute | solution.py:526
  18.3 0.8 %collective-permute-done.2.theirs_ref = bf16[2048,128]{1,0:T(8,128)(2,1)S(1)} collective-permute-done((bf16[2048,128]{1,0:T(8,128)(2,1)S(1)}, bf16[2048,128]{1,0:T(8,128)(2,1)S(1)}, u32[]{:S(2)}, u32[]{:S(2)}) %collective-permute-start.2) | collective-permute-done | bytes 524320 | tf_op jit(solution)/shard_map/ppermute | solution.py:528
  19.2 9.7 %attend_step.2 = (f32[16,128,128]{2,1,0:T(8,128)S(1)}, f32[16,8,128]{2,1,0:T(8,128)S(1)}, bf16[2,1024,1024]{2,1,0:T(8,128)(2,1)S(1)}) custom-call(s32[512]{0:T(512)S(1)} %reshape.13.lists_ref, s32[64]{0:T(128)S(1)} %reshape.14.counts_ref, bf16[2,128,1024]{2,1,0:T(8,128)(2,1)S(1)} %get-tuple-element.27.q_ref, ...), custom_call_target="tpu_custom_call" | custom-call | flops 1024 | bytes 1024 | tf_op jit(solution)/shard_map/attend_step/pallas_call | solution.py:512
  28.9 2.6 %collective-permute-start.3 = (bf16[2048,128]{1,0:T(8,128)(2,1)S(1)}, bf16[2048,128]{1,0:T(8,128)(2,1)S(1)}, u32[]{:S(2)}, u32[]{:S(2)}) collective-permute-start(bf16[2048,128]{1,0:T(8,128)(2,1)S(1)} %collective-permute-done.1.mine_ref), channel_id=1, source_target_pairs={{0,1},{1,0},{2,3},{3,2},{4,5},{5,4},{6,7},{7,6},{8,9},{9,8},{10,11... | collective-permute-start | bytes 1572872 | tf_op jit(solution)/shard_map/ppermute | solution.py:528
  31.5 1.5 %collective-permute-done.3.theirs_ref = bf16[2048,128]{1,0:T(8,128)(2,1)S(1)} collective-permute-done((bf16[2048,128]{1,0:T(8,128)(2,1)S(1)}, bf16[2048,128]{1,0:T(8,128)(2,1)S(1)}, u32[]{:S(2)}, u32[]{:S(2)}) %collective-permute-start.3) | collective-permute-done | bytes 524320 | tf_op jit(solution)/shard_map/ppermute | solution.py:528
  33.0 3.8 %attend_last.1 = (bf16[128,1024]{1,0:T(8,128)(2,1)S(1)}, bf16[2,128,1024]{2,1,0:T(8,128)(2,1)S(1)}, bf16[2,1024,1024]{2,1,0:T(8,128)(2,1)S(1)}) custom-call(s32[512]{0:T(512)S(1)} %reshape.13.lists_ref, s32[64]{0:T(128)S(1)} %reshape.14.counts_ref, bf16[2,128,1024]{2,1,0:T(8,128)(2,1)S(1)} %get-tuple-element.27.q_ref, ...), custom_call_target="tpu_custom_call" | custom-call | flops 1024 | bytes 1024 | tf_op jit(solution)/shard_map/attend_last/pallas_call | solution.py:532
  37.2 3.0 %attend_step.3 = (f32[16,128,128]{2,1,0:T(8,128)S(1)}, f32[16,8,128]{2,1,0:T(8,128)S(1)}) custom-call(s32[512]{0:T(512)S(1)} %reshape.13.lists_ref, s32[64]{0:T(128)S(1)} %reshape.14.counts_ref, bf16[2,128,1024]{2,1,0:T(8,128)(2,1)S(1)} %get-tuple-element.27.q_ref, bf16[2048,128]{1,0:T(8,128)(2,1)S(1)} %collective-permute-done.1.mine_ref, ...), custom_call_target="tpu_custom_call" | custom-call | flops 1024 | bytes 1024 | tf_op jit(solution)/shard_map/attend_step/pallas_call | solution.py:512
  40.7 0.8 %finish.1 = (bf16[128,1024]{1,0:T(8,128)(2,1)S(1)}, bf16[2,128,1024]{2,1,0:T(8,128)(2,1)S(1)}) custom-call(f32[16,128,128]{2,1,0:T(8,128)S(1)} %get-tuple-element.45.acc_ref, f32[16,8,128]{2,1,0:T(8,128)S(1)} %get-tuple-element.46.stat_ref, bf16[2,1024,1024]{2,1,0:T(8,128)(2,1)S(1)} %get-tuple-element.38.give_weight_ref.weight_ref), custom_call_target="tpu_custom_call" | custom-call | flops 1024 | bytes 1024 | tf_op jit(solution)/shard_map/finish/pallas_call | solution.py:588
  41.7 1.5 %collective-permute-start.5 = (bf16[128,1024]{1,0:T(8,128)(2,1)S(1)}, bf16[128,1024]{1,0:T(8,128)(2,1)S(1)}, u32[]{:S(2)}, u32[]{:S(2)}) collective-permute-start(bf16[128,1024]{1,0:T(8,128)(2,1)S(1)} %project_onward.2), channel_id=1, source_target_pairs={{0,2},{1,3},{2,0},{3,1},{4,6},{5,7},{6,4},{7,5},{8,10},{9,11},{10,... | collective-permute-start | bytes 786440 | tf_op jit(solution)/shard_map/ppermute | solution.py:563
  43.9 1.6 %collective-permute-start.7 = (bf16[128,1024]{1,0:T(8,128)(2,1)S(1)}, bf16[128,1024]{1,0:T(8,128)(2,1)S(1)}, u32[]{:S(2)}, u32[]{:S(2)}) collective-permute-start(bf16[128,1024]{1,0:T(8,128)(2,1)S(1)} %project_onward.3), channel_id=1, source_target_pairs={{0,2},{1,3},{2,0},{3,1},{4,6},{5,7},{6,4},{7,5},{8,10},{9,11},{10,... | collective-permute-start | bytes 786440 | tf_op jit(solution)/shard_map/ppermute | solution.py:563
  45.5 1.3 %project_near.2.refs_0_ = f32[128,1024]{1,0:T(8,128)S(1)} custom-call(bf16[128,1024]{1,0:T(8,128)(2,1)S(1)} %get-tuple-element.39.attended_ref, bf16[2,1024,1024]{2,1,0:T(8,128)(2,1)S(1)} %get-tuple-element.40.weight_ref, bf16[2,128,1024]{2,1,0:T(8,128)(2,1)S(1)} %collective-permute-done.4.got_ref, bf16[2,128,4096]{2,1,0:T(8,128)(2,1)} %residual_ref.3), custom_call_target="tpu_custom_call" | custom-call | flops 1024 | bytes 1024 | tf_op jit(solution)/shard_map/project_near/pallas_call | solution.py:567
  46.8 4.0 %collective-permute-done.5.refs_1_ = bf16[128,1024]{1,0:T(8,128)(2,1)S(1)} collective-permute-done((bf16[128,1024]{1,0:T(8,128)(2,1)S(1)}, bf16[128,1024]{1,0:T(8,128)(2,1)S(1)}, u32[]{:S(2)}, u32[]{:S(2)}) %collective-permute-start.5) | collective-permute-done | bytes 262176 | tf_op jit(solution)/shard_map/ppermute | solution.py:563
  51.0 1.3 %project_near.3.refs_0_ = f32[128,1024]{1,0:T(8,128)S(1)} custom-call(bf16[128,1024]{1,0:T(8,128)(2,1)S(1)} %get-tuple-element.47.attended_ref, bf16[2,1024,1024]{2,1,0:T(8,128)(2,1)S(1)} %get-tuple-element.40.weight_ref, bf16[2,128,1024]{2,1,0:T(8,128)(2,1)S(1)} %collective-permute-done.6.got_ref, bf16[2,128,4096]{2,1,0:T(8,128)(2,1)} %residual_ref.3), custom_call_target="tpu_custom_call" | custom-call | flops 1024 | bytes 1024 | tf_op jit(solution)/shard_map/project_near/pallas_call | solution.py:567
  52.4 3.5 %collective-permute-done.7.refs_1_ = bf16[128,1024]{1,0:T(8,128)(2,1)S(1)} collective-permute-done((bf16[128,1024]{1,0:T(8,128)(2,1)S(1)}, bf16[128,1024]{1,0:T(8,128)(2,1)S(1)}, u32[]{:S(2)}, u32[]{:S(2)}) %collective-permute-start.7) | collective-permute-done | bytes 262176 | tf_op jit(solution)/shard_map/ppermute | solution.py:563
  56.7 1.4 %collective-permute-start.9 = (f32[16,128]{1,0:T(8,128)S(1)}, f32[16,128]{1,0:T(8,128)S(1)}, u32[]{:S(2)}, u32[]{:S(2)}) collective-permute-start(f32[16,128]{1,0:T(8,128)S(1)} %constant_dynamic-update-slice_fusion.refs_2_), channel_id=1, source_target_pairs={{0,2},{1,3},{2,0},{3,1},{4,6},{5,7},{6,4},{7,5},{8,10},{9,11},{10,... | collective-permute-start | bytes 24584 | tf_op jit(solution)/shard_map/ppermute | solution.py:620
  58.1 1.7 %collective-permute-done.8.refs_3_ = f32[16,128]{1,0:T(8,128)S(1)} collective-permute-done((f32[16,128]{1,0:T(8,128)S(1)}, f32[16,128]{1,0:T(8,128)S(1)}, u32[]{:S(2)}, u32[]{:S(2)}) %collective-permute-start.8) | collective-permute-done | bytes 8224 | tf_op jit(solution)/shard_map/ppermute | solution.py:620
  59.8 0.7 %collective-permute-done.9.refs_4_ = f32[16,128]{1,0:T(8,128)S(1)} collective-permute-done((f32[16,128]{1,0:T(8,128)S(1)}, f32[16,128]{1,0:T(8,128)S(1)}, u32[]{:S(2)}, u32[]{:S(2)}) %collective-permute-start.9) | collective-permute-done | bytes 8224 | tf_op jit(solution)/shard_map/ppermute | solution.py:620
  60.5 1.2 %norm.1 = (bf16[2,128,1024]{2,1,0:T(8,128)(2,1)}, bf16[2,128,1024]{2,1,0:T(8,128)(2,1)}) custom-call(f32[128,1024]{1,0:T(8,128)S(1)} %get-tuple-element.42.refs_0_, f32[128,1024]{1,0:T(8,128)S(1)} %get-tuple-element.49.refs_1_, f32[16,128]{1,0:T(8,128)S(1)} %constant_dynamic-update-slice_fusion.refs_2_, f32[16,128]{1,0:T(8,128)S(1)} %collective-permute-done.8.refs_3_, ...), custom_call_target="tpu_custom_call" | custom-call | flops 1024 | bytes 1024 | tf_op jit(solution)/shard_map/norm/pallas_call | solution.py:624
  (19 shorter events, 3.3 us)
Async XLA Ops:
  1.7 15.5 %collective-permute-start = (bf16[2048,128]{1,0:T(8,128)(2,1)S(1)}, bf16[2048,128]{1,0:T(8,128)(2,1)S(1)}, u32[]{:S(2)}, u32[]{:S(2)}) collective-permute-start(bf16[2048,128]{1,0:T(8,128)(2,1)S(1)} %pack.1.kv_ref), channel_id=1, source_target_pairs={{0,4},{1,9},{2,6},{3,11},{4,0},{5,13},{6,2},{7,15},{8,12},{9,1},{1... | collective-permute-start | bytes 1572872 | tf_op jit(solution)/shard_map/ppermute | solution.py:526
  17.2 1.9 %collective-permute-start.2 = (bf16[2048,128]{1,0:T(8,128)(2,1)S(1)}, bf16[2048,128]{1,0:T(8,128)(2,1)S(1)}, u32[]{:S(2)}, u32[]{:S(2)}) collective-permute-start(bf16[2048,128]{1,0:T(8,128)(2,1)S(1)} %collective-permute-done.mine_ref), channel_id=1, source_target_pairs={{0,1},{1,0},{2,3},{3,2},{4,5},{5,4},{6,7},{7,6},{8,9},{9,8},{10,11... | collective-permute-start | bytes 1572872 | tf_op jit(solution)/shard_map/ppermute | solution.py:528
  17.6 11.3 %collective-permute-start.1 = (bf16[2048,128]{1,0:T(8,128)(2,1)S(1)}, bf16[2048,128]{1,0:T(8,128)(2,1)S(1)}, u32[]{:S(2)}, u32[]{:S(2)}) collective-permute-start(bf16[2048,128]{1,0:T(8,128)(2,1)S(1)} %collective-permute-done.mine_ref), channel_id=1, source_target_pairs={{1,5},{3,7},{5,1},{7,3},{9,13},{11,15},{13,9},{15,11},{17,21},{19,... | collective-permute-start | bytes 1572872 | tf_op jit(solution)/shard_map/ppermute | solution.py:526
  28.9 4.1 %collective-permute-start.3 = (bf16[2048,128]{1,0:T(8,128)(2,1)S(1)}, bf16[2048,128]{1,0:T(8,128)(2,1)S(1)}, u32[]{:S(2)}, u32[]{:S(2)}) collective-permute-start(bf16[2048,128]{1,0:T(8,128)(2,1)S(1)} %collective-permute-done.1.mine_ref), channel_id=1, source_target_pairs={{0,1},{1,0},{2,3},{3,2},{4,5},{5,4},{6,7},{7,6},{8,9},{9,8},{10,11... | collective-permute-start | bytes 1572872 | tf_op jit(solution)/shard_map/ppermute | solution.py:528
  36.8 3.4 %collective-permute-start.4 = (bf16[2,128,1024]{2,1,0:T(8,128)(2,1)S(1)}, bf16[2,128,1024]{2,1,0:T(8,128)(2,1)S(1)}, u32[]{:S(2)}, u32[]{:S(2)}) collective-permute-start(bf16[2,128,1024]{2,1,0:T(8,128)(2,1)S(1)} %get-tuple-element.41), channel_id=1, source_target_pairs={{0,1},{1,0},{2,3},{3,2},{4,5},{5,4},{6,7},{7,6},{8,9},{9,8},{10,11... | collective-permute-start | bytes 1572872 | tf_op jit(solution)/shard_map/ppermute | solution.py:581
  41.5 2.0 %collective-permute-start.6 = (bf16[2,128,1024]{2,1,0:T(8,128)(2,1)S(1)}, bf16[2,128,1024]{2,1,0:T(8,128)(2,1)S(1)}, u32[]{:S(2)}, u32[]{:S(2)}) collective-permute-start(bf16[2,128,1024]{2,1,0:T(8,128)(2,1)S(1)} %get-tuple-element.48), channel_id=1, source_target_pairs={{0,1},{1,0},{2,3},{3,2},{4,5},{5,4},{6,7},{7,6},{8,9},{9,8},{10,11... | collective-permute-start | bytes 1572872 | tf_op jit(solution)/shard_map/ppermute | solution.py:600
  41.7 9.1 %collective-permute-start.5 = (bf16[128,1024]{1,0:T(8,128)(2,1)S(1)}, bf16[128,1024]{1,0:T(8,128)(2,1)S(1)}, u32[]{:S(2)}, u32[]{:S(2)}) collective-permute-start(bf16[128,1024]{1,0:T(8,128)(2,1)S(1)} %project_onward.2), channel_id=1, source_target_pairs={{0,2},{1,3},{2,0},{3,1},{4,6},{5,7},{6,4},{7,5},{8,10},{9,11},{10,... | collective-permute-start | bytes 786440 | tf_op jit(solution)/shard_map/ppermute | solution.py:563
  43.9 12.0 %collective-permute-start.7 = (bf16[128,1024]{1,0:T(8,128)(2,1)S(1)}, bf16[128,1024]{1,0:T(8,128)(2,1)S(1)}, u32[]{:S(2)}, u32[]{:S(2)}) collective-permute-start(bf16[128,1024]{1,0:T(8,128)(2,1)S(1)} %project_onward.3), channel_id=1, source_target_pairs={{0,2},{1,3},{2,0},{3,1},{4,6},{5,7},{6,4},{7,5},{8,10},{9,11},{10,... | collective-permute-start | bytes 786440 | tf_op jit(solution)/shard_map/ppermute | solution.py:563
  51.0 7.1 %copy-start = (bf16[1024]{0:T(1024)(128)(2,1)S(1)}, bf16[1024]{0:T(1024)(128)(2,1)}, u32[]{:S(2)}) copy-start(bf16[1024]{0:T(1024)(128)(2,1)} %param.19) | copy-start | bytes 6148
  56.1 2.0 %collective-permute-start.10 = (f32[16,128]{1,0:T(8,128)S(1)}, f32[16,128]{1,0:T(8,128)S(1)}, u32[]{:S(2)}, u32[]{:S(2)}) collective-permute-start(f32[16,128]{1,0:T(8,128)S(1)} %constant_dynamic-update-slice_fusion.refs_2_), channel_id=1, source_target_pairs={{0,3},{1,0},{2,1},{3,2},{4,7},{5,4},{6,5},{7,6},{8,11},{9,8},{10,9... | collective-permute-start | bytes 24584 | tf_op jit(solution)/shard_map/ppermute | solution.py:620
  56.7 3.1 %collective-permute-start.8 = (f32[16,128]{1,0:T(8,128)S(1)}, f32[16,128]{1,0:T(8,128)S(1)}, u32[]{:S(2)}, u32[]{:S(2)}) collective-permute-start(f32[16,128]{1,0:T(8,128)S(1)} %constant_dynamic-update-slice_fusion.refs_2_), channel_id=1, source_target_pairs={{0,1},{1,2},{2,3},{3,0},{4,5},{5,6},{6,7},{7,4},{8,9},{9,10},{10,1... | collective-permute-start | bytes 24584 | tf_op jit(solution)/shard_map/ppermute | solution.py:620
  56.7 3.7 %collective-permute-start.9 = (f32[16,128]{1,0:T(8,128)S(1)}, f32[16,128]{1,0:T(8,128)S(1)}, u32[]{:S(2)}, u32[]{:S(2)}) collective-permute-start(f32[16,128]{1,0:T(8,128)S(1)} %constant_dynamic-update-slice_fusion.refs_2_), channel_id=1, source_target_pairs={{0,2},{1,3},{2,0},{3,1},{4,6},{5,7},{6,4},{7,5},{8,10},{9,11},{10,... | collective-permute-start | bytes 24584 | tf_op jit(solution)/shard_map/ppermute | solution.py:620

commit v4 on v3

--- a/solution.py
+++ b/solution.py
@@ -20,7 +20,6 @@
 TO_LOG2 = math.log2(math.e) / math.sqrt(HD)
 
 VMEM_LIMIT = 24 * 1024 * 1024
-NT = (((1,), (1,)), ((), ()))
 
 
 def key_group(heads):
@@ -59,16 +58,15 @@
 
 
 def shard_scores(lists_ref, counts_ref, q_ref, kv_ref, flipped_ref, source, sources, head, cont):
-    conts = q_ref.shape[0]
+    conts = q_ref.shape[1]
     pairs = kv_ref.shape[0] // 2 // HD
     place = (head * conts + cont) * sources + source
     count = counts_ref[place]
     blocks = [lists_ref[place * TILES + t] for t in range(TILES)]
-    query = q_ref[cont, :, pl.ds(pl.multiple_of(head * HD, HD), HD)]
     keys = jnp.concatenate(
         [kv_ref[pl.ds(pl.multiple_of(b * BLK, BLK), BLK), :] for b in blocks], axis=0
     )
-    scores = lax.dot_general(keys, query, NT, preferred_element_type=jnp.float32)
+    scores = jnp.dot(keys, q_ref[head, cont], preferred_element_type=jnp.float32)
     lane = lax.broadcasted_iota(jnp.int32, (HD, HD), 1)
     halves = []
     for t, b in enumerate(blocks):
@@ -152,19 +150,19 @@
     stat_ref,
     q_ref,
     flipped_ref,
+    rows_ref,
     ck_ref,
     cv_ref,
     own_ref,
     sems,
 ):
-    conts, length, width = q_ref.shape
-    heads = width // HD
+    heads, conts, _, length = q_ref.shape
     lanes = group_lanes(heads)
     copies = start_all(
         [
             pltpu.make_async_copy(cont_values_ref.at[:, :, lanes], cv_ref, sems.at[0]),
             pltpu.make_async_copy(cont_keys_ref.at[:, :, lanes], ck_ref, sems.at[1]),
-            pltpu.make_async_copy(queries_ref, q_ref, sems.at[2]),
+            pltpu.make_async_copy(queries_ref, rows_ref, sems.at[2]),
         ]
     )
     own = lax.axis_index("ctx")
@@ -175,13 +173,17 @@
     copies[1].wait()
     copies[2].wait()
 
-    def one_head(head, carry):
+    for head in range(heads):
+        for cont in range(conts):
+            q_ref[head, cont] = rows_ref[cont, :, head * HD : (head + 1) * HD].T
+
+    together = 4 // conts
+
+    def some_heads(index, carry):
+        work = [(index * together + j, cont) for j in range(together) for cont in range(conts)]
         made = []
-        for cont in range(conts):
-            query = q_ref[cont, :, pl.ds(pl.multiple_of(head * HD, HD), HD)]
-            scores = lax.dot_general(
-                ck_ref[cont], query, NT, preferred_element_type=jnp.float32
-            )
+        for head, cont in work:
+            scores = jnp.dot(ck_ref[cont], q_ref[head, cont], preferred_element_type=jnp.float32)
             key = lax.broadcasted_iota(jnp.int32, scores.shape, 0)
             row = lax.broadcasted_iota(jnp.int32, scores.shape, 1)
             scores = jnp.where(key <= row, scores, VERY_LOW)
@@ -192,18 +194,18 @@
                 ([(scores, True)] + tiles, jnp.concatenate([own_ref[cont], values], axis=1))
             )
         states = []
-        for cont in range(conts):
+        for got in made:
             start = (
                 jnp.full((1, length), VERY_LOW, jnp.float32),
                 jnp.zeros((1, length), jnp.float32),
                 jnp.zeros((HD, length), jnp.float32),
             )
-            states.append(absorb(start, *made[cont]))
-        for cont in range(conts):
-            store_state(acc_ref, stat_ref, head * conts + cont, states[cont])
+            states.append(absorb(start, *got))
+        for (head, cont), state in zip(work, states):
+            store_state(acc_ref, stat_ref, head * conts + cont, state)
         return carry
 
-    lax.fori_loop(0, heads, one_head, 0)
+    lax.fori_loop(0, heads // together, some_heads, 0)
 
 
 def arrivals(step, sources):
@@ -227,9 +229,8 @@
 def absorb_arrivals(
     step, sources, chosen, lists_ref, counts_ref, q_ref, kv_refs, flipped_ref, before, after
 ):
-    conts, _, width = q_ref.shape
-    heads = width // HD
-    together = 2 // len(chosen)
+    heads, conts = q_ref.shape[:2]
+    together = 4 // len(chosen)
     one_of_two = sources == 4 and step == 2
     for part, (source, valid) in enumerate(arrivals(step, sources)):
         held = before if part == 0 or one_of_two else after
@@ -357,7 +358,7 @@
         (acc_ref, stat_ref),
     )
     finish_and_give(
-        cont, q_ref.shape[0], acc_ref, stat_ref, give_weight_ref, attended_ref, give_ref
+        cont, q_ref.shape[1], acc_ref, stat_ref, give_weight_ref, attended_ref, give_ref
     )
     for copy in copies:
         copy.wait()
@@ -493,11 +494,12 @@
 
     *state, q = pl.pallas_call(
         functools.partial(first_kernel, sources),
-        out_shape=state_shape + (array(queries.shape, jnp.bfloat16),),
+        out_shape=state_shape + (array((heads, conts, HD, length), jnp.bfloat16),),
         in_specs=[smem, smem, vmem] + [hbm] * 3,
         out_specs=(vmem,) * 3,
         scratch_shapes=[
             flipped,
+            pltpu.VMEM(queries.shape, jnp.bfloat16),
             pltpu.VMEM((conts, length, HD), jnp.bfloat16),
             pltpu.VMEM((conts, length, HD), jnp.bfloat16),
             pltpu.VMEM((conts, HD, length), jnp.bfloat16),

time: 62 us -> 57.6 us (0.929)
  Pallas kernels: 29.8 us -> 24 us
  waiting for transfers between devices: 16.9 us -> 18.3 us
    pallas_call x2, Pallas kernels: 12.7 us -> 9.01 us  [attend_step(): pl.pallas_call(functools.partial(middle_kernel, step, sources, chosen, wi...]
    ppermute x2, waiting for transfers between devices: 4.37 us -> 5.73 us  [shards(): mine = lax.ppermute(sent, ('ctx', 'tp'), across(step))]
    pallas_call x1, Pallas kernels: 6.3 us -> 4.94 us  [shards(): pl.pallas_call(functools.partial(first_kernel, sources), out_shape=state_...]
    pallas_call x1, Pallas kernels: 3.8 us -> 3.06 us  [shards(): pl.pallas_call(functools.partial(last_kernel, steps, sources, 0), out_sha...]
  transfers between devices with their start and end apart: 11 -> 11, of which waited for: 8 -> 8; matrix products, arithmetic and copies ran while one was open for 3% -> 3% of each run, Pallas kernels for 36% -> 30%
where the time goes in v4:
time: 57.6 us; the launch traced here: 57.3 us
  Pallas kernels  24 us (42%)
  waiting for transfers between devices  18.3 us (32%)
  starting transfers between devices  12.4 us (22%)
  local copies, waits for them, and re-layouts  1.74 us (3%)
  between operations  0.75 us (1%)
    pallas_call x2, Pallas kernels, attend_step(): pl.pallas_call(functools.partial(middle_kernel, step, sources, chosen, wi...  9.01 us
    ppermute x2, waiting for transfers between devices, onward(): far.append(lax.ppermute(parts[k - 1], 'tp', to_chip))  7.55 us
    ppermute x2, waiting for transfers between devices, shards(): mine = lax.ppermute(sent, ('ctx', 'tp'), across(step))  5.73 us
    pallas_call x1, Pallas kernels, shards(): pl.pallas_call(functools.partial(first_kernel, sources), out_shape=state_...  4.94 us
    ppermute x2, starting transfers between devices, shards(): mine = lax.ppermute(sent, ('ctx', 'tp'), across(step))  3.77 us
    ppermute x2, starting transfers between devices, onward(): far.append(lax.ppermute(parts[k - 1], 'tp', to_chip))  3.06 us
    pallas_call x1, Pallas kernels, shards(): pl.pallas_call(functools.partial(last_kernel, steps, sources, 0), out_sha...  3.06 us
    ppermute x2, starting transfers between devices, shards(): theirs = lax.ppermute(mine, 'tp', sibling)  2.96 us
  transfers between devices with their start and end apart: 11, of which 8 were waited for; matrix products, arithmetic and copies ran while one was open for 3% of the time, Pallas kernels for 30%

profile of v4, /device:TPU:0, one launch (start us, length us, event | category | flops | bytes accessed | tf_op | source)
XLA Modules:
  0.0 57.3 jit_solution(8869360823935645373)
XLA Ops:
  0.6 1.1 %pack.1.kv_ref = bf16[2048,128]{1,0:T(8,128)(2,1)S(1)} custom-call(bf16[1024,256]{1,0:T(8,128)(2,1)} %keys_ref.1, bf16[1024,256]{1,0:T(8,128)(2,1)} %values_ref.1), custom_call_target="tpu_custom_call" | custom-call | flops 1024 | bytes 1024 | tf_op jit(solution)/shard_map/pack/pallas_call | solution.py:453
  1.7 3.1 %collective-permute-start = (bf16[2048,128]{1,0:T(8,128)(2,1)S(1)}, bf16[2048,128]{1,0:T(8,128)(2,1)S(1)}, u32[]{:S(2)}, u32[]{:S(2)}) collective-permute-start(bf16[2048,128]{1,0:T(8,128)(2,1)S(1)} %pack.1.kv_ref), channel_id=1, source_target_pairs={{0,4},{1,9},{2,6},{3,11},{4,0},{5,13},{6,2},{7,15},{8,12},{9,1},{1... | collective-permute-start | bytes 1572872 | tf_op jit(solution)/shard_map/ppermute | solution.py:528
  4.8 0.8 %copy.13 = s32[8,2,4]{2,1,0:T(2,128)S(1)} copy(s32[8,2,4]{0,2,1:T(4,128)} %param.16) | data formatting | bytes 512 | tf_op args[6]
  5.7 0.9 %reshape.13.lists_ref = s32[512]{0:T(512)S(1)} reshape(s32[8,2,4,8]{3,2,1,0:T(4,128)} %param.15) | data formatting | bytes 4096 | tf_op jit(solution)/shard_map/reshape | solution.py:485
  6.6 4.9 %attend_own.1 = (f32[16,128,128]{2,1,0:T(8,128)S(1)}, f32[16,8,128]{2,1,0:T(8,128)S(1)}, bf16[8,2,128,128]{3,2,1,0:T(8,128)(2,1)S(1)}) custom-call(s32[512]{0:T(512)S(1)} %reshape.13.lists_ref, s32[64]{0:T(128)S(1)} %reshape.14.counts_ref, bf16[2048,128]{1,0:T(8,128)(2,1)S(1)} %pack.1.kv_ref, bf16[2,128,1024]{2,1,0:T(8,128)(2,1)} %queries_ref.1, ...), custom_call_target="tpu_custom_call" | custom-call | flops 1024 | bytes 1024 | tf_op jit(solution)/shard_map/attend_own/pallas_call | solution.py:495
  11.5 5.7 %collective-permute-done.mine_ref = bf16[2048,128]{1,0:T(8,128)(2,1)S(1)} collective-permute-done((bf16[2048,128]{1,0:T(8,128)(2,1)S(1)}, bf16[2048,128]{1,0:T(8,128)(2,1)S(1)}, u32[]{:S(2)}, u32[]{:S(2)}) %collective-permute-start) | collective-permute-done | bytes 524320 | tf_op jit(solution)/shard_map/ppermute | solution.py:528
  17.6 0.7 %collective-permute-start.1 = (bf16[2048,128]{1,0:T(8,128)(2,1)S(1)}, bf16[2048,128]{1,0:T(8,128)(2,1)S(1)}, u32[]{:S(2)}, u32[]{:S(2)}) collective-permute-start(bf16[2048,128]{1,0:T(8,128)(2,1)S(1)} %collective-permute-done.mine_ref), channel_id=1, source_target_pairs={{1,5},{3,7},{5,1},{7,3},{9,13},{11,15},{13,9},{15,11},{17,21},{19,... | collective-permute-start | bytes 1572872 | tf_op jit(solution)/shard_map/ppermute | solution.py:528
  18.3 0.8 %collective-permute-done.2.theirs_ref = bf16[2048,128]{1,0:T(8,128)(2,1)S(1)} collective-permute-done((bf16[2048,128]{1,0:T(8,128)(2,1)S(1)}, bf16[2048,128]{1,0:T(8,128)(2,1)S(1)}, u32[]{:S(2)}, u32[]{:S(2)}) %collective-permute-start.2) | collective-permute-done | bytes 524320 | tf_op jit(solution)/shard_map/ppermute | solution.py:530
  19.2 6.8 %attend_step.2 = (f32[16,128,128]{2,1,0:T(8,128)S(1)}, f32[16,8,128]{2,1,0:T(8,128)S(1)}, bf16[2,1024,1024]{2,1,0:T(8,128)(2,1)S(1)}) custom-call(s32[512]{0:T(512)S(1)} %reshape.13.lists_ref, s32[64]{0:T(128)S(1)} %reshape.14.counts_ref, bf16[8,2,128,128]{3,2,1,0:T(8,128)(2,1)S(1)} %get-tuple-element.27.q_ref, ...), custom_call_target="tpu_custom_call" | custom-call | flops 1024 | bytes 1024 | tf_op jit(solution)/shard_map/attend_step/pallas_call | solution.py:514
  26.0 2.6 %collective-permute-start.3 = (bf16[2048,128]{1,0:T(8,128)(2,1)S(1)}, bf16[2048,128]{1,0:T(8,128)(2,1)S(1)}, u32[]{:S(2)}, u32[]{:S(2)}) collective-permute-start(bf16[2048,128]{1,0:T(8,128)(2,1)S(1)} %collective-permute-done.1.mine_ref), channel_id=1, source_target_pairs={{0,1},{1,0},{2,3},{3,2},{4,5},{5,4},{6,7},{7,6},{8,9},{9,8},{10,11... | collective-permute-start | bytes 1572872 | tf_op jit(solution)/shard_map/ppermute | solution.py:530
  28.5 1.5 %collective-permute-done.3.theirs_ref = bf16[2048,128]{1,0:T(8,128)(2,1)S(1)} collective-permute-done((bf16[2048,128]{1,0:T(8,128)(2,1)S(1)}, bf16[2048,128]{1,0:T(8,128)(2,1)S(1)}, u32[]{:S(2)}, u32[]{:S(2)}) %collective-permute-start.3) | collective-permute-done | bytes 524320 | tf_op jit(solution)/shard_map/ppermute | solution.py:530
  30.1 3.1 %attend_last.1 = (bf16[128,1024]{1,0:T(8,128)(2,1)S(1)}, bf16[2,128,1024]{2,1,0:T(8,128)(2,1)S(1)}, bf16[2,1024,1024]{2,1,0:T(8,128)(2,1)S(1)}) custom-call(s32[512]{0:T(512)S(1)} %reshape.13.lists_ref, s32[64]{0:T(128)S(1)} %reshape.14.counts_ref, bf16[8,2,128,128]{3,2,1,0:T(8,128)(2,1)S(1)} %get-tuple-element.27.q_ref, ...), custom_call_target="tpu_custom_call" | custom-call | flops 1024 | bytes 1024 | tf_op jit(solution)/shard_map/attend_last/pallas_call | solution.py:534
  33.6 2.2 %attend_step.3 = (f32[16,128,128]{2,1,0:T(8,128)S(1)}, f32[16,8,128]{2,1,0:T(8,128)S(1)}) custom-call(s32[512]{0:T(512)S(1)} %reshape.13.lists_ref, s32[64]{0:T(128)S(1)} %reshape.14.counts_ref, bf16[8,2,128,128]{3,2,1,0:T(8,128)(2,1)S(1)} %get-tuple-element.27.q_ref, bf16[2048,128]{1,0:T(8,128)(2,1)S(1)} %collective-permute-done.1.mine_ref, ...), custom_call_target="tpu_custom_call" | custom-call | flops 1024 | bytes 1024 | tf_op jit(solution)/shard_map/attend_step/pallas_call | solution.py:514
  36.3 0.8 %finish.1 = (bf16[128,1024]{1,0:T(8,128)(2,1)S(1)}, bf16[2,128,1024]{2,1,0:T(8,128)(2,1)S(1)}) custom-call(f32[16,128,128]{2,1,0:T(8,128)S(1)} %get-tuple-element.45.acc_ref, f32[16,8,128]{2,1,0:T(8,128)S(1)} %get-tuple-element.46.stat_ref, bf16[2,1024,1024]{2,1,0:T(8,128)(2,1)S(1)} %get-tuple-element.38.give_weight_ref.weight_ref), custom_call_target="tpu_custom_call" | custom-call | flops 1024 | bytes 1024 | tf_op jit(solution)/shard_map/finish/pallas_call | solution.py:590
  37.3 1.5 %collective-permute-start.5 = (bf16[128,1024]{1,0:T(8,128)(2,1)S(1)}, bf16[128,1024]{1,0:T(8,128)(2,1)S(1)}, u32[]{:S(2)}, u32[]{:S(2)}) collective-permute-start(bf16[128,1024]{1,0:T(8,128)(2,1)S(1)} %project_onward.2), channel_id=1, source_target_pairs={{0,2},{1,3},{2,0},{3,1},{4,6},{5,7},{6,4},{7,5},{8,10},{9,11},{10,... | collective-permute-start | bytes 786440 | tf_op jit(solution)/shard_map/ppermute | solution.py:565
  39.5 1.6 %collective-permute-start.7 = (bf16[128,1024]{1,0:T(8,128)(2,1)S(1)}, bf16[128,1024]{1,0:T(8,128)(2,1)S(1)}, u32[]{:S(2)}, u32[]{:S(2)}) collective-permute-start(bf16[128,1024]{1,0:T(8,128)(2,1)S(1)} %project_onward.3), channel_id=1, source_target_pairs={{0,2},{1,3},{2,0},{3,1},{4,6},{5,7},{6,4},{7,5},{8,10},{9,11},{10,... | collective-permute-start | bytes 786440 | tf_op jit(solution)/shard_map/ppermute | solution.py:565
  41.1 1.3 %project_near.2.refs_0_ = f32[128,1024]{1,0:T(8,128)S(1)} custom-call(bf16[128,1024]{1,0:T(8,128)(2,1)S(1)} %get-tuple-element.39.attended_ref, bf16[2,1024,1024]{2,1,0:T(8,128)(2,1)S(1)} %get-tuple-element.40.weight_ref, bf16[2,128,1024]{2,1,0:T(8,128)(2,1)S(1)} %collective-permute-done.4.got_ref, bf16[2,128,4096]{2,1,0:T(8,128)(2,1)} %residual_ref.3), custom_call_target="tpu_custom_call" | custom-call | flops 1024 | bytes 1024 | tf_op jit(solution)/shard_map/project_near/pallas_call | solution.py:569
  42.4 4.0 %collective-permute-done.5.refs_1_ = bf16[128,1024]{1,0:T(8,128)(2,1)S(1)} collective-permute-done((bf16[128,1024]{1,0:T(8,128)(2,1)S(1)}, bf16[128,1024]{1,0:T(8,128)(2,1)S(1)}, u32[]{:S(2)}, u32[]{:S(2)}) %collective-permute-start.5) | collective-permute-done | bytes 262176 | tf_op jit(solution)/shard_map/ppermute | solution.py:565
  46.6 1.3 %project_near.3.refs_0_ = f32[128,1024]{1,0:T(8,128)S(1)} custom-call(bf16[128,1024]{1,0:T(8,128)(2,1)S(1)} %get-tuple-element.47.attended_ref, bf16[2,1024,1024]{2,1,0:T(8,128)(2,1)S(1)} %get-tuple-element.40.weight_ref, bf16[2,128,1024]{2,1,0:T(8,128)(2,1)S(1)} %collective-permute-done.6.got_ref, bf16[2,128,4096]{2,1,0:T(8,128)(2,1)} %residual_ref.3), custom_call_target="tpu_custom_call" | custom-call | flops 1024 | bytes 1024 | tf_op jit(solution)/shard_map/project_near/pallas_call | solution.py:569
  47.9 3.6 %collective-permute-done.7.refs_1_ = bf16[128,1024]{1,0:T(8,128)(2,1)S(1)} collective-permute-done((bf16[128,1024]{1,0:T(8,128)(2,1)S(1)}, bf16[128,1024]{1,0:T(8,128)(2,1)S(1)}, u32[]{:S(2)}, u32[]{:S(2)}) %collective-permute-start.7) | collective-permute-done | bytes 262176 | tf_op jit(solution)/shard_map/ppermute | solution.py:565
  52.3 1.3 %collective-permute-start.9 = (f32[16,128]{1,0:T(8,128)S(1)}, f32[16,128]{1,0:T(8,128)S(1)}, u32[]{:S(2)}, u32[]{:S(2)}) collective-permute-start(f32[16,128]{1,0:T(8,128)S(1)} %constant_dynamic-update-slice_fusion.refs_2_), channel_id=1, source_target_pairs={{0,2},{1,3},{2,0},{3,1},{4,6},{5,7},{6,4},{7,5},{8,10},{9,11},{10,... | collective-permute-start | bytes 24584 | tf_op jit(solution)/shard_map/ppermute | solution.py:622
  53.7 1.7 %collective-permute-done.8.refs_3_ = f32[16,128]{1,0:T(8,128)S(1)} collective-permute-done((f32[16,128]{1,0:T(8,128)S(1)}, f32[16,128]{1,0:T(8,128)S(1)}, u32[]{:S(2)}, u32[]{:S(2)}) %collective-permute-start.8) | collective-permute-done | bytes 8224 | tf_op jit(solution)/shard_map/ppermute | solution.py:622
  55.4 0.7 %collective-permute-done.9.refs_4_ = f32[16,128]{1,0:T(8,128)S(1)} collective-permute-done((f32[16,128]{1,0:T(8,128)S(1)}, f32[16,128]{1,0:T(8,128)S(1)}, u32[]{:S(2)}, u32[]{:S(2)}) %collective-permute-start.9) | collective-permute-done | bytes 8224 | tf_op jit(solution)/shard_map/ppermute | solution.py:622
  56.1 1.2 %norm.1 = (bf16[2,128,1024]{2,1,0:T(8,128)(2,1)}, bf16[2,128,1024]{2,1,0:T(8,128)(2,1)}) custom-call(f32[128,1024]{1,0:T(8,128)S(1)} %get-tuple-element.42.refs_0_, f32[128,1024]{1,0:T(8,128)S(1)} %get-tuple-element.49.refs_1_, f32[16,128]{1,0:T(8,128)S(1)} %constant_dynamic-update-slice_fusion.refs_2_, f32[16,128]{1,0:T(8,128)S(1)} %collective-permute-done.8.refs_3_, ...), custom_call_target="tpu_custom_call" | custom-call | flops 1024 | bytes 1024 | tf_op jit(solution)/shard_map/norm/pallas_call | solution.py:626
  (19 shorter events, 3.4 us)
Async XLA Ops:
  1.7 15.5 %collective-permute-start = (bf16[2048,128]{1,0:T(8,128)(2,1)S(1)}, bf16[2048,128]{1,0:T(8,128)(2,1)S(1)}, u32[]{:S(2)}, u32[]{:S(2)}) collective-permute-start(bf16[2048,128]{1,0:T(8,128)(2,1)S(1)} %pack.1.kv_ref), channel_id=1, source_target_pairs={{0,4},{1,9},{2,6},{3,11},{4,0},{5,13},{6,2},{7,15},{8,12},{9,1},{1... | collective-permute-start | bytes 1572872 | tf_op jit(solution)/shard_map/ppermute | solution.py:528
  17.2 1.9 %collective-permute-start.2 = (bf16[2048,128]{1,0:T(8,128)(2,1)S(1)}, bf16[2048,128]{1,0:T(8,128)(2,1)S(1)}, u32[]{:S(2)}, u32[]{:S(2)}) collective-permute-start(bf16[2048,128]{1,0:T(8,128)(2,1)S(1)} %collective-permute-done.mine_ref), channel_id=1, source_target_pairs={{0,1},{1,0},{2,3},{3,2},{4,5},{5,4},{6,7},{7,6},{8,9},{9,8},{10,11... | collective-permute-start | bytes 1572872 | tf_op jit(solution)/shard_map/ppermute | solution.py:530
  17.6 8.3 %collective-permute-start.1 = (bf16[2048,128]{1,0:T(8,128)(2,1)S(1)}, bf16[2048,128]{1,0:T(8,128)(2,1)S(1)}, u32[]{:S(2)}, u32[]{:S(2)}) collective-permute-start(bf16[2048,128]{1,0:T(8,128)(2,1)S(1)} %collective-permute-done.mine_ref), channel_id=1, source_target_pairs={{1,5},{3,7},{5,1},{7,3},{9,13},{11,15},{13,9},{15,11},{17,21},{19,... | collective-permute-start | bytes 1572872 | tf_op jit(solution)/shard_map/ppermute | solution.py:528
  26.0 4.1 %collective-permute-start.3 = (bf16[2048,128]{1,0:T(8,128)(2,1)S(1)}, bf16[2048,128]{1,0:T(8,128)(2,1)S(1)}, u32[]{:S(2)}, u32[]{:S(2)}) collective-permute-start(bf16[2048,128]{1,0:T(8,128)(2,1)S(1)} %collective-permute-done.1.mine_ref), channel_id=1, source_target_pairs={{0,1},{1,0},{2,3},{3,2},{4,5},{5,4},{6,7},{7,6},{8,9},{9,8},{10,11... | collective-permute-start | bytes 1572872 | tf_op jit(solution)/shard_map/ppermute | solution.py:530
  33.2 2.7 %collective-permute-start.4 = (bf16[2,128,1024]{2,1,0:T(8,128)(2,1)S(1)}, bf16[2,128,1024]{2,1,0:T(8,128)(2,1)S(1)}, u32[]{:S(2)}, u32[]{:S(2)}) collective-permute-start(bf16[2,128,1024]{2,1,0:T(8,128)(2,1)S(1)} %get-tuple-element.41), channel_id=1, source_target_pairs={{0,1},{1,0},{2,3},{3,2},{4,5},{5,4},{6,7},{7,6},{8,9},{9,8},{10,11... | collective-permute-start | bytes 1572872 | tf_op jit(solution)/shard_map/ppermute | solution.py:583
  37.1 2.0 %collective-permute-start.6 = (bf16[2,128,1024]{2,1,0:T(8,128)(2,1)S(1)}, bf16[2,128,1024]{2,1,0:T(8,128)(2,1)S(1)}, u32[]{:S(2)}, u32[]{:S(2)}) collective-permute-start(bf16[2,128,1024]{2,1,0:T(8,128)(2,1)S(1)} %get-tuple-element.48), channel_id=1, source_target_pairs={{0,1},{1,0},{2,3},{3,2},{4,5},{5,4},{6,7},{7,6},{8,9},{9,8},{10,11... | collective-permute-start | bytes 1572872 | tf_op jit(solution)/shard_map/ppermute | solution.py:602
  37.3 9.1 %collective-permute-start.5 = (bf16[128,1024]{1,0:T(8,128)(2,1)S(1)}, bf16[128,1024]{1,0:T(8,128)(2,1)S(1)}, u32[]{:S(2)}, u32[]{:S(2)}) collective-permute-start(bf16[128,1024]{1,0:T(8,128)(2,1)S(1)} %project_onward.2), channel_id=1, source_target_pairs={{0,2},{1,3},{2,0},{3,1},{4,6},{5,7},{6,4},{7,5},{8,10},{9,11},{10,... | collective-permute-start | bytes 786440 | tf_op jit(solution)/shard_map/ppermute | solution.py:565
  39.5 12.0 %collective-permute-start.7 = (bf16[128,1024]{1,0:T(8,128)(2,1)S(1)}, bf16[128,1024]{1,0:T(8,128)(2,1)S(1)}, u32[]{:S(2)}, u32[]{:S(2)}) collective-permute-start(bf16[128,1024]{1,0:T(8,128)(2,1)S(1)} %project_onward.3), channel_id=1, source_target_pairs={{0,2},{1,3},{2,0},{3,1},{4,6},{5,7},{6,4},{7,5},{8,10},{9,11},{10,... | collective-permute-start | bytes 786440 | tf_op jit(solution)/shard_map/ppermute | solution.py:565
  46.6 7.1 %copy-start = (bf16[1024]{0:T(1024)(128)(2,1)S(1)}, bf16[1024]{0:T(1024)(128)(2,1)}, u32[]{:S(2)}) copy-start(bf16[1024]{0:T(1024)(128)(2,1)} %param.19) | copy-start | bytes 6148
  51.7 2.0 %collective-permute-start.10 = (f32[16,128]{1,0:T(8,128)S(1)}, f32[16,128]{1,0:T(8,128)S(1)}, u32[]{:S(2)}, u32[]{:S(2)}) collective-permute-start(f32[16,128]{1,0:T(8,128)S(1)} %constant_dynamic-update-slice_fusion.refs_2_), channel_id=1, source_target_pairs={{0,3},{1,0},{2,1},{3,2},{4,7},{5,4},{6,5},{7,6},{8,11},{9,8},{10,9... | collective-permute-start | bytes 24584 | tf_op jit(solution)/shard_map/ppermute | solution.py:622
  52.3 3.1 %collective-permute-start.8 = (f32[16,128]{1,0:T(8,128)S(1)}, f32[16,128]{1,0:T(8,128)S(1)}, u32[]{:S(2)}, u32[]{:S(2)}) collective-permute-start(f32[16,128]{1,0:T(8,128)S(1)} %constant_dynamic-update-slice_fusion.refs_2_), channel_id=1, source_target_pairs={{0,1},{1,2},{2,3},{3,0},{4,5},{5,6},{6,7},{7,4},{8,9},{9,10},{10,1... | collective-permute-start | bytes 24584 | tf_op jit(solution)/shard_map/ppermute | solution.py:622
  52.3 3.8 %collective-permute-start.9 = (f32[16,128]{1,0:T(8,128)S(1)}, f32[16,128]{1,0:T(8,128)S(1)}, u32[]{:S(2)}, u32[]{:S(2)}) collective-permute-start(f32[16,128]{1,0:T(8,128)S(1)} %constant_dynamic-update-slice_fusion.refs_2_), channel_id=1, source_target_pairs={{0,2},{1,3},{2,0},{3,1},{4,6},{5,7},{6,4},{7,5},{8,10},{9,11},{10,... | collective-permute-start | bytes 24584 | tf_op jit(solution)/shard_map/ppermute | solution.py:622

commit v5 on v4

v5 whole, which is shorter than its diff:
```python
import functools
import math

import jax
import jax.numpy as jnp
from jax import lax
from jax.experimental import pallas as pl
from jax.experimental.pallas import tpu as pltpu
from jax.sharding import PartitionSpec as P

HEADS = 32
KVH = 2
HD = 128
BLK = 64
TILES = 8
CORES = 2
TOGETHER = 4

VERY_LOW = -1e30
TO_LOG2 = math.log2(math.e) / math.sqrt(HD)

VMEM_LIMIT = 24 * 1024 * 1024


def key_group(heads):
    return lax.axis_index("tp") * heads // (HEADS // KVH)


def group_lanes(heads):
    return pl.ds(pl.multiple_of(key_group(heads) * HD, HD), HD)


def pack_keys_kernel(heads, keys_ref, packed_ref, sems):
    copy = pltpu.make_async_copy(keys_ref.at[:, group_lanes(heads)], packed_ref, sems.at[0])
    copy.start()
    copy.wait()


def pack_values_kernel(heads, values_ref, packed_ref, values_buf, sems):
    copy = pltpu.make_async_copy(values_ref.at[:, group_lanes(heads)], values_buf, sems.at[0])
    copy.start()
    copy.wait()
    for p in range(packed_ref.shape[0] // HD):
        rows = slice(p * HD, (p + 1) * HD)
        packed_ref[rows, :] = values_buf[rows, :].T


def both_ways(values_refs, flipped_ref):
    total = flipped_ref.shape[0] // 2
    for part, values_ref in enumerate(values_refs):
        rows = values_ref.shape[0]
        for p in range(rows // HD):
            pair = values_ref[p * HD : (p + 1) * HD, :]
            at = part * rows + p * HD
            flipped_ref[at : at + HD, :] = pair
            flipped_ref[total + at : total + at + HD, :] = jnp.concatenate(
                [pair[:, BLK:], pair[:, :BLK]], axis=1
            )


def shard_scores(lists_ref, counts_ref, q_refs, keys_ref, flipped_ref, source, head, cont):
    pairs = keys_ref.shape[0] // HD
    count = counts_ref[cont, source, head]
    blocks = [lists_ref[head, cont, source, t] for t in range(TILES)]
    keys = jnp.concatenate(
        [keys_ref[pl.ds(pl.multiple_of(b * BLK, BLK), BLK), :] for b in blocks], axis=0
    )
    scores = jnp.dot(keys, q_refs[cont][head], preferred_element_type=jnp.float32)
    lane = lax.broadcasted_iota(jnp.int32, (HD, HD), 1)
    halves = []
    for t, b in enumerate(blocks):
        spot = ((b + t) % 2 * pairs + b // 2) * HD
        halves.append(flipped_ref[pl.ds(pl.multiple_of(spot, HD), HD), :])
    values = jnp.concatenate(
        [jnp.where(lane < BLK, a, b) for a, b in zip(halves[::2], halves[1::2])], axis=1
    )
    tiles = [
        (scores[t * BLK : (t + 1) * BLK], t < count) for t in range(TILES)
    ]
    return tiles, values


def fold(op, tile):
    return functools.reduce(op, [tile[i : i + 8] for i in range(0, tile.shape[0], 8)])


def absorb(state, tiles, values):
    top, total, acc = state
    tops = [
        jnp.where(live, fold(jnp.maximum, tile), VERY_LOW) for tile, live in tiles
    ]
    best = jnp.max(functools.reduce(jnp.maximum, tops), axis=0, keepdims=True)
    new_top = jnp.maximum(top, best)
    weights = [
        jnp.exp2((tile - jnp.where(live, new_top, -VERY_LOW)) * TO_LOG2) for tile, live in tiles
    ]
    factor = jnp.exp2((top - new_top) * TO_LOG2)
    sums = functools.reduce(jnp.add, [fold(jnp.add, w) for w in weights])
    total = total * factor + jnp.sum(sums, axis=0, keepdims=True)
    rounded = jnp.concatenate([w.astype(jnp.bfloat16) for w in weights], axis=0)
    acc = acc * factor + jnp.dot(values, rounded, preferred_element_type=jnp.float32)
    return new_top, total, acc


def load_state(acc_ref, stat_ref, index):
    both = stat_ref[index]
    return both[0:1], both[1:2], acc_ref[index]


def store_state(acc_ref, stat_ref, index, state):
    top, total, acc = state
    stat_ref[index] = jnp.concatenate([top, total] + [total] * 6, axis=0)
    acc_ref[index] = acc


def start_all(copies):
    for copy in copies:
        copy.start()
    return copies


def weight_copies(weight_ref, target, sems, sibling):
    chips, _, share = target.shape
    place = lax.axis_index("tp")
    chip, core = place // CORES, place % CORES
    held = 1 - core if sibling else core
    copies = []
    for k in range(chips):
        start = (lax.rem(chip + k, chips) * CORES + held) * share
        copies.append(
            pltpu.make_async_copy(
                weight_ref.at[:, pl.ds(pl.multiple_of(start, HD), share)],
                target.at[k],
                sems.at[k],
            )
        )
    return copies


def first_kernel(
    cont,
    lists_ref,
    counts_ref,
    keys_ref,
    values_ref,
    queries_ref,
    cont_keys_ref,
    cont_values_ref,
    acc_ref,
    stat_ref,
    q_ref,
    flipped_ref,
    rows_ref,
    ck_ref,
    cv_ref,
    own_ref,
    sems,
):
    heads, _, length = q_ref.shape
    lanes = group_lanes(heads)
    copies = start_all(
        [
            pltpu.make_async_copy(cont_values_ref.at[cont, :, lanes], cv_ref, sems.at[0]),
            pltpu.make_async_copy(cont_keys_ref.at[cont, :, lanes], ck_ref, sems.at[1]),
            pltpu.make_async_copy(queries_ref.at[cont], rows_ref, sems.at[2]),
        ]
    )
    own = lax.axis_index("ctx")
    both_ways([values_ref], flipped_ref)
    copies[0].wait()
    own_ref[...] = cv_ref[...].T
    copies[1].wait()
    copies[2].wait()
    for head in range(heads):
        q_ref[head] = rows_ref[:, head * HD : (head + 1) * HD].T

    def some_heads(index, carry):
        work = [index * TOGETHER + j for j in range(TOGETHER)]
        made = []
        for head in work:
            scores = jnp.dot(ck_ref[...], q_ref[head], preferred_element_type=jnp.float32)
            key = lax.broadcasted_iota(jnp.int32, scores.shape, 0)
            row = lax.broadcasted_iota(jnp.int32, scores.shape, 1)
            scores = jnp.where(key <= row, scores, VERY_LOW)
            tiles, values = shard_scores(
                lists_ref, counts_ref, {cont: q_ref}, keys_ref, flipped_ref, own, head, cont
            )
            made.append(
                ([(scores, True)] + tiles, jnp.concatenate([own_ref[...], values], axis=1))
            )
        states = []
        for got in made:
            start = (
                jnp.full((1, length), VERY_LOW, jnp.float32),
                jnp.zeros((1, length), jnp.float32),
                jnp.zeros((HD, length), jnp.float32),
            )
            states.append(absorb(start, *got))
        for head, state in zip(work, states):
            store_state(acc_ref, stat_ref, head, state)
        return carry

    lax.fori_loop(0, heads // TOGETHER, some_heads, 0)


def arrivals(step, sources):
    spot = lax.axis_index("ctx")
    core = lax.axis_index("tp") % CORES
    if sources == 4:
        if step == 1:
            mine = jnp.bitwise_xor(spot, 1 + core)
            return ((mine, True), (jnp.bitwise_xor(mine, 3), True))
        far = jnp.bitwise_xor(spot, 3)
        return ((far, core == 1), (far, core == 0))
    mine = jnp.where(core == 0, spot - step, spot + step)
    theirs = jnp.where(core == 0, spot + step, spot - step)
    return tuple((s, (s >= 0) & (s < sources)) for s in (mine, theirs))


def steps_of(sources):
    return 2 if sources == 4 else sources - 1


def absorb_shard(
    source, lists_ref, counts_ref, q_refs, keys_ref, values_refs, flipped_ref, before, after
):
    heads = next(iter(q_refs.values())).shape[0]
    together = TOGETHER // len(q_refs)
    both_ways(values_refs, flipped_ref)

    def some_heads(index, carry):
        work = [(index * together + j, cont) for j in range(together) for cont in q_refs]
        states = [load_state(*before[cont], head) for head, cont in work]
        made = [
            shard_scores(lists_ref, counts_ref, q_refs, keys_ref, flipped_ref, source, head, cont)
            for head, cont in work
        ]
        states = [absorb(state, *got) for state, got in zip(states, made)]
        for (head, cont), state in zip(work, states):
            store_state(*after[cont], head, state)
        return carry

    lax.fori_loop(0, heads // together, some_heads, 0)


def hand_on(before, after):
    for source_ref, target_ref in zip(before, after):
        target_ref[...] = source_ref[...]


def by_cont(refs):
    return {cont: refs[2 * cont : 2 * cont + 2] for cont in range(len(refs) // 2)}


def middle_kernel(
    step, part, sources, conts, pieces, with_weight, lists_ref, counts_ref, *refs
):
    q_refs, refs = dict(enumerate(refs[:conts])), refs[conts:]
    keys_ref, values_refs, refs = refs[0], refs[1 : 1 + pieces], refs[1 + pieces :]
    before, refs = refs[: 2 * conts], refs[2 * conts :]
    if with_weight:
        weight_ref, *refs = refs
    after, refs = refs[: 2 * conts], refs[2 * conts :]
    if with_weight:
        give_ref, flipped_ref, sems = refs
        copies = start_all(weight_copies(weight_ref, give_ref, sems, True))
    else:
        (flipped_ref,) = refs
    source, valid = arrivals(step, sources)[part]

    def absorb_part():
        shard = (source, lists_ref, counts_ref, q_refs, keys_ref, values_refs, flipped_ref)
        absorb_shard(*shard, by_cont(before), by_cont(after))

    if valid is True:
        absorb_part()
    else:
        pl.when(valid)(absorb_part)
        pl.when(jnp.logical_not(valid))(lambda: hand_on(before, after))
    if with_weight:
        for copy in copies:
            copy.wait()


def finish_and_give(acc_ref, stat_ref, weight_ref, attended_ref, give_ref):
    for head in range(attended_ref.shape[1] // HD):
        _, total, acc = load_state(acc_ref, stat_ref, head)
        attended_ref[:, head * HD : (head + 1) * HD] = (acc / total).T.astype(jnp.bfloat16)
    for k in range(weight_ref.shape[0]):
        give_ref[k] = jnp.dot(
            attended_ref[...], weight_ref[k], preferred_element_type=jnp.float32
        ).astype(give_ref.dtype)


def last_kernel(
    step,
    sources,
    cont,
    lists_ref,
    counts_ref,
    q_ref,
    mine_keys_ref,
    mine_values_ref,
    their_keys_ref,
    their_values_ref,
    acc_in,
    stat_in,
    give_weight_ref,
    *refs,
):
    if cont == 0:
        weight_ref, attended_ref, give_ref, keep_weight_ref, *refs, sems = refs
        copies = start_all(weight_copies(weight_ref, keep_weight_ref, sems, False))
    else:
        attended_ref, give_ref, *refs = refs
    acc_ref, stat_ref, flipped_ref = refs
    before, after = (acc_in, stat_in), (acc_ref, stat_ref)
    held = (mine_keys_ref, [mine_values_ref]), (their_keys_ref, [their_values_ref])
    parts = arrivals(step, sources)
    one_of_two = sources == 4
    for part, (source, valid) in enumerate(parts):

        def absorb_part():
            shard = (source, lists_ref, counts_ref, {cont: q_ref}, *held[part], flipped_ref)
            first = part == 0 or one_of_two
            absorb_shard(*shard, {cont: before if first else after}, {cont: after})

        pl.when(valid)(absorb_part)
        if part == 0 and not one_of_two:
            pl.when(jnp.logical_not(valid))(lambda: hand_on(before, after))
    finish_and_give(acc_ref, stat_ref, give_weight_ref, attended_ref, give_ref)
    if cont == 0:
        for copy in copies:
            copy.wait()


def onward_kernel(attended_ref, weight_ref, got_ref, *onward_refs):
    for k, onward_ref in enumerate(onward_refs, 1):
        onward_ref[...] = (
            jnp.dot(attended_ref[...], weight_ref[k], preferred_element_type=jnp.float32)
            + got_ref[k].astype(jnp.float32)
        ).astype(jnp.bfloat16)


def near_kernel(cont, attended_ref, weight_ref, got_ref, residual_ref, near_ref, own_ref, sem):
    share = near_ref.shape[1]
    start = pl.multiple_of(lax.axis_index("tp") * share, HD)
    copy = pltpu.make_async_copy(
        residual_ref.at[cont, :, pl.ds(start, share)], own_ref, sem.at[0]
    )
    copy.start()
    near_ref[...] = jnp.dot(
        attended_ref[...], weight_ref[0], preferred_element_type=jnp.float32
    ) + got_ref[0].astype(jnp.float32)
    copy.wait()
    near_ref[...] += own_ref[...].astype(jnp.float32)


def sum_kernel(count, *refs):
    near_ref, fars, (total_ref, squares_ref) = refs[0], refs[1 : 1 + count], refs[1 + count :]
    total = near_ref[...]
    for far_ref in fars:
        total = total + far_ref[...].astype(jnp.float32)
    total_ref[...] = total
    sums = jnp.sum(total * total, axis=1, keepdims=True)
    squares_ref[...] = jnp.broadcast_to(sums, (sums.shape[0], HD)).T[:8]


def norm_kernel(conts, members, model_width, *refs):
    totals, squares = refs[:conts], refs[conts : conts + members]
    gain_ref, stream_ref, normed_ref = refs[conts + members :]
    gain = gain_ref[...].astype(jnp.float32)
    for cont in range(conts):
        row = functools.reduce(jnp.add, [ref[cont * 8 : cont * 8 + 1, :] for ref in squares])
        scale = lax.rsqrt(row / model_width + 1e-05)
        scale = jnp.broadcast_to(scale, (HD, scale.shape[1])).T[:, 0:1]
        total = totals[cont][...]
        stream_ref[cont] = total.astype(jnp.bfloat16)
        normed_ref[cont] = (total * scale * gain).astype(jnp.bfloat16)


def shards(
    queries,
    cont_keys,
    cont_values,
    prompt_keys,
    prompt_values,
    block_lists,
    tile_counts,
    out_weight,
    residual,
    norm_gain,
    *,
    sources,
    members,
):
    conts, length, width = queries.shape
    heads = width // HD
    rows_dev = prompt_keys.shape[0]
    model_width = residual.shape[2]
    share = norm_gain.shape[0]
    chips = members // CORES
    place = lax.axis_index("tp")
    pairs = heads * conts
    params = pltpu.CompilerParams(vmem_limit_bytes=VMEM_LIMIT)
    smem = pl.BlockSpec(memory_space=pltpu.SMEM)
    vmem = pl.BlockSpec(memory_space=pltpu.VMEM)
    hbm = pl.BlockSpec(memory_space=pltpu.HBM)

    def array(shape, dtype):
        return jax.ShapeDtypeStruct(shape, dtype)

    def cost(flops=1024):
        return pl.CostEstimate(flops=flops, bytes_accessed=1024, transcendentals=0)

    def in_hbm(x):
        return pltpu.with_memory_space_constraint(x, pltpu.HBM)

    kept = array((rows_dev, HD), jnp.bfloat16)
    keys = pl.pallas_call(
        functools.partial(pack_keys_kernel, heads),
        out_shape=kept,
        in_specs=[hbm],
        out_specs=vmem,
        scratch_shapes=[pltpu.SemaphoreType.DMA((1,))],
        compiler_params=params,
        cost_estimate=cost(),
        name="pack_keys",
    )(in_hbm(prompt_keys))
    values = pl.pallas_call(
        functools.partial(pack_values_kernel, heads),
        out_shape=kept,
        in_specs=[hbm],
        out_specs=vmem,
        scratch_shapes=[
            pltpu.VMEM((rows_dev, HD), jnp.bfloat16),
            pltpu.SemaphoreType.DMA((1,)),
        ],
        compiler_params=params,
        cost_estimate=cost(),
        name="pack_values",
    )(in_hbm(prompt_values))

    def across(step):
        def target(z, t):
            if sources == 4 and step == 1:
                return z ^ (1 + t % CORES)
            if sources == 4:
                return z ^ 1 if t % CORES == 1 else None
            to = z + step if t % CORES == 0 else z - step
            return to if 0 <= to < sources else None

        return [
            (z * members + t, target(z, t) * members + t)
            for z in range(sources)
            for t in range(members)
            if target(z, t) is not None
        ]

    sibling = [(t, t ^ 1) for t in range(members)]
    steps = steps_of(sources)
    lists = in_hbm(block_lists)
    counts = in_hbm(tile_counts.transpose(1, 2, 0))
    state_shape = (
        array((heads, HD, length), jnp.float32),
        array((heads, 8, length), jnp.float32),
    )
    flipped = pltpu.VMEM((2 * rows_dev, HD), jnp.bfloat16)
    weight_shape = array((chips, width, share), jnp.bfloat16)

    def attend_own(cont, keys):
        *state, q = pl.pallas_call(
            functools.partial(first_kernel, cont),
            out_shape=state_shape + (array((heads, HD, length), jnp.bfloat16),),
            in_specs=[smem, smem, vmem, vmem] + [hbm] * 3,
            out_specs=(vmem,) * 3,
            scratch_shapes=[
                flipped,
                pltpu.VMEM((length, width), jnp.bfloat16),
                pltpu.VMEM((length, HD), jnp.bfloat16),
                pltpu.VMEM((length, HD), jnp.bfloat16),
                pltpu.VMEM((HD, length), jnp.bfloat16),
                pltpu.SemaphoreType.DMA((3,)),
            ],
            compiler_params=params,
            cost_estimate=cost(),
            name="attend_own",
        )(
            lists,
            counts,
            keys,
            values,
            in_hbm(queries),
            in_hbm(cont_keys),
            in_hbm(cont_values),
        )
        return tuple(state), q

    def attend_step(step, part, with_weight, states, held):
        flat = [x for state in states for x in state]
        made = pl.pallas_call(
            functools.partial(
                middle_kernel, step, part, sources, conts, len(held) - 1, with_weight
            ),
            out_shape=state_shape * conts + ((weight_shape,) if with_weight else ()),
            in_specs=[smem, smem] + [vmem] * (3 * conts + len(held)) + [hbm] * with_weight,
            out_specs=(vmem,) * (2 * conts + with_weight),
            scratch_shapes=[flipped] + [pltpu.SemaphoreType.DMA((chips,))] * with_weight,
            compiler_params=params,
            cost_estimate=cost(),
            name="attend_step",
        )(lists, counts, *qs, *held, *flat, *([in_hbm(out_weight)] * with_weight))
        return tuple(made[2 * c : 2 * c + 2] for c in range(conts)), made[2 * conts :]

    states, qs = [], []
    for step in range(1, steps + 1):
        sent = mine if sources == 4 and step == 2 else (keys, values)
        mine_keys, mine_values = [lax.ppermute(x, ("ctx", "tp"), across(step)) for x in sent]
        own_keys = keys
        if step == 1:
            state, q = attend_own(0, keys)
            states.append(state)
            qs.append(q)
        mine_keys, own_keys, states = lax.optimization_barrier(
            (mine_keys, own_keys, tuple(states))
        )
        if step == 1:
            states = list(states)
            for cont in range(1, conts):
                state, q = attend_own(cont, own_keys)
                states.append(state)
                qs.append(q)
        their_keys = lax.ppermute(mine_keys, "tp", sibling)
        mine_values, states = lax.optimization_barrier((mine_values, tuple(states)))
        their_values = [
            lax.ppermute(x, "tp", sibling)
            for x in jnp.split(mine_values, 2 if step < steps else 1)
        ]
        mine, theirs = (mine_keys, mine_values), (their_keys, *their_values)
        if step < steps:
            states, (give_weight,) = attend_step(step, 0, True, states, mine)
            states, _ = attend_step(step, 1, False, states, theirs)

    def attend_last(cont):
        fetch = cont == 0
        return pl.pallas_call(
            functools.partial(last_kernel, steps, sources, cont),
            out_shape=(
                array((length, width), jnp.bfloat16),
                array((chips, length, share), jnp.bfloat16),
            )
            + (weight_shape,) * fetch,
            in_specs=[smem, smem] + [vmem] * 8 + [hbm] * fetch,
            out_specs=(vmem,) * (2 + fetch),
            scratch_shapes=[pltpu.VMEM(a.shape, a.dtype) for a in state_shape]
            + [flipped]
            + [pltpu.SemaphoreType.DMA((chips,))] * fetch,
            compiler_params=params,
            cost_estimate=cost(),
            name="attend_last",
        )(
            lists,
            counts,
            qs[cont],
            *mine,
            *theirs,
            *states[cont],
            give_weight,
            *([in_hbm(out_weight)] * fetch),
        )

    def onward(attended, got):
        parts = pl.pallas_call(
            onward_kernel,
            out_shape=(array((length, share), jnp.bfloat16),) * (chips - 1),
            in_specs=[vmem] * 3,
            out_specs=(vmem,) * (chips - 1),
            compiler_params=params,
            cost_estimate=cost(),
            name="project_onward",
        )(attended, keep_weight, got)
        far = []
        for k in range(1, chips):
            to_chip = [
                (t, (t // CORES + k) % chips * CORES + t % CORES) for t in range(members)
            ]
            far.append(lax.ppermute(parts[k - 1], "tp", to_chip))
        return parts, far

    def near(cont, attended, got):
        return pl.pallas_call(
            functools.partial(near_kernel, cont),
            out_shape=array((length, share), jnp.float32),
            in_specs=[vmem] * 3 + [hbm],
            out_specs=vmem,
            scratch_shapes=[
                pltpu.VMEM((length, share), jnp.bfloat16),
                pltpu.SemaphoreType.DMA((1,)),
            ],
            compiler_params=params,
            cost_estimate=cost(),
            name="project_near",
        )(attended, keep_weight, got, in_hbm(residual))

    attended, give, keep_weight = attend_last(0)
    nears, fars = [], []
    for cont in range(conts):
        got = lax.ppermute(give, "tp", sibling)
        here = attended
        if cont + 1 < conts:
            attended, give = attend_last(cont + 1)
            got, give = lax.optimization_barrier((got, give))
        _, far = onward(here, got)
        fars.append(far)
        nears.append(near(cont, here, got))

    totals, squares = [], []
    for cont in range(conts):
        total, square = pl.pallas_call(
            functools.partial(sum_kernel, chips - 1),
            out_shape=(array((length, share), jnp.float32), array((8, length), jnp.float32)),
            in_specs=[vmem] * chips,
            out_specs=(vmem,) * 2,
            compiler_params=params,
            cost_estimate=cost(),
            name="add_up",
        )(nears[cont], *fars[cont])
        totals.append(total)
        squares.append(square)
    squares = jnp.concatenate(squares, axis=0)
    all_squares = [squares] + [
        lax.ppermute(squares, "tp", [(t, (t + k) % members) for t in range(members)])
        for k in range(1, members)
    ]
    out = array((conts, length, share), jnp.bfloat16)
    return pl.pallas_call(
        functools.partial(norm_kernel, conts, members, model_width),
        out_shape=(out, out),
        in_specs=[vmem] * (conts + members + 1),
        out_specs=(vmem, vmem),
        compiler_params=params,
        cost_estimate=cost(),
        name="norm",
    )(*totals, *all_squares, norm_gain.reshape(1, share))


def solution(mesh):
    placed = (
        P(("grp", "ctx"), None, "tp"),
        P(("grp", "ctx"), None, None),
        P(("grp", "ctx"), None, None),
        P(("grp", "ctx"), None),
        P(("grp", "ctx"), None),
        P("tp", ("grp", "ctx"), None, None),
        P("tp", ("grp", "ctx"), None),
        P("tp", None),
        P(("grp", "ctx"), None, None),
        P("tp"),
    )
    return jax.shard_map(
        functools.partial(
            shards, sources=mesh.shape["ctx"], members=mesh.shape["tp"]
        ),
        mesh=mesh,
        in_specs=placed,
        out_specs=(P(("grp", "ctx"), None, "tp"), P(("grp", "ctx"), None, "tp")),
        check_vma=False,
    )
```

time: 57.6 us -> 62.6 us (1.087); the launches traced: 57.3 us -> 61.5 us
  Pallas kernels: 24 us -> 31.3 us
  waiting for transfers between devices: 18.3 us -> 13 us
  starting transfers between devices: 12.4 us -> 16.4 us
  local copies, waits for them, and re-layouts: 1.74 us -> 0.04 us
    pallas_call x6 -> x8, Pallas kernels: 18.9 us -> 26.2 us  [the longest x2 8.8 us: attend_step(): pl.pallas_call(functools.partial(middle_kernel, step, part, sources, cont...]
    ppermute x4 -> x9, waiting for transfers between devices: 8.12 us -> 3.53 us  [the longest x4 2.07 us: shards(): lax.ppermute(x, ('ctx', 'tp'), across(step))]
    ppermute x4 -> x9, starting transfers between devices: 6.73 us -> 9.94 us  [the longest x3 4.78 us: shards(): lax.ppermute(x, 'tp', sibling)]
    ppermute x3, waiting for transfers between devices: 2.41 us -> 1.36 us  [shards(): lax.ppermute(squares, 'tp', [(t, (t + k) % members) for t in range(member...]
    ppermute x3, starting transfers between devices: 2.01 us -> 2.96 us  [shards(): lax.ppermute(squares, 'tp', [(t, (t + k) % members) for t in range(member...]
    reshape x2 -> x0, local copies, waits for them, and re-layouts: 0.95 us -> none  [the longest x1 0.86 us: shards(): lists = block_lists.reshape(-1)]
    unnamed x4 -> x3, local copies, waits for them, and re-layouts: 0.78 us -> 0.01 us
  transfers between devices with their start and end apart: 11 -> 16, of which waited for: 8 -> 9; matrix products, arithmetic and copies ran while one was open for 3% -> 0% of each run, Pallas kernels for 30% -> 41%
where the time goes in v5:
time: 62.6 us; the launch traced here: 61.5 us
  Pallas kernels  31.3 us (50%)
  starting transfers between devices  16.4 us (26%)
  waiting for transfers between devices  13 us (21%)
  between operations  0.81 us (1%)
    pallas_call x2, Pallas kernels, attend_step(): pl.pallas_call(functools.partial(middle_kernel, step, part, sources, cont...  8.8 us
    ppermute x2, waiting for transfers between devices, onward(): far.append(lax.ppermute(parts[k - 1], 'tp', to_chip))  8.08 us
    pallas_call x2, Pallas kernels, attend_own(): pl.pallas_call(functools.partial(first_kernel, cont), out_shape=state_sha...  7.89 us
    pallas_call x2, Pallas kernels, attend_last(): pl.pallas_call(functools.partial(last_kernel, steps, sources, cont), out_...  7.42 us
    ppermute x3, starting transfers between devices, shards(): lax.ppermute(x, 'tp', sibling)  4.78 us
    ppermute x4, starting transfers between devices, shards(): lax.ppermute(x, ('ctx', 'tp'), across(step))  4.51 us
    ppermute x3, starting transfers between devices, shards(): lax.ppermute(squares, 'tp', [(t, (t + k) % members) for t in range(member...  2.96 us
    ppermute x2, starting transfers between devices, onward(): far.append(lax.ppermute(parts[k - 1], 'tp', to_chip))  2.87 us
  transfers between devices with their start and end apart: 16, of which 9 were waited for; matrix products, arithmetic and copies ran while one was open for 0% of the time, Pallas kernels for 41%

profile of v5, /device:TPU:0, one launch (start us, length us, event | category | flops | bytes accessed | tf_op | source)
XLA Modules:
  0.0 61.5 jit_solution(13198986610472702967)
XLA Ops:
  0.6 1.0 %pack_keys.1.keys_ref = bf16[1024,128]{1,0:T(8,128)(2,1)S(1)} custom-call(bf16[1024,256]{1,0:T(8,128)(2,1)} %keys_ref.1), custom_call_target="tpu_custom_call" | custom-call | flops 1024 | bytes 1024 | tf_op jit(solution)/shard_map/pack_keys/pallas_call | solution.py:420
  1.6 3.1 %collective-permute-start = (bf16[1024,128]{1,0:T(8,128)(2,1)S(1)}, bf16[1024,128]{1,0:T(8,128)(2,1)S(1)}, u32[]{:S(2)}, u32[]{:S(2)}) collective-permute-start(bf16[1024,128]{1,0:T(8,128)(2,1)S(1)} %pack_keys.1.keys_ref), channel_id=1, source_target_pairs={{0,4},{1,9},{2,6},{3,11},{4,0},{5,13},{6,2},{7,15},{8,12},{9,1},{1... | collective-permute-start | bytes 786440 | tf_op jit(solution)/shard_map/ppermute | solution.py:518
  4.7 1.1 %pack_values.1.values_ref = bf16[1024,128]{1,0:T(8,128)(2,1)S(1)} custom-call(bf16[1024,256]{1,0:T(8,128)(2,1)} %values_ref.1), custom_call_target="tpu_custom_call" | custom-call | flops 1024 | bytes 1024 | tf_op jit(solution)/shard_map/pack_values/pallas_call | solution.py:430
  5.9 3.9 %attend_own.2 = (f32[8,128,128]{2,1,0:T(8,128)S(1)}, f32[8,8,128]{2,1,0:T(8,128)S(1)}, bf16[8,128,128]{2,1,0:T(8,128)(2,1)S(1)}) custom-call(s32[8,2,4,8]{3,2,1,0:T(4,128)} %lists_ref.11, s32[2,4,8]{2,1,0:T(4,128)} %bitcast.1, bf16[1024,128]{1,0:T(8,128)(2,1)S(1)} %pack_keys.1.keys_ref, bf16[1024,128]{1,0:T(8,128)(2,1)S(1)} %pack_values.1.values_ref, ...), custom_call_target="tpu_custom_call" | custom-call | flops 1024 | bytes 1024 | tf_op jit(solution)/shard_map/attend_own/pallas_call | solution.py:472
  9.8 1.6 %collective-permute-done.refs_2_ = bf16[1024,128]{1,0:T(8,128)(2,1)S(1)} collective-permute-done((bf16[1024,128]{1,0:T(8,128)(2,1)S(1)}, bf16[1024,128]{1,0:T(8,128)(2,1)S(1)}, u32[]{:S(2)}, u32[]{:S(2)}) %collective-permute-start) | collective-permute-done | bytes 262176 | tf_op jit(solution)/shard_map/ppermute | solution.py:518
  12.1 0.7 %collective-permute-start.1 = (bf16[1024,128]{1,0:T(8,128)(2,1)S(1)}, bf16[1024,128]{1,0:T(8,128)(2,1)S(1)}, u32[]{:S(2)}, u32[]{:S(2)}) collective-permute-start(bf16[1024,128]{1,0:T(8,128)(2,1)S(1)} %collective-permute-done.refs_2_), channel_id=1, source_target_pairs={{1,5},{3,7},{5,1},{7,3},{9,13},{11,15},{13,9},{15,11},{17,21},{19,... | collective-permute-start | bytes 786440 | tf_op jit(solution)/shard_map/ppermute | solution.py:518
  12.7 3.9 %attend_own.3 = (f32[8,128,128]{2,1,0:T(8,128)S(1)}, f32[8,8,128]{2,1,0:T(8,128)S(1)}, bf16[8,128,128]{2,1,0:T(8,128)(2,1)S(1)}) custom-call(s32[8,2,4,8]{3,2,1,0:T(4,128)} %lists_ref.11, s32[2,4,8]{2,1,0:T(4,128)} %bitcast.2, bf16[1024,128]{1,0:T(8,128)(2,1)S(1)} %pack_keys.1.keys_ref, bf16[1024,128]{1,0:T(8,128)(2,1)S(1)} %pack_values.1.values_ref, ...), custom_call_target="tpu_custom_call" | custom-call | flops 1024 | bytes 1024 | tf_op jit(solution)/shard_map/attend_own/pallas_call | solution.py:472
  17.1 0.7 %collective-permute-start.6 = (bf16[1024,128]{1,0:T(8,128)(2,1)S(1)}, bf16[1024,128]{1,0:T(8,128)(2,1)S(1)}, u32[]{:S(2)}, u32[]{:S(2)}) collective-permute-start(bf16[1024,128]{1,0:T(8,128)(2,1)S(1)} %collective-permute-done.3.refs_3_), channel_id=1, source_target_pairs={{1,5},{3,7},{5,1},{7,3},{9,13},{11,15},{13,9},{15,11},{17,21},{19,... | collective-permute-start | bytes 786440 | tf_op jit(solution)/shard_map/ppermute | solution.py:518
  17.8 4.2 %collective-permute-start.4 = (bf16[512,128]{1,0:T(8,128)(2,1)S(1)}, bf16[512,128]{1,0:T(8,128)(2,1)S(1)}, u32[]{:S(2)}, u32[]{:S(2)}) collective-permute-start(bf16[512,128]{1,0:T(8,128)(2,1)S(1)} %get-tuple-element.93), channel_id=1, source_target_pairs={{0,1},{1,0},{2,3},{3,2},{4,5},{5,4},{6,7},{7,6},{8,9},{9,8},{10,11... | collective-permute-start | bytes 393224 | tf_op jit(solution)/shard_map/ppermute | solution.py:536
  22.1 4.4 %attend_step.2 = (f32[8,128,128]{2,1,0:T(8,128)S(1)}, f32[8,8,128]{2,1,0:T(8,128)S(1)}, f32[8,128,128]{2,1,0:T(8,128)S(1)}, f32[8,8,128]{2,1,0:T(8,128)S(1)}, bf16[2,1024,1024]{2,1,0:T(8,128)(2,1)S(1)}) custom-call(s32[8,2,4,8]{3,2,1,0:T(4,128)} %lists_ref.11, s32[2,4,8]{2,1,0:T(4,128)} %bitcast.3, bf16[8,128,128]{2,1,0:T(8,128)(2,1)S(1)} %get-tuple-element.47.refs_0_.q_ref, ...), custom_call_target="tpu_custom_call" | custom-call | flops 1024 | bytes 1024 | tf_op jit(solution)/shard_map/attend_step/pallas_call | solution.py:501
  26.5 4.4 %attend_step.3 = (f32[8,128,128]{2,1,0:T(8,128)S(1)}, f32[8,8,128]{2,1,0:T(8,128)S(1)}, f32[8,128,128]{2,1,0:T(8,128)S(1)}, f32[8,8,128]{2,1,0:T(8,128)S(1)}) custom-call(s32[8,2,4,8]{3,2,1,0:T(4,128)} %lists_ref.11, s32[2,4,8]{2,1,0:T(4,128)} %bitcast.4, bf16[8,128,128]{2,1,0:T(8,128)(2,1)S(1)} %get-tuple-element.47.refs_0_.q_ref, ...), custom_call_target="tpu_custom_call" | custom-call | flops 1024 | bytes 1024 | tf_op jit(solution)/shard_map/attend_step/pallas_call | solution.py:501
  31.5 1.1 %collective-permute-done.8.their_values_ref = bf16[1024,128]{1,0:T(8,128)(2,1)S(1)} collective-permute-done((bf16[1024,128]{1,0:T(8,128)(2,1)S(1)}, bf16[1024,128]{1,0:T(8,128)(2,1)S(1)}, u32[]{:S(2)}, u32[]{:S(2)}) %collective-permute-start.8) | collective-permute-done | bytes 262176 | tf_op jit(solution)/shard_map/ppermute | solution.py:536
  33.0 3.7 %attend_last.2 = (bf16[128,1024]{1,0:T(8,128)(2,1)S(1)}, bf16[2,128,1024]{2,1,0:T(8,128)(2,1)S(1)}, bf16[2,1024,1024]{2,1,0:T(8,128)(2,1)S(1)}) custom-call(s32[8,2,4,8]{3,2,1,0:T(4,128)} %lists_ref.11, s32[2,4,8]{2,1,0:T(4,128)} %bitcast.5, bf16[8,128,128]{2,1,0:T(8,128)(2,1)S(1)} %get-tuple-element.47.refs_0_.q_ref, ...), custom_call_target="tpu_custom_call" | custom-call | flops 1024 | bytes 1024 | tf_op jit(solution)/shard_map/attend_last/pallas_call | solution.py:546
  37.1 3.7 %attend_last.3 = (bf16[128,1024]{1,0:T(8,128)(2,1)S(1)}, bf16[2,128,1024]{2,1,0:T(8,128)(2,1)S(1)}) custom-call(s32[8,2,4,8]{3,2,1,0:T(4,128)} %lists_ref.11, s32[2,4,8]{2,1,0:T(4,128)} %bitcast.6, bf16[8,128,128]{2,1,0:T(8,128)(2,1)S(1)} %get-tuple-element.52.refs_1_.q_ref, bf16[1024,128]{1,0:T(8,128)(2,1)S(1)} %collective-permute-done.1.mine_keys_ref, ...), custom_call_target="tpu_custom_call" | custom-call | flops 1024 | bytes 1024 | tf_op jit(solution)/shard_map/attend_last/pallas_call | solution.py:546
  41.5 1.6 %collective-permute-start.10 = (bf16[128,1024]{1,0:T(8,128)(2,1)S(1)}, bf16[128,1024]{1,0:T(8,128)(2,1)S(1)}, u32[]{:S(2)}, u32[]{:S(2)}) collective-permute-start(bf16[128,1024]{1,0:T(8,128)(2,1)S(1)} %project_onward.2), channel_id=1, source_target_pairs={{0,2},{1,3},{2,0},{3,1},{4,6},{5,7},{6,4},{7,5},{8,10},{9,11},{10,... | collective-permute-start | bytes 786440 | tf_op jit(solution)/shard_map/ppermute | solution.py:587
  43.6 1.3 %collective-permute-start.12 = (bf16[128,1024]{1,0:T(8,128)(2,1)S(1)}, bf16[128,1024]{1,0:T(8,128)(2,1)S(1)}, u32[]{:S(2)}, u32[]{:S(2)}) collective-permute-start(bf16[128,1024]{1,0:T(8,128)(2,1)S(1)} %project_onward.3), channel_id=1, source_target_pairs={{0,2},{1,3},{2,0},{3,1},{4,6},{5,7},{6,4},{7,5},{8,10},{9,11},{10,... | collective-permute-start | bytes 786440 | tf_op jit(solution)/shard_map/ppermute | solution.py:587
  44.9 1.3 %project_near.2.refs_0_ = f32[128,1024]{1,0:T(8,128)S(1)} custom-call(bf16[128,1024]{1,0:T(8,128)(2,1)S(1)} %get-tuple-element.79.attended_ref, bf16[2,1024,1024]{2,1,0:T(8,128)(2,1)S(1)} %get-tuple-element.80.weight_ref, bf16[2,128,1024]{2,1,0:T(8,128)(2,1)S(1)} %collective-permute-done.9.got_ref, bf16[2,128,4096]{2,1,0:T(8,128)(2,1)} %residual_ref.3), custom_call_target="tpu_custom_call" | custom-call | flops 1024 | bytes 1024 | tf_op jit(solution)/shard_map/project_near/pallas_call | solution.py:591
  46.2 4.5 %collective-permute-done.10.refs_1_ = bf16[128,1024]{1,0:T(8,128)(2,1)S(1)} collective-permute-done((bf16[128,1024]{1,0:T(8,128)(2,1)S(1)}, bf16[128,1024]{1,0:T(8,128)(2,1)S(1)}, u32[]{:S(2)}, u32[]{:S(2)}) %collective-permute-start.10) | collective-permute-done | bytes 262176 | tf_op jit(solution)/shard_map/ppermute | solution.py:587
  50.9 1.3 %project_near.3.refs_0_ = f32[128,1024]{1,0:T(8,128)S(1)} custom-call(bf16[128,1024]{1,0:T(8,128)(2,1)S(1)} %get-tuple-element.87.attended_ref, bf16[2,1024,1024]{2,1,0:T(8,128)(2,1)S(1)} %get-tuple-element.80.weight_ref, bf16[2,128,1024]{2,1,0:T(8,128)(2,1)S(1)} %collective-permute-done.11.got_ref, bf16[2,128,4096]{2,1,0:T(8,128)(2,1)} %residual_ref.3), custom_call_target="tpu_custom_call" | custom-call | flops 1024 | bytes 1024 | tf_op jit(solution)/shard_map/project_near/pallas_call | solution.py:591
  52.2 3.5 %collective-permute-done.12.refs_1_ = bf16[128,1024]{1,0:T(8,128)(2,1)S(1)} collective-permute-done((bf16[128,1024]{1,0:T(8,128)(2,1)S(1)}, bf16[128,1024]{1,0:T(8,128)(2,1)S(1)}, u32[]{:S(2)}, u32[]{:S(2)}) %collective-permute-start.12) | collective-permute-done | bytes 262176 | tf_op jit(solution)/shard_map/ppermute | solution.py:587
  56.0 1.6 %collective-permute-start.14 = (f32[16,128]{1,0:T(8,128)S(1)}, f32[16,128]{1,0:T(8,128)S(1)}, u32[]{:S(2)}, u32[]{:S(2)}) collective-permute-start(f32[16,128]{1,0:T(8,128)S(1)} %constant_dynamic-update-slice_fusion.refs_2_), channel_id=1, source_target_pairs={{0,2},{1,3},{2,0},{3,1},{4,6},{5,7},{6,4},{7,5},{8,10},{9,11},{10,... | collective-permute-start | bytes 24584 | tf_op jit(solution)/shard_map/ppermute | solution.py:632
  57.6 1.4 %collective-permute-start.15 = (f32[16,128]{1,0:T(8,128)S(1)}, f32[16,128]{1,0:T(8,128)S(1)}, u32[]{:S(2)}, u32[]{:S(2)}) collective-permute-start(f32[16,128]{1,0:T(8,128)S(1)} %constant_dynamic-update-slice_fusion.refs_2_), channel_id=1, source_target_pairs={{0,3},{1,0},{2,1},{3,2},{4,7},{5,4},{6,5},{7,6},{8,11},{9,8},{10,9... | collective-permute-start | bytes 24584 | tf_op jit(solution)/shard_map/ppermute | solution.py:632
  59.1 0.7 %collective-permute-done.14.refs_4_ = f32[16,128]{1,0:T(8,128)S(1)} collective-permute-done((f32[16,128]{1,0:T(8,128)S(1)}, f32[16,128]{1,0:T(8,128)S(1)}, u32[]{:S(2)}, u32[]{:S(2)}) %collective-permute-start.14) | collective-permute-done | bytes 8224 | tf_op jit(solution)/shard_map/ppermute | solution.py:632
  60.3 1.2 %norm.1 = (bf16[2,128,1024]{2,1,0:T(8,128)(2,1)}, bf16[2,128,1024]{2,1,0:T(8,128)(2,1)}) custom-call(f32[128,1024]{1,0:T(8,128)S(1)} %get-tuple-element.86.refs_0_, f32[128,1024]{1,0:T(8,128)S(1)} %get-tuple-element.89.refs_1_, f32[16,128]{1,0:T(8,128)S(1)} %constant_dynamic-update-slice_fusion.refs_2_, f32[16,128]{1,0:T(8,128)S(1)} %collective-permute-done.13.refs_3_, ...), custom_call_target="tpu_custom_call" | custom-call | flops 1024 | bytes 1024 | tf_op jit(solution)/shard_map/norm/pallas_call | solution.py:636
  (29 shorter events, 4.8 us)
Async XLA Ops:
  1.6 9.9 %collective-permute-start = (bf16[1024,128]{1,0:T(8,128)(2,1)S(1)}, bf16[1024,128]{1,0:T(8,128)(2,1)S(1)}, u32[]{:S(2)}, u32[]{:S(2)}) collective-permute-start(bf16[1024,128]{1,0:T(8,128)(2,1)S(1)} %pack_keys.1.keys_ref), channel_id=1, source_target_pairs={{0,4},{1,9},{2,6},{3,11},{4,0},{5,13},{6,2},{7,15},{8,12},{9,1},{1... | collective-permute-start | bytes 786440 | tf_op jit(solution)/shard_map/ppermute | solution.py:518
  5.8 11.3 %collective-permute-start.3 = (bf16[1024,128]{1,0:T(8,128)(2,1)S(1)}, bf16[1024,128]{1,0:T(8,128)(2,1)S(1)}, u32[]{:S(2)}, u32[]{:S(2)}) collective-permute-start(bf16[1024,128]{1,0:T(8,128)(2,1)S(1)} %pack_values.1.values_ref), channel_id=1, source_target_pairs={{0,4},{1,9},{2,6},{3,11},{4,0},{5,13},{6,2},{7,15},{8,12},{9,1},{1... | collective-permute-start | bytes 786440 | tf_op jit(solution)/shard_map/ppermute | solution.py:518
  11.5 15.0 %collective-permute-start.2 = (bf16[1024,128]{1,0:T(8,128)(2,1)S(1)}, bf16[1024,128]{1,0:T(8,128)(2,1)S(1)}, u32[]{:S(2)}, u32[]{:S(2)}) collective-permute-start(bf16[1024,128]{1,0:T(8,128)(2,1)S(1)} %collective-permute-done.refs_2_), channel_id=1, source_target_pairs={{0,1},{1,0},{2,3},{3,2},{4,5},{5,4},{6,7},{7,6},{8,9},{9,8},{10,11... | collective-permute-start | bytes 786440 | tf_op jit(solution)/shard_map/ppermute | solution.py:533
  12.1 18.9 %collective-permute-start.1 = (bf16[1024,128]{1,0:T(8,128)(2,1)S(1)}, bf16[1024,128]{1,0:T(8,128)(2,1)S(1)}, u32[]{:S(2)}, u32[]{:S(2)}) collective-permute-start(bf16[1024,128]{1,0:T(8,128)(2,1)S(1)} %collective-permute-done.refs_2_), channel_id=1, source_target_pairs={{1,5},{3,7},{5,1},{7,3},{9,13},{11,15},{13,9},{15,11},{17,21},{19,... | collective-permute-start | bytes 786440 | tf_op jit(solution)/shard_map/ppermute | solution.py:518
  17.1 13.8 %collective-permute-start.6 = (bf16[1024,128]{1,0:T(8,128)(2,1)S(1)}, bf16[1024,128]{1,0:T(8,128)(2,1)S(1)}, u32[]{:S(2)}, u32[]{:S(2)}) collective-permute-start(bf16[1024,128]{1,0:T(8,128)(2,1)S(1)} %collective-permute-done.3.refs_3_), channel_id=1, source_target_pairs={{1,5},{3,7},{5,1},{7,3},{9,13},{11,15},{13,9},{15,11},{17,21},{19,... | collective-permute-start | bytes 786440 | tf_op jit(solution)/shard_map/ppermute | solution.py:518
  17.8 8.7 %collective-permute-start.4 = (bf16[512,128]{1,0:T(8,128)(2,1)S(1)}, bf16[512,128]{1,0:T(8,128)(2,1)S(1)}, u32[]{:S(2)}, u32[]{:S(2)}) collective-permute-start(bf16[512,128]{1,0:T(8,128)(2,1)S(1)} %get-tuple-element.93), channel_id=1, source_target_pairs={{0,1},{1,0},{2,3},{3,2},{4,5},{5,4},{6,7},{7,6},{8,9},{9,8},{10,11... | collective-permute-start | bytes 393224 | tf_op jit(solution)/shard_map/ppermute | solution.py:536
  22.0 4.5 %collective-permute-start.5 = (bf16[512,128]{1,0:T(8,128)(2,1)S(1)}, bf16[512,128]{1,0:T(8,128)(2,1)S(1)}, u32[]{:S(2)}, u32[]{:S(2)}) collective-permute-start(bf16[512,128]{1,0:T(8,128)(2,1)S(1)} %get-tuple-element.92), channel_id=1, source_target_pairs={{0,1},{1,0},{2,3},{3,2},{4,5},{5,4},{6,7},{7,6},{8,9},{9,8},{10,11... | collective-permute-start | bytes 393224 | tf_op jit(solution)/shard_map/ppermute | solution.py:536
  30.9 1.7 %collective-permute-start.8 = (bf16[1024,128]{1,0:T(8,128)(2,1)S(1)}, bf16[1024,128]{1,0:T(8,128)(2,1)S(1)}, u32[]{:S(2)}, u32[]{:S(2)}) collective-permute-start(bf16[1024,128]{1,0:T(8,128)(2,1)S(1)} %collective-permute-done.6.mine_values_ref), channel_id=1, source_target_pairs={{0,1},{1,0},{2,3},{3,2},{4,5},{5,4},{6,7},{7,6},{8,9},{9,8},{10,11... | collective-permute-start | bytes 786440 | tf_op jit(solution)/shard_map/ppermute | solution.py:536
  31.4 1.5 %collective-permute-start.7 = (bf16[1024,128]{1,0:T(8,128)(2,1)S(1)}, bf16[1024,128]{1,0:T(8,128)(2,1)S(1)}, u32[]{:S(2)}, u32[]{:S(2)}) collective-permute-start(bf16[1024,128]{1,0:T(8,128)(2,1)S(1)} %collective-permute-done.1.mine_keys_ref), channel_id=1, source_target_pairs={{0,1},{1,0},{2,3},{3,2},{4,5},{5,4},{6,7},{7,6},{8,9},{9,8},{10,11... | collective-permute-start | bytes 786440 | tf_op jit(solution)/shard_map/ppermute | solution.py:533
  36.7 4.1 %collective-permute-start.9 = (bf16[2,128,1024]{2,1,0:T(8,128)(2,1)S(1)}, bf16[2,128,1024]{2,1,0:T(8,128)(2,1)S(1)}, u32[]{:S(2)}, u32[]{:S(2)}) collective-permute-start(bf16[2,128,1024]{2,1,0:T(8,128)(2,1)S(1)} %get-tuple-element.81), channel_id=1, source_target_pairs={{0,1},{1,0},{2,3},{3,2},{4,5},{5,4},{6,7},{7,6},{8,9},{9,8},{10,11... | collective-permute-start | bytes 1572872 | tf_op jit(solution)/shard_map/ppermute | solution.py:608
  40.9 2.2 %collective-permute-start.11 = (bf16[2,128,1024]{2,1,0:T(8,128)(2,1)S(1)}, bf16[2,128,1024]{2,1,0:T(8,128)(2,1)S(1)}, u32[]{:S(2)}, u32[]{:S(2)}) collective-permute-start(bf16[2,128,1024]{2,1,0:T(8,128)(2,1)S(1)} %get-tuple-element.88), channel_id=1, source_target_pairs={{0,1},{1,0},{2,3},{3,2},{4,5},{5,4},{6,7},{7,6},{8,9},{9,8},{10,11... | collective-permute-start | bytes 1572872 | tf_op jit(solution)/shard_map/ppermute | solution.py:608
  41.5 9.2 %collective-permute-start.10 = (bf16[128,1024]{1,0:T(8,128)(2,1)S(1)}, bf16[128,1024]{1,0:T(8,128)(2,1)S(1)}, u32[]{:S(2)}, u32[]{:S(2)}) collective-permute-start(bf16[128,1024]{1,0:T(8,128)(2,1)S(1)} %project_onward.2), channel_id=1, source_target_pairs={{0,2},{1,3},{2,0},{3,1},{4,6},{5,7},{6,4},{7,5},{8,10},{9,11},{10,... | collective-permute-start | bytes 786440 | tf_op jit(solution)/shard_map/ppermute | solution.py:587
  43.6 12.2 %collective-permute-start.12 = (bf16[128,1024]{1,0:T(8,128)(2,1)S(1)}, bf16[128,1024]{1,0:T(8,128)(2,1)S(1)}, u32[]{:S(2)}, u32[]{:S(2)}) collective-permute-start(bf16[128,1024]{1,0:T(8,128)(2,1)S(1)} %project_onward.3), channel_id=1, source_target_pairs={{0,2},{1,3},{2,0},{3,1},{4,6},{5,7},{6,4},{7,5},{8,10},{9,11},{10,... | collective-permute-start | bytes 786440 | tf_op jit(solution)/shard_map/ppermute | solution.py:587
  50.9 8.0 %copy-start = (bf16[1024]{0:T(1024)(128)(2,1)S(1)}, bf16[1024]{0:T(1024)(128)(2,1)}, u32[]{:S(2)}) copy-start(bf16[1024]{0:T(1024)(128)(2,1)} %param.19) | copy-start | bytes 6148
  56.0 3.1 %collective-permute-start.13 = (f32[16,128]{1,0:T(8,128)S(1)}, f32[16,128]{1,0:T(8,128)S(1)}, u32[]{:S(2)}, u32[]{:S(2)}) collective-permute-start(f32[16,128]{1,0:T(8,128)S(1)} %constant_dynamic-update-slice_fusion.refs_2_), channel_id=1, source_target_pairs={{0,1},{1,2},{2,3},{3,0},{4,5},{5,6},{6,7},{7,4},{8,9},{9,10},{10,1... | collective-permute-start | bytes 24584 | tf_op jit(solution)/shard_map/ppermute | solution.py:632
  56.0 3.7 %collective-permute-start.14 = (f32[16,128]{1,0:T(8,128)S(1)}, f32[16,128]{1,0:T(8,128)S(1)}, u32[]{:S(2)}, u32[]{:S(2)}) collective-permute-start(f32[16,128]{1,0:T(8,128)S(1)} %constant_dynamic-update-slice_fusion.refs_2_), channel_id=1, source_target_pairs={{0,2},{1,3},{2,0},{3,1},{4,6},{5,7},{6,4},{7,5},{8,10},{9,11},{10,... | collective-permute-start | bytes 24584 | tf_op jit(solution)/shard_map/ppermute | solution.py:632
  57.6 2.8 %collective-permute-start.15 = (f32[16,128]{1,0:T(8,128)S(1)}, f32[16,128]{1,0:T(8,128)S(1)}, u32[]{:S(2)}, u32[]{:S(2)}) collective-permute-start(f32[16,128]{1,0:T(8,128)S(1)} %constant_dynamic-update-slice_fusion.refs_2_), channel_id=1, source_target_pairs={{0,3},{1,0},{2,1},{3,2},{4,7},{5,4},{6,5},{7,6},{8,11},{9,8},{10,9... | collective-permute-start | bytes 24584 | tf_op jit(solution)/shard_map/ppermute | solution.py:632

commit v6 on v5

--- a/solution.py
+++ b/solution.py
@@ -14,7 +14,7 @@
 BLK = 64
 TILES = 8
 CORES = 2
-TOGETHER = 4
+TOGETHER = 8
 
 VERY_LOW = -1e30
 TO_LOG2 = math.log2(math.e) / math.sqrt(HD)
@@ -138,69 +138,75 @@
 
 
 def first_kernel(
-    cont,
-    lists_ref,
-    counts_ref,
+    conts,
+    lists_hbm,
+    counts_hbm,
     keys_ref,
     values_ref,
     queries_ref,
     cont_keys_ref,
     cont_values_ref,
-    acc_ref,
-    stat_ref,
-    q_ref,
-    flipped_ref,
-    rows_ref,
-    ck_ref,
-    cv_ref,
-    own_ref,
-    sems,
+    *refs,
 ):
-    heads, _, length = q_ref.shape
+    states, refs = by_cont(refs[: 2 * conts]), refs[2 * conts :]
+    q_refs, refs = refs[:conts], refs[conts:]
+    lists_kept, counts_kept, lists_ref, counts_ref, *refs = refs
+    flipped_ref, rows_ref, ck_ref, cv_ref, own_ref, sems = refs
+    heads, _, length = q_refs[0].shape
     lanes = group_lanes(heads)
     copies = start_all(
         [
-            pltpu.make_async_copy(cont_values_ref.at[cont, :, lanes], cv_ref, sems.at[0]),
-            pltpu.make_async_copy(cont_keys_ref.at[cont, :, lanes], ck_ref, sems.at[1]),
-            pltpu.make_async_copy(queries_ref.at[cont], rows_ref, sems.at[2]),
+            pltpu.make_async_copy(cont_values_ref.at[:, :, lanes], cv_ref, sems.at[0]),
+            pltpu.make_async_copy(queries_ref, rows_ref, sems.at[1]),
+            pltpu.make_async_copy(cont_keys_ref.at[:, :, lanes], ck_ref, sems.at[2]),
+            pltpu.make_async_copy(lists_hbm, lists_ref, sems.at[3]),
+            pltpu.make_async_copy(counts_hbm, counts_ref, sems.at[4]),
+            pltpu.make_async_copy(lists_hbm, lists_kept, sems.at[5]),
+            pltpu.make_async_copy(counts_hbm, counts_kept, sems.at[6]),
         ]
     )
     own = lax.axis_index("ctx")
     both_ways([values_ref], flipped_ref)
     copies[0].wait()
-    own_ref[...] = cv_ref[...].T
+    for cont in range(conts):
+        own_ref[cont] = cv_ref[cont].T
     copies[1].wait()
-    copies[2].wait()
-    for head in range(heads):
-        q_ref[head] = rows_ref[:, head * HD : (head + 1) * HD].T
+    for cont in range(conts):
+        for head in range(heads):
+            q_refs[cont][head] = rows_ref[cont, :, head * HD : (head + 1) * HD].T
+    for copy in copies[2:]:
+        copy.wait()
+    together = TOGETHER // conts
 
     def some_heads(index, carry):
-        work = [index * TOGETHER + j for j in range(TOGETHER)]
+        work = [(index * together + j, cont) for j in range(together) for cont in range(conts)]
         made = []
-        for head in work:
-            scores = jnp.dot(ck_ref[...], q_ref[head], preferred_element_type=jnp.float32)
+        for head, cont in work:
+            scores = jnp.dot(
+                ck_ref[cont], q_refs[cont][head], preferred_element_type=jnp.float32
+            )
             key = lax.broadcasted_iota(jnp.int32, scores.shape, 0)
             row = lax.broadcasted_iota(jnp.int32, scores.shape, 1)
             scores = jnp.where(key <= row, scores, VERY_LOW)
             tiles, values = shard_scores(
-                lists_ref, counts_ref, {cont: q_ref}, keys_ref, flipped_ref, own, head, cont
+                lists_ref, counts_ref, q_refs, keys_ref, flipped_ref, own, head, cont
             )
             made.append(
-                ([(scores, True)] + tiles, jnp.concatenate([own_ref[...], values], axis=1))
-            )
-        states = []
+                ([(scores, True)] + tiles, jnp.concatenate([own_ref[cont], values], axis=1))
+            )
+        after = []
         for got in made:
             start = (
                 jnp.full((1, length), VERY_LOW, jnp.float32),
                 jnp.zeros((1, length), jnp.float32),
                 jnp.zeros((HD, length), jnp.float32),
             )
-            states.append(absorb(start, *got))
-        for head, state in zip(work, states):
-            store_state(acc_ref, stat_ref, head, state)
+            after.append(absorb(start, *got))
+        for (head, cont), state in zip(work, after):
+            store_state(*states[cont], head, state)
         return carry
 
-    lax.fori_loop(0, heads // TOGETHER, some_heads, 0)
+    lax.fori_loop(0, heads // together, some_heads, 0)
 
 
 def arrivals(step, sources):
@@ -221,12 +227,32 @@
     return 2 if sources == 4 else sources - 1
 
 
+def lists_copies(lists_kept, counts_kept, lists_ref, counts_ref, sems):
+    return start_all(
+        [
+            pltpu.make_async_copy(lists_kept, lists_ref, sems.at[0]),
+            pltpu.make_async_copy(counts_kept, counts_ref, sems.at[1]),
+        ]
+    )
+
+
 def absorb_shard(
-    source, lists_ref, counts_ref, q_refs, keys_ref, values_refs, flipped_ref, before, after
+    pending,
+    source,
+    lists_ref,
+    counts_ref,
+    q_refs,
+    keys_ref,
+    values_refs,
+    flipped_ref,
+    before,
+    after,
 ):
     heads = next(iter(q_refs.values())).shape[0]
-    together = TOGETHER // len(q_refs)
+    together = min(heads, TOGETHER // len(q_refs))
     both_ways(values_refs, flipped_ref)
+    for copy in pending:
+        copy.wait()
 
     def some_heads(index, carry):
         work = [(index * together + j, cont) for j in range(together) for cont in q_refs]
@@ -253,7 +279,7 @@
 
 
 def middle_kernel(
-    step, part, sources, conts, pieces, with_weight, lists_ref, counts_ref, *refs
+    step, part, sources, conts, pieces, with_weight, lists_kept, counts_kept, *refs
 ):
     q_refs, refs = dict(enumerate(refs[:conts])), refs[conts:]
     keys_ref, values_refs, refs = refs[0], refs[1 : 1 + pieces], refs[1 + pieces :]
@@ -262,14 +288,14 @@
         weight_ref, *refs = refs
     after, refs = refs[: 2 * conts], refs[2 * conts :]
     if with_weight:
-        give_ref, flipped_ref, sems = refs
+        give_ref, *refs, sems = refs
         copies = start_all(weight_copies(weight_ref, give_ref, sems, True))
-    else:
-        (flipped_ref,) = refs
+    flipped_ref, lists_ref, counts_ref, list_sems = refs
     source, valid = arrivals(step, sources)[part]
 
     def absorb_part():
-        shard = (source, lists_ref, counts_ref, q_refs, keys_ref, values_refs, flipped_ref)
+        pending = lists_copies(lists_kept, counts_kept, lists_ref, counts_ref, list_sems)
+        shard = (pending, source, lists_ref, counts_ref, q_refs, keys_ref, values_refs, flipped_ref)
         absorb_shard(*shard, by_cont(before), by_cont(after))
 
     if valid is True:
@@ -296,8 +322,8 @@
     step,
     sources,
     cont,
-    lists_ref,
-    counts_ref,
+    lists_kept,
+    counts_kept,
     q_ref,
     mine_keys_ref,
     mine_values_ref,
@@ -313,7 +339,7 @@
         copies = start_all(weight_copies(weight_ref, keep_weight_ref, sems, False))
     else:
         attended_ref, give_ref, *refs = refs
-    acc_ref, stat_ref, flipped_ref = refs
+    acc_ref, stat_ref, flipped_ref, lists_ref, counts_ref, list_sems = refs
     before, after = (acc_in, stat_in), (acc_ref, stat_ref)
     held = (mine_keys_ref, [mine_values_ref]), (their_keys_ref, [their_values_ref])
     parts = arrivals(step, sources)
@@ -321,9 +347,12 @@
     for part, (source, valid) in enumerate(parts):
 
         def absorb_part():
-            shard = (source, lists_ref, counts_ref, {cont: q_ref}, *held[part], flipped_ref)
+            pending = lists_copies(lists_kept, counts_kept, lists_ref, counts_ref, list_sems)
+            shard = (pending, source, lists_ref, counts_ref, {cont: q_ref}, *held[part])
             first = part == 0 or one_of_two
-            absorb_shard(*shard, {cont: before if first else after}, {cont: after})
+            absorb_shard(
+                *shard, flipped_ref, {cont: before if first else after}, {cont: after}
+            )
 
         pl.when(valid)(absorb_part)
         if part == 0 and not one_of_two:
@@ -403,7 +432,6 @@
     place = lax.axis_index("tp")
     pairs = heads * conts
     params = pltpu.CompilerParams(vmem_limit_bytes=VMEM_LIMIT)
-    smem = pl.BlockSpec(memory_space=pltpu.SMEM)
     vmem = pl.BlockSpec(memory_space=pltpu.VMEM)
     hbm = pl.BlockSpec(memory_space=pltpu.HBM)
 
@@ -468,33 +496,31 @@
     flipped = pltpu.VMEM((2 * rows_dev, HD), jnp.bfloat16)
     weight_shape = array((chips, width, share), jnp.bfloat16)
 
-    def attend_own(cont, keys):
-        *state, q = pl.pallas_call(
-            functools.partial(first_kernel, cont),
-            out_shape=state_shape + (array((heads, HD, length), jnp.bfloat16),),
-            in_specs=[smem, smem, vmem, vmem] + [hbm] * 3,
-            out_specs=(vmem,) * 3,
-            scratch_shapes=[
-                flipped,
-                pltpu.VMEM((length, width), jnp.bfloat16),
-                pltpu.VMEM((length, HD), jnp.bfloat16),
-                pltpu.VMEM((length, HD), jnp.bfloat16),
-                pltpu.VMEM((HD, length), jnp.bfloat16),
-                pltpu.SemaphoreType.DMA((3,)),
-            ],
-            compiler_params=params,
-            cost_estimate=cost(),
-            name="attend_own",
-        )(
-            lists,
-            counts,
-            keys,
-            values,
-            in_hbm(queries),
-            in_hbm(cont_keys),
-            in_hbm(cont_values),
-        )
-        return tuple(state), q
+    list_shapes = (array(lists.shape, jnp.int32), array(counts.shape, jnp.int32))
+    list_scratch = [pltpu.SMEM(x.shape, x.dtype) for x in list_shapes]
+    with_lists = [flipped] + list_scratch + [pltpu.SemaphoreType.DMA((2,))]
+    *made, lists_kept, counts_kept = pl.pallas_call(
+        functools.partial(first_kernel, conts),
+        out_shape=state_shape * conts
+        + (array((heads, HD, length), jnp.bfloat16),) * conts
+        + list_shapes,
+        in_specs=[hbm, hbm, vmem, vmem] + [hbm] * 3,
+        out_specs=(vmem,) * (3 * conts + 2),
+        scratch_shapes=list_scratch
+        + [
+            flipped,
+            pltpu.VMEM(queries.shape, jnp.bfloat16),
+            pltpu.VMEM((conts, length, HD), jnp.bfloat16),
+            pltpu.VMEM((conts, length, HD), jnp.bfloat16),
+            pltpu.VMEM((conts, HD, length), jnp.bfloat16),
+            pltpu.SemaphoreType.DMA((7,)),
+        ],
+        compiler_params=params,
+        cost_estimate=cost(),
+        name="attend_own",
+    )(lists, counts, keys, values, in_hbm(queries), in_hbm(cont_keys), in_hbm(cont_values))
+    states = tuple(made[2 * c : 2 * c + 2] for c in range(conts))
+    qs = made[2 * conts :]
 
     def attend_step(step, part, with_weight, states, held):
         flat = [x for state in states for x in state]
@@ -503,33 +529,19 @@
                 middle_kernel, step, part, sources, conts, len(held) - 1, with_weight
             ),
             out_shape=state_shape * conts + ((weight_shape,) if with_weight else ()),
-            in_specs=[smem, smem] + [vmem] * (3 * conts + len(held)) + [hbm] * with_weight,
+            in_specs=[vmem] * (2 + 3 * conts + len(held)) + [hbm] * with_weight,
             out_specs=(vmem,) * (2 * conts + with_weight),
-            scratch_shapes=[flipped] + [pltpu.SemaphoreType.DMA((chips,))] * with_weight,
+            scratch_shapes=with_lists + [pltpu.SemaphoreType.DMA((chips,))] * with_weight,
             compiler_params=params,
             cost_estimate=cost(),
             name="attend_step",
-        )(lists, counts, *qs, *held, *flat, *([in_hbm(out_weight)] * with_weight))
+        )(lists_kept, counts_kept, *qs, *held, *flat, *([in_hbm(out_weight)] * with_weight))
         return tuple(made[2 * c : 2 * c + 2] for c in range(conts)), made[2 * conts :]
 
-    states, qs = [], []
     for step in range(1, steps + 1):
         sent = mine if sources == 4 and step == 2 else (keys, values)
         mine_keys, mine_values = [lax.ppermute(x, ("ctx", "tp"), across(step)) for x in sent]
-        own_keys = keys
-        if step == 1:
-            state, q = attend_own(0, keys)
-            states.append(state)
-            qs.append(q)
-        mine_keys, own_keys, states = lax.optimization_barrier(
-            (mine_keys, own_keys, tuple(states))
-        )
-        if step == 1:
-            states = list(states)
-            for cont in range(1, conts):
-                state, q = attend_own(cont, own_keys)
-                states.append(state)
-                qs.append(q)
+        mine_keys, states = lax.optimization_barrier((mine_keys, tuple(states)))
         their_keys = lax.ppermute(mine_keys, "tp", sibling)
         mine_values, states = lax.optimization_barrier((mine_values, tuple(states)))
         their_values = [
@@ -550,17 +562,17 @@
                 array((chips, length, share), jnp.bfloat16),
             )
             + (weight_shape,) * fetch,
-            in_specs=[smem, smem] + [vmem] * 8 + [hbm] * fetch,
+            in_specs=[vmem] * 10 + [hbm] * fetch,
             out_specs=(vmem,) * (2 + fetch),
             scratch_shapes=[pltpu.VMEM(a.shape, a.dtype) for a in state_shape]
-            + [flipped]
+            + with_lists
             + [pltpu.SemaphoreType.DMA((chips,))] * fetch,
             compiler_params=params,
             cost_estimate=cost(),
             name="attend_last",
         )(
-            lists,
-            counts,
+            lists_kept,
+            counts_kept,
             qs[cont],
             *mine,
             *theirs,

time: 62.6 us -> 58 us (0.927); the launches traced: 61.5 us -> 57.6 us
  Pallas kernels: 31.3 us -> 25.3 us
  waiting for transfers between devices: 13 us -> 16.8 us
  starting transfers between devices: 16.4 us -> 14.6 us
    ppermute x4, waiting for transfers between devices: 2.07 us -> 5.92 us  [shards(): lax.ppermute(x, ('ctx', 'tp'), across(step))]
    pallas_call x2 -> x1, Pallas kernels: 7.89 us -> 4.05 us  [shards(): pl.pallas_call(functools.partial(first_kernel, conts), out_shape=state_sh...]
    ppermute x3, starting transfers between devices: 4.78 us -> 2.94 us  [shards(): lax.ppermute(x, 'tp', sibling)]
    pallas_call x2, Pallas kernels: 8.8 us -> 7.47 us  [attend_step(): pl.pallas_call(functools.partial(middle_kernel, step, part, sources, cont...]
    pallas_call x2, Pallas kernels: 7.42 us -> 6.64 us  [attend_last(): pl.pallas_call(functools.partial(last_kernel, steps, sources, cont), out_...]
  transfers between devices with their start and end apart: 16 -> 16, of which waited for: 9 -> 9; matrix products, arithmetic and copies ran while one was open for 0% -> 0% of each run, Pallas kernels for 41% -> 34%
where the time goes in v6:
time: 58 us; the launch traced here: 57.6 us
  Pallas kernels  25.3 us (44%)
  waiting for transfers between devices  16.8 us (29%)
  starting transfers between devices  14.6 us (25%)
  between operations  0.81 us (1%)
    ppermute x2, waiting for transfers between devices, onward(): far.append(lax.ppermute(parts[k - 1], 'tp', to_chip))  8.07 us
    pallas_call x2, Pallas kernels, attend_step(): pl.pallas_call(functools.partial(middle_kernel, step, part, sources, cont...  7.47 us
    pallas_call x2, Pallas kernels, attend_last(): pl.pallas_call(functools.partial(last_kernel, steps, sources, cont), out_...  6.64 us
    ppermute x4, waiting for transfers between devices, shards(): lax.ppermute(x, ('ctx', 'tp'), across(step))  5.92 us
    ppermute x4, starting transfers between devices, shards(): lax.ppermute(x, ('ctx', 'tp'), across(step))  4.51 us
    pallas_call x1, Pallas kernels, shards(): pl.pallas_call(functools.partial(first_kernel, conts), out_shape=state_sh...  4.05 us
    ppermute x3, starting transfers between devices, shards(): lax.ppermute(squares, 'tp', [(t, (t + k) % members) for t in range(member...  2.97 us
    ppermute x3, starting transfers between devices, shards(): lax.ppermute(x, 'tp', sibling)  2.94 us
  transfers between devices with their start and end apart: 16, of which 9 were waited for; matrix products, arithmetic and copies ran while one was open for 0% of the time, Pallas kernels for 34%

profile of v6, /device:TPU:0, one launch (start us, length us, event | category | flops | bytes accessed | tf_op | source)
XLA Modules:
  0.0 57.6 jit_solution(13795432579908880894)
XLA Ops:
  0.6 1.0 %pack_keys.1.keys_ref = bf16[1024,128]{1,0:T(8,128)(2,1)S(1)} custom-call(bf16[1024,256]{1,0:T(8,128)(2,1)} %keys_ref.1), custom_call_target="tpu_custom_call" | custom-call | flops 1024 | bytes 1024 | tf_op jit(solution)/shard_map/pack_keys/pallas_call | solution.py:448
  1.6 3.1 %collective-permute-start = (bf16[1024,128]{1,0:T(8,128)(2,1)S(1)}, bf16[1024,128]{1,0:T(8,128)(2,1)S(1)}, u32[]{:S(2)}, u32[]{:S(2)}) collective-permute-start(bf16[1024,128]{1,0:T(8,128)(2,1)S(1)} %pack_keys.1.keys_ref), channel_id=1, source_target_pairs={{0,4},{1,9},{2,6},{3,11},{4,0},{5,13},{6,2},{7,15},{8,12},{9,1},{1... | collective-permute-start | bytes 786440 | tf_op jit(solution)/shard_map/ppermute | solution.py:543
  4.7 1.1 %pack_values.1.values_ref = bf16[1024,128]{1,0:T(8,128)(2,1)S(1)} custom-call(bf16[1024,256]{1,0:T(8,128)(2,1)} %values_ref.1), custom_call_target="tpu_custom_call" | custom-call | flops 1024 | bytes 1024 | tf_op jit(solution)/shard_map/pack_values/pallas_call | solution.py:458
  5.9 4.0 %attend_own.1 = (f32[8,128,128]{2,1,0:T(8,128)S(1)}, f32[8,8,128]{2,1,0:T(8,128)S(1)}, f32[8,128,128]{2,1,0:T(8,128)S(1)}, f32[8,8,128]{2,1,0:T(8,128)S(1)}, bf1...) custom-call(s32[8,2,4,8]{3,2,1,0:T(4,128)} %lists_hbm.1, ...), custom_call_target="tpu_custom_call" | custom-call | flops 1024 | bytes 1024 | tf_op jit(solution)/shard_map/attend_own/pallas_call | solution.py:502
  9.9 1.5 %collective-permute-done.refs_2_ = bf16[1024,128]{1,0:T(8,128)(2,1)S(1)} collective-permute-done((bf16[1024,128]{1,0:T(8,128)(2,1)S(1)}, bf16[1024,128]{1,0:T(8,128)(2,1)S(1)}, u32[]{:S(2)}, u32[]{:S(2)}) %collective-permute-start) | collective-permute-done | bytes 262176 | tf_op jit(solution)/shard_map/ppermute | solution.py:543
  12.1 0.7 %collective-permute-start.1 = (bf16[1024,128]{1,0:T(8,128)(2,1)S(1)}, bf16[1024,128]{1,0:T(8,128)(2,1)S(1)}, u32[]{:S(2)}, u32[]{:S(2)}) collective-permute-start(bf16[1024,128]{1,0:T(8,128)(2,1)S(1)} %collective-permute-done.refs_2_), channel_id=1, source_target_pairs={{1,5},{3,7},{5,1},{7,3},{9,13},{11,15},{13,9},{15,11},{17,21},{19,... | collective-permute-start | bytes 786440 | tf_op jit(solution)/shard_map/ppermute | solution.py:543
  12.7 4.4 %collective-permute-done.3.refs_3_ = bf16[1024,128]{1,0:T(8,128)(2,1)S(1)} collective-permute-done((bf16[1024,128]{1,0:T(8,128)(2,1)S(1)}, bf16[1024,128]{1,0:T(8,128)(2,1)S(1)}, u32[]{:S(2)}, u32[]{:S(2)}) %collective-permute-start.3) | collective-permute-done | bytes 262176 | tf_op jit(solution)/shard_map/ppermute | solution.py:543
  17.1 0.7 %collective-permute-start.6 = (bf16[1024,128]{1,0:T(8,128)(2,1)S(1)}, bf16[1024,128]{1,0:T(8,128)(2,1)S(1)}, u32[]{:S(2)}, u32[]{:S(2)}) collective-permute-start(bf16[1024,128]{1,0:T(8,128)(2,1)S(1)} %collective-permute-done.3.refs_3_), channel_id=1, source_target_pairs={{1,5},{3,7},{5,1},{7,3},{9,13},{11,15},{13,9},{15,11},{17,21},{19,... | collective-permute-start | bytes 786440 | tf_op jit(solution)/shard_map/ppermute | solution.py:543
  17.8 2.4 %collective-permute-start.4 = (bf16[512,128]{1,0:T(8,128)(2,1)S(1)}, bf16[512,128]{1,0:T(8,128)(2,1)S(1)}, u32[]{:S(2)}, u32[]{:S(2)}) collective-permute-start(bf16[512,128]{1,0:T(8,128)(2,1)S(1)} %get-tuple-element.99), channel_id=1, source_target_pairs={{0,1},{1,0},{2,3},{3,2},{4,5},{5,4},{6,7},{7,6},{8,9},{9,8},{10,11... | collective-permute-start | bytes 393224 | tf_op jit(solution)/shard_map/ppermute | solution.py:548
  20.2 3.7 %attend_step.2 = (f32[8,128,128]{2,1,0:T(8,128)S(1)}, f32[8,8,128]{2,1,0:T(8,128)S(1)}, f32[8,128,128]{2,1,0:T(8,128)S(1)}, f32[8,8,128]{2,1,0:T(8,128)S(1)}, bf16[2,1024,1024]{2,1,0:T(8,128)(2,1)S(1)}) custom-call(s32[8,2,4,8]{3,2,1,0:T(4,128)S(1)} %get-tuple-element.50.lists_kept, s32[2,4,8]{2,1,0:T(4,128)S(1)} %get-tuple-element.51.counts_kept, ...), custom_call_target="tpu_custom_call" | custom-call | flops 1024 | bytes 1024 | tf_op jit(solution)/shard_map/attend_step/pallas_call | solution.py:527
  24.0 3.7 %attend_step.3 = (f32[8,128,128]{2,1,0:T(8,128)S(1)}, f32[8,8,128]{2,1,0:T(8,128)S(1)}, f32[8,128,128]{2,1,0:T(8,128)S(1)}, f32[8,8,128]{2,1,0:T(8,128)S(1)}) custom-call(s32[8,2,4,8]{3,2,1,0:T(4,128)S(1)} %get-tuple-element.50.lists_kept, s32[2,4,8]{2,1,0:T(4,128)S(1)} %get-tuple-element.51.counts_kept, ...), custom_call_target="tpu_custom_call" | custom-call | flops 1024 | bytes 1024 | tf_op jit(solution)/shard_map/attend_step/pallas_call | solution.py:527
  28.4 1.1 %collective-permute-done.8.their_values_ref = bf16[1024,128]{1,0:T(8,128)(2,1)S(1)} collective-permute-done((bf16[1024,128]{1,0:T(8,128)(2,1)S(1)}, bf16[1024,128]{1,0:T(8,128)(2,1)S(1)}, u32[]{:S(2)}, u32[]{:S(2)}) %collective-permute-start.8) | collective-permute-done | bytes 262176 | tf_op jit(solution)/shard_map/ppermute | solution.py:548
  29.8 3.2 %attend_last.2 = (bf16[128,1024]{1,0:T(8,128)(2,1)S(1)}, bf16[2,128,1024]{2,1,0:T(8,128)(2,1)S(1)}, bf16[2,1024,1024]{2,1,0:T(8,128)(2,1)S(1)}) custom-call(s32[8,2,4,8]{3,2,1,0:T(4,128)S(1)} %get-tuple-element.50.lists_kept, s32[2,4,8]{2,1,0:T(4,128)S(1)} %get-tuple-element.51.counts_kept, bf16[8,128,128]{2,1,0:T(8,128)(2,1)S(1)} %get-tuple-element.52.refs_0_.q_ref, ...), custom_call_target="tpu_custom_call" | custom-call | flops 1024 | bytes 1024 | tf_op jit(solution)/shard_map/attend_last/pallas_call | solution.py:558
  33.5 3.4 %attend_last.3 = (bf16[128,1024]{1,0:T(8,128)(2,1)S(1)}, bf16[2,128,1024]{2,1,0:T(8,128)(2,1)S(1)}) custom-call(s32[8,2,4,8]{3,2,1,0:T(4,128)S(1)} %get-tuple-element.50.lists_kept, s32[2,4,8]{2,1,0:T(4,128)S(1)} %get-tuple-element.51.counts_kept, bf16[8,128,128]{2,1,0:T(8,128)(2,1)S(1)} %get-tuple-element.58.refs_1_.q_ref, ...), custom_call_target="tpu_custom_call" | custom-call | flops 1024 | bytes 1024 | tf_op jit(solution)/shard_map/attend_last/pallas_call | solution.py:558
  37.6 1.6 %collective-permute-start.10 = (bf16[128,1024]{1,0:T(8,128)(2,1)S(1)}, bf16[128,1024]{1,0:T(8,128)(2,1)S(1)}, u32[]{:S(2)}, u32[]{:S(2)}) collective-permute-start(bf16[128,1024]{1,0:T(8,128)(2,1)S(1)} %project_onward.2), channel_id=1, source_target_pairs={{0,2},{1,3},{2,0},{3,1},{4,6},{5,7},{6,4},{7,5},{8,10},{9,11},{10,... | collective-permute-start | bytes 786440 | tf_op jit(solution)/shard_map/ppermute | solution.py:599
  39.6 1.3 %collective-permute-start.12 = (bf16[128,1024]{1,0:T(8,128)(2,1)S(1)}, bf16[128,1024]{1,0:T(8,128)(2,1)S(1)}, u32[]{:S(2)}, u32[]{:S(2)}) collective-permute-start(bf16[128,1024]{1,0:T(8,128)(2,1)S(1)} %project_onward.3), channel_id=1, source_target_pairs={{0,2},{1,3},{2,0},{3,1},{4,6},{5,7},{6,4},{7,5},{8,10},{9,11},{10,... | collective-permute-start | bytes 786440 | tf_op jit(solution)/shard_map/ppermute | solution.py:599
  40.9 1.3 %project_near.2.refs_0_ = f32[128,1024]{1,0:T(8,128)S(1)} custom-call(bf16[128,1024]{1,0:T(8,128)(2,1)S(1)} %get-tuple-element.85.attended_ref, bf16[2,1024,1024]{2,1,0:T(8,128)(2,1)S(1)} %get-tuple-element.86.weight_ref, bf16[2,128,1024]{2,1,0:T(8,128)(2,1)S(1)} %collective-permute-done.9.got_ref, bf16[2,128,4096]{2,1,0:T(8,128)(2,1)} %residual_ref.3), custom_call_target="tpu_custom_call" | custom-call | flops 1024 | bytes 1024 | tf_op jit(solution)/shard_map/project_near/pallas_call | solution.py:603
  42.3 4.5 %collective-permute-done.10.refs_1_ = bf16[128,1024]{1,0:T(8,128)(2,1)S(1)} collective-permute-done((bf16[128,1024]{1,0:T(8,128)(2,1)S(1)}, bf16[128,1024]{1,0:T(8,128)(2,1)S(1)}, u32[]{:S(2)}, u32[]{:S(2)}) %collective-permute-start.10) | collective-permute-done | bytes 262176 | tf_op jit(solution)/shard_map/ppermute | solution.py:599
  47.0 1.3 %project_near.3.refs_0_ = f32[128,1024]{1,0:T(8,128)S(1)} custom-call(bf16[128,1024]{1,0:T(8,128)(2,1)S(1)} %get-tuple-element.93.attended_ref, bf16[2,1024,1024]{2,1,0:T(8,128)(2,1)S(1)} %get-tuple-element.86.weight_ref, bf16[2,128,1024]{2,1,0:T(8,128)(2,1)S(1)} %collective-permute-done.11.got_ref, bf16[2,128,4096]{2,1,0:T(8,128)(2,1)} %residual_ref.3), custom_call_target="tpu_custom_call" | custom-call | flops 1024 | bytes 1024 | tf_op jit(solution)/shard_map/project_near/pallas_call | solution.py:603
  48.3 3.6 %collective-permute-done.12.refs_1_ = bf16[128,1024]{1,0:T(8,128)(2,1)S(1)} collective-permute-done((bf16[128,1024]{1,0:T(8,128)(2,1)S(1)}, bf16[128,1024]{1,0:T(8,128)(2,1)S(1)}, u32[]{:S(2)}, u32[]{:S(2)}) %collective-permute-start.12) | collective-permute-done | bytes 262176 | tf_op jit(solution)/shard_map/ppermute | solution.py:599
  52.1 1.6 %collective-permute-start.14 = (f32[16,128]{1,0:T(8,128)S(1)}, f32[16,128]{1,0:T(8,128)S(1)}, u32[]{:S(2)}, u32[]{:S(2)}) collective-permute-start(f32[16,128]{1,0:T(8,128)S(1)} %constant_dynamic-update-slice_fusion.refs_2_), channel_id=1, source_target_pairs={{0,2},{1,3},{2,0},{3,1},{4,6},{5,7},{6,4},{7,5},{8,10},{9,11},{10,... | collective-permute-start | bytes 24584 | tf_op jit(solution)/shard_map/ppermute | solution.py:644
  53.6 1.4 %collective-permute-start.15 = (f32[16,128]{1,0:T(8,128)S(1)}, f32[16,128]{1,0:T(8,128)S(1)}, u32[]{:S(2)}, u32[]{:S(2)}) collective-permute-start(f32[16,128]{1,0:T(8,128)S(1)} %constant_dynamic-update-slice_fusion.refs_2_), channel_id=1, source_target_pairs={{0,3},{1,0},{2,1},{3,2},{4,7},{5,4},{6,5},{7,6},{8,11},{9,8},{10,9... | collective-permute-start | bytes 24584 | tf_op jit(solution)/shard_map/ppermute | solution.py:644
  55.1 0.7 %collective-permute-done.14.refs_4_ = f32[16,128]{1,0:T(8,128)S(1)} collective-permute-done((f32[16,128]{1,0:T(8,128)S(1)}, f32[16,128]{1,0:T(8,128)S(1)}, u32[]{:S(2)}, u32[]{:S(2)}) %collective-permute-start.14) | collective-permute-done | bytes 8224 | tf_op jit(solution)/shard_map/ppermute | solution.py:644
  56.4 1.2 %norm.1 = (bf16[2,128,1024]{2,1,0:T(8,128)(2,1)}, bf16[2,128,1024]{2,1,0:T(8,128)(2,1)}) custom-call(f32[128,1024]{1,0:T(8,128)S(1)} %get-tuple-element.92.refs_0_, f32[128,1024]{1,0:T(8,128)S(1)} %get-tuple-element.95.refs_1_, f32[16,128]{1,0:T(8,128)S(1)} %constant_dynamic-update-slice_fusion.refs_2_, f32[16,128]{1,0:T(8,128)S(1)} %collective-permute-done.13.refs_3_, ...), custom_call_target="tpu_custom_call" | custom-call | flops 1024 | bytes 1024 | tf_op jit(solution)/shard_map/norm/pallas_call | solution.py:648
  (28 shorter events, 4.4 us)
Async XLA Ops:
  1.6 9.9 %collective-permute-start = (bf16[1024,128]{1,0:T(8,128)(2,1)S(1)}, bf16[1024,128]{1,0:T(8,128)(2,1)S(1)}, u32[]{:S(2)}, u32[]{:S(2)}) collective-permute-start(bf16[1024,128]{1,0:T(8,128)(2,1)S(1)} %pack_keys.1.keys_ref), channel_id=1, source_target_pairs={{0,4},{1,9},{2,6},{3,11},{4,0},{5,13},{6,2},{7,15},{8,12},{9,1},{1... | collective-permute-start | bytes 786440 | tf_op jit(solution)/shard_map/ppermute | solution.py:543
  5.8 11.3 %collective-permute-start.3 = (bf16[1024,128]{1,0:T(8,128)(2,1)S(1)}, bf16[1024,128]{1,0:T(8,128)(2,1)S(1)}, u32[]{:S(2)}, u32[]{:S(2)}) collective-permute-start(bf16[1024,128]{1,0:T(8,128)(2,1)S(1)} %pack_values.1.values_ref), channel_id=1, source_target_pairs={{0,4},{1,9},{2,6},{3,11},{4,0},{5,13},{6,2},{7,15},{8,12},{9,1},{1... | collective-permute-start | bytes 786440 | tf_op jit(solution)/shard_map/ppermute | solution.py:543
  11.5 12.5 %collective-permute-start.2 = (bf16[1024,128]{1,0:T(8,128)(2,1)S(1)}, bf16[1024,128]{1,0:T(8,128)(2,1)S(1)}, u32[]{:S(2)}, u32[]{:S(2)}) collective-permute-start(bf16[1024,128]{1,0:T(8,128)(2,1)S(1)} %collective-permute-done.refs_2_), channel_id=1, source_target_pairs={{0,1},{1,0},{2,3},{3,2},{4,5},{5,4},{6,7},{7,6},{8,9},{9,8},{10,11... | collective-permute-start | bytes 786440 | tf_op jit(solution)/shard_map/ppermute | solution.py:545
  12.1 15.7 %collective-permute-start.1 = (bf16[1024,128]{1,0:T(8,128)(2,1)S(1)}, bf16[1024,128]{1,0:T(8,128)(2,1)S(1)}, u32[]{:S(2)}, u32[]{:S(2)}) collective-permute-start(bf16[1024,128]{1,0:T(8,128)(2,1)S(1)} %collective-permute-done.refs_2_), channel_id=1, source_target_pairs={{1,5},{3,7},{5,1},{7,3},{9,13},{11,15},{13,9},{15,11},{17,21},{19,... | collective-permute-start | bytes 786440 | tf_op jit(solution)/shard_map/ppermute | solution.py:543
  17.1 10.7 %collective-permute-start.6 = (bf16[1024,128]{1,0:T(8,128)(2,1)S(1)}, bf16[1024,128]{1,0:T(8,128)(2,1)S(1)}, u32[]{:S(2)}, u32[]{:S(2)}) collective-permute-start(bf16[1024,128]{1,0:T(8,128)(2,1)S(1)} %collective-permute-done.3.refs_3_), channel_id=1, source_target_pairs={{1,5},{3,7},{5,1},{7,3},{9,13},{11,15},{13,9},{15,11},{17,21},{19,... | collective-permute-start | bytes 786440 | tf_op jit(solution)/shard_map/ppermute | solution.py:543
  17.8 6.2 %collective-permute-start.4 = (bf16[512,128]{1,0:T(8,128)(2,1)S(1)}, bf16[512,128]{1,0:T(8,128)(2,1)S(1)}, u32[]{:S(2)}, u32[]{:S(2)}) collective-permute-start(bf16[512,128]{1,0:T(8,128)(2,1)S(1)} %get-tuple-element.99), channel_id=1, source_target_pairs={{0,1},{1,0},{2,3},{3,2},{4,5},{5,4},{6,7},{7,6},{8,9},{9,8},{10,11... | collective-permute-start | bytes 393224 | tf_op jit(solution)/shard_map/ppermute | solution.py:548
  20.2 3.8 %collective-permute-start.5 = (bf16[512,128]{1,0:T(8,128)(2,1)S(1)}, bf16[512,128]{1,0:T(8,128)(2,1)S(1)}, u32[]{:S(2)}, u32[]{:S(2)}) collective-permute-start(bf16[512,128]{1,0:T(8,128)(2,1)S(1)} %get-tuple-element.98), channel_id=1, source_target_pairs={{0,1},{1,0},{2,3},{3,2},{4,5},{5,4},{6,7},{7,6},{8,9},{9,8},{10,11... | collective-permute-start | bytes 393224 | tf_op jit(solution)/shard_map/ppermute | solution.py:548
  27.8 1.7 %collective-permute-start.8 = (bf16[1024,128]{1,0:T(8,128)(2,1)S(1)}, bf16[1024,128]{1,0:T(8,128)(2,1)S(1)}, u32[]{:S(2)}, u32[]{:S(2)}) collective-permute-start(bf16[1024,128]{1,0:T(8,128)(2,1)S(1)} %collective-permute-done.6.mine_values_ref), channel_id=1, source_target_pairs={{0,1},{1,0},{2,3},{3,2},{4,5},{5,4},{6,7},{7,6},{8,9},{9,8},{10,11... | collective-permute-start | bytes 786440 | tf_op jit(solution)/shard_map/ppermute | solution.py:548
  28.3 1.5 %collective-permute-start.7 = (bf16[1024,128]{1,0:T(8,128)(2,1)S(1)}, bf16[1024,128]{1,0:T(8,128)(2,1)S(1)}, u32[]{:S(2)}, u32[]{:S(2)}) collective-permute-start(bf16[1024,128]{1,0:T(8,128)(2,1)S(1)} %collective-permute-done.1.mine_keys_ref), channel_id=1, source_target_pairs={{0,1},{1,0},{2,3},{3,2},{4,5},{5,4},{6,7},{7,6},{8,9},{9,8},{10,11... | collective-permute-start | bytes 786440 | tf_op jit(solution)/shard_map/ppermute | solution.py:545
  33.1 3.8 %collective-permute-start.9 = (bf16[2,128,1024]{2,1,0:T(8,128)(2,1)S(1)}, bf16[2,128,1024]{2,1,0:T(8,128)(2,1)S(1)}, u32[]{:S(2)}, u32[]{:S(2)}) collective-permute-start(bf16[2,128,1024]{2,1,0:T(8,128)(2,1)S(1)} %get-tuple-element.87), channel_id=1, source_target_pairs={{0,1},{1,0},{2,3},{3,2},{4,5},{5,4},{6,7},{7,6},{8,9},{9,8},{10,11... | collective-permute-start | bytes 1572872 | tf_op jit(solution)/shard_map/ppermute | solution.py:620
  36.9 2.2 %collective-permute-start.11 = (bf16[2,128,1024]{2,1,0:T(8,128)(2,1)S(1)}, bf16[2,128,1024]{2,1,0:T(8,128)(2,1)S(1)}, u32[]{:S(2)}, u32[]{:S(2)}) collective-permute-start(bf16[2,128,1024]{2,1,0:T(8,128)(2,1)S(1)} %get-tuple-element.94), channel_id=1, source_target_pairs={{0,1},{1,0},{2,3},{3,2},{4,5},{5,4},{6,7},{7,6},{8,9},{9,8},{10,11... | collective-permute-start | bytes 1572872 | tf_op jit(solution)/shard_map/ppermute | solution.py:620
  37.6 9.2 %collective-permute-start.10 = (bf16[128,1024]{1,0:T(8,128)(2,1)S(1)}, bf16[128,1024]{1,0:T(8,128)(2,1)S(1)}, u32[]{:S(2)}, u32[]{:S(2)}) collective-permute-start(bf16[128,1024]{1,0:T(8,128)(2,1)S(1)} %project_onward.2), channel_id=1, source_target_pairs={{0,2},{1,3},{2,0},{3,1},{4,6},{5,7},{6,4},{7,5},{8,10},{9,11},{10,... | collective-permute-start | bytes 786440 | tf_op jit(solution)/shard_map/ppermute | solution.py:599
  39.6 12.2 %collective-permute-start.12 = (bf16[128,1024]{1,0:T(8,128)(2,1)S(1)}, bf16[128,1024]{1,0:T(8,128)(2,1)S(1)}, u32[]{:S(2)}, u32[]{:S(2)}) collective-permute-start(bf16[128,1024]{1,0:T(8,128)(2,1)S(1)} %project_onward.3), channel_id=1, source_target_pairs={{0,2},{1,3},{2,0},{3,1},{4,6},{5,7},{6,4},{7,5},{8,10},{9,11},{10,... | collective-permute-start | bytes 786440 | tf_op jit(solution)/shard_map/ppermute | solution.py:599
  47.0 8.0 %copy-start = (bf16[1024]{0:T(1024)(128)(2,1)S(1)}, bf16[1024]{0:T(1024)(128)(2,1)}, u32[]{:S(2)}) copy-start(bf16[1024]{0:T(1024)(128)(2,1)} %param.19) | copy-start | bytes 6148
  52.0 3.1 %collective-permute-start.13 = (f32[16,128]{1,0:T(8,128)S(1)}, f32[16,128]{1,0:T(8,128)S(1)}, u32[]{:S(2)}, u32[]{:S(2)}) collective-permute-start(f32[16,128]{1,0:T(8,128)S(1)} %constant_dynamic-update-slice_fusion.refs_2_), channel_id=1, source_target_pairs={{0,1},{1,2},{2,3},{3,0},{4,5},{5,6},{6,7},{7,4},{8,9},{9,10},{10,1... | collective-permute-start | bytes 24584 | tf_op jit(solution)/shard_map/ppermute | solution.py:644
  52.1 3.7 %collective-permute-start.14 = (f32[16,128]{1,0:T(8,128)S(1)}, f32[16,128]{1,0:T(8,128)S(1)}, u32[]{:S(2)}, u32[]{:S(2)}) collective-permute-start(f32[16,128]{1,0:T(8,128)S(1)} %constant_dynamic-update-slice_fusion.refs_2_), channel_id=1, source_target_pairs={{0,2},{1,3},{2,0},{3,1},{4,6},{5,7},{6,4},{7,5},{8,10},{9,11},{10,... | collective-permute-start | bytes 24584 | tf_op jit(solution)/shard_map/ppermute | solution.py:644
  53.6 2.8 %collective-permute-start.15 = (f32[16,128]{1,0:T(8,128)S(1)}, f32[16,128]{1,0:T(8,128)S(1)}, u32[]{:S(2)}, u32[]{:S(2)}) collective-permute-start(f32[16,128]{1,0:T(8,128)S(1)} %constant_dynamic-update-slice_fusion.refs_2_), channel_id=1, source_target_pairs={{0,3},{1,0},{2,1},{3,2},{4,7},{5,4},{6,5},{7,6},{8,11},{9,8},{10,9... | collective-permute-start | bytes 24584 | tf_op jit(solution)/shard_map/ppermute | solution.py:644

commit v7 on v6

v7 whole, which is shorter than its diff:
```python
import functools
import math

import jax
import jax.numpy as jnp
from jax import lax
from jax.experimental import pallas as pl
from jax.experimental.pallas import tpu as pltpu
from jax.sharding import PartitionSpec as P

HEADS = 32
KVH = 2
HD = 128
BLK = 64
TILES = 8
CORES = 2
TOGETHER = 8

VERY_LOW = -1e30
TO_LOG2 = math.log2(math.e) / math.sqrt(HD)

VMEM_LIMIT = 24 * 1024 * 1024


def key_group(heads):
    return lax.axis_index("tp") * heads // (HEADS // KVH)


def group_lanes(heads):
    return pl.ds(pl.multiple_of(key_group(heads) * HD, HD), HD)


def pack_keys_kernel(heads, keys_ref, packed_ref, sems):
    copy = pltpu.make_async_copy(keys_ref.at[:, group_lanes(heads)], packed_ref, sems.at[0])
    copy.start()
    copy.wait()


def pack_values_kernel(heads, values_ref, packed_ref, values_buf, sems):
    copy = pltpu.make_async_copy(values_ref.at[:, group_lanes(heads)], values_buf, sems.at[0])
    copy.start()
    copy.wait()
    for p in range(packed_ref.shape[0] // HD):
        rows = slice(p * HD, (p + 1) * HD)
        packed_ref[rows, :] = values_buf[rows, :].T


def both_ways(values_ref, flipped_ref):
    rows = values_ref.shape[0]
    for p in range(rows // HD):
        pair = values_ref[p * HD : (p + 1) * HD, :]
        flipped_ref[p * HD : (p + 1) * HD, :] = pair
        flipped_ref[rows + p * HD : rows + (p + 1) * HD, :] = jnp.concatenate(
            [pair[:, BLK:], pair[:, :BLK]], axis=1
        )


def used_tiles(lists_ref, counts_ref, source, sources, place):
    at = place * sources + source
    return [lists_ref[at * TILES + t] for t in range(TILES)], counts_ref[at]


def shard_scores(blocks, count, query, keys_ref):
    keys = jnp.concatenate(
        [keys_ref[pl.ds(pl.multiple_of(b * BLK, BLK), BLK), :] for b in blocks], axis=0
    )
    scores = jnp.dot(keys, query, preferred_element_type=jnp.float32)
    return [(scores[t * BLK : (t + 1) * BLK], t < count) for t in range(TILES)]


def shard_values(blocks, flipped_ref):
    pairs = flipped_ref.shape[0] // 2 // HD
    lane = lax.broadcasted_iota(jnp.int32, (HD, HD), 1)
    halves = []
    for t, b in enumerate(blocks):
        spot = ((b + t) % 2 * pairs + b // 2) * HD
        halves.append(flipped_ref[pl.ds(pl.multiple_of(spot, HD), HD), :])
    return jnp.concatenate(
        [jnp.where(lane < BLK, a, b) for a, b in zip(halves[::2], halves[1::2])], axis=1
    )


def fold(op, tile):
    return functools.reduce(op, [tile[i : i + 8] for i in range(0, tile.shape[0], 8)])


def weigh(top, total, tiles):
    tops = [
        jnp.where(live, fold(jnp.maximum, tile), VERY_LOW) for tile, live in tiles
    ]
    best = jnp.max(functools.reduce(jnp.maximum, tops), axis=0, keepdims=True)
    new_top = jnp.maximum(top, best)
    weights = [
        jnp.exp2((tile - jnp.where(live, new_top, -VERY_LOW)) * TO_LOG2) for tile, live in tiles
    ]
    factor = jnp.exp2((top - new_top) * TO_LOG2)
    sums = functools.reduce(jnp.add, [fold(jnp.add, w) for w in weights])
    total = total * factor + jnp.sum(sums, axis=0, keepdims=True)
    rounded = jnp.concatenate([w.astype(jnp.bfloat16) for w in weights], axis=0)
    return (new_top, total, factor), rounded


def put_stat(stat_ref, head, stat):
    top, total, factor = stat
    stat_ref[head] = jnp.concatenate([top, total, factor] + [factor] * 5, axis=0)


def start_all(copies):
    for copy in copies:
        copy.start()
    return copies


def weight_copies(weight_ref, target, sems, sibling):
    chips, _, share = target.shape
    place = lax.axis_index("tp")
    chip, core = place // CORES, place % CORES
    held = 1 - core if sibling else core
    copies = []
    for k in range(chips):
        start = (lax.rem(chip + k, chips) * CORES + held) * share
        copies.append(
            pltpu.make_async_copy(
                weight_ref.at[:, pl.ds(pl.multiple_of(start, HD), share)],
                target.at[k],
                sems.at[k],
            )
        )
    return copies


def first_kernel(
    sources,
    conts,
    lists_ref,
    counts_ref,
    keys_ref,
    values_ref,
    queries_ref,
    cont_keys_ref,
    cont_values_ref,
    *refs,
):
    acc_refs, stat_refs, q_refs = refs[:conts], refs[conts : 2 * conts], refs[2 * conts : 3 * conts]
    flipped_ref, rows_ref, ck_ref, cv_ref, own_ref, sems = refs[3 * conts :]
    heads, _, length = q_refs[0].shape
    lanes = group_lanes(heads)
    copies = start_all(
        [
            pltpu.make_async_copy(cont_values_ref.at[:, :, lanes], cv_ref, sems.at[0]),
            pltpu.make_async_copy(queries_ref, rows_ref, sems.at[1]),
            pltpu.make_async_copy(cont_keys_ref.at[:, :, lanes], ck_ref, sems.at[2]),
        ]
    )
    own = lax.axis_index("ctx")
    both_ways(values_ref, flipped_ref)
    copies[0].wait()
    for cont in range(conts):
        own_ref[cont] = cv_ref[cont].T
    copies[1].wait()
    for cont in range(conts):
        for head in range(heads):
            q_refs[cont][head] = rows_ref[cont, :, head * HD : (head + 1) * HD].T
    copies[2].wait()
    together = TOGETHER // conts

    def some_heads(index, carry):
        work = [(index * together + j, cont) for j in range(together) for cont in range(conts)]
        made = []
        for head, cont in work:
            query = q_refs[cont][head]
            scores = jnp.dot(ck_ref[cont], query, preferred_element_type=jnp.float32)
            key = lax.broadcasted_iota(jnp.int32, scores.shape, 0)
            row = lax.broadcasted_iota(jnp.int32, scores.shape, 1)
            scores = jnp.where(key <= row, scores, VERY_LOW)
            blocks, count = used_tiles(
                lists_ref, counts_ref, own, sources, head * conts + cont
            )
            tiles = [(scores, True)] + shard_scores(blocks, count, query, keys_ref)
            values = jnp.concatenate([own_ref[cont], shard_values(blocks, flipped_ref)], axis=1)
            made.append((tiles, values))
        after = []
        for tiles, values in made:
            stat, rounded = weigh(
                jnp.full((1, length), VERY_LOW, jnp.float32),
                jnp.zeros((1, length), jnp.float32),
                tiles,
            )
            after.append((stat, jnp.dot(values, rounded, preferred_element_type=jnp.float32)))
        for (head, cont), (stat, acc) in zip(work, after):
            put_stat(stat_refs[cont], head, stat)
            acc_refs[cont][head] = acc
        return carry

    lax.fori_loop(0, heads // together, some_heads, 0)


def arrivals(step, sources):
    spot = lax.axis_index("ctx")
    core = lax.axis_index("tp") % CORES
    if sources == 4:
        if step == 1:
            mine = jnp.bitwise_xor(spot, 1 + core)
            return ((mine, True), (jnp.bitwise_xor(mine, 3), True))
        far = jnp.bitwise_xor(spot, 3)
        return ((far, core == 1), (far, core == 0))
    mine = jnp.where(core == 0, spot - step, spot + step)
    theirs = jnp.where(core == 0, spot + step, spot - step)
    return tuple((s, (s >= 0) & (s < sources)) for s in (mine, theirs))


def steps_of(sources):
    return 2 if sources == 4 else sources - 1


def terms_of(step, sources):
    parts = [(which, *part) for which, part in enumerate(arrivals(step, sources))]
    return [parts] if sources == 4 and step == 2 else [[part] for part in parts]


def if_there(valid, count, body):
    def work():
        lax.fori_loop(0, count, body, 0)

    if valid is True:
        work()
    else:
        pl.when(valid)(work)


def scores_kernel(step, term, sources, conts, lists_ref, counts_ref, *refs):
    candidates = terms_of(step, sources)[term]
    q_refs, refs = refs[:conts], refs[conts:]
    stat_in, refs = refs[:conts], refs[conts:]
    key_refs, refs = refs[: len(candidates)], refs[len(candidates) :]
    stat_refs, weight_refs = refs[:conts], refs[conts:]
    heads = q_refs[0].shape[0]
    together = TOGETHER // conts
    for (_, source, valid), keys_ref in zip(candidates, key_refs):

        def some_heads(index, carry):
            work = [
                (index * together + j, cont) for j in range(together) for cont in range(conts)
            ]
            made = []
            for head, cont in work:
                blocks, count = used_tiles(
                    lists_ref, counts_ref, source, sources, head * conts + cont
                )
                made.append(shard_scores(blocks, count, q_refs[cont][head], keys_ref))
            after = []
            for (head, cont), tiles in zip(work, made):
                stat = stat_in[cont][head]
                after.append(weigh(stat[0:1], stat[1:2], tiles))
            for (head, cont), (stat, rounded) in zip(work, after):
                put_stat(stat_refs[cont], head, stat)
                weight_refs[cont][head] = rounded
            return carry

        if_there(valid, heads // together, some_heads)
    if len(candidates) == 1 and valid is not True:

        @pl.when(jnp.logical_not(valid))
        def _():
            for before, after in zip(stat_in, stat_refs):
                after[...] = before[...]


def sums_kernel(step, sources, conts, lists_ref, counts_ref, *refs):
    terms = terms_of(step, sources)
    acc_in, refs = refs[:conts], refs[conts:]
    value_refs, refs = refs[: len(terms)], refs[len(terms) :]
    held = []
    for _ in terms:
        held.append((refs[:conts], refs[conts : 2 * conts]))
        refs = refs[2 * conts :]
    weight_ref, refs = refs[0], refs[1:]
    acc_refs, (give_ref, *flipped_refs, sems) = refs[:conts], refs[conts:]
    copies = start_all(weight_copies(weight_ref, give_ref, sems, True))
    heads = acc_refs[0].shape[0]
    together = TOGETHER // conts
    groups = [[0, 1]] if all(t[0][2] is True for t in terms) else [[t] for t in range(len(terms))]
    for values_ref, flipped_ref in zip(value_refs, flipped_refs):
        both_ways(values_ref, flipped_ref)
    for group in groups:
        before = acc_in if group[0] == 0 else acc_refs

        def some_heads(index, carry):
            work = [
                (index * together + j, cont) for j in range(together) for cont in range(conts)
            ]
            after = []
            for head, cont in work:
                acc = before[cont][head]
                for term in group:
                    _, source, _ = terms[term][0]
                    stat_refs, weight_refs = held[term]
                    blocks, _ = used_tiles(
                        lists_ref, counts_ref, source, sources, head * conts + cont
                    )
                    acc = acc * stat_refs[cont][head, 2:3, :] + jnp.dot(
                        shard_values(blocks, flipped_refs[term]),
                        weight_refs[cont][head],
                        preferred_element_type=jnp.float32,
                    )
                after.append(acc)
            for (head, cont), acc in zip(work, after):
                acc_refs[cont][head] = acc
            return carry

        valid = terms[group[0]][0][2]
        if_there(valid, heads // together, some_heads)
        if valid is not True and group[0] == 0:

            @pl.when(jnp.logical_not(valid))
            def _():
                for source_ref, target_ref in zip(acc_in, acc_refs):
                    target_ref[...] = source_ref[...]

    for copy in copies:
        copy.wait()


def last_kernel(step, sources, conts, cont, fetch, lists_ref, counts_ref, *refs):
    terms = terms_of(step, sources)
    acc_in, refs = refs[0], refs[1:]
    value_refs, refs = refs[:2], refs[2:]
    held = [refs[2 * t : 2 * t + 2] for t in range(len(terms))]
    give_weight_ref, *refs = refs[2 * len(terms) :]
    if fetch:
        weight_ref, attended_ref, give_ref, keep_weight_ref, acc_ref, flipped_ref, sems = refs
        copies = start_all(weight_copies(weight_ref, keep_weight_ref, sems, False))
    else:
        attended_ref, give_ref, acc_ref, flipped_ref = refs
    heads = acc_in.shape[0]
    together = min(heads, TOGETHER)
    before = acc_in
    for number, (candidates, (stat_ref, weights_ref)) in enumerate(zip(terms, held)):
        for which, source, valid in candidates:

            def absorb():
                both_ways(value_refs[which], flipped_ref)

                def some_heads(index, carry):
                    work = [index * together + j for j in range(together)]
                    after = []
                    for head in work:
                        blocks, _ = used_tiles(
                            lists_ref, counts_ref, source, sources, head * conts + cont
                        )
                        after.append(
                            before[head] * stat_ref[head, 2:3, :]
                            + jnp.dot(
                                shard_values(blocks, flipped_ref),
                                weights_ref[head],
                                preferred_element_type=jnp.float32,
                            )
                        )
                    for head, acc in zip(work, after):
                        acc_ref[head] = acc
                    return carry

                lax.fori_loop(0, heads // together, some_heads, 0)

            pl.when(valid)(absorb)
        if len(candidates) == 1 and number == 0:

            @pl.when(jnp.logical_not(valid))
            def _():
                acc_ref[...] = acc_in[...]

        before = acc_ref
    stat_ref = held[-1][0]
    for head in range(heads):
        attended_ref[:, head * HD : (head + 1) * HD] = (
            (acc_ref[head] / stat_ref[head, 1:2, :]).T.astype(jnp.bfloat16)
        )
    for k in range(give_weight_ref.shape[0]):
        give_ref[k] = jnp.dot(
            attended_ref[...], give_weight_ref[k], preferred_element_type=jnp.float32
        ).astype(give_ref.dtype)
    if fetch:
        for copy in copies:
            copy.wait()


def onward_kernel(attended_ref, weight_ref, got_ref, *onward_refs):
    for k, onward_ref in enumerate(onward_refs, 1):
        onward_ref[...] = (
            jnp.dot(attended_ref[...], weight_ref[k], preferred_element_type=jnp.float32)
            + got_ref[k].astype(jnp.float32)
        ).astype(jnp.bfloat16)


def near_kernel(cont, attended_ref, weight_ref, got_ref, residual_ref, near_ref, own_ref, sem):
    share = near_ref.shape[1]
    start = pl.multiple_of(lax.axis_index("tp") * share, HD)
    copy = pltpu.make_async_copy(
        residual_ref.at[cont, :, pl.ds(start, share)], own_ref, sem.at[0]
    )
    copy.start()
    near_ref[...] = jnp.dot(
        attended_ref[...], weight_ref[0], preferred_element_type=jnp.float32
    ) + got_ref[0].astype(jnp.float32)
    copy.wait()
    near_ref[...] += own_ref[...].astype(jnp.float32)


def sum_kernel(count, *refs):
    near_ref, fars, (total_ref, squares_ref) = refs[0], refs[1 : 1 + count], refs[1 + count :]
    total = near_ref[...]
    for far_ref in fars:
        total = total + far_ref[...].astype(jnp.float32)
    total_ref[...] = total
    sums = jnp.sum(total * total, axis=1, keepdims=True)
    squares_ref[...] = jnp.broadcast_to(sums, (sums.shape[0], HD)).T[:8]


def stream_kernel(conts, *refs):
    for cont in range(conts):
        refs[conts][cont] = refs[cont][...].astype(jnp.bfloat16)


def norm_kernel(conts, model_width, *refs):
    totals, squares = refs[:conts], refs[conts:-2]
    gain_ref, normed_ref = refs[-2:]
    gain = gain_ref[...].astype(jnp.float32)
    for cont in range(conts):
        row = functools.reduce(jnp.add, [ref[cont * 8 : cont * 8 + 1, :] for ref in squares])
        scale = lax.rsqrt(row / model_width + 1e-05)
        scale = jnp.broadcast_to(scale, (HD, scale.shape[1])).T[:, 0:1]
        total = totals[cont][...]
        normed_ref[cont] = (total * scale * gain).astype(jnp.bfloat16)


def shards(
    queries,
    cont_keys,
    cont_values,
    prompt_keys,
    prompt_values,
    block_lists,
    tile_counts,
    out_weight,
    residual,
    norm_gain,
    *,
    sources,
    members,
):
    conts, length, width = queries.shape
    heads = width // HD
    rows_dev = prompt_keys.shape[0]
    model_width = residual.shape[2]
    share = norm_gain.shape[0]
    chips = members // CORES
    place = lax.axis_index("tp")
    pairs = heads * conts
    params = pltpu.CompilerParams(vmem_limit_bytes=VMEM_LIMIT)
    vmem = pl.BlockSpec(memory_space=pltpu.VMEM)
    hbm = pl.BlockSpec(memory_space=pltpu.HBM)

    def array(shape, dtype):
        return jax.ShapeDtypeStruct(shape, dtype)

    def cost(flops=1024):
        return pl.CostEstimate(flops=flops, bytes_accessed=1024, transcendentals=0)

    def in_hbm(x):
        return pltpu.with_memory_space_constraint(x, pltpu.HBM)

    kept = array((rows_dev, HD), jnp.bfloat16)
    keys = pl.pallas_call(
        functools.partial(pack_keys_kernel, heads),
        out_shape=kept,
        in_specs=[hbm],
        out_specs=vmem,
        scratch_shapes=[pltpu.SemaphoreType.DMA((1,))],
        compiler_params=params,
        cost_estimate=cost(),
        name="pack_keys",
    )(in_hbm(prompt_keys))
    values = pl.pallas_call(
        functools.partial(pack_values_kernel, heads),
        out_shape=kept,
        in_specs=[hbm],
        out_specs=vmem,
        scratch_shapes=[
            pltpu.VMEM((rows_dev, HD), jnp.bfloat16),
            pltpu.SemaphoreType.DMA((1,)),
        ],
        compiler_params=params,
        cost_estimate=cost(),
        name="pack_values",
    )(in_hbm(prompt_values))

    def across(step):
        def target(z, t):
            if sources == 4 and step == 1:
                return z ^ (1 + t % CORES)
            if sources == 4:
                return z ^ 1 if t % CORES == 1 else None
            to = z + step if t % CORES == 0 else z - step
            return to if 0 <= to < sources else None

        return [
            (z * members + t, target(z, t) * members + t)
            for z in range(sources)
            for t in range(members)
            if target(z, t) is not None
        ]

    sibling = [(t, t ^ 1) for t in range(members)]
    steps = steps_of(sources)
    smem = pl.BlockSpec(memory_space=pltpu.SMEM)
    lists = block_lists.reshape(-1)
    counts = tile_counts.reshape(-1)
    flipped = pltpu.VMEM((2 * rows_dev, HD), jnp.bfloat16)
    weight_shape = array((chips, width, share), jnp.bfloat16)
    accs_shape = (array((heads, HD, length), jnp.float32),) * conts
    stats_shape = (array((heads, 8, length), jnp.float32),) * conts
    qs_shape = (array((heads, HD, length), jnp.bfloat16),) * conts
    rounded_shape = (array((heads, TILES * BLK, length), jnp.bfloat16),) * conts

    made = pl.pallas_call(
        functools.partial(first_kernel, sources, conts),
        out_shape=accs_shape + stats_shape + qs_shape,
        in_specs=[smem, smem, vmem, vmem] + [hbm] * 3,
        out_specs=(vmem,) * (3 * conts),
        scratch_shapes=[
            flipped,
            pltpu.VMEM(queries.shape, jnp.bfloat16),
            pltpu.VMEM((conts, length, HD), jnp.bfloat16),
            pltpu.VMEM((conts, length, HD), jnp.bfloat16),
            pltpu.VMEM((conts, HD, length), jnp.bfloat16),
            pltpu.SemaphoreType.DMA((3,)),
        ],
        compiler_params=params,
        cost_estimate=cost(),
        name="attend_own",
    )(lists, counts, keys, values, in_hbm(queries), in_hbm(cont_keys), in_hbm(cont_values))
    accs, stats, qs = (tuple(made[i * conts : (i + 1) * conts]) for i in range(3))

    def scores(step, term, stats, keys):
        made = pl.pallas_call(
            functools.partial(scores_kernel, step, term, sources, conts),
            out_shape=stats_shape + rounded_shape,
            in_specs=[smem, smem] + [vmem] * (2 * conts + len(keys)),
            out_specs=(vmem,) * (2 * conts),
            compiler_params=params,
            cost_estimate=cost(),
            name="scores",
        )(lists, counts, *qs, *stats, *keys)
        return tuple(made[:conts]), tuple(made[conts:])

    def weighted_sums(step, accs, values, held):
        *accs, give_weight = pl.pallas_call(
            functools.partial(sums_kernel, step, sources, conts),
            out_shape=accs_shape + (weight_shape,),
            in_specs=[smem, smem] + [vmem] * (conts + 2 + 4 * conts) + [hbm],
            out_specs=(vmem,) * (conts + 1),
            scratch_shapes=[flipped, flipped, pltpu.SemaphoreType.DMA((chips,))],
            compiler_params=params,
            cost_estimate=cost(),
            name="weighted_sums",
        )(
            lists,
            counts,
            *accs,
            *values,
            *[x for stats, rounded in held for x in (*stats, *rounded)],
            in_hbm(out_weight),
        )
        return tuple(accs), give_weight

    for step in range(1, steps + 1):
        sent = mine if sources == 4 and step == 2 else (keys, values)
        mine_keys, mine_values = [lax.ppermute(x, ("ctx", "tp"), across(step)) for x in sent]
        mine_keys, accs, stats = lax.optimization_barrier((mine_keys, accs, stats))
        their_keys = jnp.concatenate(
            [lax.ppermute(x, "tp", sibling) for x in jnp.split(mine_keys, 2)]
        )
        held = []
        if sources == 4 and step == 2:
            held.append(scores(step, 0, stats, (mine_keys, their_keys)))
        else:
            held.append(scores(step, 0, stats, (mine_keys,)))
            held.append(scores(step, 1, held[0][0], (their_keys,)))
        stats = held[-1][0]
        mine_keys, mine_values, held, stats = lax.optimization_barrier(
            (mine_keys, mine_values, held, stats)
        )
        their_values = lax.ppermute(mine_values, "tp", sibling)
        mine = (mine_keys, mine_values)
        if step < steps:
            accs, give_weight = weighted_sums(step, accs, (mine_values, their_values), held)

    def attend_last(cont):
        fetch = cont == 0
        terms = [x for stats, rounded in held for x in (stats[cont], rounded[cont])]
        return pl.pallas_call(
            functools.partial(last_kernel, steps, sources, conts, cont, fetch),
            out_shape=(
                array((length, width), jnp.bfloat16),
                array((chips, length, share), jnp.bfloat16),
            )
            + (weight_shape,) * fetch,
            in_specs=[smem, smem] + [vmem] * (4 + len(terms)) + [hbm] * fetch,
            out_specs=(vmem,) * (2 + fetch),
            scratch_shapes=[pltpu.VMEM((heads, HD, length), jnp.float32), flipped]
            + [pltpu.SemaphoreType.DMA((chips,))] * fetch,
            compiler_params=params,
            cost_estimate=cost(),
            name="attend_last",
        )(
            lists,
            counts,
            accs[cont],
            mine_values,
            their_values,
            *terms,
            give_weight,
            *([in_hbm(out_weight)] * fetch),
        )

    def onward(attended, got):
        parts = pl.pallas_call(
            onward_kernel,
            out_shape=(array((length, share), jnp.bfloat16),) * (chips - 1),
            in_specs=[vmem] * 3,
            out_specs=(vmem,) * (chips - 1),
            compiler_params=params,
            cost_estimate=cost(),
            name="project_onward",
        )(attended, keep_weight, got)
        far = []
        for k in range(1, chips):
            to_chip = [
                (t, (t // CORES + k) % chips * CORES + t % CORES) for t in range(members)
            ]
            far.append(lax.ppermute(parts[k - 1], "tp", to_chip))
        return parts, far

    def near(cont, attended, got):
        return pl.pallas_call(
            functools.partial(near_kernel, cont),
            out_shape=array((length, share), jnp.float32),
            in_specs=[vmem] * 3 + [hbm],
            out_specs=vmem,
            scratch_shapes=[
                pltpu.VMEM((length, share), jnp.bfloat16),
                pltpu.SemaphoreType.DMA((1,)),
            ],
            compiler_params=params,
            cost_estimate=cost(),
            name="project_near",
        )(attended, keep_weight, got, in_hbm(residual))

    attended, give, keep_weight = attend_last(0)
    nears, fars = [], []
    for cont in range(conts):
        got = lax.ppermute(give, "tp", sibling)
        here = attended
        if cont + 1 < conts:
            attended, give = attend_last(cont + 1)
            got, give = lax.optimization_barrier((got, give))
        _, far = onward(here, got)
        fars.append(far)
        nears.append(near(cont, here, got))

    totals, squares = [], []
    for cont in range(conts):
        total, square = pl.pallas_call(
            functools.partial(sum_kernel, chips - 1),
            out_shape=(array((length, share), jnp.float32), array((8, length), jnp.float32)),
            in_specs=[vmem] * chips,
            out_specs=(vmem,) * 2,
            compiler_params=params,
            cost_estimate=cost(),
            name="add_up",
        )(nears[cont], *fars[cont])
        totals.append(total)
        squares.append(square)
    squares = jnp.concatenate(squares, axis=0)
    squares = squares + lax.ppermute(squares, "tp", sibling)
    all_squares = [squares] + [
        lax.ppermute(
            squares,
            "tp",
            [(t, (t // CORES + k) % chips * CORES + t % CORES) for t in range(members)],
        )
        for k in range(1, chips)
    ]
    out = array((conts, length, share), jnp.bfloat16)
    stream = pl.pallas_call(
        functools.partial(stream_kernel, conts),
        out_shape=out,
        in_specs=[vmem] * conts,
        out_specs=vmem,
        compiler_params=params,
        cost_estimate=cost(),
        name="stream",
    )(*totals)
    normed = pl.pallas_call(
        functools.partial(norm_kernel, conts, model_width),
        out_shape=out,
        in_specs=[vmem] * (conts + chips + 1),
        out_specs=vmem,
        compiler_params=params,
        cost_estimate=cost(),
        name="norm",
    )(*totals, *all_squares, norm_gain.reshape(1, share))
    return stream, normed


def solution(mesh):
    placed = (
        P(("grp", "ctx"), None, "tp"),
        P(("grp", "ctx"), None, None),
        P(("grp", "ctx"), None, None),
        P(("grp", "ctx"), None),
        P(("grp", "ctx"), None),
        P("tp", ("grp", "ctx"), None, None),
        P("tp", ("grp", "ctx"), None),
        P("tp", None),
        P(("grp", "ctx"), None, None),
        P("tp"),
    )
    return jax.shard_map(
        functools.partial(
            shards, sources=mesh.shape["ctx"], members=mesh.shape["tp"]
        ),
        mesh=mesh,
        in_specs=placed,
        out_specs=(P(("grp", "ctx"), None, "tp"), P(("grp", "ctx"), None, "tp")),
        check_vma=False,
    )
```

time: 58 us -> 59.2 us (1.021)
  waiting for transfers between devices: 16.8 us -> 13.3 us
  Pallas kernels: 25.3 us -> 27.4 us
  local copies, waits for them, and re-layouts: 0.04 us -> 1.78 us
  starting transfers between devices: 14.6 us -> 15.5 us
    ppermute x4, waiting for transfers between devices: 5.92 us -> 0.15 us  [shards(): lax.ppermute(x, ('ctx', 'tp'), across(step))]
    ppermute x3 -> x4, starting transfers between devices: 2.94 us -> 5.43 us  [shards(): lax.ppermute(x, 'tp', sibling)]
    ppermute x5 -> x4, waiting for transfers between devices: 1.73 us -> 3.82 us  [the longest x2 1.35 us: shards(): their_values = lax.ppermute(mine_values, 'tp', sibling)]
    pallas_call x6 -> x9, Pallas kernels: 19.4 us -> 21.4 us  [the longest x3 6.21 us: scores(): pl.pallas_call(functools.partial(scores_kernel, step, term, sources, cont...]
    ppermute x5 -> x4, starting transfers between devices: 3.62 us -> 2.18 us  [the longest x1 1.49 us: shards(): lax.ppermute(squares, 'tp', [(t, (t // CORES + k) % chips * CORES + t % C...]
    reshape x0 -> x2, local copies, waits for them, and re-layouts: none -> 0.95 us  [the longest x1 0.86 us: shards(): lists = block_lists.reshape(-1)]
    unnamed x3 -> x4, local copies, waits for them, and re-layouts: 0.01 us -> 0.78 us
    ppermute x3 -> x4, waiting for transfers between devices: 1.08 us -> 1.27 us  [shards(): lax.ppermute(x, 'tp', sibling)]
  transfers between devices with their start and end apart: 16 -> 16, of which waited for: 9 -> 8; matrix products, arithmetic and copies ran while one was open for 0% -> 3% of each run, Pallas kernels for 34% -> 38%
where the time goes in v7:
time: 59.2 us; the launch traced here: 58.9 us
  Pallas kernels  27.4 us (46%)
  starting transfers between devices  15.5 us (26%)
  waiting for transfers between devices  13.3 us (22%)
  local copies, waits for them, and re-layouts  1.78 us (3%)
  between operations  0.84 us (1%)
    ppermute x2, waiting for transfers between devices, onward(): far.append(lax.ppermute(parts[k - 1], 'tp', to_chip))  8.09 us
    pallas_call x3, Pallas kernels, scores(): pl.pallas_call(functools.partial(scores_kernel, step, term, sources, cont...  6.21 us
    ppermute x4, starting transfers between devices, shards(): lax.ppermute(x, 'tp', sibling)  5.43 us
    pallas_call x2, Pallas kernels, attend_last(): pl.pallas_call(functools.partial(last_kernel, steps, sources, conts, cont...  5.29 us
    ppermute x4, starting transfers between devices, shards(): lax.ppermute(x, ('ctx', 'tp'), across(step))  4.53 us
    pallas_call x1, Pallas kernels, shards(): pl.pallas_call(functools.partial(first_kernel, sources, conts), out_shape...  4.41 us
    pallas_call x1, Pallas kernels, weighted_sums(): pl.pallas_call(functools.partial(sums_kernel, step, sources, conts), out_...  3.66 us
    ppermute x2, starting transfers between devices, onward(): far.append(lax.ppermute(parts[k - 1], 'tp', to_chip))  2.68 us
  transfers between devices with their start and end apart: 16, of which 8 were waited for; matrix products, arithmetic and copies ran while one was open for 3% of the time, Pallas kernels for 38%

profile of v7, /device:TPU:0, one launch (start us, length us, event | category | flops | bytes accessed | tf_op | source)
XLA Modules:
  0.0 58.9 jit_solution(5194221210839100804)
XLA Ops:
  0.6 1.0 %pack_keys.1.keys_ref = bf16[1024,128]{1,0:T(8,128)(2,1)S(1)} custom-call(bf16[1024,256]{1,0:T(8,128)(2,1)} %keys_ref.1), custom_call_target="tpu_custom_call" | custom-call | flops 1024 | bytes 1024 | tf_op jit(solution)/shard_map/pack_keys/pallas_call | solution.py:473
  1.6 3.1 %collective-permute-start = (bf16[1024,128]{1,0:T(8,128)(2,1)S(1)}, bf16[1024,128]{1,0:T(8,128)(2,1)S(1)}, u32[]{:S(2)}, u32[]{:S(2)}) collective-permute-start(bf16[1024,128]{1,0:T(8,128)(2,1)S(1)} %pack_keys.1.keys_ref), channel_id=1, source_target_pairs={{0,4},{1,9},{2,6},{3,11},{4,0},{5,13},{6,2},{7,15},{8,12},{9,1},{1... | collective-permute-start | bytes 786440 | tf_op jit(solution)/shard_map/ppermute | solution.py:578
  4.7 1.1 %pack_values.1.values_ref = bf16[1024,128]{1,0:T(8,128)(2,1)S(1)} custom-call(bf16[1024,256]{1,0:T(8,128)(2,1)} %values_ref.1), custom_call_target="tpu_custom_call" | custom-call | flops 1024 | bytes 1024 | tf_op jit(solution)/shard_map/pack_values/pallas_call | solution.py:483
  6.7 0.9 %reshape.13.lists_ref = s32[512]{0:T(512)S(1)} reshape(s32[8,2,4,8]{3,2,1,0:T(4,128)} %param.15) | data formatting | bytes 4096 | tf_op jit(solution)/shard_map/reshape | solution.py:516
  7.6 4.4 %attend_own.1 = (f32[8,128,128]{2,1,0:T(8,128)S(1)}, f32[8,128,128]{2,1,0:T(8,128)S(1)}, f32[8,8,128]{2,1,0:T(8,128)S(1)}, f32[8,8,128]{2,1,0:T(8,128)S(1)}, bf1...) custom-call(s32[512]{0:T(512)S(1)} %reshape.13.lists_ref, s32[64]{0:T(128)S(1)} %reshape.14.counts_ref, ...), custom_call_target="tpu_custom_call" | custom-call | flops 1024 | bytes 1024 | tf_op jit(solution)/shard_map/attend_own/pallas_call | solution.py:525
  12.8 2.0 %scores.3 = (f32[8,8,128]{2,1,0:T(8,128)S(1)}, f32[8,8,128]{2,1,0:T(8,128)S(1)}, bf16[8,512,128]{2,1,0:T(8,128)(2,1)S(1)}, bf16[8,512,128]{2,1,0:T(8,128)(2,1)S(1)}) custom-call(s32[512]{0:T(512)S(1)} %reshape.13.lists_ref, s32[64]{0:T(128)S(1)} %reshape.14.counts_ref, bf16[8,128,128]{2,1,0:T(8,128)(2,1)S(1)} %get-tuple-element.66.refs_0_, ...), custom_call_target="tpu_custom_call" | custom-call | flops 1024 | bytes 1024 | tf_op jit(solution)/shard_map/scores/pallas_call | solution.py:545
  14.9 2.1 %scores.4 = (f32[8,8,128]{2,1,0:T(8,128)S(1)}, f32[8,8,128]{2,1,0:T(8,128)S(1)}, bf16[8,512,128]{2,1,0:T(8,128)(2,1)S(1)}, bf16[8,512,128]{2,1,0:T(8,128)(2,1)S(1)}) custom-call(s32[512]{0:T(512)S(1)} %reshape.13.lists_ref, s32[64]{0:T(128)S(1)} %reshape.14.counts_ref, bf16[8,128,128]{2,1,0:T(8,128)(2,1)S(1)} %get-tuple-element.66.refs_0_, ...), custom_call_target="tpu_custom_call" | custom-call | flops 1024 | bytes 1024 | tf_op jit(solution)/shard_map/scores/pallas_call | solution.py:545
  18.9 3.7 %weighted_sums.1 = (f32[8,128,128]{2,1,0:T(8,128)S(1)}, f32[8,128,128]{2,1,0:T(8,128)S(1)}, bf16[2,1024,1024]{2,1,0:T(8,128)(2,1)S(1)}) custom-call(s32[512]{0:T(512)S(1)} %reshape.13.lists_ref, s32[64]{0:T(128)S(1)} %reshape.14.counts_ref, f32[8,128,128]{2,1,0:T(8,128)S(1)} %get-tuple-element.79.refs_0_, f32[8,128,128]{2,1,0:T(8,128)S(1)} %get-tuple-element.80.refs_1_, ...), custom_call_target="tpu_custom_call" | custom-call | flops 1024 | bytes 1024 | tf_op jit(solution)/shard_map/weighted_sums/pallas_call | solution.py:557
  22.6 4.6 %collective-permute-start.7 = (bf16[512,128]{1,0:T(8,128)(2,1)S(1)}, bf16[512,128]{1,0:T(8,128)(2,1)S(1)}, u32[]{:S(2)}, u32[]{:S(2)}) collective-permute-start(bf16[512,128]{1,0:T(8,128)(2,1)S(1)} %get-tuple-element.120), channel_id=1, source_target_pairs={{0,1},{1,0},{2,3},{3,2},{4,5},{5,4},{6,7},{7,6},{8,9},{9,8},{10,11... | collective-permute-start | bytes 393224 | tf_op jit(solution)/shard_map/ppermute | solution.py:581
  27.3 0.9 %collective-permute-done.7 = bf16[512,128]{1,0:T(8,128)(2,1)S(1)} collective-permute-done((bf16[512,128]{1,0:T(8,128)(2,1)S(1)}, bf16[512,128]{1,0:T(8,128)(2,1)S(1)}, u32[]{:S(2)}, u32[]{:S(2)}) %collective-permute-start.7) | collective-permute-done | bytes 131104 | tf_op jit(solution)/shard_map/ppermute | solution.py:581
  28.6 2.1 %scores.5 = (f32[8,8,128]{2,1,0:T(8,128)S(1)}, f32[8,8,128]{2,1,0:T(8,128)S(1)}, bf16[8,512,128]{2,1,0:T(8,128)(2,1)S(1)}, bf16[8,512,128]{2,1,0:T(8,128)(2,1)S(1)}) custom-call(s32[512]{0:T(512)S(1)} %reshape.13.lists_ref, s32[64]{0:T(128)S(1)} %reshape.14.counts_ref, bf16[8,128,128]{2,1,0:T(8,128)(2,1)S(1)} %get-tuple-element.66.refs_0_, ...), custom_call_target="tpu_custom_call" | custom-call | flops 1024 | bytes 1024 | tf_op jit(solution)/shard_map/scores/pallas_call | solution.py:545
  30.9 1.3 %collective-permute-done.9.refs_2_ = bf16[1024,128]{1,0:T(8,128)(2,1)S(1)} collective-permute-done((bf16[1024,128]{1,0:T(8,128)(2,1)S(1)}, bf16[1024,128]{1,0:T(8,128)(2,1)S(1)}, u32[]{:S(2)}, u32[]{:S(2)}) %collective-permute-start.9) | collective-permute-done | bytes 262176 | tf_op jit(solution)/shard_map/ppermute | solution.py:593
  32.3 2.8 %attend_last.2 = (bf16[128,1024]{1,0:T(8,128)(2,1)S(1)}, bf16[2,128,1024]{2,1,0:T(8,128)(2,1)S(1)}, bf16[2,1024,1024]{2,1,0:T(8,128)(2,1)S(1)}) custom-call(s32[512]{0:T(512)S(1)} %reshape.13.lists_ref, s32[64]{0:T(128)S(1)} %reshape.14.counts_ref, f32[8,128,128]{2,1,0:T(8,128)S(1)} %get-tuple-element.94.refs_0_, ...), custom_call_target="tpu_custom_call" | custom-call | flops 1024 | bytes 1024 | tf_op jit(solution)/shard_map/attend_last/pallas_call | solution.py:601
  35.4 2.5 %attend_last.3 = (bf16[128,1024]{1,0:T(8,128)(2,1)S(1)}, bf16[2,128,1024]{2,1,0:T(8,128)(2,1)S(1)}) custom-call(s32[512]{0:T(512)S(1)} %reshape.13.lists_ref, s32[64]{0:T(128)S(1)} %reshape.14.counts_ref, f32[8,128,128]{2,1,0:T(8,128)S(1)} %get-tuple-element.109.refs_0_, bf16[1024,128]{1,0:T(8,128)(2,1)S(1)} %collective-permute-done.6.refs_1_, ...), custom_call_target="tpu_custom_call" | custom-call | flops 1024 | bytes 1024 | tf_op jit(solution)/shard_map/attend_last/pallas_call | solution.py:601
  38.7 1.6 %collective-permute-start.11 = (bf16[128,1024]{1,0:T(8,128)(2,1)S(1)}, bf16[128,1024]{1,0:T(8,128)(2,1)S(1)}, u32[]{:S(2)}, u32[]{:S(2)}) collective-permute-start(bf16[128,1024]{1,0:T(8,128)(2,1)S(1)} %project_onward.2), channel_id=1, source_target_pairs={{0,2},{1,3},{2,0},{3,1},{4,6},{5,7},{6,4},{7,5},{8,10},{9,11},{10,... | collective-permute-start | bytes 786440 | tf_op jit(solution)/shard_map/ppermute | solution.py:641
  40.7 1.1 %collective-permute-start.13 = (bf16[128,1024]{1,0:T(8,128)(2,1)S(1)}, bf16[128,1024]{1,0:T(8,128)(2,1)S(1)}, u32[]{:S(2)}, u32[]{:S(2)}) collective-permute-start(bf16[128,1024]{1,0:T(8,128)(2,1)S(1)} %project_onward.3), channel_id=1, source_target_pairs={{0,2},{1,3},{2,0},{3,1},{4,6},{5,7},{6,4},{7,5},{8,10},{9,11},{10,... | collective-permute-start | bytes 786440 | tf_op jit(solution)/shard_map/ppermute | solution.py:641
  41.8 1.3 %project_near.2.refs_0_ = f32[128,1024]{1,0:T(8,128)S(1)} custom-call(bf16[128,1024]{1,0:T(8,128)(2,1)S(1)} %get-tuple-element.106.attended_ref, bf16[2,1024,1024]{2,1,0:T(8,128)(2,1)S(1)} %get-tuple-element.107.weight_ref, bf16[2,128,1024]{2,1,0:T(8,128)(2,1)S(1)} %collective-permute-done.10.got_ref, bf16[2,128,4096]{2,1,0:T(8,128)(2,1)} %residual_ref.3), custom_call_target="tpu_custom_call" | custom-call | flops 1024 | bytes 1024 | tf_op jit(solution)/shard_map/project_near/pallas_call | solution.py:645
  43.2 4.7 %collective-permute-done.11.refs_1_ = bf16[128,1024]{1,0:T(8,128)(2,1)S(1)} collective-permute-done((bf16[128,1024]{1,0:T(8,128)(2,1)S(1)}, bf16[128,1024]{1,0:T(8,128)(2,1)S(1)}, u32[]{:S(2)}, u32[]{:S(2)}) %collective-permute-start.11) | collective-permute-done | bytes 262176 | tf_op jit(solution)/shard_map/ppermute | solution.py:641
  48.1 1.3 %project_near.3.refs_0_ = f32[128,1024]{1,0:T(8,128)S(1)} custom-call(bf16[128,1024]{1,0:T(8,128)(2,1)S(1)} %get-tuple-element.115.attended_ref, bf16[2,1024,1024]{2,1,0:T(8,128)(2,1)S(1)} %get-tuple-element.107.weight_ref, bf16[2,128,1024]{2,1,0:T(8,128)(2,1)S(1)} %collective-permute-done.12.got_ref, bf16[2,128,4096]{2,1,0:T(8,128)(2,1)} %residual_ref.3), custom_call_target="tpu_custom_call" | custom-call | flops 1024 | bytes 1024 | tf_op jit(solution)/shard_map/project_near/pallas_call | solution.py:645
  49.4 3.3 %collective-permute-done.13.refs_1_ = bf16[128,1024]{1,0:T(8,128)(2,1)S(1)} collective-permute-done((bf16[128,1024]{1,0:T(8,128)(2,1)S(1)}, bf16[128,1024]{1,0:T(8,128)(2,1)S(1)}, u32[]{:S(2)}, u32[]{:S(2)}) %collective-permute-start.13) | collective-permute-done | bytes 262176 | tf_op jit(solution)/shard_map/ppermute | solution.py:641
  53.0 1.2 %collective-permute-done.14 = f32[16,128]{1,0:T(8,128)S(1)} collective-permute-done((f32[16,128]{1,0:T(8,128)S(1)}, f32[16,128]{1,0:T(8,128)S(1)}, u32[]{:S(2)}, u32[]{:S(2)}) %collective-permute-start.14) | collective-permute-done | bytes 8224 | tf_op jit(solution)/shard_map/ppermute | solution.py:685
  54.2 1.5 %collective-permute-start.15 = (f32[16,128]{1,0:T(8,128)S(1)}, f32[16,128]{1,0:T(8,128)S(1)}, u32[]{:S(2)}, u32[]{:S(2)}) collective-permute-start(f32[16,128]{1,0:T(8,128)S(1)} %add.3.refs_2_), channel_id=1, source_target_pairs={{0,2},{1,3},{2,0},{3,1},{4,6},{5,7},{6,4},{7,5},{8,10},{9,11},{10,... | collective-permute-start | bytes 24584 | tf_op jit(solution)/shard_map/ppermute | solution.py:687
  56.5 1.3 %collective-permute-done.15.refs_3_ = f32[16,128]{1,0:T(8,128)S(1)} collective-permute-done((f32[16,128]{1,0:T(8,128)S(1)}, f32[16,128]{1,0:T(8,128)S(1)}, u32[]{:S(2)}, u32[]{:S(2)}) %collective-permute-start.15) | collective-permute-done | bytes 8224 | tf_op jit(solution)/shard_map/ppermute | solution.py:687
  57.8 1.0 %norm.1 = bf16[2,128,1024]{2,1,0:T(8,128)(2,1)} custom-call(f32[128,1024]{1,0:T(8,128)S(1)} %get-tuple-element.114.refs_0_, f32[128,1024]{1,0:T(8,128)S(1)} %get-tuple-element.117.refs_1_, f32[16,128]{1,0:T(8,128)S(1)} %add.3.refs_2_, f32[16,128]{1,0:T(8,128)S(1)} %collective-permute-done.15.refs_3_, bf16[1,1024]{1,0:T(2,128)(2,1)S(1)} %reshape.15.refs_4_), custom_call_target="tpu_custom_call" | custom-call | flops 1024 | bytes 1024 | tf_op jit(solution)/shard_map/norm/pallas_call | solution.py:704
  (38 shorter events, 7.1 us)
Async XLA Ops:
  1.6 10.4 %collective-permute-start = (bf16[1024,128]{1,0:T(8,128)(2,1)S(1)}, bf16[1024,128]{1,0:T(8,128)(2,1)S(1)}, u32[]{:S(2)}, u32[]{:S(2)}) collective-permute-start(bf16[1024,128]{1,0:T(8,128)(2,1)S(1)} %pack_keys.1.keys_ref), channel_id=1, source_target_pairs={{0,4},{1,9},{2,6},{3,11},{4,0},{5,13},{6,2},{7,15},{8,12},{9,1},{1... | collective-permute-start | bytes 786440 | tf_op jit(solution)/shard_map/ppermute | solution.py:578
  5.8 11.3 %collective-permute-start.1 = (bf16[1024,128]{1,0:T(8,128)(2,1)S(1)}, bf16[1024,128]{1,0:T(8,128)(2,1)S(1)}, u32[]{:S(2)}, u32[]{:S(2)}) collective-permute-start(bf16[1024,128]{1,0:T(8,128)(2,1)S(1)} %pack_values.1.values_ref), channel_id=1, source_target_pairs={{0,4},{1,9},{2,6},{3,11},{4,0},{5,13},{6,2},{7,15},{8,12},{9,1},{1... | collective-permute-start | bytes 786440 | tf_op jit(solution)/shard_map/ppermute | solution.py:578
  12.1 2.8 %collective-permute-start.2 = (bf16[512,128]{1,0:T(8,128)(2,1)S(1)}, bf16[512,128]{1,0:T(8,128)(2,1)S(1)}, u32[]{:S(2)}, u32[]{:S(2)}) collective-permute-start(bf16[512,128]{1,0:T(8,128)(2,1)S(1)} %get-tuple-element.122), channel_id=1, source_target_pairs={{0,1},{1,0},{2,3},{3,2},{4,5},{5,4},{6,7},{7,6},{8,9},{9,8},{10,11... | collective-permute-start | bytes 393224 | tf_op jit(solution)/shard_map/ppermute | solution.py:581
  12.7 2.1 %collective-permute-start.3 = (bf16[512,128]{1,0:T(8,128)(2,1)S(1)}, bf16[512,128]{1,0:T(8,128)(2,1)S(1)}, u32[]{:S(2)}, u32[]{:S(2)}) collective-permute-start(bf16[512,128]{1,0:T(8,128)(2,1)S(1)} %get-tuple-element.123), channel_id=1, source_target_pairs={{0,1},{1,0},{2,3},{3,2},{4,5},{5,4},{6,7},{7,6},{8,9},{9,8},{10,11... | collective-permute-start | bytes 393224 | tf_op jit(solution)/shard_map/ppermute | solution.py:581
  17.1 1.8 %collective-permute-start.5 = (bf16[1024,128]{1,0:T(8,128)(2,1)S(1)}, bf16[1024,128]{1,0:T(8,128)(2,1)S(1)}, u32[]{:S(2)}, u32[]{:S(2)}) collective-permute-start(bf16[1024,128]{1,0:T(8,128)(2,1)S(1)} %collective-permute-done.1.refs_2_), channel_id=1, source_target_pairs={{0,1},{1,0},{2,3},{3,2},{4,5},{5,4},{6,7},{7,6},{8,9},{9,8},{10,11... | collective-permute-start | bytes 786440 | tf_op jit(solution)/shard_map/ppermute | solution.py:593
  17.5 5.0 %collective-permute-start.4 = (bf16[1024,128]{1,0:T(8,128)(2,1)S(1)}, bf16[1024,128]{1,0:T(8,128)(2,1)S(1)}, u32[]{:S(2)}, u32[]{:S(2)}) collective-permute-start(bf16[1024,128]{1,0:T(8,128)(2,1)S(1)} %collective-permute-done.refs_4_), channel_id=1, source_target_pairs={{1,5},{3,7},{5,1},{7,3},{9,13},{11,15},{13,9},{15,11},{17,21},{19,... | collective-permute-start | bytes 786440 | tf_op jit(solution)/shard_map/ppermute | solution.py:578
  18.2 12.5 %collective-permute-start.6 = (bf16[1024,128]{1,0:T(8,128)(2,1)S(1)}, bf16[1024,128]{1,0:T(8,128)(2,1)S(1)}, u32[]{:S(2)}, u32[]{:S(2)}) collective-permute-start(bf16[1024,128]{1,0:T(8,128)(2,1)S(1)} %collective-permute-done.1.refs_2_), channel_id=1, source_target_pairs={{1,5},{3,7},{5,1},{7,3},{9,13},{11,15},{13,9},{15,11},{17,21},{19,... | collective-permute-start | bytes 786440 | tf_op jit(solution)/shard_map/ppermute | solution.py:578
  22.6 5.6 %collective-permute-start.7 = (bf16[512,128]{1,0:T(8,128)(2,1)S(1)}, bf16[512,128]{1,0:T(8,128)(2,1)S(1)}, u32[]{:S(2)}, u32[]{:S(2)}) collective-permute-start(bf16[512,128]{1,0:T(8,128)(2,1)S(1)} %get-tuple-element.120), channel_id=1, source_target_pairs={{0,1},{1,0},{2,3},{3,2},{4,5},{5,4},{6,7},{7,6},{8,9},{9,8},{10,11... | collective-permute-start | bytes 393224 | tf_op jit(solution)/shard_map/ppermute | solution.py:581
  27.2 1.3 %collective-permute-start.8 = (bf16[512,128]{1,0:T(8,128)(2,1)S(1)}, bf16[512,128]{1,0:T(8,128)(2,1)S(1)}, u32[]{:S(2)}, u32[]{:S(2)}) collective-permute-start(bf16[512,128]{1,0:T(8,128)(2,1)S(1)} %get-tuple-element.121), channel_id=1, source_target_pairs={{0,1},{1,0},{2,3},{3,2},{4,5},{5,4},{6,7},{7,6},{8,9},{9,8},{10,11... | collective-permute-start | bytes 393224 | tf_op jit(solution)/shard_map/ppermute | solution.py:581
  30.7 1.6 %collective-permute-start.9 = (bf16[1024,128]{1,0:T(8,128)(2,1)S(1)}, bf16[1024,128]{1,0:T(8,128)(2,1)S(1)}, u32[]{:S(2)}, u32[]{:S(2)}) collective-permute-start(bf16[1024,128]{1,0:T(8,128)(2,1)S(1)} %collective-permute-done.6.refs_1_), channel_id=1, source_target_pairs={{0,1},{1,0},{2,3},{3,2},{4,5},{5,4},{6,7},{7,6},{8,9},{9,8},{10,11... | collective-permute-start | bytes 786440 | tf_op jit(solution)/shard_map/ppermute | solution.py:593
  35.1 2.7 %collective-permute-start.10 = (bf16[2,128,1024]{2,1,0:T(8,128)(2,1)S(1)}, bf16[2,128,1024]{2,1,0:T(8,128)(2,1)S(1)}, u32[]{:S(2)}, u32[]{:S(2)}) collective-permute-start(bf16[2,128,1024]{2,1,0:T(8,128)(2,1)S(1)} %get-tuple-element.108), channel_id=1, source_target_pairs={{0,1},{1,0},{2,3},{3,2},{4,5},{5,4},{6,7},{7,6},{8,9},{9,8},{10,11... | collective-permute-start | bytes 1572872 | tf_op jit(solution)/shard_map/ppermute | solution.py:662
  37.9 2.4 %collective-permute-start.12 = (bf16[2,128,1024]{2,1,0:T(8,128)(2,1)S(1)}, bf16[2,128,1024]{2,1,0:T(8,128)(2,1)S(1)}, u32[]{:S(2)}, u32[]{:S(2)}) collective-permute-start(bf16[2,128,1024]{2,1,0:T(8,128)(2,1)S(1)} %get-tuple-element.116), channel_id=1, source_target_pairs={{0,1},{1,0},{2,3},{3,2},{4,5},{5,4},{6,7},{7,6},{8,9},{9,8},{10,11... | collective-permute-start | bytes 1572872 | tf_op jit(solution)/shard_map/ppermute | solution.py:662
  38.7 9.2 %collective-permute-start.11 = (bf16[128,1024]{1,0:T(8,128)(2,1)S(1)}, bf16[128,1024]{1,0:T(8,128)(2,1)S(1)}, u32[]{:S(2)}, u32[]{:S(2)}) collective-permute-start(bf16[128,1024]{1,0:T(8,128)(2,1)S(1)} %project_onward.2), channel_id=1, source_target_pairs={{0,2},{1,3},{2,0},{3,1},{4,6},{5,7},{6,4},{7,5},{8,10},{9,11},{10,... | collective-permute-start | bytes 786440 | tf_op jit(solution)/shard_map/ppermute | solution.py:641
  40.7 12.1 %collective-permute-start.13 = (bf16[128,1024]{1,0:T(8,128)(2,1)S(1)}, bf16[128,1024]{1,0:T(8,128)(2,1)S(1)}, u32[]{:S(2)}, u32[]{:S(2)}) collective-permute-start(bf16[128,1024]{1,0:T(8,128)(2,1)S(1)} %project_onward.3), channel_id=1, source_target_pairs={{0,2},{1,3},{2,0},{3,1},{4,6},{5,7},{6,4},{7,5},{8,10},{9,11},{10,... | collective-permute-start | bytes 786440 | tf_op jit(solution)/shard_map/ppermute | solution.py:641
  48.1 7.6 %copy-start = (bf16[1024]{0:T(1024)(128)(2,1)S(1)}, bf16[1024]{0:T(1024)(128)(2,1)}, u32[]{:S(2)}) copy-start(bf16[1024]{0:T(1024)(128)(2,1)} %param.19) | copy-start | bytes 6148
  53.0 1.2 %collective-permute-start.14 = (f32[16,128]{1,0:T(8,128)S(1)}, f32[16,128]{1,0:T(8,128)S(1)}, u32[]{:S(2)}, u32[]{:S(2)}) collective-permute-start(f32[16,128]{1,0:T(8,128)S(1)} %constant_dynamic-update-slice_fusion), channel_id=1, source_target_pairs={{0,1},{1,0},{2,3},{3,2},{4,5},{5,4},{6,7},{7,6},{8,9},{9,8},{10,11... | collective-permute-start | bytes 24584 | tf_op jit(solution)/shard_map/ppermute | solution.py:685
  54.2 3.7 %collective-permute-start.15 = (f32[16,128]{1,0:T(8,128)S(1)}, f32[16,128]{1,0:T(8,128)S(1)}, u32[]{:S(2)}, u32[]{:S(2)}) collective-permute-start(f32[16,128]{1,0:T(8,128)S(1)} %add.3.refs_2_), channel_id=1, source_target_pairs={{0,2},{1,3},{2,0},{3,1},{4,6},{5,7},{6,4},{7,5},{8,10},{9,11},{10,... | collective-permute-start | bytes 24584 | tf_op jit(solution)/shard_map/ppermute | solution.py:687

commit v8 on v7

v8 whole, which is shorter than its diff:
```python
import functools
import math

import jax
import jax.numpy as jnp
from jax import lax
from jax.experimental import pallas as pl
from jax.experimental.pallas import tpu as pltpu
from jax.sharding import PartitionSpec as P

HEADS = 32
KVH = 2
HD = 128
BLK = 64
TILES = 8
CORES = 2
TOGETHER = 4

VERY_LOW = -1e30
TO_LOG2 = math.log2(math.e) / math.sqrt(HD)

VMEM_LIMIT = 28 * 1024 * 1024


def key_group(heads):
    return lax.axis_index("tp") * heads // (HEADS // KVH)


def group_lanes(heads):
    return pl.ds(pl.multiple_of(key_group(heads) * HD, HD), HD)


def pack_kernel(heads, transposed, rows_ref, packed_ref, buffer, sems):
    target = buffer if transposed else packed_ref
    copy = pltpu.make_async_copy(rows_ref.at[:, group_lanes(heads)], target, sems.at[0])
    copy.start()
    copy.wait()
    if transposed:
        for p in range(packed_ref.shape[0] // HD):
            rows = slice(p * HD, (p + 1) * HD)
            packed_ref[rows, :] = buffer[rows, :].T


def side_by_side(keys_ref):
    return jnp.concatenate(
        [keys_ref[p : p + HD, :] for p in range(0, keys_ref.shape[0], HD)], axis=1
    )


def with_ones(values):
    return jnp.concatenate([values, jnp.ones_like(values)], axis=1)


def block_bias(mask, width):
    block = lax.broadcasted_iota(jnp.int32, (1, width), 1) // BLK
    used = jnp.bitwise_and(jnp.right_shift(mask, block), 1)
    return jnp.where(used == 1, 0.0, VERY_LOW)


def weigh(top, scores, store):
    best = jnp.max(scores, axis=1, keepdims=True)
    new_top = jnp.maximum(top, best)
    for p in range(0, scores.shape[1], HD):
        store(p, jnp.exp2((scores[:, p : p + HD] - new_top) * TO_LOG2).astype(jnp.bfloat16))
    return new_top, jnp.exp2((top - new_top) * TO_LOG2)


def twice(x):
    return jnp.concatenate([x, x], axis=1)


def start_all(copies):
    for copy in copies:
        copy.start()
    return copies


def weight_copies(weight_ref, target, sems, sibling):
    chips, _, share = target.shape
    place = lax.axis_index("tp")
    chip, core = place // CORES, place % CORES
    held = 1 - core if sibling else core
    copies = []
    for k in range(chips):
        start = (lax.rem(chip + k, chips) * CORES + held) * share
        copies.append(
            pltpu.make_async_copy(
                weight_ref.at[:, pl.ds(pl.multiple_of(start, HD), share)],
                target.at[k],
                sems.at[k],
            )
        )
    return copies


def first_kernel(
    sources,
    conts,
    masks_ref,
    keys_ref,
    values_ref,
    queries_ref,
    cont_keys_ref,
    cont_values_ref,
    *refs,
):
    acc_refs, top_refs, q_refs = refs[:conts], refs[conts : 2 * conts], refs[2 * conts : 3 * conts]
    rows_ref, ck_ref, cv_ref, weights_ref, sems = refs[3 * conts :]
    length = cv_ref.shape[1]
    heads = q_refs[0].shape[0] // length
    shard = keys_ref.shape[0]
    lanes = group_lanes(heads)
    copies = start_all(
        [
            pltpu.make_async_copy(queries_ref, rows_ref, sems.at[0]),
            pltpu.make_async_copy(cont_keys_ref.at[:, :, lanes], ck_ref, sems.at[1]),
            pltpu.make_async_copy(cont_values_ref.at[:, :, lanes], cv_ref, sems.at[2]),
        ]
    )
    own = lax.axis_index("ctx")
    copies[0].wait()
    for cont in range(conts):
        for head in range(heads):
            q_refs[cont][head * length : (head + 1) * length, :] = rows_ref[
                cont, :, head * HD : (head + 1) * HD
            ]
    copies[1].wait()
    own_keys = [ck_ref[cont].T for cont in range(conts)]
    copies[2].wait()
    row = lax.broadcasted_iota(jnp.int32, (length, length), 0)
    column = lax.broadcasted_iota(jnp.int32, (length, length), 1)
    causal = jnp.where(column <= row, 0.0, VERY_LOW)

    def some_heads(index, carry):
        here = pl.ds(pl.multiple_of(index * TOGETHER * length, length), TOGETHER * length)
        keys = side_by_side(keys_ref)
        for cont in range(conts):
            query = q_refs[cont][here, :]
            scores = jnp.dot(query, keys, preferred_element_type=jnp.float32)
            owns = jnp.dot(query, own_keys[cont], preferred_element_type=jnp.float32)
            for j in range(TOGETHER):
                rows = slice(j * length, (j + 1) * length)
                mask = masks_ref[((index * TOGETHER + j) * conts + cont) * sources + own]
                both = jnp.concatenate(
                    [owns[rows] + causal, scores[rows] + block_bias(mask, shard)], axis=1
                )

                def store(p, weights, rows=rows, cont=cont):
                    weights_ref[cont, rows, p : p + HD] = weights

                top, _ = weigh(jnp.full((length, HD), VERY_LOW, jnp.float32), both, store)
                at = pl.ds(pl.multiple_of((index * TOGETHER + j) * length, length), length)
                top_refs[cont][at, :] = top
        for cont in range(conts):
            values = jnp.concatenate([cv_ref[cont], values_ref[...]], axis=0)
            acc_refs[cont][here, :] = jnp.dot(
                weights_ref[cont], with_ones(values), preferred_element_type=jnp.float32
            )
        return carry

    lax.fori_loop(0, heads // TOGETHER, some_heads, 0)


def arrivals(step, sources):
    spot = lax.axis_index("ctx")
    core = lax.axis_index("tp") % CORES
    if sources == 4:
        if step == 1:
            mine = jnp.bitwise_xor(spot, 1 + core)
            return ((mine, True), (jnp.bitwise_xor(mine, 3), True))
        far = jnp.bitwise_xor(spot, 3)
        return ((far, core == 1), (far, core == 0))
    mine = jnp.where(core == 0, spot - step, spot + step)
    theirs = jnp.where(core == 0, spot + step, spot - step)
    return tuple((s, (s >= 0) & (s < sources)) for s in (mine, theirs))


def steps_of(sources):
    return 2 if sources == 4 else sources - 1


def terms_of(step, sources):
    parts = [(which, *part) for which, part in enumerate(arrivals(step, sources))]
    return [parts] if sources == 4 and step == 2 else [[part] for part in parts]


def if_there(valid, work):
    if valid is True:
        work()
    else:
        pl.when(valid)(work)


def scores_kernel(step, term, sources, conts, length, masks_ref, *refs):
    candidates = terms_of(step, sources)[term]
    q_refs, refs = refs[:conts], refs[conts:]
    top_in, refs = refs[:conts], refs[conts:]
    key_refs, refs = refs[: len(candidates)], refs[len(candidates) :]
    top_refs, factor_refs, weight_refs = (refs[i * conts : (i + 1) * conts] for i in range(3))
    heads = q_refs[0].shape[0] // length
    for (_, source, valid), keys_ref in zip(candidates, key_refs):

        def some_heads(index, carry):
            here = pl.ds(pl.multiple_of(index * TOGETHER * length, length), TOGETHER * length)
            keys = side_by_side(keys_ref)
            for cont in range(conts):
                scores = jnp.dot(q_refs[cont][here, :], keys, preferred_element_type=jnp.float32)
                for j in range(TOGETHER):
                    place = index * TOGETHER + j
                    at = pl.ds(pl.multiple_of(place * length, length), length)
                    mask = masks_ref[(place * conts + cont) * sources + source]
                    masked = scores[j * length : (j + 1) * length] + block_bias(
                        mask, keys_ref.shape[0]
                    )

                    def store(p, weights, at=at, cont=cont):
                        weight_refs[cont][at, p : p + HD] = weights

                    top, factor = weigh(top_in[cont][at, :], masked, store)
                    top_refs[cont][at, :] = top
                    factor_refs[cont][at, :] = factor
            return carry

        def work():
            lax.fori_loop(0, heads // TOGETHER, some_heads, 0)

        if_there(valid, work)
    if len(candidates) == 1 and valid is not True:

        @pl.when(jnp.logical_not(valid))
        def _():
            for before, after in zip(top_in, top_refs):
                after[...] = before[...]


def add_term(before, factor_ref, weights_ref, values_ref, after):
    rows, width = after.shape
    values = with_ones(values_ref[...])
    piece = 512

    def some_rows(index, carry):
        at = pl.ds(pl.multiple_of(index * piece, piece), piece)
        after[at, :] = before[at, :] * twice(factor_ref[at, :]) + jnp.dot(
            weights_ref[at, :], values, preferred_element_type=jnp.float32
        )
        return carry

    lax.fori_loop(0, rows // piece, some_rows, 0)


def sums_kernel(step, sources, conts, *refs):
    terms = terms_of(step, sources)
    acc_in, refs = refs[:conts], refs[conts:]
    value_refs, refs = refs[: len(terms)], refs[len(terms) :]
    held = []
    for _ in terms:
        held.append((refs[:conts], refs[conts : 2 * conts]))
        refs = refs[2 * conts :]
    weight_ref, refs = refs[0], refs[1:]
    acc_refs, (give_ref, sems) = refs[:conts], refs[conts:]
    copies = start_all(weight_copies(weight_ref, give_ref, sems, True))
    for number, ([(_, _, valid)], (factor_refs, weight_refs)) in enumerate(zip(terms, held)):
        before = acc_refs if number else acc_in

        def work():
            for cont in range(conts):
                add_term(
                    before[cont],
                    factor_refs[cont],
                    weight_refs[cont],
                    value_refs[number],
                    acc_refs[cont],
                )

        if_there(valid, work)
        if valid is not True and number == 0:

            @pl.when(jnp.logical_not(valid))
            def _():
                for source_ref, target_ref in zip(acc_in, acc_refs):
                    target_ref[...] = source_ref[...]

    for copy in copies:
        copy.wait()


def last_kernel(step, sources, fetch, *refs):
    terms = terms_of(step, sources)
    acc_in, refs = refs[0], refs[1:]
    value_refs, refs = refs[:2], refs[2:]
    held = [refs[2 * t : 2 * t + 2] for t in range(len(terms))]
    give_weight_ref, *refs = refs[2 * len(terms) :]
    if fetch:
        weight_ref, attended_ref, give_ref, keep_weight_ref, acc_ref, sems = refs
        copies = start_all(weight_copies(weight_ref, keep_weight_ref, sems, False))
    else:
        attended_ref, give_ref, acc_ref = refs
    before = acc_in
    for number, (candidates, (factor_ref, weights_ref)) in enumerate(zip(terms, held)):
        for which, _, valid in candidates:

            @pl.when(valid)
            def _():
                add_term(before, factor_ref, weights_ref, value_refs[which], acc_ref)

        if len(candidates) == 1 and number == 0:

            @pl.when(jnp.logical_not(valid))
            def _():
                acc_ref[...] = acc_in[...]

        before = acc_ref
    length = attended_ref.shape[0]
    for head in range(attended_ref.shape[1] // HD):
        at = slice(head * length, (head + 1) * length)
        attended_ref[:, head * HD : (head + 1) * HD] = (
            acc_ref[at, :HD] / acc_ref[at, HD:]
        ).astype(jnp.bfloat16)
    for k in range(give_weight_ref.shape[0]):
        give_ref[k] = jnp.dot(
            attended_ref[...], give_weight_ref[k], preferred_element_type=jnp.float32
        ).astype(give_ref.dtype)
    if fetch:
        for copy in copies:
            copy.wait()


def onward_kernel(attended_ref, weight_ref, got_ref, *onward_refs):
    for k, onward_ref in enumerate(onward_refs, 1):
        onward_ref[...] = (
            jnp.dot(attended_ref[...], weight_ref[k], preferred_element_type=jnp.float32)
            + got_ref[k].astype(jnp.float32)
        ).astype(jnp.bfloat16)


def near_kernel(cont, attended_ref, weight_ref, got_ref, residual_ref, near_ref, own_ref, sem):
    share = near_ref.shape[1]
    start = pl.multiple_of(lax.axis_index("tp") * share, HD)
    copy = pltpu.make_async_copy(
        residual_ref.at[cont, :, pl.ds(start, share)], own_ref, sem.at[0]
    )
    copy.start()
    near_ref[...] = jnp.dot(
        attended_ref[...], weight_ref[0], preferred_element_type=jnp.float32
    ) + got_ref[0].astype(jnp.float32)
    copy.wait()
    near_ref[...] += own_ref[...].astype(jnp.float32)


def sum_kernel(count, *refs):
    near_ref, fars, (total_ref, squares_ref) = refs[0], refs[1 : 1 + count], refs[1 + count :]
    total = near_ref[...]
    for far_ref in fars:
        total = total + far_ref[...].astype(jnp.float32)
    total_ref[...] = total
    sums = jnp.sum(total * total, axis=1, keepdims=True)
    squares_ref[...] = jnp.broadcast_to(sums, (sums.shape[0], HD)).T[:8]


def stream_kernel(conts, *refs):
    for cont in range(conts):
        refs[conts][cont] = refs[cont][...].astype(jnp.bfloat16)


def norm_kernel(conts, model_width, *refs):
    totals, squares = refs[:conts], refs[conts:-2]
    gain_ref, normed_ref = refs[-2:]
    gain = gain_ref[...].astype(jnp.float32)
    for cont in range(conts):
        row = functools.reduce(jnp.add, [ref[cont * 8 : cont * 8 + 1, :] for ref in squares])
        scale = lax.rsqrt(row / model_width + 1e-05)
        scale = jnp.broadcast_to(scale, (HD, scale.shape[1])).T[:, 0:1]
        total = totals[cont][...]
        normed_ref[cont] = (total * scale * gain).astype(jnp.bfloat16)


def shards(
    queries,
    cont_keys,
    cont_values,
    prompt_keys,
    prompt_values,
    block_lists,
    tile_counts,
    out_weight,
    residual,
    norm_gain,
    *,
    sources,
    members,
):
    conts, length, width = queries.shape
    heads = width // HD
    rows_dev = prompt_keys.shape[0]
    model_width = residual.shape[2]
    share = norm_gain.shape[0]
    chips = members // CORES
    place = lax.axis_index("tp")
    pairs = heads * conts
    params = pltpu.CompilerParams(vmem_limit_bytes=VMEM_LIMIT)
    vmem = pl.BlockSpec(memory_space=pltpu.VMEM)
    hbm = pl.BlockSpec(memory_space=pltpu.HBM)

    def array(shape, dtype):
        return jax.ShapeDtypeStruct(shape, dtype)

    def cost(flops=1024):
        return pl.CostEstimate(flops=flops, bytes_accessed=1024, transcendentals=0)

    def in_hbm(x):
        return pltpu.with_memory_space_constraint(x, pltpu.HBM)

    def pack(x, transposed, name):
        shape = (rows_dev, HD)
        return pl.pallas_call(
            functools.partial(pack_kernel, heads, transposed),
            out_shape=array(shape, jnp.bfloat16),
            in_specs=[hbm],
            out_specs=vmem,
            scratch_shapes=[pltpu.VMEM(shape, jnp.bfloat16), pltpu.SemaphoreType.DMA((1,))],
            compiler_params=params,
            cost_estimate=cost(),
            name=name,
        )(in_hbm(x))

    keys = pack(prompt_keys, True, "pack_keys")
    values = pack(prompt_values, False, "pack_values")

    def across(step):
        def target(z, t):
            if sources == 4 and step == 1:
                return z ^ (1 + t % CORES)
            if sources == 4:
                return z ^ 1 if t % CORES == 1 else None
            to = z + step if t % CORES == 0 else z - step
            return to if 0 <= to < sources else None

        return [
            (z * members + t, target(z, t) * members + t)
            for z in range(sources)
            for t in range(members)
            if target(z, t) is not None
        ]

    sibling = [(t, t ^ 1) for t in range(members)]
    steps = steps_of(sources)
    smem = pl.BlockSpec(memory_space=pltpu.SMEM)
    live = jnp.arange(TILES) < tile_counts[..., None]
    masks = jnp.sum(jnp.where(live, jnp.left_shift(1, block_lists), 0), axis=-1).reshape(-1)
    rows = heads * length
    weight_shape = array((chips, width, share), jnp.bfloat16)
    accs_shape = (array((rows, 2 * HD), jnp.float32),) * conts
    tops_shape = (array((rows, HD), jnp.float32),) * conts
    qs_shape = (array((rows, HD), jnp.bfloat16),) * conts
    rounded_shape = (array((rows, rows_dev), jnp.bfloat16),) * conts

    made = pl.pallas_call(
        functools.partial(first_kernel, sources, conts),
        out_shape=accs_shape + tops_shape + qs_shape,
        in_specs=[smem, vmem, vmem] + [hbm] * 3,
        out_specs=(vmem,) * (3 * conts),
        scratch_shapes=[
            pltpu.VMEM(queries.shape, jnp.bfloat16),
            pltpu.VMEM((conts, length, HD), jnp.bfloat16),
            pltpu.VMEM((conts, length, HD), jnp.bfloat16),
            pltpu.VMEM((conts, TOGETHER * length, length + rows_dev), jnp.bfloat16),
            pltpu.SemaphoreType.DMA((3,)),
        ],
        compiler_params=params,
        cost_estimate=cost(),
        name="attend_own",
    )(masks, keys, values, in_hbm(queries), in_hbm(cont_keys), in_hbm(cont_values))
    accs, tops, qs = (tuple(made[i * conts : (i + 1) * conts]) for i in range(3))

    def scores(step, term, tops, keys):
        made = pl.pallas_call(
            functools.partial(scores_kernel, step, term, sources, conts, length),
            out_shape=tops_shape + tops_shape + rounded_shape,
            in_specs=[smem] + [vmem] * (2 * conts + len(keys)),
            out_specs=(vmem,) * (3 * conts),
            compiler_params=params,
            cost_estimate=cost(),
            name="scores",
        )(masks, *qs, *tops, *keys)
        tops, factors, rounded = (tuple(made[i * conts : (i + 1) * conts]) for i in range(3))
        return tops, (factors, rounded)

    def weighted_sums(step, accs, values, held):
        *accs, give_weight = pl.pallas_call(
            functools.partial(sums_kernel, step, sources, conts),
            out_shape=accs_shape + (weight_shape,),
            in_specs=[vmem] * (conts + 2 + 4 * conts) + [hbm],
            out_specs=(vmem,) * (conts + 1),
            scratch_shapes=[pltpu.SemaphoreType.DMA((chips,))],
            compiler_params=params,
            cost_estimate=cost(),
            name="weighted_sums",
        )(
            *accs,
            *values,
            *[x for factors, rounded in held for x in (*factors, *rounded)],
            in_hbm(out_weight),
        )
        return tuple(accs), give_weight

    for step in range(1, steps + 1):
        sent = mine if sources == 4 and step == 2 else (keys, values)
        mine_keys, mine_values = [lax.ppermute(x, ("ctx", "tp"), across(step)) for x in sent]
        mine_keys, accs, tops = lax.optimization_barrier((mine_keys, accs, tops))
        their_keys = jnp.concatenate(
            [lax.ppermute(x, "tp", sibling) for x in jnp.split(mine_keys, 2)]
        )
        held = []
        if sources == 4 and step == 2:
            tops, made = scores(step, 0, tops, (mine_keys, their_keys))
            held.append(made)
        else:
            for term, source_keys in enumerate((mine_keys, their_keys)):
                tops, made = scores(step, term, tops, (source_keys,))
                held.append(made)
        mine_keys, mine_values, held, tops = lax.optimization_barrier(
            (mine_keys, mine_values, held, tops)
        )
        their_values = lax.ppermute(mine_values, "tp", sibling)
        mine = (mine_keys, mine_values)
        if step < steps:
            accs, give_weight = weighted_sums(step, accs, (mine_values, their_values), held)

    def attend_last(cont):
        fetch = cont == 0
        terms = [x for factors, rounded in held for x in (factors[cont], rounded[cont])]
        return pl.pallas_call(
            functools.partial(last_kernel, steps, sources, fetch),
            out_shape=(
                array((length, width), jnp.bfloat16),
                array((chips, length, share), jnp.bfloat16),
            )
            + (weight_shape,) * fetch,
            in_specs=[vmem] * (4 + len(terms)) + [hbm] * fetch,
            out_specs=(vmem,) * (2 + fetch),
            scratch_shapes=[pltpu.VMEM((rows, 2 * HD), jnp.float32)]
            + [pltpu.SemaphoreType.DMA((chips,))] * fetch,
            compiler_params=params,
            cost_estimate=cost(),
            name="attend_last",
        )(
            accs[cont],
            mine_values,
            their_values,
            *terms,
            give_weight,
            *([in_hbm(out_weight)] * fetch),
        )

    def onward(attended, got):
        parts = pl.pallas_call(
            onward_kernel,
            out_shape=(array((length, share), jnp.bfloat16),) * (chips - 1),
            in_specs=[vmem] * 3,
            out_specs=(vmem,) * (chips - 1),
            compiler_params=params,
            cost_estimate=cost(),
            name="project_onward",
        )(attended, keep_weight, got)
        far = []
        for k in range(1, chips):
            to_chip = [
                (t, (t // CORES + k) % chips * CORES + t % CORES) for t in range(members)
            ]
            far.append(lax.ppermute(parts[k - 1], "tp", to_chip))
        return parts, far

    def near(cont, attended, got):
        return pl.pallas_call(
            functools.partial(near_kernel, cont),
            out_shape=array((length, share), jnp.float32),
            in_specs=[vmem] * 3 + [hbm],
            out_specs=vmem,
            scratch_shapes=[
                pltpu.VMEM((length, share), jnp.bfloat16),
                pltpu.SemaphoreType.DMA((1,)),
            ],
            compiler_params=params,
            cost_estimate=cost(),
            name="project_near",
        )(attended, keep_weight, got, in_hbm(residual))

    attended, give, keep_weight = attend_last(0)
    nears, fars = [], []
    for cont in range(conts):
        got = lax.ppermute(give, "tp", sibling)
        here = attended
        if cont + 1 < conts:
            attended, give = attend_last(cont + 1)
            got, give = lax.optimization_barrier((got, give))
        _, far = onward(here, got)
        fars.append(far)
        nears.append(near(cont, here, got))

    totals, squares = [], []
    for cont in range(conts):
        total, square = pl.pallas_call(
            functools.partial(sum_kernel, chips - 1),
            out_shape=(array((length, share), jnp.float32), array((8, length), jnp.float32)),
            in_specs=[vmem] * chips,
            out_specs=(vmem,) * 2,
            compiler_params=params,
            cost_estimate=cost(),
            name="add_up",
        )(nears[cont], *fars[cont])
        totals.append(total)
        squares.append(square)
    squares = jnp.concatenate(squares, axis=0)
    squares = squares + lax.ppermute(squares, "tp", sibling)
    all_squares = [squares] + [
        lax.ppermute(
            squares,
            "tp",
            [(t, (t // CORES + k) % chips * CORES + t % CORES) for t in range(members)],
        )
        for k in range(1, chips)
    ]
    out = array((conts, length, share), jnp.bfloat16)
    stream = pl.pallas_call(
        functools.partial(stream_kernel, conts),
        out_shape=out,
        in_specs=[vmem] * conts,
        out_specs=vmem,
        compiler_params=params,
        cost_estimate=cost(),
        name="stream",
    )(*totals)
    normed = pl.pallas_call(
        functools.partial(norm_kernel, conts, model_width),
        out_shape=out,
        in_specs=[vmem] * (conts + chips + 1),
        out_specs=vmem,
        compiler_params=params,
        cost_estimate=cost(),
        name="norm",
    )(*totals, *all_squares, norm_gain.reshape(1, share))
    return stream, normed


def solution(mesh):
    placed = (
        P(("grp", "ctx"), None, "tp"),
        P(("grp", "ctx"), None, None),
        P(("grp", "ctx"), None, None),
        P(("grp", "ctx"), None),
        P(("grp", "ctx"), None),
        P("tp", ("grp", "ctx"), None, None),
        P("tp", ("grp", "ctx"), None),
        P("tp", None),
        P(("grp", "ctx"), None, None),
        P("tp"),
    )
    return jax.shard_map(
        functools.partial(
            shards, sources=mesh.shape["ctx"], members=mesh.shape["tp"]
        ),
        mesh=mesh,
        in_specs=placed,
        out_specs=(P(("grp", "ctx"), None, "tp"), P(("grp", "ctx"), None, "tp")),
        check_vma=False,
    )
```

time: 59.2 us -> 63.4 us (1.071)
  Pallas kernels: 27.4 us -> 31.8 us
  other arithmetic: 0.04 us -> 1.22 us
  local copies, waits for them, and re-layouts: 1.78 us -> 0.93 us
    pallas_call x3, Pallas kernels: 6.21 us -> 10.4 us  [scores(): pl.pallas_call(functools.partial(scores_kernel, step, term, sources, cont...]
    pallas_call x1, Pallas kernels: 4.41 us -> 5.93 us  [shards(): pl.pallas_call(functools.partial(first_kernel, sources, conts), out_shape...]
    pallas_call x4, Pallas kernels: 7.34 us -> 6.09 us  [the longest x2 4.04 us: attend_last(): pl.pallas_call(functools.partial(last_kernel, steps, sources, fetch), out...]
    reduce_sum x0 -> x1, other arithmetic: none -> 1.18 us  [shards(): jnp.sum(jnp.where(live, jnp.left_shift(1, block_lists), 0), axis=-1)]
    reshape x2 -> x1, local copies, waits for them, and re-layouts: 0.95 us -> 0.1 us  [shards(): jnp.sum(jnp.where(live, jnp.left_shift(1, block_lists), 0), axis=-1)]
  transfers between devices with their start and end apart: 16 -> 16, of which waited for: 8 -> 7; matrix products, arithmetic and copies ran while one was open for 3% -> 3% of each run, Pallas kernels for 38% -> 43%
where the time goes in v8:
time: 63.4 us; the launch traced here: 63.1 us
  Pallas kernels  31.8 us (50%)
  starting transfers between devices  15.4 us (24%)
  waiting for transfers between devices  12.9 us (20%)
  other arithmetic  1.22 us (2%)
  local copies, waits for them, and re-layouts  0.93 us (1%)
  between operations  0.85 us (1%)
    pallas_call x3, Pallas kernels, scores(): pl.pallas_call(functools.partial(scores_kernel, step, term, sources, cont...  10.4 us
    ppermute x2, waiting for transfers between devices, onward(): far.append(lax.ppermute(parts[k - 1], 'tp', to_chip))  7.92 us
    pallas_call x1, Pallas kernels, shards(): pl.pallas_call(functools.partial(first_kernel, sources, conts), out_shape...  5.93 us
    ppermute x4, starting transfers between devices, shards(): lax.ppermute(x, 'tp', sibling)  4.98 us
    ppermute x4, starting transfers between devices, shards(): lax.ppermute(x, ('ctx', 'tp'), across(step))  4.53 us
    pallas_call x2, Pallas kernels, attend_last(): pl.pallas_call(functools.partial(last_kernel, steps, sources, fetch), out...  4.04 us
    pallas_call x1, Pallas kernels, weighted_sums(): pl.pallas_call(functools.partial(sums_kernel, step, sources, conts), out_...  3.58 us
    ppermute x2, starting transfers between devices, onward(): far.append(lax.ppermute(parts[k - 1], 'tp', to_chip))  2.83 us
  transfers between devices with their start and end apart: 16, of which 7 were waited for; matrix products, arithmetic and copies ran while one was open for 3% of the time, Pallas kernels for 43%

profile of v8, /device:TPU:0, one launch (start us, length us, event | category | flops | bytes accessed | tf_op | source)
XLA Modules:
  0.0 63.1 jit_solution(15303081225771864250)
XLA Ops:
  0.6 1.1 %pack_keys.1.keys_ref = bf16[1024,128]{1,0:T(8,128)(2,1)S(1)} custom-call(bf16[1024,256]{1,0:T(8,128)(2,1)} %rows_ref.2), custom_call_target="tpu_custom_call" | custom-call | flops 1024 | bytes 1024 | tf_op jit(solution)/shard_map/pack_keys/pallas_call | solution.py:415
  1.7 3.1 %collective-permute-start = (bf16[1024,128]{1,0:T(8,128)(2,1)S(1)}, bf16[1024,128]{1,0:T(8,128)(2,1)S(1)}, u32[]{:S(2)}, u32[]{:S(2)}) collective-permute-start(bf16[1024,128]{1,0:T(8,128)(2,1)S(1)} %pack_keys.1.keys_ref), channel_id=1, source_target_pairs={{0,4},{1,9},{2,6},{3,11},{4,0},{5,13},{6,2},{7,15},{8,12},{9,1},{1... | collective-permute-start | bytes 786440 | tf_op jit(solution)/shard_map/ppermute | solution.py:508
  4.8 1.0 %pack_values.1.values_ref = bf16[1024,128]{1,0:T(8,128)(2,1)S(1)} custom-call(bf16[1024,256]{1,0:T(8,128)(2,1)} %rows_ref.3), custom_call_target="tpu_custom_call" | custom-call | flops 1024 | bytes 1024 | tf_op jit(solution)/shard_map/pack_values/pallas_call | solution.py:415
  6.7 1.2 %select_reduce_fusion = s32[8,2,4]{2,1,0:T(2,128)S(1)} fusion(s32[8,2,4,8]{3,2,1,0:T(4,128)} %param.15, s32[8,2,4]{2,1,0:T(2,128)S(1)} %copy.13), kind=kLoop, calls=%fused_computation.2 | loop fusion | flops 1984 | bytes 2560 | tf_op jit(solution)/shard_map/reduce_sum | solution.py:449
  7.9 5.9 %attend_own.1 = (f32[1024,256]{1,0:T(8,128)S(1)}, f32[1024,256]{1,0:T(8,128)S(1)}, f32[1024,128]{1,0:T(8,128)S(1)}, f32[1024,128]{1,0:T(8,128)S(1)}, bf16[1024,1...) custom-call(s32[64]{0:T(128)S(1)} %reshape.11.masks_ref, bf16[1024,128]{1,0:T(8,128)(2,1)S(1)} %pack_keys.1.keys_ref, ...), custom_call_target="tpu_custom_call" | custom-call | flops 1024 | bytes 1024 | tf_op jit(solution)/shard_map/attend_own/pallas_call | solution.py:457
  14.6 3.1 %scores.3 = (f32[1024,128]{1,0:T(8,128)S(1)}, f32[1024,128]{1,0:T(8,128)S(1)}, f32[1024,128]{1,0:T(8,128)S(1)}, f32[1024,128]{1,0:T(8,128)S(1)}, bf16[1024,1024]...) custom-call(s32[64]{0:T(128)S(1)} %reshape.11.masks_ref, bf16[1024,128]{1,0:T(8,128)(2,1)S(1)} %get-tuple-element.70.refs_0_, ...), custom_call_target="tpu_custom_call" | custom-call | flops 1024 | bytes 1024 | tf_op jit(solution)/shard_map/scores/pallas_call | solution.py:476
  17.8 3.2 %scores.4 = (f32[1024,128]{1,0:T(8,128)S(1)}, f32[1024,128]{1,0:T(8,128)S(1)}, f32[1024,128]{1,0:T(8,128)S(1)}, f32[1024,128]{1,0:T(8,128)S(1)}, bf16[1024,1024]...) custom-call(s32[64]{0:T(128)S(1)} %reshape.11.masks_ref, bf16[1024,128]{1,0:T(8,128)(2,1)S(1)} %get-tuple-element.70.refs_0_, ...), custom_call_target="tpu_custom_call" | custom-call | flops 1024 | bytes 1024 | tf_op jit(solution)/shard_map/scores/pallas_call | solution.py:476
  22.9 3.6 %weighted_sums.1 = (f32[1024,256]{1,0:T(8,128)S(1)}, f32[1024,256]{1,0:T(8,128)S(1)}, bf16[2,1024,1024]{2,1,0:T(8,128)(2,1)S(1)}) custom-call(f32[1024,256]{1,0:T(8,128)S(1)} %get-tuple-element.87.refs_0_, f32[1024,256]{1,0:T(8,128)S(1)} %get-tuple-element.88.refs_1_, bf16[1024,128]{1,0:T(8,128)(2,1)S(1)} %collective-permute-done.1.refs_2_, ...), custom_call_target="tpu_custom_call" | custom-call | flops 1024 | bytes 1024 | tf_op jit(solution)/shard_map/weighted_sums/pallas_call | solution.py:489
  26.5 4.2 %collective-permute-start.7 = (bf16[512,128]{1,0:T(8,128)(2,1)S(1)}, bf16[512,128]{1,0:T(8,128)(2,1)S(1)}, u32[]{:S(2)}, u32[]{:S(2)}) collective-permute-start(bf16[512,128]{1,0:T(8,128)(2,1)S(1)} %get-tuple-element.128), channel_id=1, source_target_pairs={{0,1},{1,0},{2,3},{3,2},{4,5},{5,4},{6,7},{7,6},{8,9},{9,8},{10,11... | collective-permute-start | bytes 393224 | tf_op jit(solution)/shard_map/ppermute | solution.py:511
  30.8 0.9 %collective-permute-done.7 = bf16[512,128]{1,0:T(8,128)(2,1)S(1)} collective-permute-done((bf16[512,128]{1,0:T(8,128)(2,1)S(1)}, bf16[512,128]{1,0:T(8,128)(2,1)S(1)}, u32[]{:S(2)}, u32[]{:S(2)}) %collective-permute-start.7) | collective-permute-done | bytes 131104 | tf_op jit(solution)/shard_map/ppermute | solution.py:511
  32.1 4.1 %scores.5 = (f32[1024,128]{1,0:T(8,128)}, f32[1024,128]{1,0:T(8,128)}, f32[1024,128]{1,0:T(8,128)S(1)}, f32[1024,128]{1,0:T(8,128)S(1)}, bf16[1024,1024]{1,0:T(8,128)(2,1)S(1)}, /*index=5*/bf16[1024,1024]{1,0:T(8,128)(2,1)S(1)}) custom-call(s32[64]{0:T(128)S(1)} %reshape.11.masks_ref, bf16[1024,128]{1,0:T(8,128)(2,1)S(1)} %get-tuple-element.70.refs_0_, ...), custom_call_target="tpu_custom_call" | custom-call | flops 1024 | bytes 1024 | tf_op jit(solution)/shard_map/scores/pallas_call | solution.py:476
  36.4 1.4 %collective-permute-done.9.refs_2_ = bf16[1024,128]{1,0:T(8,128)(2,1)S(1)} collective-permute-done((bf16[1024,128]{1,0:T(8,128)(2,1)S(1)}, bf16[1024,128]{1,0:T(8,128)(2,1)S(1)}, u32[]{:S(2)}, u32[]{:S(2)}) %collective-permute-start.9) | collective-permute-done | bytes 262176 | tf_op jit(solution)/shard_map/ppermute | solution.py:524
  37.8 2.2 %attend_last.2 = (bf16[128,1024]{1,0:T(8,128)(2,1)S(1)}, bf16[2,128,1024]{2,1,0:T(8,128)(2,1)S(1)}, bf16[2,1024,1024]{2,1,0:T(8,128)(2,1)S(1)}) custom-call(f32[1024,256]{1,0:T(8,128)S(1)} %get-tuple-element.102.refs_0_, bf16[1024,128]{1,0:T(8,128)(2,1)S(1)} %collective-permute-done.6.refs_1_, bf16[1024,128]{1,0:T(8,128)(2,1)S(1)} %collective-permute-done.9.refs_2_, ...), custom_call_target="tpu_custom_call" | custom-call | flops 1024 | bytes 1024 | tf_op jit(solution)/shard_map/attend_last/pallas_call | solution.py:532
  40.2 1.8 %attend_last.3 = (bf16[128,1024]{1,0:T(8,128)(2,1)S(1)}, bf16[2,128,1024]{2,1,0:T(8,128)(2,1)S(1)}) custom-call(f32[1024,256]{1,0:T(8,128)S(1)} %get-tuple-element.117.refs_0_, bf16[1024,128]{1,0:T(8,128)(2,1)S(1)} %collective-permute-done.6.refs_1_, bf16[1024,128]{1,0:T(8,128)(2,1)S(1)} %collective-permute-done.9.refs_2_, ...), custom_call_target="tpu_custom_call" | custom-call | flops 1024 | bytes 1024 | tf_op jit(solution)/shard_map/attend_last/pallas_call | solution.py:532
  42.9 1.7 %collective-permute-start.11 = (bf16[128,1024]{1,0:T(8,128)(2,1)S(1)}, bf16[128,1024]{1,0:T(8,128)(2,1)S(1)}, u32[]{:S(2)}, u32[]{:S(2)}) collective-permute-start(bf16[128,1024]{1,0:T(8,128)(2,1)S(1)} %project_onward.2), channel_id=1, source_target_pairs={{0,2},{1,3},{2,0},{3,1},{4,6},{5,7},{6,4},{7,5},{8,10},{9,11},{10,... | collective-permute-start | bytes 786440 | tf_op jit(solution)/shard_map/ppermute | solution.py:570
  45.1 1.1 %collective-permute-start.13 = (bf16[128,1024]{1,0:T(8,128)(2,1)S(1)}, bf16[128,1024]{1,0:T(8,128)(2,1)S(1)}, u32[]{:S(2)}, u32[]{:S(2)}) collective-permute-start(bf16[128,1024]{1,0:T(8,128)(2,1)S(1)} %project_onward.3), channel_id=1, source_target_pairs={{0,2},{1,3},{2,0},{3,1},{4,6},{5,7},{6,4},{7,5},{8,10},{9,11},{10,... | collective-permute-start | bytes 786440 | tf_op jit(solution)/shard_map/ppermute | solution.py:570
  46.2 1.3 %project_near.2.refs_0_ = f32[128,1024]{1,0:T(8,128)S(1)} custom-call(bf16[128,1024]{1,0:T(8,128)(2,1)S(1)} %get-tuple-element.114.attended_ref, bf16[2,1024,1024]{2,1,0:T(8,128)(2,1)S(1)} %get-tuple-element.115.weight_ref, bf16[2,128,1024]{2,1,0:T(8,128)(2,1)S(1)} %collective-permute-done.10.got_ref, bf16[2,128,4096]{2,1,0:T(8,128)(2,1)} %residual_ref.3), custom_call_target="tpu_custom_call" | custom-call | flops 1024 | bytes 1024 | tf_op jit(solution)/shard_map/project_near/pallas_call | solution.py:574
  47.5 4.6 %collective-permute-done.11.refs_1_ = bf16[128,1024]{1,0:T(8,128)(2,1)S(1)} collective-permute-done((bf16[128,1024]{1,0:T(8,128)(2,1)S(1)}, bf16[128,1024]{1,0:T(8,128)(2,1)S(1)}, u32[]{:S(2)}, u32[]{:S(2)}) %collective-permute-start.11) | collective-permute-done | bytes 262176 | tf_op jit(solution)/shard_map/ppermute | solution.py:570
  52.3 1.3 %project_near.3.refs_0_ = f32[128,1024]{1,0:T(8,128)S(1)} custom-call(bf16[128,1024]{1,0:T(8,128)(2,1)S(1)} %get-tuple-element.123.attended_ref, bf16[2,1024,1024]{2,1,0:T(8,128)(2,1)S(1)} %get-tuple-element.115.weight_ref, bf16[2,128,1024]{2,1,0:T(8,128)(2,1)S(1)} %collective-permute-done.12.got_ref, bf16[2,128,4096]{2,1,0:T(8,128)(2,1)} %residual_ref.3), custom_call_target="tpu_custom_call" | custom-call | flops 1024 | bytes 1024 | tf_op jit(solution)/shard_map/project_near/pallas_call | solution.py:574
  53.7 3.3 %collective-permute-done.13.refs_1_ = bf16[128,1024]{1,0:T(8,128)(2,1)S(1)} collective-permute-done((bf16[128,1024]{1,0:T(8,128)(2,1)S(1)}, bf16[128,1024]{1,0:T(8,128)(2,1)S(1)}, u32[]{:S(2)}, u32[]{:S(2)}) %collective-permute-start.13) | collective-permute-done | bytes 262176 | tf_op jit(solution)/shard_map/ppermute | solution.py:570
  57.2 1.2 %collective-permute-done.14 = f32[16,128]{1,0:T(8,128)S(1)} collective-permute-done((f32[16,128]{1,0:T(8,128)S(1)}, f32[16,128]{1,0:T(8,128)S(1)}, u32[]{:S(2)}, u32[]{:S(2)}) %collective-permute-start.14) | collective-permute-done | bytes 8224 | tf_op jit(solution)/shard_map/ppermute | solution.py:614
  58.4 1.7 %collective-permute-start.15 = (f32[16,128]{1,0:T(8,128)S(1)}, f32[16,128]{1,0:T(8,128)S(1)}, u32[]{:S(2)}, u32[]{:S(2)}) collective-permute-start(f32[16,128]{1,0:T(8,128)S(1)} %add.3.refs_2_), channel_id=1, source_target_pairs={{0,2},{1,3},{2,0},{3,1},{4,6},{5,7},{6,4},{7,5},{8,10},{9,11},{10,... | collective-permute-start | bytes 24584 | tf_op jit(solution)/shard_map/ppermute | solution.py:616
  60.9 1.1 %collective-permute-done.15.refs_3_ = f32[16,128]{1,0:T(8,128)S(1)} collective-permute-done((f32[16,128]{1,0:T(8,128)S(1)}, f32[16,128]{1,0:T(8,128)S(1)}, u32[]{:S(2)}, u32[]{:S(2)}) %collective-permute-start.15) | collective-permute-done | bytes 8224 | tf_op jit(solution)/shard_map/ppermute | solution.py:616
  62.0 1.0 %norm.1 = bf16[2,128,1024]{2,1,0:T(8,128)(2,1)} custom-call(f32[128,1024]{1,0:T(8,128)S(1)} %get-tuple-element.122.refs_0_, f32[128,1024]{1,0:T(8,128)S(1)} %get-tuple-element.125.refs_1_, f32[16,128]{1,0:T(8,128)S(1)} %add.3.refs_2_, f32[16,128]{1,0:T(8,128)S(1)} %collective-permute-done.15.refs_3_, bf16[1,1024]{1,0:T(2,128)(2,1)S(1)} %reshape.12.refs_4_), custom_call_target="tpu_custom_call" | custom-call | flops 1024 | bytes 1024 | tf_op jit(solution)/shard_map/norm/pallas_call | solution.py:633
  (38 shorter events, 7.0 us)
Async XLA Ops:
  1.7 12.2 %collective-permute-start = (bf16[1024,128]{1,0:T(8,128)(2,1)S(1)}, bf16[1024,128]{1,0:T(8,128)(2,1)S(1)}, u32[]{:S(2)}, u32[]{:S(2)}) collective-permute-start(bf16[1024,128]{1,0:T(8,128)(2,1)S(1)} %pack_keys.1.keys_ref), channel_id=1, source_target_pairs={{0,4},{1,9},{2,6},{3,11},{4,0},{5,13},{6,2},{7,15},{8,12},{9,1},{1... | collective-permute-start | bytes 786440 | tf_op jit(solution)/shard_map/ppermute | solution.py:508
  5.8 15.2 %collective-permute-start.1 = (bf16[1024,128]{1,0:T(8,128)(2,1)S(1)}, bf16[1024,128]{1,0:T(8,128)(2,1)S(1)}, u32[]{:S(2)}, u32[]{:S(2)}) collective-permute-start(bf16[1024,128]{1,0:T(8,128)(2,1)S(1)} %pack_values.1.values_ref), channel_id=1, source_target_pairs={{0,4},{1,9},{2,6},{3,11},{4,0},{5,13},{6,2},{7,15},{8,12},{9,1},{1... | collective-permute-start | bytes 786440 | tf_op jit(solution)/shard_map/ppermute | solution.py:508
  13.9 3.9 %collective-permute-start.2 = (bf16[512,128]{1,0:T(8,128)(2,1)S(1)}, bf16[512,128]{1,0:T(8,128)(2,1)S(1)}, u32[]{:S(2)}, u32[]{:S(2)}) collective-permute-start(bf16[512,128]{1,0:T(8,128)(2,1)S(1)} %get-tuple-element.130), channel_id=1, source_target_pairs={{0,1},{1,0},{2,3},{3,2},{4,5},{5,4},{6,7},{7,6},{8,9},{9,8},{10,11... | collective-permute-start | bytes 393224 | tf_op jit(solution)/shard_map/ppermute | solution.py:511
  14.6 3.2 %collective-permute-start.3 = (bf16[512,128]{1,0:T(8,128)(2,1)S(1)}, bf16[512,128]{1,0:T(8,128)(2,1)S(1)}, u32[]{:S(2)}, u32[]{:S(2)}) collective-permute-start(bf16[512,128]{1,0:T(8,128)(2,1)S(1)} %get-tuple-element.131), channel_id=1, source_target_pairs={{0,1},{1,0},{2,3},{3,2},{4,5},{5,4},{6,7},{7,6},{8,9},{9,8},{10,11... | collective-permute-start | bytes 393224 | tf_op jit(solution)/shard_map/ppermute | solution.py:511
  21.0 1.9 %collective-permute-start.5 = (bf16[1024,128]{1,0:T(8,128)(2,1)S(1)}, bf16[1024,128]{1,0:T(8,128)(2,1)S(1)}, u32[]{:S(2)}, u32[]{:S(2)}) collective-permute-start(bf16[1024,128]{1,0:T(8,128)(2,1)S(1)} %collective-permute-done.1.refs_2_), channel_id=1, source_target_pairs={{0,1},{1,0},{2,3},{3,2},{4,5},{5,4},{6,7},{7,6},{8,9},{9,8},{10,11... | collective-permute-start | bytes 786440 | tf_op jit(solution)/shard_map/ppermute | solution.py:524
  21.5 5.0 %collective-permute-start.4 = (bf16[1024,128]{1,0:T(8,128)(2,1)S(1)}, bf16[1024,128]{1,0:T(8,128)(2,1)S(1)}, u32[]{:S(2)}, u32[]{:S(2)}) collective-permute-start(bf16[1024,128]{1,0:T(8,128)(2,1)S(1)} %collective-permute-done.refs_4_), channel_id=1, source_target_pairs={{1,5},{3,7},{5,1},{7,3},{9,13},{11,15},{13,9},{15,11},{17,21},{19,... | collective-permute-start | bytes 786440 | tf_op jit(solution)/shard_map/ppermute | solution.py:508
  22.2 14.0 %collective-permute-start.6 = (bf16[1024,128]{1,0:T(8,128)(2,1)S(1)}, bf16[1024,128]{1,0:T(8,128)(2,1)S(1)}, u32[]{:S(2)}, u32[]{:S(2)}) collective-permute-start(bf16[1024,128]{1,0:T(8,128)(2,1)S(1)} %collective-permute-done.1.refs_2_), channel_id=1, source_target_pairs={{1,5},{3,7},{5,1},{7,3},{9,13},{11,15},{13,9},{15,11},{17,21},{19,... | collective-permute-start | bytes 786440 | tf_op jit(solution)/shard_map/ppermute | solution.py:508
  26.5 5.2 %collective-permute-start.7 = (bf16[512,128]{1,0:T(8,128)(2,1)S(1)}, bf16[512,128]{1,0:T(8,128)(2,1)S(1)}, u32[]{:S(2)}, u32[]{:S(2)}) collective-permute-start(bf16[512,128]{1,0:T(8,128)(2,1)S(1)} %get-tuple-element.128), channel_id=1, source_target_pairs={{0,1},{1,0},{2,3},{3,2},{4,5},{5,4},{6,7},{7,6},{8,9},{9,8},{10,11... | collective-permute-start | bytes 393224 | tf_op jit(solution)/shard_map/ppermute | solution.py:511
  30.7 1.3 %collective-permute-start.8 = (bf16[512,128]{1,0:T(8,128)(2,1)S(1)}, bf16[512,128]{1,0:T(8,128)(2,1)S(1)}, u32[]{:S(2)}, u32[]{:S(2)}) collective-permute-start(bf16[512,128]{1,0:T(8,128)(2,1)S(1)} %get-tuple-element.129), channel_id=1, source_target_pairs={{0,1},{1,0},{2,3},{3,2},{4,5},{5,4},{6,7},{7,6},{8,9},{9,8},{10,11... | collective-permute-start | bytes 393224 | tf_op jit(solution)/shard_map/ppermute | solution.py:511
  36.2 1.5 %collective-permute-start.9 = (bf16[1024,128]{1,0:T(8,128)(2,1)S(1)}, bf16[1024,128]{1,0:T(8,128)(2,1)S(1)}, u32[]{:S(2)}, u32[]{:S(2)}) collective-permute-start(bf16[1024,128]{1,0:T(8,128)(2,1)S(1)} %collective-permute-done.6.refs_1_), channel_id=1, source_target_pairs={{0,1},{1,0},{2,3},{3,2},{4,5},{5,4},{6,7},{7,6},{8,9},{9,8},{10,11... | collective-permute-start | bytes 786440 | tf_op jit(solution)/shard_map/ppermute | solution.py:524
  40.0 2.0 %collective-permute-start.10 = (bf16[2,128,1024]{2,1,0:T(8,128)(2,1)S(1)}, bf16[2,128,1024]{2,1,0:T(8,128)(2,1)S(1)}, u32[]{:S(2)}, u32[]{:S(2)}) collective-permute-start(bf16[2,128,1024]{2,1,0:T(8,128)(2,1)S(1)} %get-tuple-element.116), channel_id=1, source_target_pairs={{0,1},{1,0},{2,3},{3,2},{4,5},{5,4},{6,7},{7,6},{8,9},{9,8},{10,11... | collective-permute-start | bytes 1572872 | tf_op jit(solution)/shard_map/ppermute | solution.py:591
  42.1 2.6 %collective-permute-start.12 = (bf16[2,128,1024]{2,1,0:T(8,128)(2,1)S(1)}, bf16[2,128,1024]{2,1,0:T(8,128)(2,1)S(1)}, u32[]{:S(2)}, u32[]{:S(2)}) collective-permute-start(bf16[2,128,1024]{2,1,0:T(8,128)(2,1)S(1)} %get-tuple-element.124), channel_id=1, source_target_pairs={{0,1},{1,0},{2,3},{3,2},{4,5},{5,4},{6,7},{7,6},{8,9},{9,8},{10,11... | collective-permute-start | bytes 1572872 | tf_op jit(solution)/shard_map/ppermute | solution.py:591
  42.9 9.2 %collective-permute-start.11 = (bf16[128,1024]{1,0:T(8,128)(2,1)S(1)}, bf16[128,1024]{1,0:T(8,128)(2,1)S(1)}, u32[]{:S(2)}, u32[]{:S(2)}) collective-permute-start(bf16[128,1024]{1,0:T(8,128)(2,1)S(1)} %project_onward.2), channel_id=1, source_target_pairs={{0,2},{1,3},{2,0},{3,1},{4,6},{5,7},{6,4},{7,5},{8,10},{9,11},{10,... | collective-permute-start | bytes 786440 | tf_op jit(solution)/shard_map/ppermute | solution.py:570
  45.1 11.9 %collective-permute-start.13 = (bf16[128,1024]{1,0:T(8,128)(2,1)S(1)}, bf16[128,1024]{1,0:T(8,128)(2,1)S(1)}, u32[]{:S(2)}, u32[]{:S(2)}) collective-permute-start(bf16[128,1024]{1,0:T(8,128)(2,1)S(1)} %project_onward.3), channel_id=1, source_target_pairs={{0,2},{1,3},{2,0},{3,1},{4,6},{5,7},{6,4},{7,5},{8,10},{9,11},{10,... | collective-permute-start | bytes 786440 | tf_op jit(solution)/shard_map/ppermute | solution.py:570
  52.3 7.7 %copy-start = (bf16[1024]{0:T(1024)(128)(2,1)S(1)}, bf16[1024]{0:T(1024)(128)(2,1)}, u32[]{:S(2)}) copy-start(bf16[1024]{0:T(1024)(128)(2,1)} %param.19) | copy-start | bytes 6148
  57.2 1.2 %collective-permute-start.14 = (f32[16,128]{1,0:T(8,128)S(1)}, f32[16,128]{1,0:T(8,128)S(1)}, u32[]{:S(2)}, u32[]{:S(2)}) collective-permute-start(f32[16,128]{1,0:T(8,128)S(1)} %constant_dynamic-update-slice_fusion), channel_id=1, source_target_pairs={{0,1},{1,0},{2,3},{3,2},{4,5},{5,4},{6,7},{7,6},{8,9},{9,8},{10,11... | collective-permute-start | bytes 24584 | tf_op jit(solution)/shard_map/ppermute | solution.py:614
  58.4 3.7 %collective-permute-start.15 = (f32[16,128]{1,0:T(8,128)S(1)}, f32[16,128]{1,0:T(8,128)S(1)}, u32[]{:S(2)}, u32[]{:S(2)}) collective-permute-start(f32[16,128]{1,0:T(8,128)S(1)} %add.3.refs_2_), channel_id=1, source_target_pairs={{0,2},{1,3},{2,0},{3,1},{4,6},{5,7},{6,4},{7,5},{8,10},{9,11},{10,... | collective-permute-start | bytes 24584 | tf_op jit(solution)/shard_map/ppermute | solution.py:616

commit v9 on v7

--- a/solution.py
+++ b/solution.py
@@ -30,19 +30,22 @@
     return pl.ds(pl.multiple_of(key_group(heads) * HD, HD), HD)
 
 
-def pack_keys_kernel(heads, keys_ref, packed_ref, sems):
-    copy = pltpu.make_async_copy(keys_ref.at[:, group_lanes(heads)], packed_ref, sems.at[0])
+def pack_kernel(heads, transposed, rows_ref, packed_ref, half_ref, buffer, sems):
+    target = buffer if transposed else packed_ref
+    copy = pltpu.make_async_copy(rows_ref.at[:, group_lanes(heads)], target, sems.at[0])
     copy.start()
     copy.wait()
-
-
-def pack_values_kernel(heads, values_ref, packed_ref, values_buf, sems):
-    copy = pltpu.make_async_copy(values_ref.at[:, group_lanes(heads)], values_buf, sems.at[0])
-    copy.start()
-    copy.wait()
-    for p in range(packed_ref.shape[0] // HD):
-        rows = slice(p * HD, (p + 1) * HD)
-        packed_ref[rows, :] = values_buf[rows, :].T
+    if transposed:
+        for p in range(packed_ref.shape[0] // HD):
+            rows = slice(p * HD, (p + 1) * HD)
+            packed_ref[rows, :] = buffer[rows, :].T
+    half = half_ref.shape[0]
+    start = lax.axis_index("tp") % CORES * half
+    half_ref[...] = packed_ref[pl.ds(pl.multiple_of(start, half), half), :]
+
+
+def of_sibling(both_ref):
+    return both_ref.at[1 - lax.axis_index("tp") % CORES]
 
 
 def both_ways(values_ref, flipped_ref):
@@ -195,33 +198,28 @@
     lax.fori_loop(0, heads // together, some_heads, 0)
 
 
-def arrivals(step, sources):
+def steps_of(sources):
+    return 2 if sources == 4 else sources - 1
+
+
+def far_step(step, sources):
+    return sources == 4 and step == 2
+
+
+def terms_of(step, sources):
     spot = lax.axis_index("ctx")
     core = lax.axis_index("tp") % CORES
+    if far_step(step, sources):
+        return [(jnp.bitwise_xor(spot, 3), True)]
     if sources == 4:
-        if step == 1:
-            mine = jnp.bitwise_xor(spot, 1 + core)
-            return ((mine, True), (jnp.bitwise_xor(mine, 3), True))
-        far = jnp.bitwise_xor(spot, 3)
-        return ((far, core == 1), (far, core == 0))
+        mine = jnp.bitwise_xor(spot, 1 + core)
+        return [(mine, True), (jnp.bitwise_xor(mine, 3), True)]
     mine = jnp.where(core == 0, spot - step, spot + step)
     theirs = jnp.where(core == 0, spot + step, spot - step)
-    return tuple((s, (s >= 0) & (s < sources)) for s in (mine, theirs))
-
-
-def steps_of(sources):
-    return 2 if sources == 4 else sources - 1
-
-
-def terms_of(step, sources):
-    parts = [(which, *part) for which, part in enumerate(arrivals(step, sources))]
-    return [parts] if sources == 4 and step == 2 else [[part] for part in parts]
-
-
-def if_there(valid, count, body):
-    def work():
-        lax.fori_loop(0, count, body, 0)
-
+    return [(s, (s >= 0) & (s < sources)) for s in (mine, theirs)]
+
+
+def if_there(valid, work):
     if valid is True:
         work()
     else:
@@ -229,36 +227,38 @@
 
 
 def scores_kernel(step, term, sources, conts, lists_ref, counts_ref, *refs):
-    candidates = terms_of(step, sources)[term]
+    source, valid = terms_of(step, sources)[term]
     q_refs, refs = refs[:conts], refs[conts:]
     stat_in, refs = refs[:conts], refs[conts:]
-    key_refs, refs = refs[: len(candidates)], refs[len(candidates) :]
+    keys_ref, *refs = refs
+    if term == 1:
+        keys_ref = of_sibling(keys_ref)
     stat_refs, weight_refs = refs[:conts], refs[conts:]
     heads = q_refs[0].shape[0]
     together = TOGETHER // conts
-    for (_, source, valid), keys_ref in zip(candidates, key_refs):
-
-        def some_heads(index, carry):
-            work = [
-                (index * together + j, cont) for j in range(together) for cont in range(conts)
-            ]
-            made = []
-            for head, cont in work:
-                blocks, count = used_tiles(
-                    lists_ref, counts_ref, source, sources, head * conts + cont
-                )
-                made.append(shard_scores(blocks, count, q_refs[cont][head], keys_ref))
-            after = []
-            for (head, cont), tiles in zip(work, made):
-                stat = stat_in[cont][head]
-                after.append(weigh(stat[0:1], stat[1:2], tiles))
-            for (head, cont), (stat, rounded) in zip(work, after):
-                put_stat(stat_refs[cont], head, stat)
-                weight_refs[cont][head] = rounded
-            return carry
-
-        if_there(valid, heads // together, some_heads)
-    if len(candidates) == 1 and valid is not True:
+
+    def some_heads(index, carry):
+        work = [(index * together + j, cont) for j in range(together) for cont in range(conts)]
+        made = []
+        for head, cont in work:
+            blocks, count = used_tiles(
+                lists_ref, counts_ref, source, sources, head * conts + cont
+            )
+            made.append(shard_scores(blocks, count, q_refs[cont][head], keys_ref))
+        after = []
+        for (head, cont), tiles in zip(work, made):
+            stat = stat_in[cont][head]
+            after.append(weigh(stat[0:1], stat[1:2], tiles))
+        for (head, cont), (stat, rounded) in zip(work, after):
+            put_stat(stat_refs[cont], head, stat)
+            weight_refs[cont][head] = rounded
+        return carry
+
+    def work():
+        lax.fori_loop(0, heads // together, some_heads, 0)
+
+    if_there(valid, work)
+    if valid is not True:
 
         @pl.when(jnp.logical_not(valid))
         def _():
@@ -269,7 +269,7 @@
 def sums_kernel(step, sources, conts, lists_ref, counts_ref, *refs):
     terms = terms_of(step, sources)
     acc_in, refs = refs[:conts], refs[conts:]
-    value_refs, refs = refs[: len(terms)], refs[len(terms) :]
+    value_refs, refs = (refs[0], of_sibling(refs[1])), refs[2:]
     held = []
     for _ in terms:
         held.append((refs[:conts], refs[conts : 2 * conts]))
@@ -279,7 +279,8 @@
     copies = start_all(weight_copies(weight_ref, give_ref, sems, True))
     heads = acc_refs[0].shape[0]
     together = TOGETHER // conts
-    groups = [[0, 1]] if all(t[0][2] is True for t in terms) else [[t] for t in range(len(terms))]
+    apart = any(valid is not True for _, valid in terms)
+    groups = [[0], [1]] if apart else [[0, 1]]
     for values_ref, flipped_ref in zip(value_refs, flipped_refs):
         both_ways(values_ref, flipped_ref)
     for group in groups:
@@ -293,10 +294,9 @@
             for head, cont in work:
                 acc = before[cont][head]
                 for term in group:
-                    _, source, _ = terms[term][0]
                     stat_refs, weight_refs = held[term]
                     blocks, _ = used_tiles(
-                        lists_ref, counts_ref, source, sources, head * conts + cont
+                        lists_ref, counts_ref, terms[term][0], sources, head * conts + cont
                     )
                     acc = acc * stat_refs[cont][head, 2:3, :] + jnp.dot(
                         shard_values(blocks, flipped_refs[term]),
@@ -308,8 +308,11 @@
                 acc_refs[cont][head] = acc
             return carry
 
-        valid = terms[group[0]][0][2]
-        if_there(valid, heads // together, some_heads)
+        def work():
+            lax.fori_loop(0, heads // together, some_heads, 0)
+
+        valid = terms[group[0]][1]
+        if_there(valid, work)
         if valid is not True and group[0] == 0:
 
             @pl.when(jnp.logical_not(valid))
@@ -324,7 +327,9 @@
 def last_kernel(step, sources, conts, cont, fetch, lists_ref, counts_ref, *refs):
     terms = terms_of(step, sources)
     acc_in, refs = refs[0], refs[1:]
-    value_refs, refs = refs[:2], refs[2:]
+    value_refs, refs = refs[: len(terms)], refs[len(terms) :]
+    if len(terms) == 2:
+        value_refs = (value_refs[0], of_sibling(value_refs[1]))
     held = [refs[2 * t : 2 * t + 2] for t in range(len(terms))]
     give_weight_ref, *refs = refs[2 * len(terms) :]
     if fetch:
@@ -335,35 +340,34 @@
     heads = acc_in.shape[0]
     together = min(heads, TOGETHER)
     before = acc_in
-    for number, (candidates, (stat_ref, weights_ref)) in enumerate(zip(terms, held)):
-        for which, source, valid in candidates:
-
-            def absorb():
-                both_ways(value_refs[which], flipped_ref)
-
-                def some_heads(index, carry):
-                    work = [index * together + j for j in range(together)]
-                    after = []
-                    for head in work:
-                        blocks, _ = used_tiles(
-                            lists_ref, counts_ref, source, sources, head * conts + cont
+    for number, ((source, valid), (stat_ref, weights_ref)) in enumerate(zip(terms, held)):
+
+        def absorb():
+            both_ways(value_refs[number], flipped_ref)
+
+            def some_heads(index, carry):
+                work = [index * together + j for j in range(together)]
+                after = []
+                for head in work:
+                    blocks, _ = used_tiles(
+                        lists_ref, counts_ref, source, sources, head * conts + cont
+                    )
+                    after.append(
+                        before[head] * stat_ref[head, 2:3, :]
+                        + jnp.dot(
+                            shard_values(blocks, flipped_ref),
+                            weights_ref[head],
+                            preferred_element_type=jnp.float32,
                         )
-                        after.append(
-                            before[head] * stat_ref[head, 2:3, :]
-                            + jnp.dot(
-                                shard_values(blocks, flipped_ref),
-                                weights_ref[head],
-                                preferred_element_type=jnp.float32,
-                            )
-                        )
-                    for head, acc in zip(work, after):
-                        acc_ref[head] = acc
-                    return carry
-
-                lax.fori_loop(0, heads // together, some_heads, 0)
-
-            pl.when(valid)(absorb)
-        if len(candidates) == 1 and number == 0:
+                    )
+                for head, acc in zip(work, after):
+                    acc_ref[head] = acc
+                return carry
+
+            lax.fori_loop(0, heads // together, some_heads, 0)
+
+        if_there(valid, absorb)
+        if valid is not True and number == 0:
 
             @pl.when(jnp.logical_not(valid))
             def _():
@@ -469,37 +473,35 @@
     def in_hbm(x):
         return pltpu.with_memory_space_constraint(x, pltpu.HBM)
 
-    kept = array((rows_dev, HD), jnp.bfloat16)
-    keys = pl.pallas_call(
-        functools.partial(pack_keys_kernel, heads),
-        out_shape=kept,
-        in_specs=[hbm],
-        out_specs=vmem,
-        scratch_shapes=[pltpu.SemaphoreType.DMA((1,))],
-        compiler_params=params,
-        cost_estimate=cost(),
-        name="pack_keys",
-    )(in_hbm(prompt_keys))
-    values = pl.pallas_call(
-        functools.partial(pack_values_kernel, heads),
-        out_shape=kept,
-        in_specs=[hbm],
-        out_specs=vmem,
-        scratch_shapes=[
-            pltpu.VMEM((rows_dev, HD), jnp.bfloat16),
-            pltpu.SemaphoreType.DMA((1,)),
-        ],
-        compiler_params=params,
-        cost_estimate=cost(),
-        name="pack_values",
-    )(in_hbm(prompt_values))
+    half_dev = rows_dev // CORES
+
+    def pack(x, transposed, name):
+        return pl.pallas_call(
+            functools.partial(pack_kernel, heads, transposed),
+            out_shape=(
+                array((rows_dev, HD), jnp.bfloat16),
+                array((half_dev, HD), jnp.bfloat16),
+            ),
+            in_specs=[hbm],
+            out_specs=(vmem, vmem),
+            scratch_shapes=[
+                pltpu.VMEM((rows_dev, HD), jnp.bfloat16),
+                pltpu.SemaphoreType.DMA((1,)),
+            ],
+            compiler_params=params,
+            cost_estimate=cost(),
+            name=name,
+        )(in_hbm(x))
+
+    keys, far_keys = pack(prompt_keys, False, "pack_keys")
+    values, far_values = pack(prompt_values, True, "pack_values")
 
     def across(step):
         def target(z, t):
             if sources == 4 and step == 1:
                 return z ^ (1 + t % CORES)
             if sources == 4:
-                return z ^ 1 if t % CORES == 1 else None
+                return z ^ 3
             to = z + step if t % CORES == 0 else z - step
             return to if 0 <= to < sources else None
 
@@ -545,12 +547,12 @@
         made = pl.pallas_call(
             functools.partial(scores_kernel, step, term, sources, conts),
             out_shape=stats_shape + rounded_shape,
-            in_specs=[smem, smem] + [vmem] * (2 * conts + len(keys)),
+            in_specs=[smem, smem] + [vmem] * (2 * conts + 1),
             out_specs=(vmem,) * (2 * conts),
             compiler_params=params,
             cost_estimate=cost(),
             name="scores",
-        )(lists, counts, *qs, *stats, *keys)
+        )(lists, counts, *qs, *stats, keys)
         return tuple(made[:conts]), tuple(made[conts:])
 
     def weighted_sums(step, accs, values, held):
@@ -573,27 +575,31 @@
         )
         return tuple(accs), give_weight
 
+    pairs = [[t, t + 1] for t in range(0, members, CORES)]
+
+    def both_cores(x):
+        return lax.all_to_all(jnp.stack([x] * CORES), "tp", 0, 0, axis_index_groups=pairs)
+
     for step in range(1, steps + 1):
-        sent = mine if sources == 4 and step == 2 else (keys, values)
+        far = far_step(step, sources)
+        sent = (far_keys, far_values) if far else (keys, values)
         mine_keys, mine_values = [lax.ppermute(x, ("ctx", "tp"), across(step)) for x in sent]
         mine_keys, accs, stats = lax.optimization_barrier((mine_keys, accs, stats))
-        their_keys = jnp.concatenate(
-            [lax.ppermute(x, "tp", sibling) for x in jnp.split(mine_keys, 2)]
-        )
-        held = []
-        if sources == 4 and step == 2:
-            held.append(scores(step, 0, stats, (mine_keys, their_keys)))
+        both_keys = both_cores(mine_keys)
+        if far:
+            held = [scores(step, 0, stats, both_keys.reshape(rows_dev, HD))]
         else:
-            held.append(scores(step, 0, stats, (mine_keys,)))
-            held.append(scores(step, 1, held[0][0], (their_keys,)))
+            held = [scores(step, 0, stats, mine_keys)]
+            held.append(scores(step, 1, held[0][0], both_keys))
         stats = held[-1][0]
-        mine_keys, mine_values, held, stats = lax.optimization_barrier(
-            (mine_keys, mine_values, held, stats)
-        )
-        their_values = lax.ppermute(mine_values, "tp", sibling)
-        mine = (mine_keys, mine_values)
+        mine_values, held, stats = lax.optimization_barrier((mine_values, held, stats))
+        both_values = both_cores(mine_values)
+        if far:
+            last_values = (both_values.reshape(rows_dev, HD),)
+        else:
+            last_values = (mine_values, both_values)
         if step < steps:
-            accs, give_weight = weighted_sums(step, accs, (mine_values, their_values), held)
+            accs, give_weight = weighted_sums(step, accs, last_values, held)
 
     def attend_last(cont):
         fetch = cont == 0
@@ -605,7 +611,9 @@
                 array((chips, length, share), jnp.bfloat16),
             )
             + (weight_shape,) * fetch,
-            in_specs=[smem, smem] + [vmem] * (4 + len(terms)) + [hbm] * fetch,
+            in_specs=[smem, smem]
+            + [vmem] * (2 + len(last_values) + len(terms))
+            + [hbm] * fetch,
             out_specs=(vmem,) * (2 + fetch),
             scratch_shapes=[pltpu.VMEM((heads, HD, length), jnp.float32), flipped]
             + [pltpu.SemaphoreType.DMA((chips,))] * fetch,
@@ -616,8 +624,7 @@
             lists,
             counts,
             accs[cont],
-            mine_values,
-            their_values,
+            *last_values,
             *terms,
             give_weight,
             *([in_hbm(out_weight)] * fetch),

time: 59.2 us -> 79.1 us (1.34)
  blocking collectives: 0 us -> 12 us
  local copies, waits for them, and re-layouts: 1.78 us -> 6.35 us
  waiting for transfers between devices: 13.3 us -> 10.1 us
  other arithmetic: 0.04 us -> 2.97 us
  Pallas kernels: 27.4 us -> 30.1 us
    all_to_all x0 -> x3, blocking collectives: none -> 12 us  [both_cores(): lax.all_to_all(jnp.stack([x] * CORES), 'tp', 0, 0, axis_index_groups=pairs)]
    ppermute x6 -> x0, starting transfers between devices: 6.08 us -> none  [the longest x4 5.43 us: shards(): lax.ppermute(x, 'tp', sibling)]
    unnamed x4 -> x16, local copies, waits for them, and re-layouts: 0.78 us -> 5.39 us
    all_to_all x0 -> x1, starting transfers between devices: none -> 3.49 us  [both_cores(): lax.all_to_all(jnp.stack([x] * CORES), 'tp', 0, 0, axis_index_groups=pairs)]
    another operation x0 -> x4, other arithmetic: none -> 2.97 us  [both_cores(): jnp.stack([x] * CORES)]
    ppermute x4, starting transfers between devices: 4.53 us -> 7.24 us  [shards(): lax.ppermute(x, ('ctx', 'tp'), across(step))]
    ppermute x6 -> x0, waiting for transfers between devices: 2.62 us -> none  [the longest x2 1.35 us: shards(): their_values = lax.ppermute(mine_values, 'tp', sibling)]
    pallas_call x2, Pallas kernels: 2.05 us -> 3.46 us  [pack(): pl.pallas_call(functools.partial(pack_kernel, heads, transposed), out_sha...]
  transfers between devices with their start and end apart: 16 -> 11, of which waited for: 8 -> 4; matrix products, arithmetic and copies ran while one was open for 3% -> 5% of each run, Pallas kernels for 38% -> 30%
where the time goes in v9:
time: 79.1 us; the launch traced here: 78.4 us
  Pallas kernels  30.1 us (38%)
  starting transfers between devices  15.9 us (20%)
  blocking collectives  12 us (15%)
  waiting for transfers between devices  10.1 us (13%)
  local copies, waits for them, and re-layouts  6.35 us (8%)
  other arithmetic  2.97 us (4%)
  between operations  0.83 us (1%)
    all_to_all x3, blocking collectives, both_cores(): lax.all_to_all(jnp.stack([x] * CORES), 'tp', 0, 0, axis_index_groups=pairs)  12 us
    ppermute x2, waiting for transfers between devices, onward(): far.append(lax.ppermute(parts[k - 1], 'tp', to_chip))  7.84 us
    ppermute x4, starting transfers between devices, shards(): lax.ppermute(x, ('ctx', 'tp'), across(step))  7.24 us
    pallas_call x2, Pallas kernels, attend_last(): pl.pallas_call(functools.partial(last_kernel, steps, sources, conts, cont...  6.27 us
    pallas_call x3, Pallas kernels, scores(): pl.pallas_call(functools.partial(scores_kernel, step, term, sources, cont...  6.18 us
    unnamed x16, local copies, waits for them, and re-layouts  5.39 us
    pallas_call x1, Pallas kernels, shards(): pl.pallas_call(functools.partial(first_kernel, sources, conts), out_shape...  4.79 us
    pallas_call x1, Pallas kernels, weighted_sums(): pl.pallas_call(functools.partial(sums_kernel, step, sources, conts), out_...  3.64 us
  transfers between devices with their start and end apart: 11, of which 4 were waited for; matrix products, arithmetic and copies ran while one was open for 5% of the time, Pallas kernels for 30%

profile of v9, /device:TPU:0, one launch (start us, length us, event | category | flops | bytes accessed | tf_op | source)
XLA Modules:
  0.0 78.4 jit_solution(17288489778882611471)
XLA Ops:
  0.6 1.6 %pack_keys.1 = (bf16[1024,128]{1,0:T(8,128)(2,1)S(1)}, bf16[512,128]{1,0:T(8,128)(2,1)}) custom-call(bf16[1024,256]{1,0:T(8,128)(2,1)} %rows_ref.2), custom_call_target="tpu_custom_call" | custom-call | flops 1024 | bytes 1024 | tf_op jit(solution)/shard_map/pack_keys/pallas_call | solution.py:479
  2.3 3.1 %collective-permute-start.1 = (bf16[1024,128]{1,0:T(8,128)(2,1)S(1)}, bf16[1024,128]{1,0:T(8,128)(2,1)S(1)}, u32[]{:S(2)}, u32[]{:S(2)}) collective-permute-start(bf16[1024,128]{1,0:T(8,128)(2,1)S(1)} %get-tuple-element.65.keys_ref), channel_id=1, source_target_pairs={{0,4},{1,9},{2,6},{3,11},{4,0},{5,13},{6,2},{7,15},{8,12},{9,1},{1... | collective-permute-start | bytes 786440 | tf_op jit(solution)/shard_map/ppermute | solution.py:586
  5.3 1.8 %pack_values.1 = (bf16[1024,128]{1,0:T(8,128)(2,1)}, bf16[512,128]{1,0:T(8,128)(2,1)}) custom-call(bf16[1024,256]{1,0:T(8,128)(2,1)} %rows_ref.3), custom_call_target="tpu_custom_call" | custom-call | flops 1024 | bytes 1024 | tf_op jit(solution)/shard_map/pack_values/pallas_call | solution.py:479
  7.3 4.0 %collective-permute-start = (bf16[512,128]{1,0:T(8,128)(2,1)}, bf16[512,128]{1,0:T(8,128)(2,1)}, u32[]{:S(2)}, u32[]{:S(2)}) collective-permute-start(bf16[512,128]{1,0:T(8,128)(2,1)} %get-tuple-element.64), channel_id=1, source_target_pairs={{0,12},{1,13},{2,14},{3,15},{4,8},{5,9},{6,10},{7,11},{8,4},{9,5},... | collective-permute-start | bytes 393224 | tf_op jit(solution)/shard_map/ppermute | solution.py:586
  13.1 4.8 %attend_own.1 = (f32[8,128,128]{2,1,0:T(8,128)S(1)}, f32[8,128,128]{2,1,0:T(8,128)S(1)}, f32[8,8,128]{2,1,0:T(8,128)S(1)}, f32[8,8,128]{2,1,0:T(8,128)S(1)}, bf1...) custom-call(s32[512]{0:T(512)S(1)} %reshape.19.lists_ref, s32[64]{0:T(128)S(1)} %reshape.20.counts_ref, ...), custom_call_target="tpu_custom_call" | custom-call | flops 1024 | bytes 1024 | tf_op jit(solution)/shard_map/attend_own/pallas_call | solution.py:527
  20.4 3.5 %all-to-all-start = ((bf16[2,1024,128]{2,1,0:T(8,128)(2,1)}), bf16[2,1024,128]{2,1,0:T(8,128)(2,1)S(1)}, u32[]{:S(2)}, u32[]{:S(2)}) async-start(bf16[2,1024,128]{2,1,0:T(8,128)(2,1)} %pad_maximum_fusion), calls=%async_computation | async-start | bytes 1048576 | tf_op jit(solution)/shard_map/all_to_all | solution.py:581
  24.8 2.1 %scores.3 = (f32[8,8,128]{2,1,0:T(8,128)S(1)}, f32[8,8,128]{2,1,0:T(8,128)S(1)}, bf16[8,512,128]{2,1,0:T(8,128)(2,1)S(1)}, bf16[8,512,128]{2,1,0:T(8,128)(2,1)S(1)}) custom-call(s32[512]{0:T(512)S(1)} %reshape.19.lists_ref, s32[64]{0:T(128)S(1)} %reshape.20.counts_ref, bf16[8,128,128]{2,1,0:T(8,128)(2,1)S(1)} %get-tuple-element.73.refs_0_, ...), custom_call_target="tpu_custom_call" | custom-call | flops 1024 | bytes 1024 | tf_op jit(solution)/shard_map/scores/pallas_call | solution.py:547
  26.9 2.1 %scores.4 = (f32[8,8,128]{2,1,0:T(8,128)S(1)}, f32[8,8,128]{2,1,0:T(8,128)S(1)}, bf16[8,512,128]{2,1,0:T(8,128)(2,1)S(1)}, bf16[8,512,128]{2,1,0:T(8,128)(2,1)S(1)}) custom-call(s32[512]{0:T(512)S(1)} %reshape.19.lists_ref, s32[64]{0:T(128)S(1)} %reshape.20.counts_ref, bf16[8,128,128]{2,1,0:T(8,128)(2,1)S(1)} %get-tuple-element.73.refs_0_, ...), custom_call_target="tpu_custom_call" | custom-call | flops 1024 | bytes 1024 | tf_op jit(solution)/shard_map/scores/pallas_call | solution.py:547
  29.0 4.2 %all_to_all.20.refs_3_ = bf16[2,1024,128]{2,1,0:T(8,128)(2,1)S(1)} all-to-all(bf16[2,1024,128]{2,1,0:T(8,128)(2,1)S(1)} %pad_maximum_fusion.1), channel_id=1, replica_groups={{0,1},{2,3},{4,5},{6,7},{8,9},{10,11},{12,13},{14,15},{16,17},{18,19},{..., dimensions={0} | all-to-all | bytes 1048576 | tf_op jit(solution)/shard_map/all_to_all | solution.py:581
  35.3 3.6 %weighted_sums.1 = (f32[8,128,128]{2,1,0:T(8,128)S(1)}, f32[8,128,128]{2,1,0:T(8,128)S(1)}, bf16[2,1024,1024]{2,1,0:T(8,128)(2,1)S(1)}) custom-call(s32[512]{0:T(512)S(1)} %reshape.19.lists_ref, s32[64]{0:T(128)S(1)} %reshape.20.counts_ref, f32[8,128,128]{2,1,0:T(8,128)S(1)} %copy-done.3, f32[8,128,128]{2,1,0:T(8,128)S(1)} %copy-done.5, ...), custom_call_target="tpu_custom_call" | custom-call | flops 1024 | bytes 1024 | tf_op jit(solution)/shard_map/weighted_sums/pallas_call | solution.py:559
  39.9 3.9 %all_to_all.21 = bf16[2,512,128]{2,1,0:T(8,128)(2,1)S(1)} all-to-all(bf16[2,512,128]{2,1,0:T(8,128)(2,1)S(1)} %pad_maximum_fusion.2), channel_id=1, replica_groups={{0,1},{2,3},{4,5},{6,7},{8,9},{10,11},{12,13},{14,15},{16,17},{18,19},{..., dimensions={0} | all-to-all | bytes 524288 | tf_op jit(solution)/shard_map/all_to_all | solution.py:581
  43.9 2.1 %scores.5 = (f32[8,8,128]{2,1,0:T(8,128)S(1)}, f32[8,8,128]{2,1,0:T(8,128)S(1)}, bf16[8,512,128]{2,1,0:T(8,128)(2,1)S(1)}, bf16[8,512,128]{2,1,0:T(8,128)(2,1)S(1)}) custom-call(s32[512]{0:T(512)S(1)} %reshape.19.lists_ref, s32[64]{0:T(128)S(1)} %reshape.20.counts_ref, bf16[8,128,128]{2,1,0:T(8,128)(2,1)S(1)} %get-tuple-element.73.refs_0_, ...), custom_call_target="tpu_custom_call" | custom-call | flops 1024 | bytes 1024 | tf_op jit(solution)/shard_map/scores/pallas_call | solution.py:547
  47.0 3.9 %all_to_all.22 = bf16[2,512,128]{2,1,0:T(8,128)(2,1)S(1)} all-to-all(bf16[2,512,128]{2,1,0:T(8,128)(2,1)S(1)} %pad_maximum_fusion.3), channel_id=1, replica_groups={{0,1},{2,3},{4,5},{6,7},{8,9},{10,11},{12,13},{14,15},{16,17},{18,19},{..., dimensions={0} | all-to-all | bytes 524288 | tf_op jit(solution)/shard_map/all_to_all | solution.py:581
  50.9 4.1 %attend_last.2 = (bf16[128,1024]{1,0:T(8,128)(2,1)S(1)}, bf16[2,128,1024]{2,1,0:T(8,128)(2,1)S(1)}, bf16[2,1024,1024]{2,1,0:T(8,128)(2,1)S(1)}) custom-call(s32[512]{0:T(512)S(1)} %reshape.19.lists_ref, s32[64]{0:T(128)S(1)} %reshape.20.counts_ref, f32[8,128,128]{2,1,0:T(8,128)S(1)} %get-tuple-element.99.refs_0_, bf16[1024,128]{1,0:T(8,128)(2,1)S(1)} %bitcast.6, ...), custom_call_target="tpu_custom_call" | custom-call | flops 1024 | bytes 1024 | tf_op jit(solution)/shard_map/attend_last/pallas_call | solution.py:607
  55.3 2.1 %attend_last.3 = (bf16[128,1024]{1,0:T(8,128)(2,1)S(1)}, bf16[2,128,1024]{2,1,0:T(8,128)(2,1)S(1)}) custom-call(s32[512]{0:T(512)S(1)} %reshape.19.lists_ref, s32[64]{0:T(128)S(1)} %reshape.20.counts_ref, f32[8,128,128]{2,1,0:T(8,128)S(1)} %get-tuple-element.115.refs_0_, bf16[1024,128]{1,0:T(8,128)(2,1)S(1)} %bitcast.7, ...), custom_call_target="tpu_custom_call" | custom-call | flops 1024 | bytes 1024 | tf_op jit(solution)/shard_map/attend_last/pallas_call | solution.py:607
  58.3 1.7 %collective-permute-start.5 = (bf16[128,1024]{1,0:T(8,128)(2,1)S(1)}, bf16[128,1024]{1,0:T(8,128)(2,1)S(1)}, u32[]{:S(2)}, u32[]{:S(2)}) collective-permute-start(bf16[128,1024]{1,0:T(8,128)(2,1)S(1)} %project_onward.2), channel_id=1, source_target_pairs={{0,2},{1,3},{2,0},{3,1},{4,6},{5,7},{6,4},{7,5},{8,10},{9,11},{10,... | collective-permute-start | bytes 786440 | tf_op jit(solution)/shard_map/ppermute | solution.py:648
  60.5 1.1 %collective-permute-start.7 = (bf16[128,1024]{1,0:T(8,128)(2,1)S(1)}, bf16[128,1024]{1,0:T(8,128)(2,1)S(1)}, u32[]{:S(2)}, u32[]{:S(2)}) collective-permute-start(bf16[128,1024]{1,0:T(8,128)(2,1)S(1)} %project_onward.3), channel_id=1, source_target_pairs={{0,2},{1,3},{2,0},{3,1},{4,6},{5,7},{6,4},{7,5},{8,10},{9,11},{10,... | collective-permute-start | bytes 786440 | tf_op jit(solution)/shard_map/ppermute | solution.py:648
  61.6 1.3 %project_near.2.refs_0_ = f32[128,1024]{1,0:T(8,128)S(1)} custom-call(bf16[128,1024]{1,0:T(8,128)(2,1)S(1)} %get-tuple-element.112.attended_ref, bf16[2,1024,1024]{2,1,0:T(8,128)(2,1)S(1)} %get-tuple-element.113.weight_ref, bf16[2,128,1024]{2,1,0:T(8,128)(2,1)S(1)} %collective-permute-done.4.got_ref, bf16[2,128,4096]{2,1,0:T(8,128)(2,1)} %residual_ref.3), custom_call_target="tpu_custom_call" | custom-call | flops 1024 | bytes 1024 | tf_op jit(solution)/shard_map/project_near/pallas_call | solution.py:652
  63.0 4.5 %collective-permute-done.5.refs_1_ = bf16[128,1024]{1,0:T(8,128)(2,1)S(1)} collective-permute-done((bf16[128,1024]{1,0:T(8,128)(2,1)S(1)}, bf16[128,1024]{1,0:T(8,128)(2,1)S(1)}, u32[]{:S(2)}, u32[]{:S(2)}) %collective-permute-start.5) | collective-permute-done | bytes 262176 | tf_op jit(solution)/shard_map/ppermute | solution.py:648
  67.7 1.3 %project_near.3.refs_0_ = f32[128,1024]{1,0:T(8,128)S(1)} custom-call(bf16[128,1024]{1,0:T(8,128)(2,1)S(1)} %get-tuple-element.121.attended_ref, bf16[2,1024,1024]{2,1,0:T(8,128)(2,1)S(1)} %get-tuple-element.113.weight_ref, bf16[2,128,1024]{2,1,0:T(8,128)(2,1)S(1)} %collective-permute-done.6.got_ref, bf16[2,128,4096]{2,1,0:T(8,128)(2,1)} %residual_ref.3), custom_call_target="tpu_custom_call" | custom-call | flops 1024 | bytes 1024 | tf_op jit(solution)/shard_map/project_near/pallas_call | solution.py:652
  69.1 3.3 %collective-permute-done.7.refs_1_ = bf16[128,1024]{1,0:T(8,128)(2,1)S(1)} collective-permute-done((bf16[128,1024]{1,0:T(8,128)(2,1)S(1)}, bf16[128,1024]{1,0:T(8,128)(2,1)S(1)}, u32[]{:S(2)}, u32[]{:S(2)}) %collective-permute-start.7) | collective-permute-done | bytes 262176 | tf_op jit(solution)/shard_map/ppermute | solution.py:648
  72.6 1.2 %collective-permute-done.8 = f32[16,128]{1,0:T(8,128)S(1)} collective-permute-done((f32[16,128]{1,0:T(8,128)S(1)}, f32[16,128]{1,0:T(8,128)S(1)}, u32[]{:S(2)}, u32[]{:S(2)}) %collective-permute-start.8) | collective-permute-done | bytes 8224 | tf_op jit(solution)/shard_map/ppermute | solution.py:692
  73.7 1.7 %collective-permute-start.9 = (f32[16,128]{1,0:T(8,128)S(1)}, f32[16,128]{1,0:T(8,128)S(1)}, u32[]{:S(2)}, u32[]{:S(2)}) collective-permute-start(f32[16,128]{1,0:T(8,128)S(1)} %add.3.refs_2_), channel_id=1, source_target_pairs={{0,2},{1,3},{2,0},{3,1},{4,6},{5,7},{6,4},{7,5},{8,10},{9,11},{10,... | collective-permute-start | bytes 24584 | tf_op jit(solution)/shard_map/ppermute | solution.py:694
  76.3 1.1 %collective-permute-done.9.refs_3_ = f32[16,128]{1,0:T(8,128)S(1)} collective-permute-done((f32[16,128]{1,0:T(8,128)S(1)}, f32[16,128]{1,0:T(8,128)S(1)}, u32[]{:S(2)}, u32[]{:S(2)}) %collective-permute-start.9) | collective-permute-done | bytes 8224 | tf_op jit(solution)/shard_map/ppermute | solution.py:694
  (43 shorter events, 13.3 us)
Async XLA Ops:
  2.3 17.2 %collective-permute-start.1 = (bf16[1024,128]{1,0:T(8,128)(2,1)S(1)}, bf16[1024,128]{1,0:T(8,128)(2,1)S(1)}, u32[]{:S(2)}, u32[]{:S(2)}) collective-permute-start(bf16[1024,128]{1,0:T(8,128)(2,1)S(1)} %get-tuple-element.65.keys_ref), channel_id=1, source_target_pairs={{0,4},{1,9},{2,6},{3,11},{4,0},{5,13},{6,2},{7,15},{8,12},{9,1},{1... | collective-permute-start | bytes 786440 | tf_op jit(solution)/shard_map/ppermute | solution.py:586
  7.2 21.8 %collective-permute-start.2 = (bf16[1024,128]{1,0:T(8,128)(2,1)}, bf16[1024,128]{1,0:T(8,128)(2,1)S(1)}, u32[]{:S(2)}, u32[]{:S(2)}) collective-permute-start(bf16[1024,128]{1,0:T(8,128)(2,1)} %get-tuple-element.66.values_ref), channel_id=1, source_target_pairs={{0,4},{1,9},{2,6},{3,11},{4,0},{5,13},{6,2},{7,15},{8,12},{9,1},{1... | collective-permute-start | bytes 786440 | tf_op jit(solution)/shard_map/ppermute | solution.py:586
  7.3 31.6 %collective-permute-start = (bf16[512,128]{1,0:T(8,128)(2,1)}, bf16[512,128]{1,0:T(8,128)(2,1)}, u32[]{:S(2)}, u32[]{:S(2)}) collective-permute-start(bf16[512,128]{1,0:T(8,128)(2,1)} %get-tuple-element.64), channel_id=1, source_target_pairs={{0,12},{1,13},{2,14},{3,15},{4,8},{5,9},{6,10},{7,11},{8,4},{9,5},... | collective-permute-start | bytes 393224 | tf_op jit(solution)/shard_map/ppermute | solution.py:586
  11.3 34.6 %collective-permute-start.3 = (bf16[512,128]{1,0:T(8,128)(2,1)}, bf16[512,128]{1,0:T(8,128)(2,1)}, u32[]{:S(2)}, u32[]{:S(2)}) collective-permute-start(bf16[512,128]{1,0:T(8,128)(2,1)} %get-tuple-element.100), channel_id=1, source_target_pairs={{0,12},{1,13},{2,14},{3,15},{4,8},{5,9},{6,10},{7,11},{8,4},{9,5},... | collective-permute-start | bytes 393224 | tf_op jit(solution)/shard_map/ppermute | solution.py:586
  17.9 0.8 %copy-start.2 = (f32[8,128,128]{2,1,0:T(8,128)}, f32[8,128,128]{2,1,0:T(8,128)S(1)}, u32[]{:S(2)}) copy-start(f32[8,128,128]{2,1,0:T(8,128)S(1)} %get-tuple-element.71.refs_0_) | copy-start | bytes 1572868
  18.7 0.8 %copy-start.4 = (f32[8,128,128]{2,1,0:T(8,128)}, f32[8,128,128]{2,1,0:T(8,128)S(1)}, u32[]{:S(2)}) copy-start(f32[8,128,128]{2,1,0:T(8,128)S(1)} %get-tuple-element.72.refs_1_) | copy-start | bytes 1572868
  19.5 0.9 %copy-start = (bf16[1024,128]{1,0:T(8,128)(2,1)}, bf16[1024,128]{1,0:T(8,128)(2,1)S(1)}, u32[]{:S(2)}) copy-start(bf16[1024,128]{1,0:T(8,128)(2,1)S(1)} %collective-permute-done.1.refs_4_) | copy-start | bytes 786436
  20.4 6.5 %all-to-all-start = ((bf16[2,1024,128]{2,1,0:T(8,128)(2,1)}), bf16[2,1024,128]{2,1,0:T(8,128)(2,1)S(1)}, u32[]{:S(2)}, u32[]{:S(2)}) async-start(bf16[2,1024,128]{2,1,0:T(8,128)(2,1)} %pad_maximum_fusion), calls=%async_computation | async-start | bytes 1048576 | tf_op jit(solution)/shard_map/all_to_all | solution.py:581
  23.9 1.0 %copy-start.1 = (bf16[1024,128]{1,0:T(8,128)(2,1)S(1)}, bf16[1024,128]{1,0:T(8,128)(2,1)}, u32[]{:S(2)}) copy-start(bf16[1024,128]{1,0:T(8,128)(2,1)} %copy-done) | copy-start | bytes 786436
  33.2 1.0 %copy-start.3 = (f32[8,128,128]{2,1,0:T(8,128)S(1)}, f32[8,128,128]{2,1,0:T(8,128)}, u32[]{:S(2)}) copy-start(f32[8,128,128]{2,1,0:T(8,128)} %copy-done.2) | copy-start | bytes 1572868
  34.2 1.0 %copy-start.5 = (f32[8,128,128]{2,1,0:T(8,128)S(1)}, f32[8,128,128]{2,1,0:T(8,128)}, u32[]{:S(2)}) copy-start(f32[8,128,128]{2,1,0:T(8,128)} %copy-done.4) | copy-start | bytes 1572868
  55.1 2.3 %collective-permute-start.4 = (bf16[2,128,1024]{2,1,0:T(8,128)(2,1)S(1)}, bf16[2,128,1024]{2,1,0:T(8,128)(2,1)S(1)}, u32[]{:S(2)}, u32[]{:S(2)}) collective-permute-start(bf16[2,128,1024]{2,1,0:T(8,128)(2,1)S(1)} %get-tuple-element.114), channel_id=1, source_target_pairs={{0,1},{1,0},{2,3},{3,2},{4,5},{5,4},{6,7},{7,6},{8,9},{9,8},{10,11... | collective-permute-start | bytes 1572872 | tf_op jit(solution)/shard_map/ppermute | solution.py:669
  57.4 2.6 %collective-permute-start.6 = (bf16[2,128,1024]{2,1,0:T(8,128)(2,1)S(1)}, bf16[2,128,1024]{2,1,0:T(8,128)(2,1)S(1)}, u32[]{:S(2)}, u32[]{:S(2)}) collective-permute-start(bf16[2,128,1024]{2,1,0:T(8,128)(2,1)S(1)} %get-tuple-element.122), channel_id=1, source_target_pairs={{0,1},{1,0},{2,3},{3,2},{4,5},{5,4},{6,7},{7,6},{8,9},{9,8},{10,11... | collective-permute-start | bytes 1572872 | tf_op jit(solution)/shard_map/ppermute | solution.py:669
  58.3 9.2 %collective-permute-start.5 = (bf16[128,1024]{1,0:T(8,128)(2,1)S(1)}, bf16[128,1024]{1,0:T(8,128)(2,1)S(1)}, u32[]{:S(2)}, u32[]{:S(2)}) collective-permute-start(bf16[128,1024]{1,0:T(8,128)(2,1)S(1)} %project_onward.2), channel_id=1, source_target_pairs={{0,2},{1,3},{2,0},{3,1},{4,6},{5,7},{6,4},{7,5},{8,10},{9,11},{10,... | collective-permute-start | bytes 786440 | tf_op jit(solution)/shard_map/ppermute | solution.py:648
  60.5 11.8 %collective-permute-start.7 = (bf16[128,1024]{1,0:T(8,128)(2,1)S(1)}, bf16[128,1024]{1,0:T(8,128)(2,1)S(1)}, u32[]{:S(2)}, u32[]{:S(2)}) collective-permute-start(bf16[128,1024]{1,0:T(8,128)(2,1)S(1)} %project_onward.3), channel_id=1, source_target_pairs={{0,2},{1,3},{2,0},{3,1},{4,6},{5,7},{6,4},{7,5},{8,10},{9,11},{10,... | collective-permute-start | bytes 786440 | tf_op jit(solution)/shard_map/ppermute | solution.py:648
  67.7 7.7 %copy-start.6 = (bf16[1024]{0:T(1024)(128)(2,1)S(1)}, bf16[1024]{0:T(1024)(128)(2,1)}, u32[]{:S(2)}) copy-start(bf16[1024]{0:T(1024)(128)(2,1)} %param.19) | copy-start | bytes 6148
  72.5 1.2 %collective-permute-start.8 = (f32[16,128]{1,0:T(8,128)S(1)}, f32[16,128]{1,0:T(8,128)S(1)}, u32[]{:S(2)}, u32[]{:S(2)}) collective-permute-start(f32[16,128]{1,0:T(8,128)S(1)} %constant_dynamic-update-slice_fusion), channel_id=1, source_target_pairs={{0,1},{1,0},{2,3},{3,2},{4,5},{5,4},{6,7},{7,6},{8,9},{9,8},{10,11... | collective-permute-start | bytes 24584 | tf_op jit(solution)/shard_map/ppermute | solution.py:692
  73.7 3.7 %collective-permute-start.9 = (f32[16,128]{1,0:T(8,128)S(1)}, f32[16,128]{1,0:T(8,128)S(1)}, u32[]{:S(2)}, u32[]{:S(2)}) collective-permute-start(f32[16,128]{1,0:T(8,128)S(1)} %add.3.refs_2_), channel_id=1, source_target_pairs={{0,2},{1,3},{2,0},{3,1},{4,6},{5,7},{6,4},{7,5},{8,10},{9,11},{10,... | collective-permute-start | bytes 24584 | tf_op jit(solution)/shard_map/ppermute | solution.py:694

commit v10 on v6

--- a/solution.py
+++ b/solution.py
@@ -30,38 +30,46 @@
     return pl.ds(pl.multiple_of(key_group(heads) * HD, HD), HD)
 
 
-def pack_keys_kernel(heads, keys_ref, packed_ref, sems):
-    copy = pltpu.make_async_copy(keys_ref.at[:, group_lanes(heads)], packed_ref, sems.at[0])
-    copy.start()
-    copy.wait()
-
-
-def pack_values_kernel(heads, values_ref, packed_ref, values_buf, sems):
-    copy = pltpu.make_async_copy(values_ref.at[:, group_lanes(heads)], values_buf, sems.at[0])
-    copy.start()
-    copy.wait()
-    for p in range(packed_ref.shape[0] // HD):
-        rows = slice(p * HD, (p + 1) * HD)
-        packed_ref[rows, :] = values_buf[rows, :].T
-
-
-def both_ways(values_refs, flipped_ref):
-    total = flipped_ref.shape[0] // 2
-    for part, values_ref in enumerate(values_refs):
-        rows = values_ref.shape[0]
-        for p in range(rows // HD):
-            pair = values_ref[p * HD : (p + 1) * HD, :]
-            at = part * rows + p * HD
-            flipped_ref[at : at + HD, :] = pair
-            flipped_ref[total + at : total + at + HD, :] = jnp.concatenate(
-                [pair[:, BLK:], pair[:, :BLK]], axis=1
-            )
-
-
-def shard_scores(lists_ref, counts_ref, q_refs, keys_ref, flipped_ref, source, head, cont):
+def pack_kernel(heads, keys_ref, values_ref, packed_ref, values_buf, sems):
+    rows = keys_ref.shape[0]
+    lanes = group_lanes(heads)
+    keys_copy = pltpu.make_async_copy(
+        keys_ref.at[:, lanes], packed_ref.at[pl.ds(0, rows)], sems.at[0]
+    )
+    values_copy = pltpu.make_async_copy(values_ref.at[:, lanes], values_buf, sems.at[1])
+    values_copy.start()
+    keys_copy.start()
+    values_copy.wait()
+    for p in range(rows // HD):
+        packed_ref[rows + p * HD : rows + (p + 1) * HD, :] = values_buf[
+            p * HD : (p + 1) * HD, :
+        ].T
+    keys_copy.wait()
+
+
+def split(refs):
+    if len(refs) == 2:
+        return refs
+    rows = refs[0].shape[0] // 2
+    return refs[0].at[pl.ds(0, rows)], refs[0].at[pl.ds(rows, rows)]
+
+
+def both_ways(values_ref, flipped_ref):
+    rows = values_ref.shape[0]
+    for p in range(rows // HD):
+        pair = values_ref[p * HD : (p + 1) * HD, :]
+        flipped_ref[p * HD : (p + 1) * HD, :] = pair
+        flipped_ref[rows + p * HD : rows + (p + 1) * HD, :] = jnp.concatenate(
+            [pair[:, BLK:], pair[:, :BLK]], axis=1
+        )
+
+
+def shard_scores(lists_ref, counts_ref, q_refs, keys_ref, flipped_ref, place, head, cont):
     pairs = keys_ref.shape[0] // HD
-    count = counts_ref[cont, source, head]
-    blocks = [lists_ref[head, cont, source, t] for t in range(TILES)]
+    conts, sources, source = place
+    at = (head * conts + cont) * sources + source
+    count = counts_ref[at]
+    blocks = [lists_ref[at * TILES + t] for t in range(TILES)]
     keys = jnp.concatenate(
         [keys_ref[pl.ds(pl.multiple_of(b * BLK, BLK), BLK), :] for b in blocks], axis=0
     )
@@ -138,11 +146,11 @@
 
 
 def first_kernel(
+    sources,
     conts,
-    lists_hbm,
-    counts_hbm,
-    keys_ref,
-    values_ref,
+    lists_ref,
+    counts_ref,
+    packed_ref,
     queries_ref,
     cont_keys_ref,
     cont_values_ref,
@@ -150,8 +158,8 @@
 ):
     states, refs = by_cont(refs[: 2 * conts]), refs[2 * conts :]
     q_refs, refs = refs[:conts], refs[conts:]
-    lists_kept, counts_kept, lists_ref, counts_ref, *refs = refs
     flipped_ref, rows_ref, ck_ref, cv_ref, own_ref, sems = refs
+    keys_ref, values_ref = split([packed_ref])
     heads, _, length = q_refs[0].shape
     lanes = group_lanes(heads)
     copies = start_all(
@@ -159,14 +167,10 @@
             pltpu.make_async_copy(cont_values_ref.at[:, :, lanes], cv_ref, sems.at[0]),
             pltpu.make_async_copy(queries_ref, rows_ref, sems.at[1]),
             pltpu.make_async_copy(cont_keys_ref.at[:, :, lanes], ck_ref, sems.at[2]),
-            pltpu.make_async_copy(lists_hbm, lists_ref, sems.at[3]),
-            pltpu.make_async_copy(counts_hbm, counts_ref, sems.at[4]),
-            pltpu.make_async_copy(lists_hbm, lists_kept, sems.at[5]),
-            pltpu.make_async_copy(counts_hbm, counts_kept, sems.at[6]),
         ]
     )
-    own = lax.axis_index("ctx")
-    both_ways([values_ref], flipped_ref)
+    place = conts, sources, lax.axis_index("ctx")
+    both_ways(values_ref, flipped_ref)
     copies[0].wait()
     for cont in range(conts):
         own_ref[cont] = cv_ref[cont].T
@@ -189,7 +193,7 @@
             row = lax.broadcasted_iota(jnp.int32, scores.shape, 1)
             scores = jnp.where(key <= row, scores, VERY_LOW)
             tiles, values = shard_scores(
-                lists_ref, counts_ref, q_refs, keys_ref, flipped_ref, own, head, cont
+                lists_ref, counts_ref, q_refs, keys_ref, flipped_ref, place, head, cont
             )
             made.append(
                 ([(scores, True)] + tiles, jnp.concatenate([own_ref[cont], values], axis=1))
@@ -227,38 +231,17 @@
     return 2 if sources == 4 else sources - 1
 
 
-def lists_copies(lists_kept, counts_kept, lists_ref, counts_ref, sems):
-    return start_all(
-        [
-            pltpu.make_async_copy(lists_kept, lists_ref, sems.at[0]),
-            pltpu.make_async_copy(counts_kept, counts_ref, sems.at[1]),
-        ]
-    )
-
-
-def absorb_shard(
-    pending,
-    source,
-    lists_ref,
-    counts_ref,
-    q_refs,
-    keys_ref,
-    values_refs,
-    flipped_ref,
-    before,
-    after,
-):
+def absorb_shard(place, lists_ref, counts_ref, q_refs, held, flipped_ref, before, after):
+    keys_ref, values_ref = split(held)
     heads = next(iter(q_refs.values())).shape[0]
     together = min(heads, TOGETHER // len(q_refs))
-    both_ways(values_refs, flipped_ref)
-    for copy in pending:
-        copy.wait()
+    both_ways(values_ref, flipped_ref)
 
     def some_heads(index, carry):
         work = [(index * together + j, cont) for j in range(together) for cont in q_refs]
         states = [load_state(*before[cont], head) for head, cont in work]
         made = [
-            shard_scores(lists_ref, counts_ref, q_refs, keys_ref, flipped_ref, source, head, cont)
+            shard_scores(lists_ref, counts_ref, q_refs, keys_ref, flipped_ref, place, head, cont)
             for head, cont in work
         ]
         states = [absorb(state, *got) for state, got in zip(states, made)]
@@ -274,29 +257,31 @@
         target_ref[...] = source_ref[...]
 
 
-def by_cont(refs):
-    return {cont: refs[2 * cont : 2 * cont + 2] for cont in range(len(refs) // 2)}
+def by_cont(refs, chosen=None):
+    chosen = range(len(refs) // 2) if chosen is None else chosen
+    return {cont: refs[2 * i : 2 * i + 2] for i, cont in enumerate(chosen)}
 
 
 def middle_kernel(
-    step, part, sources, conts, pieces, with_weight, lists_kept, counts_kept, *refs
+    step, part, sources, conts, chosen, pieces, with_weight, lists_ref, counts_ref, *refs
 ):
-    q_refs, refs = dict(enumerate(refs[:conts])), refs[conts:]
-    keys_ref, values_refs, refs = refs[0], refs[1 : 1 + pieces], refs[1 + pieces :]
-    before, refs = refs[: 2 * conts], refs[2 * conts :]
+    count = len(chosen)
+    q_refs, refs = dict(zip(chosen, refs)), refs[count:]
+    held, refs = refs[:pieces], refs[pieces:]
+    before, refs = refs[: 2 * count], refs[2 * count :]
     if with_weight:
         weight_ref, *refs = refs
-    after, refs = refs[: 2 * conts], refs[2 * conts :]
+    after, refs = refs[: 2 * count], refs[2 * count :]
     if with_weight:
-        give_ref, *refs, sems = refs
+        give_ref, flipped_ref, sems = refs
         copies = start_all(weight_copies(weight_ref, give_ref, sems, True))
-    flipped_ref, lists_ref, counts_ref, list_sems = refs
+    else:
+        (flipped_ref,) = refs
     source, valid = arrivals(step, sources)[part]
 
     def absorb_part():
-        pending = lists_copies(lists_kept, counts_kept, lists_ref, counts_ref, list_sems)
-        shard = (pending, source, lists_ref, counts_ref, q_refs, keys_ref, values_refs, flipped_ref)
-        absorb_shard(*shard, by_cont(before), by_cont(after))
+        shard = ((conts, sources, source), lists_ref, counts_ref, q_refs, held, flipped_ref)
+        absorb_shard(*shard, by_cont(before, chosen), by_cont(after, chosen))
 
     if valid is True:
         absorb_part()
@@ -321,14 +306,13 @@
 def last_kernel(
     step,
     sources,
+    conts,
     cont,
-    lists_kept,
-    counts_kept,
+    lists_ref,
+    counts_ref,
     q_ref,
-    mine_keys_ref,
-    mine_values_ref,
-    their_keys_ref,
-    their_values_ref,
+    mine_ref,
+    theirs_ref,
     acc_in,
     stat_in,
     give_weight_ref,
@@ -339,16 +323,14 @@
         copies = start_all(weight_copies(weight_ref, keep_weight_ref, sems, False))
     else:
         attended_ref, give_ref, *refs = refs
-    acc_ref, stat_ref, flipped_ref, lists_ref, counts_ref, list_sems = refs
+    acc_ref, stat_ref, flipped_ref = refs
     before, after = (acc_in, stat_in), (acc_ref, stat_ref)
-    held = (mine_keys_ref, [mine_values_ref]), (their_keys_ref, [their_values_ref])
-    parts = arrivals(step, sources)
     one_of_two = sources == 4
-    for part, (source, valid) in enumerate(parts):
+    for part, (source, valid) in enumerate(arrivals(step, sources)):
 
         def absorb_part():
-            pending = lists_copies(lists_kept, counts_kept, lists_ref, counts_ref, list_sems)
-            shard = (pending, source, lists_ref, counts_ref, {cont: q_ref}, *held[part])
+            held = [(mine_ref, theirs_ref)[part]]
+            shard = ((conts, sources, source), lists_ref, counts_ref, {cont: q_ref}, held)
             first = part == 0 or one_of_two
             absorb_shard(
                 *shard, flipped_ref, {cont: before if first else after}, {cont: after}
@@ -444,30 +426,19 @@
     def in_hbm(x):
         return pltpu.with_memory_space_constraint(x, pltpu.HBM)
 
-    kept = array((rows_dev, HD), jnp.bfloat16)
-    keys = pl.pallas_call(
-        functools.partial(pack_keys_kernel, heads),
-        out_shape=kept,
-        in_specs=[hbm],
-        out_specs=vmem,
-        scratch_shapes=[pltpu.SemaphoreType.DMA((1,))],
-        compiler_params=params,
-        cost_estimate=cost(),
-        name="pack_keys",
-    )(in_hbm(prompt_keys))
-    values = pl.pallas_call(
-        functools.partial(pack_values_kernel, heads),
-        out_shape=kept,
-        in_specs=[hbm],
+    packed = pl.pallas_call(
+        functools.partial(pack_kernel, heads),
+        out_shape=array((2 * rows_dev, HD), jnp.bfloat16),
+        in_specs=[hbm] * 2,
         out_specs=vmem,
         scratch_shapes=[
             pltpu.VMEM((rows_dev, HD), jnp.bfloat16),
-            pltpu.SemaphoreType.DMA((1,)),
+            pltpu.SemaphoreType.DMA((2,)),
         ],
         compiler_params=params,
         cost_estimate=cost(),
-        name="pack_values",
-    )(in_hbm(prompt_values))
+        name="pack",
+    )(in_hbm(prompt_keys), in_hbm(prompt_values))
 
     def across(step):
         def target(z, t):
@@ -487,8 +458,9 @@
 
     sibling = [(t, t ^ 1) for t in range(members)]
     steps = steps_of(sources)
-    lists = in_hbm(block_lists)
-    counts = in_hbm(tile_counts.transpose(1, 2, 0))
+    smem = pl.BlockSpec(memory_space=pltpu.SMEM)
+    lists = block_lists.reshape(-1)
+    counts = tile_counts.reshape(-1)
     state_shape = (
         array((heads, HD, length), jnp.float32),
         array((heads, 8, length), jnp.float32),
@@ -496,87 +468,94 @@
     flipped = pltpu.VMEM((2 * rows_dev, HD), jnp.bfloat16)
     weight_shape = array((chips, width, share), jnp.bfloat16)
 
-    list_shapes = (array(lists.shape, jnp.int32), array(counts.shape, jnp.int32))
-    list_scratch = [pltpu.SMEM(x.shape, x.dtype) for x in list_shapes]
-    with_lists = [flipped] + list_scratch + [pltpu.SemaphoreType.DMA((2,))]
-    *made, lists_kept, counts_kept = pl.pallas_call(
-        functools.partial(first_kernel, conts),
-        out_shape=state_shape * conts
-        + (array((heads, HD, length), jnp.bfloat16),) * conts
-        + list_shapes,
-        in_specs=[hbm, hbm, vmem, vmem] + [hbm] * 3,
-        out_specs=(vmem,) * (3 * conts + 2),
-        scratch_shapes=list_scratch
-        + [
+    made = pl.pallas_call(
+        functools.partial(first_kernel, sources, conts),
+        out_shape=state_shape * conts + (array((heads, HD, length), jnp.bfloat16),) * conts,
+        in_specs=[smem, smem, vmem] + [hbm] * 3,
+        out_specs=(vmem,) * (3 * conts),
+        scratch_shapes=[
             flipped,
             pltpu.VMEM(queries.shape, jnp.bfloat16),
             pltpu.VMEM((conts, length, HD), jnp.bfloat16),
             pltpu.VMEM((conts, length, HD), jnp.bfloat16),
             pltpu.VMEM((conts, HD, length), jnp.bfloat16),
-            pltpu.SemaphoreType.DMA((7,)),
+            pltpu.SemaphoreType.DMA((3,)),
         ],
         compiler_params=params,
         cost_estimate=cost(),
         name="attend_own",
-    )(lists, counts, keys, values, in_hbm(queries), in_hbm(cont_keys), in_hbm(cont_values))
+    )(lists, counts, packed, in_hbm(queries), in_hbm(cont_keys), in_hbm(cont_values))
     states = tuple(made[2 * c : 2 * c + 2] for c in range(conts))
     qs = made[2 * conts :]
 
-    def attend_step(step, part, with_weight, states, held):
-        flat = [x for state in states for x in state]
+    def attend_step(step, part, chosen, with_weight, states, held):
+        flat = [x for cont in chosen for x in states[cont]]
+        count = len(chosen)
         made = pl.pallas_call(
             functools.partial(
-                middle_kernel, step, part, sources, conts, len(held) - 1, with_weight
+                middle_kernel, step, part, sources, conts, chosen, len(held), with_weight
             ),
-            out_shape=state_shape * conts + ((weight_shape,) if with_weight else ()),
-            in_specs=[vmem] * (2 + 3 * conts + len(held)) + [hbm] * with_weight,
-            out_specs=(vmem,) * (2 * conts + with_weight),
-            scratch_shapes=with_lists + [pltpu.SemaphoreType.DMA((chips,))] * with_weight,
+            out_shape=state_shape * count + ((weight_shape,) if with_weight else ()),
+            in_specs=[smem, smem] + [vmem] * (3 * count + len(held)) + [hbm] * with_weight,
+            out_specs=(vmem,) * (2 * count + with_weight),
+            scratch_shapes=[flipped] + [pltpu.SemaphoreType.DMA((chips,))] * with_weight,
             compiler_params=params,
             cost_estimate=cost(),
             name="attend_step",
-        )(lists_kept, counts_kept, *qs, *held, *flat, *([in_hbm(out_weight)] * with_weight))
-        return tuple(made[2 * c : 2 * c + 2] for c in range(conts)), made[2 * conts :]
-
+        )(
+            lists,
+            counts,
+            *[qs[cont] for cont in chosen],
+            *held,
+            *flat,
+            *([in_hbm(out_weight)] * with_weight),
+        )
+        states = list(states)
+        for i, cont in enumerate(chosen):
+            states[cont] = tuple(made[2 * i : 2 * i + 2])
+        return tuple(states), made[2 * count :]
+
+    everyone = tuple(range(conts))
+    mine, theirs = packed, None
     for step in range(1, steps + 1):
-        sent = mine if sources == 4 and step == 2 else (keys, values)
-        mine_keys, mine_values = [lax.ppermute(x, ("ctx", "tp"), across(step)) for x in sent]
-        mine_keys, states = lax.optimization_barrier((mine_keys, tuple(states)))
-        their_keys = lax.ppermute(mine_keys, "tp", sibling)
-        mine_values, states = lax.optimization_barrier((mine_values, tuple(states)))
-        their_values = [
-            lax.ppermute(x, "tp", sibling)
-            for x in jnp.split(mine_values, 2 if step < steps else 1)
-        ]
-        mine, theirs = (mine_keys, mine_values), (their_keys, *their_values)
+        sent = mine if sources == 4 and step == 2 else packed
+        mine = lax.ppermute(sent, ("ctx", "tp"), across(step))
+        mine, states = lax.optimization_barrier((mine, states))
+        rest = theirs
         if step < steps:
-            states, (give_weight,) = attend_step(step, 0, True, states, mine)
-            states, _ = attend_step(step, 1, False, states, theirs)
-
-    def attend_last(cont):
+            theirs = [lax.ppermute(x, "tp", sibling) for x in jnp.split(mine, 2)]
+            states, (give_weight,) = attend_step(step, 0, everyone, True, states, [mine])
+            states, _ = attend_step(step, 1, everyone[:1], False, states, theirs)
+        else:
+            theirs = [lax.ppermute(mine, "tp", sibling)]
+        if step > 1:
+            states, _ = attend_step(step - 1, 1, everyone[1:], False, states, rest)
+            theirs, states = lax.optimization_barrier((theirs, states))
+
+    def attend_last(cont, state):
         fetch = cont == 0
         return pl.pallas_call(
-            functools.partial(last_kernel, steps, sources, cont),
+            functools.partial(last_kernel, steps, sources, conts, cont),
             out_shape=(
                 array((length, width), jnp.bfloat16),
                 array((chips, length, share), jnp.bfloat16),
             )
             + (weight_shape,) * fetch,
-            in_specs=[vmem] * 10 + [hbm] * fetch,
+            in_specs=[smem, smem] + [vmem] * 6 + [hbm] * fetch,
             out_specs=(vmem,) * (2 + fetch),
             scratch_shapes=[pltpu.VMEM(a.shape, a.dtype) for a in state_shape]
-            + with_lists
+            + [flipped]
             + [pltpu.SemaphoreType.DMA((chips,))] * fetch,
             compiler_params=params,
             cost_estimate=cost(),
             name="attend_last",
         )(
-            lists_kept,
-            counts_kept,
+            lists,
+            counts,
             qs[cont],
-            *mine,
+            mine,
             *theirs,
-            *states[cont],
+            *state,
             give_weight,
             *([in_hbm(out_weight)] * fetch),
         )
@@ -614,13 +593,13 @@
             name="project_near",
         )(attended, keep_weight, got, in_hbm(residual))
 
-    attended, give, keep_weight = attend_last(0)
+    attended, give, keep_weight = attend_last(0, states[0])
     nears, fars = [], []
     for cont in range(conts):
         got = lax.ppermute(give, "tp", sibling)
         here = attended
         if cont + 1 < conts:
-            attended, give = attend_last(cont + 1)
+            attended, give = attend_last(cont + 1, states[cont + 1])
             got, give = lax.optimization_barrier((got, give))
         _, far = onward(here, got)
         fars.append(far)

time: 58 us -> 56.5 us (0.974)
  Pallas kernels: 25.3 us -> 23.3 us
  local copies, waits for them, and re-layouts: 0.04 us -> 1.78 us
  starting transfers between devices: 14.6 us -> 13.6 us
    pallas_call x5 -> x4, Pallas kernels: 12.7 us -> 11.2 us  [the longest x2 5.67 us: attend_last(): pl.pallas_call(functools.partial(last_kernel, steps, sources, conts, cont...]
    ppermute x3, waiting for transfers between devices: 1.36 us -> 2.56 us  [shards(): lax.ppermute(squares, 'tp', [(t, (t + k) % members) for t in range(member...]
    ppermute x9 -> x5, waiting for transfers between devices: 7.38 us -> 6.24 us  [the longest x2 6.23 us: shards(): mine = lax.ppermute(sent, ('ctx', 'tp'), across(step))]
    reshape x0 -> x2, local copies, waits for them, and re-layouts: none -> 0.95 us  [the longest x1 0.86 us: shards(): lists = block_lists.reshape(-1)]
    ppermute x3, starting transfers between devices: 2.97 us -> 2.03 us  [shards(): lax.ppermute(squares, 'tp', [(t, (t + k) % members) for t in range(member...]
    unnamed x3 -> x4, local copies, waits for them, and re-layouts: 0.01 us -> 0.78 us
    pallas_call x2 -> x3, Pallas kernels: 7.47 us -> 6.93 us  [attend_step(): pl.pallas_call(functools.partial(middle_kernel, step, part, sources, cont...]
    ppermute x9 -> x5, starting transfers between devices: 8.11 us -> 8.24 us  [the longest x2 3.77 us: shards(): mine = lax.ppermute(sent, ('ctx', 'tp'), across(step))]
  transfers between devices with their start and end apart: 16 -> 12, of which waited for: 9 -> 5; matrix products, arithmetic and copies ran while one was open for 0% -> 3% of each run, Pallas kernels for 34% -> 32%
where the time goes in v10:
time: 56.5 us; the launch traced here: 56.1 us
  Pallas kernels  23.3 us (41%)
  waiting for transfers between devices  16.7 us (30%)
  starting transfers between devices  13.6 us (24%)
  local copies, waits for them, and re-layouts  1.78 us (3%)
  between operations  0.78 us (1%)
    ppermute x2, waiting for transfers between devices, onward(): far.append(lax.ppermute(parts[k - 1], 'tp', to_chip))  7.91 us
    pallas_call x3, Pallas kernels, attend_step(): pl.pallas_call(functools.partial(middle_kernel, step, part, sources, cont...  6.93 us
    ppermute x2, waiting for transfers between devices, shards(): mine = lax.ppermute(sent, ('ctx', 'tp'), across(step))  6.23 us
    pallas_call x2, Pallas kernels, attend_last(): pl.pallas_call(functools.partial(last_kernel, steps, sources, conts, cont...  5.67 us
    pallas_call x1, Pallas kernels, shards(): pl.pallas_call(functools.partial(first_kernel, sources, conts), out_shape...  4.43 us
    ppermute x2, starting transfers between devices, shards(): mine = lax.ppermute(sent, ('ctx', 'tp'), across(step))  3.77 us
    pallas_call x2, Pallas kernels, near(): pl.pallas_call(functools.partial(near_kernel, cont), out_shape=array((len...  2.67 us
    ppermute x2, starting transfers between devices, onward(): far.append(lax.ppermute(parts[k - 1], 'tp', to_chip))  2.66 us
  transfers between devices with their start and end apart: 12, of which 5 were waited for; matrix products, arithmetic and copies ran while one was open for 3% of the time, Pallas kernels for 32%

profile of v10, /device:TPU:0, one launch (start us, length us, event | category | flops | bytes accessed | tf_op | source)
XLA Modules:
  0.0 56.1 jit_solution(16203095851125525195)
XLA Ops:
  0.6 1.1 %pack.1.packed_ref = bf16[2048,128]{1,0:T(8,128)(2,1)S(1)} custom-call(bf16[1024,256]{1,0:T(8,128)(2,1)} %keys_ref.1, bf16[1024,256]{1,0:T(8,128)(2,1)} %values_ref.1), custom_call_target="tpu_custom_call" | custom-call | flops 1024 | bytes 1024 | tf_op jit(solution)/shard_map/pack/pallas_call | solution.py:429
  1.7 3.1 %collective-permute-start = (bf16[2048,128]{1,0:T(8,128)(2,1)S(1)}, bf16[2048,128]{1,0:T(8,128)(2,1)S(1)}, u32[]{:S(2)}, u32[]{:S(2)}) collective-permute-start(bf16[2048,128]{1,0:T(8,128)(2,1)S(1)} %pack.1.packed_ref), channel_id=1, source_target_pairs={{0,4},{1,9},{2,6},{3,11},{4,0},{5,13},{6,2},{7,15},{8,12},{9,1},{1... | collective-permute-start | bytes 1572872 | tf_op jit(solution)/shard_map/ppermute | solution.py:522
  4.8 0.8 %copy.13 = s32[8,2,4]{2,1,0:T(2,128)S(1)} copy(s32[8,2,4]{0,2,1:T(4,128)} %param.16) | data formatting | bytes 512 | tf_op args[6]
  5.7 0.9 %reshape.13.lists_ref = s32[512]{0:T(512)S(1)} reshape(s32[8,2,4,8]{3,2,1,0:T(4,128)} %param.15) | data formatting | bytes 4096 | tf_op jit(solution)/shard_map/reshape | solution.py:462
  6.6 4.4 %attend_own.1 = (f32[8,128,128]{2,1,0:T(8,128)S(1)}, f32[8,8,128]{2,1,0:T(8,128)S(1)}, f32[8,128,128]{2,1,0:T(8,128)S(1)}, f32[8,8,128]{2,1,0:T(8,128)S(1)}, bf1...) custom-call(s32[512]{0:T(512)S(1)} %reshape.13.lists_ref, s32[64]{0:T(128)S(1)} %reshape.14.counts_ref, ...), custom_call_target="tpu_custom_call" | custom-call | flops 1024 | bytes 1024 | tf_op jit(solution)/shard_map/attend_own/pallas_call | solution.py:471
  11.0 6.2 %collective-permute-done.refs_2_ = bf16[2048,128]{1,0:T(8,128)(2,1)S(1)} collective-permute-done((bf16[2048,128]{1,0:T(8,128)(2,1)S(1)}, bf16[2048,128]{1,0:T(8,128)(2,1)S(1)}, u32[]{:S(2)}, u32[]{:S(2)}) %collective-permute-start) | collective-permute-done | bytes 524320 | tf_op jit(solution)/shard_map/ppermute | solution.py:522
  17.2 0.7 %collective-permute-start.1 = (bf16[2048,128]{1,0:T(8,128)(2,1)S(1)}, bf16[2048,128]{1,0:T(8,128)(2,1)S(1)}, u32[]{:S(2)}, u32[]{:S(2)}) collective-permute-start(bf16[2048,128]{1,0:T(8,128)(2,1)S(1)} %collective-permute-done.refs_2_), channel_id=1, source_target_pairs={{1,5},{3,7},{5,1},{7,3},{9,13},{11,15},{13,9},{15,11},{17,21},{19,... | collective-permute-start | bytes 1572872 | tf_op jit(solution)/shard_map/ppermute | solution.py:522
  18.0 2.4 %collective-permute-start.2 = (bf16[1024,128]{1,0:T(8,128)(2,1)S(1)}, bf16[1024,128]{1,0:T(8,128)(2,1)S(1)}, u32[]{:S(2)}, u32[]{:S(2)}) collective-permute-start(bf16[1024,128]{1,0:T(8,128)(2,1)S(1)} %get-tuple-element.85), channel_id=1, source_target_pairs={{0,1},{1,0},{2,3},{3,2},{4,5},{5,4},{6,7},{7,6},{8,9},{9,8},{10,11... | collective-permute-start | bytes 786440 | tf_op jit(solution)/shard_map/ppermute | solution.py:526
  20.4 3.2 %attend_step.3 = (f32[8,128,128]{2,1,0:T(8,128)S(1)}, f32[8,8,128]{2,1,0:T(8,128)S(1)}, f32[8,128,128]{2,1,0:T(8,128)S(1)}, f32[8,8,128]{2,1,0:T(8,128)S(1)}, bf16[2,1024,1024]{2,1,0:T(8,128)(2,1)S(1)}) custom-call(s32[512]{0:T(512)S(1)} %reshape.13.lists_ref, s32[64]{0:T(128)S(1)} %reshape.14.counts_ref, ...), custom_call_target="tpu_custom_call" | custom-call | flops 1024 | bytes 1024 | tf_op jit(solution)/shard_map/attend_step/pallas_call | solution.py:494
  23.6 1.9 %attend_step.4 = (f32[8,128,128]{2,1,0:T(8,128)S(1)}, f32[8,8,128]{2,1,0:T(8,128)S(1)}) custom-call(s32[512]{0:T(512)S(1)} %reshape.13.lists_ref, s32[64]{0:T(128)S(1)} %reshape.14.counts_ref, bf16[8,128,128]{2,1,0:T(8,128)(2,1)S(1)} %get-tuple-element.43.refs_0_.q_ref, bf16[1024,128]{1,0:T(8,128)(2,1)S(1)} %collective-permute-done.2.refs_1_, ...), custom_call_target="tpu_custom_call" | custom-call | flops 1024 | bytes 1024 | tf_op jit(solution)/shard_map/attend_step/pallas_call | solution.py:494
  25.5 2.0 %collective-permute-start.4 = (bf16[2048,128]{1,0:T(8,128)(2,1)S(1)}, bf16[2048,128]{1,0:T(8,128)(2,1)S(1)}, u32[]{:S(2)}, u32[]{:S(2)}) collective-permute-start(bf16[2048,128]{1,0:T(8,128)(2,1)S(1)} %collective-permute-done.1.mine_ref), channel_id=1, source_target_pairs={{0,1},{1,0},{2,3},{3,2},{4,5},{5,4},{6,7},{7,6},{8,9},{9,8},{10,11... | collective-permute-start | bytes 1572872 | tf_op jit(solution)/shard_map/ppermute | solution.py:530
  27.5 1.9 %attend_step.5 = (f32[8,128,128]{2,1,0:T(8,128)S(1)}, f32[8,8,128]{2,1,0:T(8,128)S(1)}) custom-call(s32[512]{0:T(512)S(1)} %reshape.13.lists_ref, s32[64]{0:T(128)S(1)} %reshape.14.counts_ref, bf16[8,128,128]{2,1,0:T(8,128)(2,1)S(1)} %get-tuple-element.49.refs_1_.refs_0_.q_ref, bf16[1024,128]{1,0:T(8,128)(2,1)S(1)} %collective-permute-done.2.refs_1_, ...), custom_call_target="tpu_custom_call" | custom-call | flops 1024 | bytes 1024 | tf_op jit(solution)/shard_map/attend_step/pallas_call | solution.py:494
  29.4 2.8 %attend_last.2 = (bf16[128,1024]{1,0:T(8,128)(2,1)S(1)}, bf16[2,128,1024]{2,1,0:T(8,128)(2,1)S(1)}, bf16[2,1024,1024]{2,1,0:T(8,128)(2,1)S(1)}) custom-call(s32[512]{0:T(512)S(1)} %reshape.13.lists_ref, s32[64]{0:T(128)S(1)} %reshape.14.counts_ref, bf16[8,128,128]{2,1,0:T(8,128)(2,1)S(1)} %get-tuple-element.43.refs_0_.q_ref, ...), custom_call_target="tpu_custom_call" | custom-call | flops 1024 | bytes 1024 | tf_op jit(solution)/shard_map/attend_last/pallas_call | solution.py:537
  32.4 2.8 %attend_last.3 = (bf16[128,1024]{1,0:T(8,128)(2,1)S(1)}, bf16[2,128,1024]{2,1,0:T(8,128)(2,1)S(1)}) custom-call(s32[512]{0:T(512)S(1)} %reshape.13.lists_ref, s32[64]{0:T(128)S(1)} %reshape.14.counts_ref, bf16[8,128,128]{2,1,0:T(8,128)(2,1)S(1)} %get-tuple-element.49.refs_1_.refs_0_.q_ref, bf16[2048,128]{1,0:T(8,128)(2,1)S(1)} %collective-permute-done.1.mine_ref, ...), custom_call_target="tpu_custom_call" | custom-call | flops 1024 | bytes 1024 | tf_op jit(solution)/shard_map/attend_last/pallas_call | solution.py:537
  36.2 1.6 %collective-permute-start.6 = (bf16[128,1024]{1,0:T(8,128)(2,1)S(1)}, bf16[128,1024]{1,0:T(8,128)(2,1)S(1)}, u32[]{:S(2)}, u32[]{:S(2)}) collective-permute-start(bf16[128,1024]{1,0:T(8,128)(2,1)S(1)} %project_onward.2), channel_id=1, source_target_pairs={{0,2},{1,3},{2,0},{3,1},{4,6},{5,7},{6,4},{7,5},{8,10},{9,11},{10,... | collective-permute-start | bytes 786440 | tf_op jit(solution)/shard_map/ppermute | solution.py:578
  38.3 1.1 %collective-permute-start.8 = (bf16[128,1024]{1,0:T(8,128)(2,1)S(1)}, bf16[128,1024]{1,0:T(8,128)(2,1)S(1)}, u32[]{:S(2)}, u32[]{:S(2)}) collective-permute-start(bf16[128,1024]{1,0:T(8,128)(2,1)S(1)} %project_onward.3), channel_id=1, source_target_pairs={{0,2},{1,3},{2,0},{3,1},{4,6},{5,7},{6,4},{7,5},{8,10},{9,11},{10,... | collective-permute-start | bytes 786440 | tf_op jit(solution)/shard_map/ppermute | solution.py:578
  39.4 1.3 %project_near.2.refs_0_ = f32[128,1024]{1,0:T(8,128)S(1)} custom-call(bf16[128,1024]{1,0:T(8,128)(2,1)S(1)} %get-tuple-element.71.attended_ref, bf16[2,1024,1024]{2,1,0:T(8,128)(2,1)S(1)} %get-tuple-element.72.weight_ref, bf16[2,128,1024]{2,1,0:T(8,128)(2,1)S(1)} %collective-permute-done.5.got_ref, bf16[2,128,4096]{2,1,0:T(8,128)(2,1)} %residual_ref.3), custom_call_target="tpu_custom_call" | custom-call | flops 1024 | bytes 1024 | tf_op jit(solution)/shard_map/project_near/pallas_call | solution.py:582
  40.7 4.8 %collective-permute-done.6.refs_1_ = bf16[128,1024]{1,0:T(8,128)(2,1)S(1)} collective-permute-done((bf16[128,1024]{1,0:T(8,128)(2,1)S(1)}, bf16[128,1024]{1,0:T(8,128)(2,1)S(1)}, u32[]{:S(2)}, u32[]{:S(2)}) %collective-permute-start.6) | collective-permute-done | bytes 262176 | tf_op jit(solution)/shard_map/ppermute | solution.py:578
  45.7 1.3 %project_near.3.refs_0_ = f32[128,1024]{1,0:T(8,128)S(1)} custom-call(bf16[128,1024]{1,0:T(8,128)(2,1)S(1)} %get-tuple-element.79.attended_ref, bf16[2,1024,1024]{2,1,0:T(8,128)(2,1)S(1)} %get-tuple-element.72.weight_ref, bf16[2,128,1024]{2,1,0:T(8,128)(2,1)S(1)} %collective-permute-done.7.got_ref, bf16[2,128,4096]{2,1,0:T(8,128)(2,1)} %residual_ref.3), custom_call_target="tpu_custom_call" | custom-call | flops 1024 | bytes 1024 | tf_op jit(solution)/shard_map/project_near/pallas_call | solution.py:582
  47.0 3.2 %collective-permute-done.8.refs_1_ = bf16[128,1024]{1,0:T(8,128)(2,1)S(1)} collective-permute-done((bf16[128,1024]{1,0:T(8,128)(2,1)S(1)}, bf16[128,1024]{1,0:T(8,128)(2,1)S(1)}, u32[]{:S(2)}, u32[]{:S(2)}) %collective-permute-start.8) | collective-permute-done | bytes 262176 | tf_op jit(solution)/shard_map/ppermute | solution.py:578
  50.3 1.5 %collective-permute-start.10 = (f32[16,128]{1,0:T(8,128)S(1)}, f32[16,128]{1,0:T(8,128)S(1)}, u32[]{:S(2)}, u32[]{:S(2)}) collective-permute-start(f32[16,128]{1,0:T(8,128)S(1)} %constant_dynamic-update-slice_fusion.refs_2_), channel_id=1, source_target_pairs={{0,2},{1,3},{2,0},{3,1},{4,6},{5,7},{6,4},{7,5},{8,10},{9,11},{10,... | collective-permute-start | bytes 24584 | tf_op jit(solution)/shard_map/ppermute | solution.py:623
  52.4 1.7 %collective-permute-done.10.refs_4_ = f32[16,128]{1,0:T(8,128)S(1)} collective-permute-done((f32[16,128]{1,0:T(8,128)S(1)}, f32[16,128]{1,0:T(8,128)S(1)}, u32[]{:S(2)}, u32[]{:S(2)}) %collective-permute-start.10) | collective-permute-done | bytes 8224 | tf_op jit(solution)/shard_map/ppermute | solution.py:623
  54.0 0.9 %collective-permute-done.9.refs_3_ = f32[16,128]{1,0:T(8,128)S(1)} collective-permute-done((f32[16,128]{1,0:T(8,128)S(1)}, f32[16,128]{1,0:T(8,128)S(1)}, u32[]{:S(2)}, u32[]{:S(2)}) %collective-permute-start.9) | collective-permute-done | bytes 8224 | tf_op jit(solution)/shard_map/ppermute | solution.py:623
  54.9 1.2 %norm.1 = (bf16[2,128,1024]{2,1,0:T(8,128)(2,1)}, bf16[2,128,1024]{2,1,0:T(8,128)(2,1)}) custom-call(f32[128,1024]{1,0:T(8,128)S(1)} %get-tuple-element.78.refs_0_, f32[128,1024]{1,0:T(8,128)S(1)} %get-tuple-element.81.refs_1_, f32[16,128]{1,0:T(8,128)S(1)} %constant_dynamic-update-slice_fusion.refs_2_, f32[16,128]{1,0:T(8,128)S(1)} %collective-permute-done.9.refs_3_, ...), custom_call_target="tpu_custom_call" | custom-call | flops 1024 | bytes 1024 | tf_op jit(solution)/shard_map/norm/pallas_call | solution.py:627
  (23 shorter events, 2.7 us)
Async XLA Ops:
  1.7 15.5 %collective-permute-start = (bf16[2048,128]{1,0:T(8,128)(2,1)S(1)}, bf16[2048,128]{1,0:T(8,128)(2,1)S(1)}, u32[]{:S(2)}, u32[]{:S(2)}) collective-permute-start(bf16[2048,128]{1,0:T(8,128)(2,1)S(1)} %pack.1.packed_ref), channel_id=1, source_target_pairs={{0,4},{1,9},{2,6},{3,11},{4,0},{5,13},{6,2},{7,15},{8,12},{9,1},{1... | collective-permute-start | bytes 1572872 | tf_op jit(solution)/shard_map/ppermute | solution.py:522
  17.2 8.3 %collective-permute-start.1 = (bf16[2048,128]{1,0:T(8,128)(2,1)S(1)}, bf16[2048,128]{1,0:T(8,128)(2,1)S(1)}, u32[]{:S(2)}, u32[]{:S(2)}) collective-permute-start(bf16[2048,128]{1,0:T(8,128)(2,1)S(1)} %collective-permute-done.refs_2_), channel_id=1, source_target_pairs={{1,5},{3,7},{5,1},{7,3},{9,13},{11,15},{13,9},{15,11},{17,21},{19,... | collective-permute-start | bytes 1572872 | tf_op jit(solution)/shard_map/ppermute | solution.py:522
  18.0 5.6 %collective-permute-start.2 = (bf16[1024,128]{1,0:T(8,128)(2,1)S(1)}, bf16[1024,128]{1,0:T(8,128)(2,1)S(1)}, u32[]{:S(2)}, u32[]{:S(2)}) collective-permute-start(bf16[1024,128]{1,0:T(8,128)(2,1)S(1)} %get-tuple-element.85), channel_id=1, source_target_pairs={{0,1},{1,0},{2,3},{3,2},{4,5},{5,4},{6,7},{7,6},{8,9},{9,8},{10,11... | collective-permute-start | bytes 786440 | tf_op jit(solution)/shard_map/ppermute | solution.py:526
  20.3 3.3 %collective-permute-start.3 = (bf16[1024,128]{1,0:T(8,128)(2,1)S(1)}, bf16[1024,128]{1,0:T(8,128)(2,1)S(1)}, u32[]{:S(2)}, u32[]{:S(2)}) collective-permute-start(bf16[1024,128]{1,0:T(8,128)(2,1)S(1)} %get-tuple-element.84), channel_id=1, source_target_pairs={{0,1},{1,0},{2,3},{3,2},{4,5},{5,4},{6,7},{7,6},{8,9},{9,8},{10,11... | collective-permute-start | bytes 786440 | tf_op jit(solution)/shard_map/ppermute | solution.py:526
  25.5 3.9 %collective-permute-start.4 = (bf16[2048,128]{1,0:T(8,128)(2,1)S(1)}, bf16[2048,128]{1,0:T(8,128)(2,1)S(1)}, u32[]{:S(2)}, u32[]{:S(2)}) collective-permute-start(bf16[2048,128]{1,0:T(8,128)(2,1)S(1)} %collective-permute-done.1.mine_ref), channel_id=1, source_target_pairs={{0,1},{1,0},{2,3},{3,2},{4,5},{5,4},{6,7},{7,6},{8,9},{9,8},{10,11... | collective-permute-start | bytes 1572872 | tf_op jit(solution)/shard_map/ppermute | solution.py:530
  32.3 2.9 %collective-permute-start.5 = (bf16[2,128,1024]{2,1,0:T(8,128)(2,1)S(1)}, bf16[2,128,1024]{2,1,0:T(8,128)(2,1)S(1)}, u32[]{:S(2)}, u32[]{:S(2)}) collective-permute-start(bf16[2,128,1024]{2,1,0:T(8,128)(2,1)S(1)} %get-tuple-element.73), channel_id=1, source_target_pairs={{0,1},{1,0},{2,3},{3,2},{4,5},{5,4},{6,7},{7,6},{8,9},{9,8},{10,11... | collective-permute-start | bytes 1572872 | tf_op jit(solution)/shard_map/ppermute | solution.py:599
  35.2 2.6 %collective-permute-start.7 = (bf16[2,128,1024]{2,1,0:T(8,128)(2,1)S(1)}, bf16[2,128,1024]{2,1,0:T(8,128)(2,1)S(1)}, u32[]{:S(2)}, u32[]{:S(2)}) collective-permute-start(bf16[2,128,1024]{2,1,0:T(8,128)(2,1)S(1)} %get-tuple-element.80), channel_id=1, source_target_pairs={{0,1},{1,0},{2,3},{3,2},{4,5},{5,4},{6,7},{7,6},{8,9},{9,8},{10,11... | collective-permute-start | bytes 1572872 | tf_op jit(solution)/shard_map/ppermute | solution.py:599
  36.2 9.2 %collective-permute-start.6 = (bf16[128,1024]{1,0:T(8,128)(2,1)S(1)}, bf16[128,1024]{1,0:T(8,128)(2,1)S(1)}, u32[]{:S(2)}, u32[]{:S(2)}) collective-permute-start(bf16[128,1024]{1,0:T(8,128)(2,1)S(1)} %project_onward.2), channel_id=1, source_target_pairs={{0,2},{1,3},{2,0},{3,1},{4,6},{5,7},{6,4},{7,5},{8,10},{9,11},{10,... | collective-permute-start | bytes 786440 | tf_op jit(solution)/shard_map/ppermute | solution.py:578
  38.3 11.9 %collective-permute-start.8 = (bf16[128,1024]{1,0:T(8,128)(2,1)S(1)}, bf16[128,1024]{1,0:T(8,128)(2,1)S(1)}, u32[]{:S(2)}, u32[]{:S(2)}) collective-permute-start(bf16[128,1024]{1,0:T(8,128)(2,1)S(1)} %project_onward.3), channel_id=1, source_target_pairs={{0,2},{1,3},{2,0},{3,1},{4,6},{5,7},{6,4},{7,5},{8,10},{9,11},{10,... | collective-permute-start | bytes 786440 | tf_op jit(solution)/shard_map/ppermute | solution.py:578
  45.6 6.7 %copy-start = (bf16[1024]{0:T(1024)(128)(2,1)S(1)}, bf16[1024]{0:T(1024)(128)(2,1)}, u32[]{:S(2)}) copy-start(bf16[1024]{0:T(1024)(128)(2,1)} %param.19) | copy-start | bytes 6148
  50.3 3.7 %collective-permute-start.10 = (f32[16,128]{1,0:T(8,128)S(1)}, f32[16,128]{1,0:T(8,128)S(1)}, u32[]{:S(2)}, u32[]{:S(2)}) collective-permute-start(f32[16,128]{1,0:T(8,128)S(1)} %constant_dynamic-update-slice_fusion.refs_2_), channel_id=1, source_target_pairs={{0,2},{1,3},{2,0},{3,1},{4,6},{5,7},{6,4},{7,5},{8,10},{9,11},{10,... | collective-permute-start | bytes 24584 | tf_op jit(solution)/shard_map/ppermute | solution.py:623
  51.9 2.2 %collective-permute-start.11 = (f32[16,128]{1,0:T(8,128)S(1)}, f32[16,128]{1,0:T(8,128)S(1)}, u32[]{:S(2)}, u32[]{:S(2)}) collective-permute-start(f32[16,128]{1,0:T(8,128)S(1)} %constant_dynamic-update-slice_fusion.refs_2_), channel_id=1, source_target_pairs={{0,3},{1,0},{2,1},{3,2},{4,7},{5,4},{6,5},{7,6},{8,11},{9,8},{10,9... | collective-permute-start | bytes 24584 | tf_op jit(solution)/shard_map/ppermute | solution.py:623
  51.9 3.1 %collective-permute-start.9 = (f32[16,128]{1,0:T(8,128)S(1)}, f32[16,128]{1,0:T(8,128)S(1)}, u32[]{:S(2)}, u32[]{:S(2)}) collective-permute-start(f32[16,128]{1,0:T(8,128)S(1)} %constant_dynamic-update-slice_fusion.refs_2_), channel_id=1, source_target_pairs={{0,1},{1,2},{2,3},{3,0},{4,5},{5,6},{6,7},{7,4},{8,9},{9,10},{10,1... | collective-permute-start | bytes 24584 | tf_op jit(solution)/shard_map/ppermute | solution.py:623

commit v11 on v10

--- a/solution.py
+++ b/solution.py
@@ -30,38 +30,32 @@
     return pl.ds(pl.multiple_of(key_group(heads) * HD, HD), HD)
 
 
-def pack_kernel(heads, keys_ref, values_ref, packed_ref, values_buf, sems):
-    rows = keys_ref.shape[0]
-    lanes = group_lanes(heads)
-    keys_copy = pltpu.make_async_copy(
-        keys_ref.at[:, lanes], packed_ref.at[pl.ds(0, rows)], sems.at[0]
-    )
-    values_copy = pltpu.make_async_copy(values_ref.at[:, lanes], values_buf, sems.at[1])
-    values_copy.start()
-    keys_copy.start()
-    values_copy.wait()
-    for p in range(rows // HD):
-        packed_ref[rows + p * HD : rows + (p + 1) * HD, :] = values_buf[
-            p * HD : (p + 1) * HD, :
-        ].T
-    keys_copy.wait()
-
-
-def split(refs):
-    if len(refs) == 2:
-        return refs
-    rows = refs[0].shape[0] // 2
-    return refs[0].at[pl.ds(0, rows)], refs[0].at[pl.ds(rows, rows)]
-
-
-def both_ways(values_ref, flipped_ref):
-    rows = values_ref.shape[0]
-    for p in range(rows // HD):
-        pair = values_ref[p * HD : (p + 1) * HD, :]
-        flipped_ref[p * HD : (p + 1) * HD, :] = pair
-        flipped_ref[rows + p * HD : rows + (p + 1) * HD, :] = jnp.concatenate(
-            [pair[:, BLK:], pair[:, :BLK]], axis=1
-        )
+def pack_keys_kernel(heads, keys_ref, packed_ref, sems):
+    copy = pltpu.make_async_copy(keys_ref.at[:, group_lanes(heads)], packed_ref, sems.at[0])
+    copy.start()
+    copy.wait()
+
+
+def pack_values_kernel(heads, values_ref, packed_ref, values_buf, sems):
+    copy = pltpu.make_async_copy(values_ref.at[:, group_lanes(heads)], values_buf, sems.at[0])
+    copy.start()
+    copy.wait()
+    for p in range(packed_ref.shape[0] // HD):
+        rows = slice(p * HD, (p + 1) * HD)
+        packed_ref[rows, :] = values_buf[rows, :].T
+
+
+def both_ways(values_refs, flipped_ref):
+    total = flipped_ref.shape[0] // 2
+    for part, values_ref in enumerate(values_refs):
+        rows = values_ref.shape[0]
+        for p in range(rows // HD):
+            pair = values_ref[p * HD : (p + 1) * HD, :]
+            at = part * rows + p * HD
+            flipped_ref[at : at + HD, :] = pair
+            flipped_ref[total + at : total + at + HD, :] = jnp.concatenate(
+                [pair[:, BLK:], pair[:, :BLK]], axis=1
+            )
 
 
 def shard_scores(lists_ref, counts_ref, q_refs, keys_ref, flipped_ref, place, head, cont):
@@ -150,7 +144,8 @@
     conts,
     lists_ref,
     counts_ref,
-    packed_ref,
+    keys_ref,
+    values_ref,
     queries_ref,
     cont_keys_ref,
     cont_values_ref,
@@ -159,7 +154,6 @@
     states, refs = by_cont(refs[: 2 * conts]), refs[2 * conts :]
     q_refs, refs = refs[:conts], refs[conts:]
     flipped_ref, rows_ref, ck_ref, cv_ref, own_ref, sems = refs
-    keys_ref, values_ref = split([packed_ref])
     heads, _, length = q_refs[0].shape
     lanes = group_lanes(heads)
     copies = start_all(
@@ -170,7 +164,7 @@
         ]
     )
     place = conts, sources, lax.axis_index("ctx")
-    both_ways(values_ref, flipped_ref)
+    both_ways([values_ref], flipped_ref)
     copies[0].wait()
     for cont in range(conts):
         own_ref[cont] = cv_ref[cont].T
@@ -232,10 +226,10 @@
 
 
 def absorb_shard(place, lists_ref, counts_ref, q_refs, held, flipped_ref, before, after):
-    keys_ref, values_ref = split(held)
+    keys_ref, *values_refs = held
     heads = next(iter(q_refs.values())).shape[0]
     together = min(heads, TOGETHER // len(q_refs))
-    both_ways(values_ref, flipped_ref)
+    both_ways(values_refs, flipped_ref)
 
     def some_heads(index, carry):
         work = [(index * together + j, cont) for j in range(together) for cont in q_refs]
@@ -311,8 +305,10 @@
     lists_ref,
     counts_ref,
     q_ref,
-    mine_ref,
-    theirs_ref,
+    mine_keys_ref,
+    mine_values_ref,
+    their_keys_ref,
+    their_values_ref,
     acc_in,
     stat_in,
     give_weight_ref,
@@ -329,7 +325,10 @@
     for part, (source, valid) in enumerate(arrivals(step, sources)):
 
         def absorb_part():
-            held = [(mine_ref, theirs_ref)[part]]
+            held = (
+                (mine_keys_ref, mine_values_ref),
+                (their_keys_ref, their_values_ref),
+            )[part]
             shard = ((conts, sources, source), lists_ref, counts_ref, {cont: q_ref}, held)
             first = part == 0 or one_of_two
             absorb_shard(
@@ -377,16 +376,20 @@
     squares_ref[...] = jnp.broadcast_to(sums, (sums.shape[0], HD)).T[:8]
 
 
-def norm_kernel(conts, members, model_width, *refs):
-    totals, squares = refs[:conts], refs[conts : conts + members]
-    gain_ref, stream_ref, normed_ref = refs[conts + members :]
+def stream_kernel(conts, *refs):
+    for cont in range(conts):
+        refs[conts][cont] = refs[cont][...].astype(jnp.bfloat16)
+
+
+def norm_kernel(conts, model_width, *refs):
+    totals, squares = refs[:conts], refs[conts:-2]
+    gain_ref, normed_ref = refs[-2:]
     gain = gain_ref[...].astype(jnp.float32)
     for cont in range(conts):
         row = functools.reduce(jnp.add, [ref[cont * 8 : cont * 8 + 1, :] for ref in squares])
         scale = lax.rsqrt(row / model_width + 1e-05)
         scale = jnp.broadcast_to(scale, (HD, scale.shape[1])).T[:, 0:1]
         total = totals[cont][...]
-        stream_ref[cont] = total.astype(jnp.bfloat16)
         normed_ref[cont] = (total * scale * gain).astype(jnp.bfloat16)
 
 
@@ -426,19 +429,30 @@
     def in_hbm(x):
         return pltpu.with_memory_space_constraint(x, pltpu.HBM)
 
-    packed = pl.pallas_call(
-        functools.partial(pack_kernel, heads),
-        out_shape=array((2 * rows_dev, HD), jnp.bfloat16),
-        in_specs=[hbm] * 2,
+    kept = array((rows_dev, HD), jnp.bfloat16)
+    keys = pl.pallas_call(
+        functools.partial(pack_keys_kernel, heads),
+        out_shape=kept,
+        in_specs=[hbm],
+        out_specs=vmem,
+        scratch_shapes=[pltpu.SemaphoreType.DMA((1,))],
+        compiler_params=params,
+        cost_estimate=cost(),
+        name="pack_keys",
+    )(in_hbm(prompt_keys))
+    values = pl.pallas_call(
+        functools.partial(pack_values_kernel, heads),
+        out_shape=kept,
+        in_specs=[hbm],
         out_specs=vmem,
         scratch_shapes=[
             pltpu.VMEM((rows_dev, HD), jnp.bfloat16),
-            pltpu.SemaphoreType.DMA((2,)),
+            pltpu.SemaphoreType.DMA((1,)),
         ],
         compiler_params=params,
         cost_estimate=cost(),
-        name="pack",
-    )(in_hbm(prompt_keys), in_hbm(prompt_values))
+        name="pack_values",
+    )(in_hbm(prompt_values))
 
     def across(step):
         def target(z, t):
@@ -471,7 +485,7 @@
     made = pl.pallas_call(
         functools.partial(first_kernel, sources, conts),
         out_shape=state_shape * conts + (array((heads, HD, length), jnp.bfloat16),) * conts,
-        in_specs=[smem, smem, vmem] + [hbm] * 3,
+        in_specs=[smem, smem, vmem, vmem] + [hbm] * 3,
         out_specs=(vmem,) * (3 * conts),
         scratch_shapes=[
             flipped,
@@ -484,7 +498,7 @@
         compiler_params=params,
         cost_estimate=cost(),
         name="attend_own",
-    )(lists, counts, packed, in_hbm(queries), in_hbm(cont_keys), in_hbm(cont_values))
+    )(lists, counts, keys, values, in_hbm(queries), in_hbm(cont_keys), in_hbm(cont_values))
     states = tuple(made[2 * c : 2 * c + 2] for c in range(conts))
     qs = made[2 * conts :]
 
@@ -516,18 +530,22 @@
         return tuple(states), made[2 * count :]
 
     everyone = tuple(range(conts))
-    mine, theirs = packed, None
+    mine, theirs = (keys, values), None
     for step in range(1, steps + 1):
-        sent = mine if sources == 4 and step == 2 else packed
-        mine = lax.ppermute(sent, ("ctx", "tp"), across(step))
-        mine, states = lax.optimization_barrier((mine, states))
+        sent = mine if sources == 4 and step == 2 else (keys, values)
+        mine_keys, mine_values = [lax.ppermute(x, ("ctx", "tp"), across(step)) for x in sent]
+        mine_keys, states = lax.optimization_barrier((mine_keys, states))
+        their_keys = lax.ppermute(mine_keys, "tp", sibling)
+        mine_values, states = lax.optimization_barrier((mine_values, states))
+        their_values = [
+            lax.ppermute(x, "tp", sibling)
+            for x in jnp.split(mine_values, 2 if step < steps else 1)
+        ]
         rest = theirs
+        mine, theirs = (mine_keys, mine_values), (their_keys, *their_values)
         if step < steps:
-            theirs = [lax.ppermute(x, "tp", sibling) for x in jnp.split(mine, 2)]
-            states, (give_weight,) = attend_step(step, 0, everyone, True, states, [mine])
+            states, (give_weight,) = attend_step(step, 0, everyone, True, states, mine)
             states, _ = attend_step(step, 1, everyone[:1], False, states, theirs)
-        else:
-            theirs = [lax.ppermute(mine, "tp", sibling)]
         if step > 1:
             states, _ = attend_step(step - 1, 1, everyone[1:], False, states, rest)
             theirs, states = lax.optimization_barrier((theirs, states))
@@ -541,7 +559,7 @@
                 array((chips, length, share), jnp.bfloat16),
             )
             + (weight_shape,) * fetch,
-            in_specs=[smem, smem] + [vmem] * 6 + [hbm] * fetch,
+            in_specs=[smem, smem] + [vmem] * 8 + [hbm] * fetch,
             out_specs=(vmem,) * (2 + fetch),
             scratch_shapes=[pltpu.VMEM(a.shape, a.dtype) for a in state_shape]
             + [flipped]
@@ -553,7 +571,7 @@
             lists,
             counts,
             qs[cont],
-            mine,
+            *mine,
             *theirs,
             *state,
             give_weight,
@@ -619,20 +637,35 @@
         totals.append(total)
         squares.append(square)
     squares = jnp.concatenate(squares, axis=0)
+    squares = squares + lax.ppermute(squares, "tp", sibling)
     all_squares = [squares] + [
-        lax.ppermute(squares, "tp", [(t, (t + k) % members) for t in range(members)])
-        for k in range(1, members)
+        lax.ppermute(
+            squares,
+            "tp",
+            [(t, (t // CORES + k) % chips * CORES + t % CORES) for t in range(members)],
+        )
+        for k in range(1, chips)
     ]
     out = array((conts, length, share), jnp.bfloat16)
-    return pl.pallas_call(
-        functools.partial(norm_kernel, conts, members, model_width),
-        out_shape=(out, out),
-        in_specs=[vmem] * (conts + members + 1),
-        out_specs=(vmem, vmem),
+    stream = pl.pallas_call(
+        functools.partial(stream_kernel, conts),
+        out_shape=out,
+        in_specs=[vmem] * conts,
+        out_specs=vmem,
+        compiler_params=params,
+        cost_estimate=cost(),
+        name="stream",
+    )(*totals)
+    normed = pl.pallas_call(
+        functools.partial(norm_kernel, conts, model_width),
+        out_shape=out,
+        in_specs=[vmem] * (conts + chips + 1),
+        out_specs=vmem,
         compiler_params=params,
         cost_estimate=cost(),
         name="norm",
     )(*totals, *all_squares, norm_gain.reshape(1, share))
+    return stream, normed
 
 
 def solution(mesh):

time: 56.5 us -> 55.5 us (0.982)
  waiting for transfers between devices: 16.7 us -> 14.3 us
  Pallas kernels: 23.3 us -> 24.9 us
    ppermute x8 -> x11, waiting for transfers between devices: 8.8 us -> 6.22 us  [the longest x4 3.74 us: shards(): lax.ppermute(x, ('ctx', 'tp'), across(step))]
    pallas_call x2 -> x4, Pallas kernels: 2.32 us -> 3.93 us  [the longest x1 1.08 us: shards(): pl.pallas_call(functools.partial(pack_values_kernel, heads), out_shape=ke...]
    ppermute x8 -> x11, starting transfers between devices: 10.3 us -> 9.68 us  [the longest x4 4.51 us: shards(): lax.ppermute(x, ('ctx', 'tp'), across(step))]
  transfers between devices with their start and end apart: 12 -> 15, of which waited for: 5 -> 5; matrix products, arithmetic and copies ran while one was open for 3% -> 3% of each run, Pallas kernels for 32% -> 36%
where the time goes in v11:
time: 55.5 us; the launch traced here: 55.1 us
  Pallas kernels  24.9 us (45%)
  waiting for transfers between devices  14.3 us (26%)
  starting transfers between devices  13.2 us (24%)
  local copies, waits for them, and re-layouts  1.76 us (3%)
  between operations  0.84 us (2%)
    ppermute x2, waiting for transfers between devices, onward(): far.append(lax.ppermute(parts[k - 1], 'tp', to_chip))  8.09 us
    pallas_call x3, Pallas kernels, attend_step(): pl.pallas_call(functools.partial(middle_kernel, step, part, sources, cont...  6.93 us
    pallas_call x2, Pallas kernels, attend_last(): pl.pallas_call(functools.partial(last_kernel, steps, sources, conts, cont...  5.71 us
    ppermute x4, starting transfers between devices, shards(): lax.ppermute(x, ('ctx', 'tp'), across(step))  4.51 us
    pallas_call x1, Pallas kernels, shards(): pl.pallas_call(functools.partial(first_kernel, sources, conts), out_shape...  4.44 us
    ppermute x4, waiting for transfers between devices, shards(): lax.ppermute(x, ('ctx', 'tp'), across(step))  3.74 us
    ppermute x3, starting transfers between devices, shards(): lax.ppermute(x, 'tp', sibling)  2.94 us
    ppermute x2, starting transfers between devices, onward(): far.append(lax.ppermute(parts[k - 1], 'tp', to_chip))  2.93 us
  transfers between devices with their start and end apart: 15, of which 5 were waited for; matrix products, arithmetic and copies ran while one was open for 3% of the time, Pallas kernels for 36%

profile of v11, /device:TPU:0, one launch (start us, length us, event | category | flops | bytes accessed | tf_op | source)
XLA Modules:
  0.0 55.1 jit_solution(13447157143843545952)
XLA Ops:
  0.6 1.0 %pack_keys.1.keys_ref = bf16[1024,128]{1,0:T(8,128)(2,1)S(1)} custom-call(bf16[1024,256]{1,0:T(8,128)(2,1)} %keys_ref.1), custom_call_target="tpu_custom_call" | custom-call | flops 1024 | bytes 1024 | tf_op jit(solution)/shard_map/pack_keys/pallas_call | solution.py:433
  1.6 3.1 %collective-permute-start = (bf16[1024,128]{1,0:T(8,128)(2,1)S(1)}, bf16[1024,128]{1,0:T(8,128)(2,1)S(1)}, u32[]{:S(2)}, u32[]{:S(2)}) collective-permute-start(bf16[1024,128]{1,0:T(8,128)(2,1)S(1)} %pack_keys.1.keys_ref), channel_id=1, source_target_pairs={{0,4},{1,9},{2,6},{3,11},{4,0},{5,13},{6,2},{7,15},{8,12},{9,1},{1... | collective-permute-start | bytes 786440 | tf_op jit(solution)/shard_map/ppermute | solution.py:536
  4.7 1.1 %pack_values.1.values_ref = bf16[1024,128]{1,0:T(8,128)(2,1)S(1)} custom-call(bf16[1024,256]{1,0:T(8,128)(2,1)} %values_ref.1), custom_call_target="tpu_custom_call" | custom-call | flops 1024 | bytes 1024 | tf_op jit(solution)/shard_map/pack_values/pallas_call | solution.py:443
  5.9 0.8 %copy.13 = s32[8,2,4]{2,1,0:T(2,128)S(1)} copy(s32[8,2,4]{0,2,1:T(4,128)} %param.16) | data formatting | bytes 512 | tf_op args[6]
  6.7 0.9 %reshape.13.lists_ref = s32[512]{0:T(512)S(1)} reshape(s32[8,2,4,8]{3,2,1,0:T(4,128)} %param.15) | data formatting | bytes 4096 | tf_op jit(solution)/shard_map/reshape | solution.py:476
  7.6 4.4 %attend_own.1 = (f32[8,128,128]{2,1,0:T(8,128)S(1)}, f32[8,8,128]{2,1,0:T(8,128)S(1)}, f32[8,128,128]{2,1,0:T(8,128)S(1)}, f32[8,8,128]{2,1,0:T(8,128)S(1)}, bf1...) custom-call(s32[512]{0:T(512)S(1)} %reshape.13.lists_ref, s32[64]{0:T(128)S(1)} %reshape.14.counts_ref, ...), custom_call_target="tpu_custom_call" | custom-call | flops 1024 | bytes 1024 | tf_op jit(solution)/shard_map/attend_own/pallas_call | solution.py:485
  13.4 3.7 %collective-permute-done.3.refs_3_ = bf16[1024,128]{1,0:T(8,128)(2,1)S(1)} collective-permute-done((bf16[1024,128]{1,0:T(8,128)(2,1)S(1)}, bf16[1024,128]{1,0:T(8,128)(2,1)S(1)}, u32[]{:S(2)}, u32[]{:S(2)}) %collective-permute-start.3) | collective-permute-done | bytes 262176 | tf_op jit(solution)/shard_map/ppermute | solution.py:536
  17.8 2.4 %collective-permute-start.4 = (bf16[512,128]{1,0:T(8,128)(2,1)S(1)}, bf16[512,128]{1,0:T(8,128)(2,1)S(1)}, u32[]{:S(2)}, u32[]{:S(2)}) collective-permute-start(bf16[512,128]{1,0:T(8,128)(2,1)S(1)} %get-tuple-element.107), channel_id=1, source_target_pairs={{0,1},{1,0},{2,3},{3,2},{4,5},{5,4},{6,7},{7,6},{8,9},{9,8},{10,11... | collective-permute-start | bytes 393224 | tf_op jit(solution)/shard_map/ppermute | solution.py:541
  20.2 3.2 %attend_step.3 = (f32[8,128,128]{2,1,0:T(8,128)S(1)}, f32[8,8,128]{2,1,0:T(8,128)S(1)}, f32[8,128,128]{2,1,0:T(8,128)S(1)}, f32[8,8,128]{2,1,0:T(8,128)S(1)}, bf16[2,1024,1024]{2,1,0:T(8,128)(2,1)S(1)}) custom-call(s32[512]{0:T(512)S(1)} %reshape.13.lists_ref, s32[64]{0:T(128)S(1)} %reshape.14.counts_ref, ...), custom_call_target="tpu_custom_call" | custom-call | flops 1024 | bytes 1024 | tf_op jit(solution)/shard_map/attend_step/pallas_call | solution.py:508
  23.5 1.9 %attend_step.4 = (f32[8,128,128]{2,1,0:T(8,128)S(1)}, f32[8,8,128]{2,1,0:T(8,128)S(1)}) custom-call(s32[512]{0:T(512)S(1)} %reshape.13.lists_ref, s32[64]{0:T(128)S(1)} %reshape.14.counts_ref, bf16[8,128,128]{2,1,0:T(8,128)(2,1)S(1)} %get-tuple-element.54.refs_0_.q_ref, bf16[1024,128]{1,0:T(8,128)(2,1)S(1)} %collective-permute-done.2.refs_1_, ...), custom_call_target="tpu_custom_call" | custom-call | flops 1024 | bytes 1024 | tf_op jit(solution)/shard_map/attend_step/pallas_call | solution.py:508
  26.0 1.9 %attend_step.5 = (f32[8,128,128]{2,1,0:T(8,128)S(1)}, f32[8,8,128]{2,1,0:T(8,128)S(1)}) custom-call(s32[512]{0:T(512)S(1)} %reshape.13.lists_ref, s32[64]{0:T(128)S(1)} %reshape.14.counts_ref, bf16[8,128,128]{2,1,0:T(8,128)(2,1)S(1)} %get-tuple-element.65.refs_1_.refs_0_.q_ref, bf16[1024,128]{1,0:T(8,128)(2,1)S(1)} %collective-permute-done.2.refs_1_, ...), custom_call_target="tpu_custom_call" | custom-call | flops 1024 | bytes 1024 | tf_op jit(solution)/shard_map/attend_step/pallas_call | solution.py:508
  27.8 2.8 %attend_last.2 = (bf16[128,1024]{1,0:T(8,128)(2,1)S(1)}, bf16[2,128,1024]{2,1,0:T(8,128)(2,1)S(1)}, bf16[2,1024,1024]{2,1,0:T(8,128)(2,1)S(1)}) custom-call(s32[512]{0:T(512)S(1)} %reshape.13.lists_ref, s32[64]{0:T(128)S(1)} %reshape.14.counts_ref, bf16[8,128,128]{2,1,0:T(8,128)(2,1)S(1)} %get-tuple-element.54.refs_0_.q_ref, ...), custom_call_target="tpu_custom_call" | custom-call | flops 1024 | bytes 1024 | tf_op jit(solution)/shard_map/attend_last/pallas_call | solution.py:555
  31.2 2.9 %attend_last.3 = (bf16[128,1024]{1,0:T(8,128)(2,1)S(1)}, bf16[2,128,1024]{2,1,0:T(8,128)(2,1)S(1)}) custom-call(s32[512]{0:T(512)S(1)} %reshape.13.lists_ref, s32[64]{0:T(128)S(1)} %reshape.14.counts_ref, bf16[8,128,128]{2,1,0:T(8,128)(2,1)S(1)} %get-tuple-element.65.refs_1_.refs_0_.q_ref, bf16[1024,128]{1,0:T(8,128)(2,1)S(1)} %collective-permute-done.1.mine_keys_ref, ...), custom_call_target="tpu_custom_call" | custom-call | flops 1024 | bytes 1024 | tf_op jit(solution)/shard_map/attend_last/pallas_call | solution.py:555
  34.7 1.6 %collective-permute-start.10 = (bf16[128,1024]{1,0:T(8,128)(2,1)S(1)}, bf16[128,1024]{1,0:T(8,128)(2,1)S(1)}, u32[]{:S(2)}, u32[]{:S(2)}) collective-permute-start(bf16[128,1024]{1,0:T(8,128)(2,1)S(1)} %project_onward.2), channel_id=1, source_target_pairs={{0,2},{1,3},{2,0},{3,1},{4,6},{5,7},{6,4},{7,5},{8,10},{9,11},{10,... | collective-permute-start | bytes 786440 | tf_op jit(solution)/shard_map/ppermute | solution.py:596
  36.7 1.4 %collective-permute-start.12 = (bf16[128,1024]{1,0:T(8,128)(2,1)S(1)}, bf16[128,1024]{1,0:T(8,128)(2,1)S(1)}, u32[]{:S(2)}, u32[]{:S(2)}) collective-permute-start(bf16[128,1024]{1,0:T(8,128)(2,1)S(1)} %project_onward.3), channel_id=1, source_target_pairs={{0,2},{1,3},{2,0},{3,1},{4,6},{5,7},{6,4},{7,5},{8,10},{9,11},{10,... | collective-permute-start | bytes 786440 | tf_op jit(solution)/shard_map/ppermute | solution.py:596
  38.1 1.3 %project_near.2.refs_0_ = f32[128,1024]{1,0:T(8,128)S(1)} custom-call(bf16[128,1024]{1,0:T(8,128)(2,1)S(1)} %get-tuple-element.93.attended_ref, bf16[2,1024,1024]{2,1,0:T(8,128)(2,1)S(1)} %get-tuple-element.94.weight_ref, bf16[2,128,1024]{2,1,0:T(8,128)(2,1)S(1)} %collective-permute-done.9.got_ref, bf16[2,128,4096]{2,1,0:T(8,128)(2,1)} %residual_ref.3), custom_call_target="tpu_custom_call" | custom-call | flops 1024 | bytes 1024 | tf_op jit(solution)/shard_map/project_near/pallas_call | solution.py:600
  39.4 4.4 %collective-permute-done.10.refs_1_ = bf16[128,1024]{1,0:T(8,128)(2,1)S(1)} collective-permute-done((bf16[128,1024]{1,0:T(8,128)(2,1)S(1)}, bf16[128,1024]{1,0:T(8,128)(2,1)S(1)}, u32[]{:S(2)}, u32[]{:S(2)}) %collective-permute-start.10) | collective-permute-done | bytes 262176 | tf_op jit(solution)/shard_map/ppermute | solution.py:596
  44.0 1.3 %project_near.3.refs_0_ = f32[128,1024]{1,0:T(8,128)S(1)} custom-call(bf16[128,1024]{1,0:T(8,128)(2,1)S(1)} %get-tuple-element.101.attended_ref, bf16[2,1024,1024]{2,1,0:T(8,128)(2,1)S(1)} %get-tuple-element.94.weight_ref, bf16[2,128,1024]{2,1,0:T(8,128)(2,1)S(1)} %collective-permute-done.11.got_ref, bf16[2,128,4096]{2,1,0:T(8,128)(2,1)} %residual_ref.3), custom_call_target="tpu_custom_call" | custom-call | flops 1024 | bytes 1024 | tf_op jit(solution)/shard_map/project_near/pallas_call | solution.py:600
  45.4 3.6 %collective-permute-done.12.refs_1_ = bf16[128,1024]{1,0:T(8,128)(2,1)S(1)} collective-permute-done((bf16[128,1024]{1,0:T(8,128)(2,1)S(1)}, bf16[128,1024]{1,0:T(8,128)(2,1)S(1)}, u32[]{:S(2)}, u32[]{:S(2)}) %collective-permute-start.12) | collective-permute-done | bytes 262176 | tf_op jit(solution)/shard_map/ppermute | solution.py:596
  49.2 1.2 %collective-permute-done.13 = f32[16,128]{1,0:T(8,128)S(1)} collective-permute-done((f32[16,128]{1,0:T(8,128)S(1)}, f32[16,128]{1,0:T(8,128)S(1)}, u32[]{:S(2)}, u32[]{:S(2)}) %collective-permute-start.13) | collective-permute-done | bytes 8224 | tf_op jit(solution)/shard_map/ppermute | solution.py:640
  50.4 1.5 %collective-permute-start.14 = (f32[16,128]{1,0:T(8,128)S(1)}, f32[16,128]{1,0:T(8,128)S(1)}, u32[]{:S(2)}, u32[]{:S(2)}) collective-permute-start(f32[16,128]{1,0:T(8,128)S(1)} %add.3.refs_2_), channel_id=1, source_target_pairs={{0,2},{1,3},{2,0},{3,1},{4,6},{5,7},{6,4},{7,5},{8,10},{9,11},{10,... | collective-permute-start | bytes 24584 | tf_op jit(solution)/shard_map/ppermute | solution.py:642
  51.9 0.8 %stream.1 = bf16[2,128,1024]{2,1,0:T(8,128)(2,1)} custom-call(f32[128,1024]{1,0:T(8,128)S(1)} %get-tuple-element.100.refs_0_, f32[128,1024]{1,0:T(8,128)S(1)} %get-tuple-element.103.refs_1_), custom_call_target="tpu_custom_call" | custom-call | flops 1024 | bytes 1024 | tf_op jit(solution)/shard_map/stream/pallas_call | solution.py:650
  52.7 1.3 %collective-permute-done.14.refs_3_ = f32[16,128]{1,0:T(8,128)S(1)} collective-permute-done((f32[16,128]{1,0:T(8,128)S(1)}, f32[16,128]{1,0:T(8,128)S(1)}, u32[]{:S(2)}, u32[]{:S(2)}) %collective-permute-start.14) | collective-permute-done | bytes 8224 | tf_op jit(solution)/shard_map/ppermute | solution.py:642
  54.1 1.0 %norm.1 = bf16[2,128,1024]{2,1,0:T(8,128)(2,1)} custom-call(f32[128,1024]{1,0:T(8,128)S(1)} %get-tuple-element.100.refs_0_, f32[128,1024]{1,0:T(8,128)S(1)} %get-tuple-element.103.refs_1_, f32[16,128]{1,0:T(8,128)S(1)} %add.3.refs_2_, f32[16,128]{1,0:T(8,128)S(1)} %collective-permute-done.14.refs_3_, bf16[1,1024]{1,0:T(2,128)(2,1)S(1)} %reshape.15.refs_4_), custom_call_target="tpu_custom_call" | custom-call | flops 1024 | bytes 1024 | tf_op jit(solution)/shard_map/norm/pallas_call | solution.py:659
  (32 shorter events, 4.8 us)
Async XLA Ops:
  1.6 10.4 %collective-permute-start = (bf16[1024,128]{1,0:T(8,128)(2,1)S(1)}, bf16[1024,128]{1,0:T(8,128)(2,1)S(1)}, u32[]{:S(2)}, u32[]{:S(2)}) collective-permute-start(bf16[1024,128]{1,0:T(8,128)(2,1)S(1)} %pack_keys.1.keys_ref), channel_id=1, source_target_pairs={{0,4},{1,9},{2,6},{3,11},{4,0},{5,13},{6,2},{7,15},{8,12},{9,1},{1... | collective-permute-start | bytes 786440 | tf_op jit(solution)/shard_map/ppermute | solution.py:536
  5.8 11.3 %collective-permute-start.3 = (bf16[1024,128]{1,0:T(8,128)(2,1)S(1)}, bf16[1024,128]{1,0:T(8,128)(2,1)S(1)}, u32[]{:S(2)}, u32[]{:S(2)}) collective-permute-start(bf16[1024,128]{1,0:T(8,128)(2,1)S(1)} %pack_values.1.values_ref), channel_id=1, source_target_pairs={{0,4},{1,9},{2,6},{3,11},{4,0},{5,13},{6,2},{7,15},{8,12},{9,1},{1... | collective-permute-start | bytes 786440 | tf_op jit(solution)/shard_map/ppermute | solution.py:536
  12.1 11.4 %collective-permute-start.2 = (bf16[1024,128]{1,0:T(8,128)(2,1)S(1)}, bf16[1024,128]{1,0:T(8,128)(2,1)S(1)}, u32[]{:S(2)}, u32[]{:S(2)}) collective-permute-start(bf16[1024,128]{1,0:T(8,128)(2,1)S(1)} %collective-permute-done.refs_2_), channel_id=1, source_target_pairs={{0,1},{1,0},{2,3},{3,2},{4,5},{5,4},{6,7},{7,6},{8,9},{9,8},{10,11... | collective-permute-start | bytes 786440 | tf_op jit(solution)/shard_map/ppermute | solution.py:538
  12.7 12.7 %collective-permute-start.1 = (bf16[1024,128]{1,0:T(8,128)(2,1)S(1)}, bf16[1024,128]{1,0:T(8,128)(2,1)S(1)}, u32[]{:S(2)}, u32[]{:S(2)}) collective-permute-start(bf16[1024,128]{1,0:T(8,128)(2,1)S(1)} %collective-permute-done.refs_2_), channel_id=1, source_target_pairs={{1,5},{3,7},{5,1},{7,3},{9,13},{11,15},{13,9},{15,11},{17,21},{19,... | collective-permute-start | bytes 786440 | tf_op jit(solution)/shard_map/ppermute | solution.py:536
  17.1 8.3 %collective-permute-start.6 = (bf16[1024,128]{1,0:T(8,128)(2,1)S(1)}, bf16[1024,128]{1,0:T(8,128)(2,1)S(1)}, u32[]{:S(2)}, u32[]{:S(2)}) collective-permute-start(bf16[1024,128]{1,0:T(8,128)(2,1)S(1)} %collective-permute-done.3.refs_3_), channel_id=1, source_target_pairs={{1,5},{3,7},{5,1},{7,3},{9,13},{11,15},{13,9},{15,11},{17,21},{19,... | collective-permute-start | bytes 786440 | tf_op jit(solution)/shard_map/ppermute | solution.py:536
  17.8 5.7 %collective-permute-start.4 = (bf16[512,128]{1,0:T(8,128)(2,1)S(1)}, bf16[512,128]{1,0:T(8,128)(2,1)S(1)}, u32[]{:S(2)}, u32[]{:S(2)}) collective-permute-start(bf16[512,128]{1,0:T(8,128)(2,1)S(1)} %get-tuple-element.107), channel_id=1, source_target_pairs={{0,1},{1,0},{2,3},{3,2},{4,5},{5,4},{6,7},{7,6},{8,9},{9,8},{10,11... | collective-permute-start | bytes 393224 | tf_op jit(solution)/shard_map/ppermute | solution.py:541
  20.2 3.3 %collective-permute-start.5 = (bf16[512,128]{1,0:T(8,128)(2,1)S(1)}, bf16[512,128]{1,0:T(8,128)(2,1)S(1)}, u32[]{:S(2)}, u32[]{:S(2)}) collective-permute-start(bf16[512,128]{1,0:T(8,128)(2,1)S(1)} %get-tuple-element.106), channel_id=1, source_target_pairs={{0,1},{1,0},{2,3},{3,2},{4,5},{5,4},{6,7},{7,6},{8,9},{9,8},{10,11... | collective-permute-start | bytes 393224 | tf_op jit(solution)/shard_map/ppermute | solution.py:541
  25.4 2.5 %collective-permute-start.8 = (bf16[1024,128]{1,0:T(8,128)(2,1)S(1)}, bf16[1024,128]{1,0:T(8,128)(2,1)S(1)}, u32[]{:S(2)}, u32[]{:S(2)}) collective-permute-start(bf16[1024,128]{1,0:T(8,128)(2,1)S(1)} %collective-permute-done.6.mine_values_ref), channel_id=1, source_target_pairs={{0,1},{1,0},{2,3},{3,2},{4,5},{5,4},{6,7},{7,6},{8,9},{9,8},{10,11... | collective-permute-start | bytes 786440 | tf_op jit(solution)/shard_map/ppermute | solution.py:541
  25.9 2.0 %collective-permute-start.7 = (bf16[1024,128]{1,0:T(8,128)(2,1)S(1)}, bf16[1024,128]{1,0:T(8,128)(2,1)S(1)}, u32[]{:S(2)}, u32[]{:S(2)}) collective-permute-start(bf16[1024,128]{1,0:T(8,128)(2,1)S(1)} %collective-permute-done.1.mine_keys_ref), channel_id=1, source_target_pairs={{0,1},{1,0},{2,3},{3,2},{4,5},{5,4},{6,7},{7,6},{8,9},{9,8},{10,11... | collective-permute-start | bytes 786440 | tf_op jit(solution)/shard_map/ppermute | solution.py:538
  30.7 3.4 %collective-permute-start.9 = (bf16[2,128,1024]{2,1,0:T(8,128)(2,1)S(1)}, bf16[2,128,1024]{2,1,0:T(8,128)(2,1)S(1)}, u32[]{:S(2)}, u32[]{:S(2)}) collective-permute-start(bf16[2,128,1024]{2,1,0:T(8,128)(2,1)S(1)} %get-tuple-element.95), channel_id=1, source_target_pairs={{0,1},{1,0},{2,3},{3,2},{4,5},{5,4},{6,7},{7,6},{8,9},{9,8},{10,11... | collective-permute-start | bytes 1572872 | tf_op jit(solution)/shard_map/ppermute | solution.py:617
  34.1 2.2 %collective-permute-start.11 = (bf16[2,128,1024]{2,1,0:T(8,128)(2,1)S(1)}, bf16[2,128,1024]{2,1,0:T(8,128)(2,1)S(1)}, u32[]{:S(2)}, u32[]{:S(2)}) collective-permute-start(bf16[2,128,1024]{2,1,0:T(8,128)(2,1)S(1)} %get-tuple-element.102), channel_id=1, source_target_pairs={{0,1},{1,0},{2,3},{3,2},{4,5},{5,4},{6,7},{7,6},{8,9},{9,8},{10,11... | collective-permute-start | bytes 1572872 | tf_op jit(solution)/shard_map/ppermute | solution.py:617
  34.7 9.2 %collective-permute-start.10 = (bf16[128,1024]{1,0:T(8,128)(2,1)S(1)}, bf16[128,1024]{1,0:T(8,128)(2,1)S(1)}, u32[]{:S(2)}, u32[]{:S(2)}) collective-permute-start(bf16[128,1024]{1,0:T(8,128)(2,1)S(1)} %project_onward.2), channel_id=1, source_target_pairs={{0,2},{1,3},{2,0},{3,1},{4,6},{5,7},{6,4},{7,5},{8,10},{9,11},{10,... | collective-permute-start | bytes 786440 | tf_op jit(solution)/shard_map/ppermute | solution.py:596
  36.7 12.3 %collective-permute-start.12 = (bf16[128,1024]{1,0:T(8,128)(2,1)S(1)}, bf16[128,1024]{1,0:T(8,128)(2,1)S(1)}, u32[]{:S(2)}, u32[]{:S(2)}) collective-permute-start(bf16[128,1024]{1,0:T(8,128)(2,1)S(1)} %project_onward.3), channel_id=1, source_target_pairs={{0,2},{1,3},{2,0},{3,1},{4,6},{5,7},{6,4},{7,5},{8,10},{9,11},{10,... | collective-permute-start | bytes 786440 | tf_op jit(solution)/shard_map/ppermute | solution.py:596
  44.0 7.9 %copy-start = (bf16[1024]{0:T(1024)(128)(2,1)S(1)}, bf16[1024]{0:T(1024)(128)(2,1)}, u32[]{:S(2)}) copy-start(bf16[1024]{0:T(1024)(128)(2,1)} %param.19) | copy-start | bytes 6148
  49.2 1.2 %collective-permute-start.13 = (f32[16,128]{1,0:T(8,128)S(1)}, f32[16,128]{1,0:T(8,128)S(1)}, u32[]{:S(2)}, u32[]{:S(2)}) collective-permute-start(f32[16,128]{1,0:T(8,128)S(1)} %constant_dynamic-update-slice_fusion), channel_id=1, source_target_pairs={{0,1},{1,0},{2,3},{3,2},{4,5},{5,4},{6,7},{7,6},{8,9},{9,8},{10,11... | collective-permute-start | bytes 24584 | tf_op jit(solution)/shard_map/ppermute | solution.py:640
  50.4 3.7 %collective-permute-start.14 = (f32[16,128]{1,0:T(8,128)S(1)}, f32[16,128]{1,0:T(8,128)S(1)}, u32[]{:S(2)}, u32[]{:S(2)}) collective-permute-start(f32[16,128]{1,0:T(8,128)S(1)} %add.3.refs_2_), channel_id=1, source_target_pairs={{0,2},{1,3},{2,0},{3,1},{4,6},{5,7},{6,4},{7,5},{8,10},{9,11},{10,... | collective-permute-start | bytes 24584 | tf_op jit(solution)/shard_map/ppermute | solution.py:642

commit v12 on v11

--- a/solution.py
+++ b/solution.py
@@ -287,14 +287,17 @@
             copy.wait()
 
 
-def finish_and_give(acc_ref, stat_ref, weight_ref, attended_ref, give_ref):
+def finish_and_give(acc_ref, stat_ref, weight_ref, attended_ref, give_refs):
     for head in range(attended_ref.shape[1] // HD):
         _, total, acc = load_state(acc_ref, stat_ref, head)
         attended_ref[:, head * HD : (head + 1) * HD] = (acc / total).T.astype(jnp.bfloat16)
+    rows = give_refs[0].shape[1]
     for k in range(weight_ref.shape[0]):
-        give_ref[k] = jnp.dot(
+        made = jnp.dot(
             attended_ref[...], weight_ref[k], preferred_element_type=jnp.float32
-        ).astype(give_ref.dtype)
+        ).astype(jnp.bfloat16)
+        for i, give_ref in enumerate(give_refs):
+            give_ref[k] = made[i * rows : (i + 1) * rows]
 
 
 def last_kernel(
@@ -302,6 +305,7 @@
     sources,
     conts,
     cont,
+    pieces,
     lists_ref,
     counts_ref,
     q_ref,
@@ -315,10 +319,11 @@
     *refs,
 ):
     if cont == 0:
-        weight_ref, attended_ref, give_ref, keep_weight_ref, *refs, sems = refs
+        weight_ref, *refs, sems = refs
+    attended_ref, give_refs, refs = refs[0], refs[1 : 1 + pieces], refs[1 + pieces :]
+    if cont == 0:
+        keep_weight_ref, *refs = refs
         copies = start_all(weight_copies(weight_ref, keep_weight_ref, sems, False))
-    else:
-        attended_ref, give_ref, *refs = refs
     acc_ref, stat_ref, flipped_ref = refs
     before, after = (acc_in, stat_in), (acc_ref, stat_ref)
     one_of_two = sources == 4
@@ -338,21 +343,30 @@
         pl.when(valid)(absorb_part)
         if part == 0 and not one_of_two:
             pl.when(jnp.logical_not(valid))(lambda: hand_on(before, after))
-    finish_and_give(acc_ref, stat_ref, give_weight_ref, attended_ref, give_ref)
+    finish_and_give(acc_ref, stat_ref, give_weight_ref, attended_ref, give_refs)
     if cont == 0:
         for copy in copies:
             copy.wait()
 
 
-def onward_kernel(attended_ref, weight_ref, got_ref, *onward_refs):
-    for k, onward_ref in enumerate(onward_refs, 1):
-        onward_ref[...] = (
+def from_sibling(got_refs, k):
+    return jnp.concatenate([ref[k] for ref in got_refs], axis=0).astype(jnp.float32)
+
+
+def onward_kernel(pieces, cuts, attended_ref, weight_ref, *refs):
+    got_refs, onward_refs = refs[:pieces], refs[pieces:]
+    for k in range(1, weight_ref.shape[0]):
+        made = (
             jnp.dot(attended_ref[...], weight_ref[k], preferred_element_type=jnp.float32)
-            + got_ref[k].astype(jnp.float32)
+            + from_sibling(got_refs, k)
         ).astype(jnp.bfloat16)
-
-
-def near_kernel(cont, attended_ref, weight_ref, got_ref, residual_ref, near_ref, own_ref, sem):
+        for start, end in zip(cuts, cuts[1:]):
+            onward_refs[0][...] = made[start:end]
+            onward_refs = onward_refs[1:]
+
+
+def near_kernel(cont, pieces, attended_ref, weight_ref, residual_ref, *refs):
+    got_refs, (near_ref, own_ref, sem) = refs[:pieces], refs[pieces:]
     share = near_ref.shape[1]
     start = pl.multiple_of(lax.axis_index("tp") * share, HD)
     copy = pltpu.make_async_copy(
@@ -361,16 +375,17 @@
     copy.start()
     near_ref[...] = jnp.dot(
         attended_ref[...], weight_ref[0], preferred_element_type=jnp.float32
-    ) + got_ref[0].astype(jnp.float32)
+    ) + from_sibling(got_refs, 0)
     copy.wait()
     near_ref[...] += own_ref[...].astype(jnp.float32)
 
 
-def sum_kernel(count, *refs):
-    near_ref, fars, (total_ref, squares_ref) = refs[0], refs[1 : 1 + count], refs[1 + count :]
+def sum_kernel(pieces, near_ref, *refs):
+    far_refs, (total_ref, squares_ref) = refs[:-2], refs[-2:]
     total = near_ref[...]
-    for far_ref in fars:
-        total = total + far_ref[...].astype(jnp.float32)
+    for k in range(0, len(far_refs), pieces):
+        parts = [ref[...] for ref in far_refs[k : k + pieces]]
+        total = total + jnp.concatenate(parts, axis=0).astype(jnp.float32)
     total_ref[...] = total
     sums = jnp.sum(total * total, axis=1, keepdims=True)
     squares_ref[...] = jnp.broadcast_to(sums, (sums.shape[0], HD)).T[:8]
@@ -534,33 +549,31 @@
     for step in range(1, steps + 1):
         sent = mine if sources == 4 and step == 2 else (keys, values)
         mine_keys, mine_values = [lax.ppermute(x, ("ctx", "tp"), across(step)) for x in sent]
-        mine_keys, states = lax.optimization_barrier((mine_keys, states))
+        mine_keys, states, theirs = lax.optimization_barrier((mine_keys, states, theirs))
         their_keys = lax.ppermute(mine_keys, "tp", sibling)
         mine_values, states = lax.optimization_barrier((mine_values, states))
         their_values = [
             lax.ppermute(x, "tp", sibling)
             for x in jnp.split(mine_values, 2 if step < steps else 1)
         ]
-        rest = theirs
-        mine, theirs = (mine_keys, mine_values), (their_keys, *their_values)
+        mine, rest, theirs = (mine_keys, mine_values), theirs, (their_keys, *their_values)
+        if rest is not None:
+            states, _ = attend_step(step - 1, 1, everyone[:1], False, states, rest)
+            theirs, first = lax.optimization_barrier((theirs, states[0]))
+            states = (first, *states[1:])
+            states, _ = attend_step(step - 1, 1, everyone[1:], False, states, rest)
         if step < steps:
             states, (give_weight,) = attend_step(step, 0, everyone, True, states, mine)
-            states, _ = attend_step(step, 1, everyone[:1], False, states, theirs)
-        if step > 1:
-            states, _ = attend_step(step - 1, 1, everyone[1:], False, states, rest)
-            theirs, states = lax.optimization_barrier((theirs, states))
 
     def attend_last(cont, state):
-        fetch = cont == 0
-        return pl.pallas_call(
-            functools.partial(last_kernel, steps, sources, conts, cont),
-            out_shape=(
-                array((length, width), jnp.bfloat16),
-                array((chips, length, share), jnp.bfloat16),
-            )
+        fetch, pieces = cont == 0, swap_pieces[cont]
+        made = pl.pallas_call(
+            functools.partial(last_kernel, steps, sources, conts, cont, pieces),
+            out_shape=(array((length, width), jnp.bfloat16),)
+            + (array((chips, length // pieces, share), jnp.bfloat16),) * pieces
             + (weight_shape,) * fetch,
             in_specs=[smem, smem] + [vmem] * 8 + [hbm] * fetch,
-            out_specs=(vmem,) * (2 + fetch),
+            out_specs=(vmem,) * (1 + pieces + fetch),
             scratch_shapes=[pltpu.VMEM(a.shape, a.dtype) for a in state_shape]
             + [flipped]
             + [pltpu.SemaphoreType.DMA((chips,))] * fetch,
@@ -577,30 +590,33 @@
             give_weight,
             *([in_hbm(out_weight)] * fetch),
         )
-
-    def onward(attended, got):
+        return made[0], made[1 : 1 + pieces], made[1 + pieces :]
+
+    def onward(cuts, attended, got):
+        cut_rows = [end - start for start, end in zip(cuts, cuts[1:])]
         parts = pl.pallas_call(
-            onward_kernel,
-            out_shape=(array((length, share), jnp.bfloat16),) * (chips - 1),
-            in_specs=[vmem] * 3,
-            out_specs=(vmem,) * (chips - 1),
+            functools.partial(onward_kernel, len(got), cuts),
+            out_shape=tuple(array((n, share), jnp.bfloat16) for n in cut_rows * (chips - 1)),
+            in_specs=[vmem] * (2 + len(got)),
+            out_specs=(vmem,) * (len(cut_rows) * (chips - 1)),
             compiler_params=params,
             cost_estimate=cost(),
             name="project_onward",
-        )(attended, keep_weight, got)
+        )(attended, keep_weight, *got)
         far = []
         for k in range(1, chips):
             to_chip = [
                 (t, (t // CORES + k) % chips * CORES + t % CORES) for t in range(members)
             ]
-            far.append(lax.ppermute(parts[k - 1], "tp", to_chip))
+            for part in parts[(k - 1) * len(cut_rows) : k * len(cut_rows)]:
+                far.append(lax.ppermute(part, "tp", to_chip))
         return parts, far
 
     def near(cont, attended, got):
         return pl.pallas_call(
-            functools.partial(near_kernel, cont),
+            functools.partial(near_kernel, cont, len(got)),
             out_shape=array((length, share), jnp.float32),
-            in_specs=[vmem] * 3 + [hbm],
+            in_specs=[vmem] * 2 + [hbm] + [vmem] * len(got),
             out_specs=vmem,
             scratch_shapes=[
                 pltpu.VMEM((length, share), jnp.bfloat16),
@@ -609,26 +625,31 @@
             compiler_params=params,
             cost_estimate=cost(),
             name="project_near",
-        )(attended, keep_weight, got, in_hbm(residual))
-
-    attended, give, keep_weight = attend_last(0, states[0])
-    nears, fars = [], []
+        )(attended, keep_weight, in_hbm(residual), *got)
+
+    swap_pieces = [1] + [4] * (conts - 1)
+    attended, give, (keep_weight,) = attend_last(0, states[0])
+    nears, fars, cuts = [], [], []
     for cont in range(conts):
-        got = lax.ppermute(give, "tp", sibling)
-        here = attended
+        got = [lax.ppermute(x, "tp", sibling) for x in give]
+        if cont > 0:
+            first = fars[-1][:: len(cuts[-1]) - 1]
+            got, first = lax.optimization_barrier((got, first))
+            fars[-1][:: len(cuts[-1]) - 1] = first
+        cuts.append((0, length))
+        parts, far = onward(cuts[-1], attended, got)
+        nears.append(near(cont, attended, got))
+        fars.append(far)
         if cont + 1 < conts:
-            attended, give = attend_last(cont + 1, states[cont + 1])
-            got, give = lax.optimization_barrier((got, give))
-        _, far = onward(here, got)
-        fars.append(far)
-        nears.append(near(cont, here, got))
+            state, parts = lax.optimization_barrier((states[cont + 1], parts))
+            attended, give, _ = attend_last(cont + 1, state)
 
     totals, squares = [], []
     for cont in range(conts):
         total, square = pl.pallas_call(
-            functools.partial(sum_kernel, chips - 1),
+            functools.partial(sum_kernel, len(cuts[cont]) - 1),
             out_shape=(array((length, share), jnp.float32), array((8, length), jnp.float32)),
-            in_specs=[vmem] * chips,
+            in_specs=[vmem] * (1 + len(fars[cont])),
             out_specs=(vmem,) * 2,
             compiler_params=params,
             cost_estimate=cost(),

time: 55.5 us -> 55.9 us (level)
  starting transfers between devices: 13.2 us -> 14.4 us
  waiting for transfers between devices: 14.3 us -> 13.7 us
    ppermute x4 -> x7, waiting for transfers between devices: 8.1 us -> 6.95 us  [the longest x2 4.39 us: onward(): far.append(lax.ppermute(part, 'tp', to_chip))]
    ppermute x4 -> x7, starting transfers between devices: 3.55 us -> 4.62 us  [the longest x2 2.96 us: onward(): far.append(lax.ppermute(part, 'tp', to_chip))]
    ppermute x3, starting transfers between devices: 2.94 us -> 3.65 us  [shards(): lax.ppermute(x, 'tp', sibling)]
  transfers between devices with their start and end apart: 15 -> 18, of which waited for: 5 -> 10; matrix products, arithmetic and copies ran while one was open for 3% -> 3% of each run, Pallas kernels for 36% -> 34%
where the time goes in v12:
time: 55.9 us; the launch traced here: 55.5 us
  Pallas kernels  24.8 us (44%)
  starting transfers between devices  14.4 us (26%)
  waiting for transfers between devices  13.7 us (25%)
  local copies, waits for them, and re-layouts  1.76 us (3%)
  between operations  0.84 us (2%)
    pallas_call x3, Pallas kernels, attend_step(): pl.pallas_call(functools.partial(middle_kernel, step, part, sources, cont...  6.92 us
    pallas_call x2, Pallas kernels, attend_last(): pl.pallas_call(functools.partial(last_kernel, steps, sources, conts, cont...  5.72 us
    ppermute x4, starting transfers between devices, shards(): lax.ppermute(x, ('ctx', 'tp'), across(step))  4.51 us
    pallas_call x1, Pallas kernels, shards(): pl.pallas_call(functools.partial(first_kernel, sources, conts), out_shape...  4.44 us
    ppermute x2, waiting for transfers between devices, onward(): far.append(lax.ppermute(part, 'tp', to_chip))  4.39 us
    ppermute x4, waiting for transfers between devices, shards(): lax.ppermute(x, ('ctx', 'tp'), across(step))  3.74 us
    ppermute x3, starting transfers between devices, shards(): lax.ppermute(x, 'tp', sibling)  3.65 us
    ppermute x2, starting transfers between devices, onward(): far.append(lax.ppermute(part, 'tp', to_chip))  2.96 us
  transfers between devices with their start and end apart: 18, of which 10 were waited for; matrix products, arithmetic and copies ran while one was open for 3% of the time, Pallas kernels for 34%

profile of v12, /device:TPU:0, one launch (start us, length us, event | category | flops | bytes accessed | tf_op | source)
XLA Modules:
  0.0 55.5 jit_solution(3605489177792788780)
XLA Ops:
  0.6 1.0 %pack_keys.1.keys_ref = bf16[1024,128]{1,0:T(8,128)(2,1)S(1)} custom-call(bf16[1024,256]{1,0:T(8,128)(2,1)} %keys_ref.1), custom_call_target="tpu_custom_call" | custom-call | flops 1024 | bytes 1024 | tf_op jit(solution)/shard_map/pack_keys/pallas_call | solution.py:448
  1.6 3.1 %collective-permute-start = (bf16[1024,128]{1,0:T(8,128)(2,1)S(1)}, bf16[1024,128]{1,0:T(8,128)(2,1)S(1)}, u32[]{:S(2)}, u32[]{:S(2)}) collective-permute-start(bf16[1024,128]{1,0:T(8,128)(2,1)S(1)} %pack_keys.1.keys_ref), channel_id=1, source_target_pairs={{0,4},{1,9},{2,6},{3,11},{4,0},{5,13},{6,2},{7,15},{8,12},{9,1},{1... | collective-permute-start | bytes 786440 | tf_op jit(solution)/shard_map/ppermute | solution.py:551
  4.7 1.1 %pack_values.1.values_ref = bf16[1024,128]{1,0:T(8,128)(2,1)S(1)} custom-call(bf16[1024,256]{1,0:T(8,128)(2,1)} %values_ref.1), custom_call_target="tpu_custom_call" | custom-call | flops 1024 | bytes 1024 | tf_op jit(solution)/shard_map/pack_values/pallas_call | solution.py:458
  5.9 0.9 %reshape.13.lists_ref = s32[512]{0:T(512)S(1)} reshape(s32[8,2,4,8]{3,2,1,0:T(4,128)} %param.15) | data formatting | bytes 4096 | tf_op jit(solution)/shard_map/reshape | solution.py:491
  7.6 4.4 %attend_own.1 = (f32[8,128,128]{2,1,0:T(8,128)S(1)}, f32[8,8,128]{2,1,0:T(8,128)S(1)}, f32[8,128,128]{2,1,0:T(8,128)S(1)}, f32[8,8,128]{2,1,0:T(8,128)S(1)}, bf1...) custom-call(s32[512]{0:T(512)S(1)} %reshape.13.lists_ref, s32[64]{0:T(128)S(1)} %reshape.14.counts_ref, ...), custom_call_target="tpu_custom_call" | custom-call | flops 1024 | bytes 1024 | tf_op jit(solution)/shard_map/attend_own/pallas_call | solution.py:500
  13.4 3.7 %collective-permute-done.2.refs_3_ = bf16[1024,128]{1,0:T(8,128)(2,1)S(1)} collective-permute-done((bf16[1024,128]{1,0:T(8,128)(2,1)S(1)}, bf16[1024,128]{1,0:T(8,128)(2,1)S(1)}, u32[]{:S(2)}, u32[]{:S(2)}) %collective-permute-start.2) | collective-permute-done | bytes 262176 | tf_op jit(solution)/shard_map/ppermute | solution.py:551
  17.8 2.4 %collective-permute-start.5 = (bf16[512,128]{1,0:T(8,128)(2,1)S(1)}, bf16[512,128]{1,0:T(8,128)(2,1)S(1)}, u32[]{:S(2)}, u32[]{:S(2)}) collective-permute-start(bf16[512,128]{1,0:T(8,128)(2,1)S(1)} %get-tuple-element.124), channel_id=1, source_target_pairs={{0,1},{1,0},{2,3},{3,2},{4,5},{5,4},{6,7},{7,6},{8,9},{9,8},{10,11... | collective-permute-start | bytes 393224 | tf_op jit(solution)/shard_map/ppermute | solution.py:556
  20.2 3.2 %attend_step.3 = (f32[8,128,128]{2,1,0:T(8,128)S(1)}, f32[8,8,128]{2,1,0:T(8,128)S(1)}, f32[8,128,128]{2,1,0:T(8,128)S(1)}, f32[8,8,128]{2,1,0:T(8,128)S(1)}, bf16[2,1024,1024]{2,1,0:T(8,128)(2,1)S(1)}) custom-call(s32[512]{0:T(512)S(1)} %reshape.13.lists_ref, s32[64]{0:T(128)S(1)} %reshape.14.counts_ref, ...), custom_call_target="tpu_custom_call" | custom-call | flops 1024 | bytes 1024 | tf_op jit(solution)/shard_map/attend_step/pallas_call | solution.py:523
  23.5 1.2 %collective-permute-start.8 = (bf16[1024,128]{1,0:T(8,128)(2,1)S(1)}, bf16[1024,128]{1,0:T(8,128)(2,1)S(1)}, u32[]{:S(2)}, u32[]{:S(2)}) collective-permute-start(bf16[1024,128]{1,0:T(8,128)(2,1)S(1)} %collective-permute-done.6.mine_values_ref), channel_id=1, source_target_pairs={{0,1},{1,0},{2,3},{3,2},{4,5},{5,4},{6,7},{7,6},{8,9},{9,8},{10,11... | collective-permute-start | bytes 786440 | tf_op jit(solution)/shard_map/ppermute | solution.py:556
  24.7 1.9 %attend_step.4 = (f32[8,128,128]{2,1,0:T(8,128)S(1)}, f32[8,8,128]{2,1,0:T(8,128)S(1)}) custom-call(s32[512]{0:T(512)S(1)} %reshape.13.lists_ref, s32[64]{0:T(128)S(1)} %reshape.14.counts_ref, bf16[8,128,128]{2,1,0:T(8,128)(2,1)S(1)} %get-tuple-element.63.refs_0_.q_ref, bf16[1024,128]{1,0:T(8,128)(2,1)S(1)} %collective-permute-done.3.refs_1_, ...), custom_call_target="tpu_custom_call" | custom-call | flops 1024 | bytes 1024 | tf_op jit(solution)/shard_map/attend_step/pallas_call | solution.py:523
  26.6 2.8 %attend_last.2 = (bf16[128,1024]{1,0:T(8,128)(2,1)S(1)}, bf16[2,128,1024]{2,1,0:T(8,128)(2,1)S(1)}, bf16[2,1024,1024]{2,1,0:T(8,128)(2,1)S(1)}) custom-call(s32[512]{0:T(512)S(1)} %reshape.13.lists_ref, s32[64]{0:T(128)S(1)} %reshape.14.counts_ref, bf16[8,128,128]{2,1,0:T(8,128)(2,1)S(1)} %get-tuple-element.63.refs_0_.q_ref, ...), custom_call_target="tpu_custom_call" | custom-call | flops 1024 | bytes 1024 | tf_op jit(solution)/shard_map/attend_last/pallas_call | solution.py:570
  30.0 1.5 %collective-permute-done.9.refs_0_ = bf16[2,128,1024]{2,1,0:T(8,128)(2,1)S(1)} collective-permute-done((bf16[2,128,1024]{2,1,0:T(8,128)(2,1)S(1)}, bf16[2,128,1024]{2,1,0:T(8,128)(2,1)S(1)}, u32[]{:S(2)}, u32[]{:S(2)}) %collective-permute-start.9) | collective-permute-done | bytes 524320 | tf_op jit(solution)/shard_map/ppermute | solution.py:634
  32.0 1.5 %collective-permute-start.14 = (bf16[128,1024]{1,0:T(8,128)(2,1)S(1)}, bf16[128,1024]{1,0:T(8,128)(2,1)S(1)}, u32[]{:S(2)}, u32[]{:S(2)}) collective-permute-start(bf16[128,1024]{1,0:T(8,128)(2,1)S(1)} %project_onward.2), channel_id=1, source_target_pairs={{0,2},{1,3},{2,0},{3,1},{4,6},{5,7},{6,4},{7,5},{8,10},{9,11},{10,... | collective-permute-start | bytes 786440 | tf_op jit(solution)/shard_map/ppermute | solution.py:612
  33.5 1.9 %attend_step.5 = (f32[8,128,128]{2,1,0:T(8,128)S(1)}, f32[8,8,128]{2,1,0:T(8,128)S(1)}) custom-call(s32[512]{0:T(512)S(1)} %reshape.13.lists_ref, s32[64]{0:T(128)S(1)} %reshape.14.counts_ref, bf16[8,128,128]{2,1,0:T(8,128)(2,1)S(1)} %get-tuple-element.69.refs_1_.refs_0_.q_ref, bf16[1024,128]{1,0:T(8,128)(2,1)S(1)} %collective-permute-done.3.refs_1_, ...), custom_call_target="tpu_custom_call" | custom-call | flops 1024 | bytes 1024 | tf_op jit(solution)/shard_map/attend_step/pallas_call | solution.py:523
  35.4 2.9 %attend_last.3 = (bf16[128,1024]{1,0:T(8,128)(2,1)S(1)}, bf16[2,32,1024]{2,1,0:T(8,128)(2,1)S(1)}, bf16[2,32,1024]{2,1,0:T(8,128)(2,1)S(1)}, bf16[2,32,1024]{2,1,0:T(8,128)(2,1)S(1)}, bf16[2,32,1024]{2,1,0:T(8,128)(2,1)S(1)}) custom-call(s32[512]{0:T(512)S(1)} %reshape.13.lists_ref, s32[64]{0:T(128)S(1)} %reshape.14.counts_ref, ...), custom_call_target="tpu_custom_call" | custom-call | flops 1024 | bytes 1024 | tf_op jit(solution)/shard_map/attend_last/pallas_call | solution.py:570
  41.1 1.5 %collective-permute-start.15 = (bf16[128,1024]{1,0:T(8,128)(2,1)S(1)}, bf16[128,1024]{1,0:T(8,128)(2,1)S(1)}, u32[]{:S(2)}, u32[]{:S(2)}) collective-permute-start(bf16[128,1024]{1,0:T(8,128)(2,1)S(1)} %project_onward.3), channel_id=1, source_target_pairs={{0,2},{1,3},{2,0},{3,1},{4,6},{5,7},{6,4},{7,5},{8,10},{9,11},{10,... | collective-permute-start | bytes 786440 | tf_op jit(solution)/shard_map/ppermute | solution.py:612
  42.6 1.3 %project_near.2.near_ref = f32[128,1024]{1,0:T(8,128)S(1)} custom-call(bf16[128,1024]{1,0:T(8,128)(2,1)S(1)} %get-tuple-element.101.attended_ref, bf16[2,1024,1024]{2,1,0:T(8,128)(2,1)S(1)} %get-tuple-element.102.weight_ref, bf16[2,128,4096]{2,1,0:T(8,128)(2,1)} %residual_ref.3, bf16[2,128,1024]{2,1,0:T(8,128)(2,1)S(1)} %collective-permute-done.9.refs_0_), custom_call_target="tpu_custom_call" | custom-call | flops 1024 | bytes 1024 | tf_op jit(solution)/shard_map/project_near/pallas_call | solution.py:616
  43.9 1.2 %project_near.3.near_ref = f32[128,1024]{1,0:T(8,128)S(1)} custom-call(bf16[128,1024]{1,0:T(8,128)(2,1)S(1)} %get-tuple-element.116.attended_ref, bf16[2,1024,1024]{2,1,0:T(8,128)(2,1)S(1)} %get-tuple-element.102.weight_ref, bf16[2,128,4096]{2,1,0:T(8,128)(2,1)} %residual_ref.3, bf16[2,32,1024]{2,1,0:T(8,128)(2,1)S(1)} %collective-permute-done.10.refs_0_, ...), custom_call_target="tpu_custom_call" | custom-call | flops 1024 | bytes 1024 | tf_op jit(solution)/shard_map/project_near/pallas_call | solution.py:616
  45.3 4.1 %collective-permute-done.15.refs_0_ = bf16[128,1024]{1,0:T(8,128)(2,1)S(1)} collective-permute-done((bf16[128,1024]{1,0:T(8,128)(2,1)S(1)}, bf16[128,1024]{1,0:T(8,128)(2,1)S(1)}, u32[]{:S(2)}, u32[]{:S(2)}) %collective-permute-start.15) | collective-permute-done | bytes 262176 | tf_op jit(solution)/shard_map/ppermute | solution.py:612
  49.6 1.2 %collective-permute-done.16 = f32[16,128]{1,0:T(8,128)S(1)} collective-permute-done((f32[16,128]{1,0:T(8,128)S(1)}, f32[16,128]{1,0:T(8,128)S(1)}, u32[]{:S(2)}, u32[]{:S(2)}) %collective-permute-start.16) | collective-permute-done | bytes 8224 | tf_op jit(solution)/shard_map/ppermute | solution.py:661
  50.8 0.9 %collective-permute-start.17 = (f32[16,128]{1,0:T(8,128)S(1)}, f32[16,128]{1,0:T(8,128)S(1)}, u32[]{:S(2)}, u32[]{:S(2)}) collective-permute-start(f32[16,128]{1,0:T(8,128)S(1)} %add.3.refs_2_), channel_id=1, source_target_pairs={{0,2},{1,3},{2,0},{3,1},{4,6},{5,7},{6,4},{7,5},{8,10},{9,11},{10,... | collective-permute-start | bytes 24584 | tf_op jit(solution)/shard_map/ppermute | solution.py:663
  51.8 0.8 %stream.1 = bf16[2,128,1024]{2,1,0:T(8,128)(2,1)} custom-call(f32[128,1024]{1,0:T(8,128)S(1)} %get-tuple-element.115.refs_0_, f32[128,1024]{1,0:T(8,128)S(1)} %get-tuple-element.121.refs_1_), custom_call_target="tpu_custom_call" | custom-call | flops 1024 | bytes 1024 | tf_op jit(solution)/shard_map/stream/pallas_call | solution.py:671
  52.6 1.9 %collective-permute-done.17.refs_3_ = f32[16,128]{1,0:T(8,128)S(1)} collective-permute-done((f32[16,128]{1,0:T(8,128)S(1)}, f32[16,128]{1,0:T(8,128)S(1)}, u32[]{:S(2)}, u32[]{:S(2)}) %collective-permute-start.17) | collective-permute-done | bytes 8224 | tf_op jit(solution)/shard_map/ppermute | solution.py:663
  54.5 1.0 %norm.1 = bf16[2,128,1024]{2,1,0:T(8,128)(2,1)} custom-call(f32[128,1024]{1,0:T(8,128)S(1)} %get-tuple-element.115.refs_0_, f32[128,1024]{1,0:T(8,128)S(1)} %get-tuple-element.121.refs_1_, f32[16,128]{1,0:T(8,128)S(1)} %add.3.refs_2_, f32[16,128]{1,0:T(8,128)S(1)} %collective-permute-done.17.refs_3_, bf16[1,1024]{1,0:T(2,128)(2,1)S(1)} %reshape.15.refs_4_), custom_call_target="tpu_custom_call" | custom-call | flops 1024 | bytes 1024 | tf_op jit(solution)/shard_map/norm/pallas_call | solution.py:680
  (38 shorter events, 7.3 us)
Async XLA Ops:
  1.6 10.4 %collective-permute-start = (bf16[1024,128]{1,0:T(8,128)(2,1)S(1)}, bf16[1024,128]{1,0:T(8,128)(2,1)S(1)}, u32[]{:S(2)}, u32[]{:S(2)}) collective-permute-start(bf16[1024,128]{1,0:T(8,128)(2,1)S(1)} %pack_keys.1.keys_ref), channel_id=1, source_target_pairs={{0,4},{1,9},{2,6},{3,11},{4,0},{5,13},{6,2},{7,15},{8,12},{9,1},{1... | collective-permute-start | bytes 786440 | tf_op jit(solution)/shard_map/ppermute | solution.py:551
  5.8 11.3 %collective-permute-start.2 = (bf16[1024,128]{1,0:T(8,128)(2,1)S(1)}, bf16[1024,128]{1,0:T(8,128)(2,1)S(1)}, u32[]{:S(2)}, u32[]{:S(2)}) collective-permute-start(bf16[1024,128]{1,0:T(8,128)(2,1)S(1)} %pack_values.1.values_ref), channel_id=1, source_target_pairs={{0,4},{1,9},{2,6},{3,11},{4,0},{5,13},{6,2},{7,15},{8,12},{9,1},{1... | collective-permute-start | bytes 786440 | tf_op jit(solution)/shard_map/ppermute | solution.py:551
  12.1 11.4 %collective-permute-start.3 = (bf16[1024,128]{1,0:T(8,128)(2,1)S(1)}, bf16[1024,128]{1,0:T(8,128)(2,1)S(1)}, u32[]{:S(2)}, u32[]{:S(2)}) collective-permute-start(bf16[1024,128]{1,0:T(8,128)(2,1)S(1)} %collective-permute-done.refs_2_), channel_id=1, source_target_pairs={{0,1},{1,0},{2,3},{3,2},{4,5},{5,4},{6,7},{7,6},{8,9},{9,8},{10,11... | collective-permute-start | bytes 786440 | tf_op jit(solution)/shard_map/ppermute | solution.py:553
  12.7 10.8 %collective-permute-start.1 = (bf16[1024,128]{1,0:T(8,128)(2,1)S(1)}, bf16[1024,128]{1,0:T(8,128)(2,1)S(1)}, u32[]{:S(2)}, u32[]{:S(2)}) collective-permute-start(bf16[1024,128]{1,0:T(8,128)(2,1)S(1)} %collective-permute-done.refs_2_), channel_id=1, source_target_pairs={{1,5},{3,7},{5,1},{7,3},{9,13},{11,15},{13,9},{15,11},{17,21},{19,... | collective-permute-start | bytes 786440 | tf_op jit(solution)/shard_map/ppermute | solution.py:551
  17.1 6.4 %collective-permute-start.6 = (bf16[1024,128]{1,0:T(8,128)(2,1)S(1)}, bf16[1024,128]{1,0:T(8,128)(2,1)S(1)}, u32[]{:S(2)}, u32[]{:S(2)}) collective-permute-start(bf16[1024,128]{1,0:T(8,128)(2,1)S(1)} %collective-permute-done.2.refs_3_), channel_id=1, source_target_pairs={{1,5},{3,7},{5,1},{7,3},{9,13},{11,15},{13,9},{15,11},{17,21},{19,... | collective-permute-start | bytes 786440 | tf_op jit(solution)/shard_map/ppermute | solution.py:551
  17.8 5.7 %collective-permute-start.5 = (bf16[512,128]{1,0:T(8,128)(2,1)S(1)}, bf16[512,128]{1,0:T(8,128)(2,1)S(1)}, u32[]{:S(2)}, u32[]{:S(2)}) collective-permute-start(bf16[512,128]{1,0:T(8,128)(2,1)S(1)} %get-tuple-element.124), channel_id=1, source_target_pairs={{0,1},{1,0},{2,3},{3,2},{4,5},{5,4},{6,7},{7,6},{8,9},{9,8},{10,11... | collective-permute-start | bytes 393224 | tf_op jit(solution)/shard_map/ppermute | solution.py:556
  20.2 3.3 %collective-permute-start.4 = (bf16[512,128]{1,0:T(8,128)(2,1)S(1)}, bf16[512,128]{1,0:T(8,128)(2,1)S(1)}, u32[]{:S(2)}, u32[]{:S(2)}) collective-permute-start(bf16[512,128]{1,0:T(8,128)(2,1)S(1)} %get-tuple-element.125), channel_id=1, source_target_pairs={{0,1},{1,0},{2,3},{3,2},{4,5},{5,4},{6,7},{7,6},{8,9},{9,8},{10,11... | collective-permute-start | bytes 393224 | tf_op jit(solution)/shard_map/ppermute | solution.py:556
  23.5 3.1 %collective-permute-start.8 = (bf16[1024,128]{1,0:T(8,128)(2,1)S(1)}, bf16[1024,128]{1,0:T(8,128)(2,1)S(1)}, u32[]{:S(2)}, u32[]{:S(2)}) collective-permute-start(bf16[1024,128]{1,0:T(8,128)(2,1)S(1)} %collective-permute-done.6.mine_values_ref), channel_id=1, source_target_pairs={{0,1},{1,0},{2,3},{3,2},{4,5},{5,4},{6,7},{7,6},{8,9},{9,8},{10,11... | collective-permute-start | bytes 786440 | tf_op jit(solution)/shard_map/ppermute | solution.py:556
  24.7 1.9 %collective-permute-start.7 = (bf16[1024,128]{1,0:T(8,128)(2,1)S(1)}, bf16[1024,128]{1,0:T(8,128)(2,1)S(1)}, u32[]{:S(2)}, u32[]{:S(2)}) collective-permute-start(bf16[1024,128]{1,0:T(8,128)(2,1)S(1)} %collective-permute-done.1.mine_keys_ref), channel_id=1, source_target_pairs={{0,1},{1,0},{2,3},{3,2},{4,5},{5,4},{6,7},{7,6},{8,9},{9,8},{10,11... | collective-permute-start | bytes 786440 | tf_op jit(solution)/shard_map/ppermute | solution.py:553
  29.4 2.1 %collective-permute-start.9 = (bf16[2,128,1024]{2,1,0:T(8,128)(2,1)S(1)}, bf16[2,128,1024]{2,1,0:T(8,128)(2,1)S(1)}, u32[]{:S(2)}, u32[]{:S(2)}) collective-permute-start(bf16[2,128,1024]{2,1,0:T(8,128)(2,1)S(1)} %get-tuple-element.103), channel_id=1, source_target_pairs={{0,1},{1,0},{2,3},{3,2},{4,5},{5,4},{6,7},{7,6},{8,9},{9,8},{10,11... | collective-permute-start | bytes 1572872 | tf_op jit(solution)/shard_map/ppermute | solution.py:634
  32.0 8.7 %collective-permute-start.14 = (bf16[128,1024]{1,0:T(8,128)(2,1)S(1)}, bf16[128,1024]{1,0:T(8,128)(2,1)S(1)}, u32[]{:S(2)}, u32[]{:S(2)}) collective-permute-start(bf16[128,1024]{1,0:T(8,128)(2,1)S(1)} %project_onward.2), channel_id=1, source_target_pairs={{0,2},{1,3},{2,0},{3,1},{4,6},{5,7},{6,4},{7,5},{8,10},{9,11},{10,... | collective-permute-start | bytes 786440 | tf_op jit(solution)/shard_map/ppermute | solution.py:612
  38.3 1.4 %collective-permute-start.10 = (bf16[2,32,1024]{2,1,0:T(8,128)(2,1)S(1)}, bf16[2,32,1024]{2,1,0:T(8,128)(2,1)S(1)}, u32[]{:S(2)}, u32[]{:S(2)}) collective-permute-start(bf16[2,32,1024]{2,1,0:T(8,128)(2,1)S(1)} %get-tuple-element.110), channel_id=1, source_target_pairs={{0,1},{1,0},{2,3},{3,2},{4,5},{5,4},{6,7},{7,6},{8,9},{9,8},{10,11... | collective-permute-start | bytes 393224 | tf_op jit(solution)/shard_map/ppermute | solution.py:634
  38.4 1.5 %collective-permute-start.11 = (bf16[2,32,1024]{2,1,0:T(8,128)(2,1)S(1)}, bf16[2,32,1024]{2,1,0:T(8,128)(2,1)S(1)}, u32[]{:S(2)}, u32[]{:S(2)}) collective-permute-start(bf16[2,32,1024]{2,1,0:T(8,128)(2,1)S(1)} %get-tuple-element.111), channel_id=1, source_target_pairs={{0,1},{1,0},{2,3},{3,2},{4,5},{5,4},{6,7},{7,6},{8,9},{9,8},{10,11... | collective-permute-start | bytes 393224 | tf_op jit(solution)/shard_map/ppermute | solution.py:634
  38.8 1.3 %collective-permute-start.12 = (bf16[2,32,1024]{2,1,0:T(8,128)(2,1)S(1)}, bf16[2,32,1024]{2,1,0:T(8,128)(2,1)S(1)}, u32[]{:S(2)}, u32[]{:S(2)}) collective-permute-start(bf16[2,32,1024]{2,1,0:T(8,128)(2,1)S(1)} %get-tuple-element.112), channel_id=1, source_target_pairs={{0,1},{1,0},{2,3},{3,2},{4,5},{5,4},{6,7},{7,6},{8,9},{9,8},{10,11... | collective-permute-start | bytes 393224 | tf_op jit(solution)/shard_map/ppermute | solution.py:634
  38.9 1.5 %collective-permute-start.13 = (bf16[2,32,1024]{2,1,0:T(8,128)(2,1)S(1)}, bf16[2,32,1024]{2,1,0:T(8,128)(2,1)S(1)}, u32[]{:S(2)}, u32[]{:S(2)}) collective-permute-start(bf16[2,32,1024]{2,1,0:T(8,128)(2,1)S(1)} %get-tuple-element.113), channel_id=1, source_target_pairs={{0,1},{1,0},{2,3},{3,2},{4,5},{5,4},{6,7},{7,6},{8,9},{9,8},{10,11... | collective-permute-start | bytes 393224 | tf_op jit(solution)/shard_map/ppermute | solution.py:634
  41.1 8.3 %collective-permute-start.15 = (bf16[128,1024]{1,0:T(8,128)(2,1)S(1)}, bf16[128,1024]{1,0:T(8,128)(2,1)S(1)}, u32[]{:S(2)}, u32[]{:S(2)}) collective-permute-start(bf16[128,1024]{1,0:T(8,128)(2,1)S(1)} %project_onward.3), channel_id=1, source_target_pairs={{0,2},{1,3},{2,0},{3,1},{4,6},{5,7},{6,4},{7,5},{8,10},{9,11},{10,... | collective-permute-start | bytes 786440 | tf_op jit(solution)/shard_map/ppermute | solution.py:612
  43.9 7.8 %copy-start = (bf16[1024]{0:T(1024)(128)(2,1)S(1)}, bf16[1024]{0:T(1024)(128)(2,1)}, u32[]{:S(2)}) copy-start(bf16[1024]{0:T(1024)(128)(2,1)} %param.19) | copy-start | bytes 6148
  49.6 1.2 %collective-permute-start.16 = (f32[16,128]{1,0:T(8,128)S(1)}, f32[16,128]{1,0:T(8,128)S(1)}, u32[]{:S(2)}, u32[]{:S(2)}) collective-permute-start(f32[16,128]{1,0:T(8,128)S(1)} %constant_dynamic-update-slice_fusion), channel_id=1, source_target_pairs={{0,1},{1,0},{2,3},{3,2},{4,5},{5,4},{6,7},{7,6},{8,9},{9,8},{10,11... | collective-permute-start | bytes 24584 | tf_op jit(solution)/shard_map/ppermute | solution.py:661
  50.8 3.7 %collective-permute-start.17 = (f32[16,128]{1,0:T(8,128)S(1)}, f32[16,128]{1,0:T(8,128)S(1)}, u32[]{:S(2)}, u32[]{:S(2)}) collective-permute-start(f32[16,128]{1,0:T(8,128)S(1)} %add.3.refs_2_), channel_id=1, source_target_pairs={{0,2},{1,3},{2,0},{3,1},{4,6},{5,7},{6,4},{7,5},{8,10},{9,11},{10,... | collective-permute-start | bytes 24584 | tf_op jit(solution)/shard_map/ppermute | solution.py:663

commit v13 on v12

--- a/solution.py
+++ b/solution.py
@@ -290,7 +290,9 @@
 def finish_and_give(acc_ref, stat_ref, weight_ref, attended_ref, give_refs):
     for head in range(attended_ref.shape[1] // HD):
         _, total, acc = load_state(acc_ref, stat_ref, head)
-        attended_ref[:, head * HD : (head + 1) * HD] = (acc / total).T.astype(jnp.bfloat16)
+        attended_ref[:, head * HD : (head + 1) * HD] = (acc * (1.0 / total)).T.astype(
+            jnp.bfloat16
+        )
     rows = give_refs[0].shape[1]
     for k in range(weight_ref.shape[0]):
         made = jnp.dot(
@@ -353,16 +355,13 @@
     return jnp.concatenate([ref[k] for ref in got_refs], axis=0).astype(jnp.float32)
 
 
-def onward_kernel(pieces, cuts, attended_ref, weight_ref, *refs):
+def onward_kernel(pieces, attended_ref, weight_ref, *refs):
     got_refs, onward_refs = refs[:pieces], refs[pieces:]
-    for k in range(1, weight_ref.shape[0]):
-        made = (
+    for k, onward_ref in enumerate(onward_refs, 1):
+        onward_ref[...] = (
             jnp.dot(attended_ref[...], weight_ref[k], preferred_element_type=jnp.float32)
             + from_sibling(got_refs, k)
         ).astype(jnp.bfloat16)
-        for start, end in zip(cuts, cuts[1:]):
-            onward_refs[0][...] = made[start:end]
-            onward_refs = onward_refs[1:]
 
 
 def near_kernel(cont, pieces, attended_ref, weight_ref, residual_ref, *refs):
@@ -380,12 +379,11 @@
     near_ref[...] += own_ref[...].astype(jnp.float32)
 
 
-def sum_kernel(pieces, near_ref, *refs):
+def sum_kernel(near_ref, *refs):
     far_refs, (total_ref, squares_ref) = refs[:-2], refs[-2:]
     total = near_ref[...]
-    for k in range(0, len(far_refs), pieces):
-        parts = [ref[...] for ref in far_refs[k : k + pieces]]
-        total = total + jnp.concatenate(parts, axis=0).astype(jnp.float32)
+    for far_ref in far_refs:
+        total = total + far_ref[...].astype(jnp.float32)
     total_ref[...] = total
     sums = jnp.sum(total * total, axis=1, keepdims=True)
     squares_ref[...] = jnp.broadcast_to(sums, (sums.shape[0], HD)).T[:8]
@@ -592,13 +590,12 @@
         )
         return made[0], made[1 : 1 + pieces], made[1 + pieces :]
 
-    def onward(cuts, attended, got):
-        cut_rows = [end - start for start, end in zip(cuts, cuts[1:])]
+    def onward(attended, got):
         parts = pl.pallas_call(
-            functools.partial(onward_kernel, len(got), cuts),
-            out_shape=tuple(array((n, share), jnp.bfloat16) for n in cut_rows * (chips - 1)),
+            functools.partial(onward_kernel, len(got)),
+            out_shape=(array((length, share), jnp.bfloat16),) * (chips - 1),
             in_specs=[vmem] * (2 + len(got)),
-            out_specs=(vmem,) * (len(cut_rows) * (chips - 1)),
+            out_specs=(vmem,) * (chips - 1),
             compiler_params=params,
             cost_estimate=cost(),
             name="project_onward",
@@ -608,8 +605,7 @@
             to_chip = [
                 (t, (t // CORES + k) % chips * CORES + t % CORES) for t in range(members)
             ]
-            for part in parts[(k - 1) * len(cut_rows) : k * len(cut_rows)]:
-                far.append(lax.ppermute(part, "tp", to_chip))
+            far.append(lax.ppermute(parts[k - 1], "tp", to_chip))
         return parts, far
 
     def near(cont, attended, got):
@@ -623,31 +619,30 @@
                 pltpu.SemaphoreType.DMA((1,)),
             ],
             compiler_params=params,
-            cost_estimate=cost(),
+            cost_estimate=cost(2**35 if cont > 0 else 1024),
             name="project_near",
         )(attended, keep_weight, in_hbm(residual), *got)
 
     swap_pieces = [1] + [4] * (conts - 1)
     attended, give, (keep_weight,) = attend_last(0, states[0])
-    nears, fars, cuts = [], [], []
+    nears, fars = [], []
     for cont in range(conts):
         got = [lax.ppermute(x, "tp", sibling) for x in give]
+        if cont + 1 < conts:
+            got, state = lax.optimization_barrier((got, states[cont + 1]))
+        parts, far = onward(attended, got)
         if cont > 0:
-            first = fars[-1][:: len(cuts[-1]) - 1]
-            got, first = lax.optimization_barrier((got, first))
-            fars[-1][:: len(cuts[-1]) - 1] = first
-        cuts.append((0, length))
-        parts, far = onward(cuts[-1], attended, got)
+            attended, fars[-1] = lax.optimization_barrier((attended, fars[-1]))
         nears.append(near(cont, attended, got))
         fars.append(far)
         if cont + 1 < conts:
-            state, parts = lax.optimization_barrier((states[cont + 1], parts))
+            state, parts = lax.optimization_barrier((state, parts))
             attended, give, _ = attend_last(cont + 1, state)
 
     totals, squares = [], []
     for cont in range(conts):
         total, square = pl.pallas_call(
-            functools.partial(sum_kernel, len(cuts[cont]) - 1),
+            sum_kernel,
             out_shape=(array((length, share), jnp.float32), array((8, length), jnp.float32)),
             in_specs=[vmem] * (1 + len(fars[cont])),
             out_specs=(vmem,) * 2,

time: 55.9 us -> 54.4 us (0.973)
  starting transfers between devices: 14.4 us -> 13.3 us
    ppermute x5, waiting for transfers between devices: 2.56 us -> 0.01 us  [shards(): got = [lax.ppermute(x, 'tp', sibling) for x in give]]
    ppermute x2, waiting for transfers between devices: 4.39 us -> 6.29 us  [onward(): far.append(lax.ppermute(parts[k - 1], 'tp', to_chip))]
    ppermute x2, starting transfers between devices: 2.96 us -> 2.15 us  [onward(): far.append(lax.ppermute(parts[k - 1], 'tp', to_chip))]
  transfers between devices with their start and end apart: 18 -> 18, of which waited for: 10 -> 5; matrix products, arithmetic and copies ran while one was open for 3% -> 3% of each run, Pallas kernels for 34% -> 36%
where the time goes in v13:
time: 54.4 us; the launch traced here: 54.1 us
  Pallas kernels  24.8 us (46%)
  waiting for transfers between devices  13.4 us (25%)
  starting transfers between devices  13.3 us (24%)
  local copies, waits for them, and re-layouts  1.76 us (3%)
  between operations  0.88 us (2%)
    pallas_call x3, Pallas kernels, attend_step(): pl.pallas_call(functools.partial(middle_kernel, step, part, sources, cont...  6.92 us
    ppermute x2, waiting for transfers between devices, onward(): far.append(lax.ppermute(parts[k - 1], 'tp', to_chip))  6.29 us
    pallas_call x2, Pallas kernels, attend_last(): pl.pallas_call(functools.partial(last_kernel, steps, sources, conts, cont...  5.72 us
    ppermute x4, starting transfers between devices, shards(): lax.ppermute(x, ('ctx', 'tp'), across(step))  4.51 us
    pallas_call x1, Pallas kernels, shards(): pl.pallas_call(functools.partial(first_kernel, sources, conts), out_shape...  4.44 us
    ppermute x4, waiting for transfers between devices, shards(): lax.ppermute(x, ('ctx', 'tp'), across(step))  3.74 us
    ppermute x3, starting transfers between devices, shards(): lax.ppermute(x, 'tp', sibling)  3.65 us
    pallas_call x2, Pallas kernels, near(): pl.pallas_call(functools.partial(near_kernel, cont, len(got)), out_shape=...  2.51 us
  transfers between devices with their start and end apart: 18, of which 5 were waited for; matrix products, arithmetic and copies ran while one was open for 3% of the time, Pallas kernels for 36%

profile of v13, /device:TPU:0, one launch (start us, length us, event | category | flops | bytes accessed | tf_op | source)
XLA Modules:
  0.0 54.1 jit_solution(10372997626990904269)
XLA Ops:
  0.6 1.0 %pack_keys.1.keys_ref = bf16[1024,128]{1,0:T(8,128)(2,1)S(1)} custom-call(bf16[1024,256]{1,0:T(8,128)(2,1)} %keys_ref.1), custom_call_target="tpu_custom_call" | custom-call | flops 1024 | bytes 1024 | tf_op jit(solution)/shard_map/pack_keys/pallas_call | solution.py:446
  1.6 3.1 %collective-permute-start = (bf16[1024,128]{1,0:T(8,128)(2,1)S(1)}, bf16[1024,128]{1,0:T(8,128)(2,1)S(1)}, u32[]{:S(2)}, u32[]{:S(2)}) collective-permute-start(bf16[1024,128]{1,0:T(8,128)(2,1)S(1)} %pack_keys.1.keys_ref), channel_id=1, source_target_pairs={{0,4},{1,9},{2,6},{3,11},{4,0},{5,13},{6,2},{7,15},{8,12},{9,1},{1... | collective-permute-start | bytes 786440 | tf_op jit(solution)/shard_map/ppermute | solution.py:549
  4.7 1.1 %pack_values.1.values_ref = bf16[1024,128]{1,0:T(8,128)(2,1)S(1)} custom-call(bf16[1024,256]{1,0:T(8,128)(2,1)} %values_ref.1), custom_call_target="tpu_custom_call" | custom-call | flops 1024 | bytes 1024 | tf_op jit(solution)/shard_map/pack_values/pallas_call | solution.py:456
  5.9 0.9 %reshape.13.lists_ref = s32[512]{0:T(512)S(1)} reshape(s32[8,2,4,8]{3,2,1,0:T(4,128)} %param.15) | data formatting | bytes 4096 | tf_op jit(solution)/shard_map/reshape | solution.py:489
  6.7 0.8 %copy.13 = s32[8,2,4]{2,1,0:T(2,128)S(1)} copy(s32[8,2,4]{0,2,1:T(4,128)} %param.16) | data formatting | bytes 512 | tf_op args[6]
  7.6 4.4 %attend_own.1 = (f32[8,128,128]{2,1,0:T(8,128)S(1)}, f32[8,8,128]{2,1,0:T(8,128)S(1)}, f32[8,128,128]{2,1,0:T(8,128)S(1)}, f32[8,8,128]{2,1,0:T(8,128)S(1)}, bf1...) custom-call(s32[512]{0:T(512)S(1)} %reshape.13.lists_ref, s32[64]{0:T(128)S(1)} %reshape.14.counts_ref, ...), custom_call_target="tpu_custom_call" | custom-call | flops 1024 | bytes 1024 | tf_op jit(solution)/shard_map/attend_own/pallas_call | solution.py:498
  13.4 3.7 %collective-permute-done.2.refs_3_ = bf16[1024,128]{1,0:T(8,128)(2,1)S(1)} collective-permute-done((bf16[1024,128]{1,0:T(8,128)(2,1)S(1)}, bf16[1024,128]{1,0:T(8,128)(2,1)S(1)}, u32[]{:S(2)}, u32[]{:S(2)}) %collective-permute-start.2) | collective-permute-done | bytes 262176 | tf_op jit(solution)/shard_map/ppermute | solution.py:549
  17.1 0.7 %collective-permute-start.6 = (bf16[1024,128]{1,0:T(8,128)(2,1)S(1)}, bf16[1024,128]{1,0:T(8,128)(2,1)S(1)}, u32[]{:S(2)}, u32[]{:S(2)}) collective-permute-start(bf16[1024,128]{1,0:T(8,128)(2,1)S(1)} %collective-permute-done.2.refs_3_), channel_id=1, source_target_pairs={{1,5},{3,7},{5,1},{7,3},{9,13},{11,15},{13,9},{15,11},{17,21},{19,... | collective-permute-start | bytes 786440 | tf_op jit(solution)/shard_map/ppermute | solution.py:549
  17.8 2.4 %collective-permute-start.5 = (bf16[512,128]{1,0:T(8,128)(2,1)S(1)}, bf16[512,128]{1,0:T(8,128)(2,1)S(1)}, u32[]{:S(2)}, u32[]{:S(2)}) collective-permute-start(bf16[512,128]{1,0:T(8,128)(2,1)S(1)} %get-tuple-element.124), channel_id=1, source_target_pairs={{0,1},{1,0},{2,3},{3,2},{4,5},{5,4},{6,7},{7,6},{8,9},{9,8},{10,11... | collective-permute-start | bytes 393224 | tf_op jit(solution)/shard_map/ppermute | solution.py:554
  20.2 3.2 %attend_step.3 = (f32[8,128,128]{2,1,0:T(8,128)S(1)}, f32[8,8,128]{2,1,0:T(8,128)S(1)}, f32[8,128,128]{2,1,0:T(8,128)S(1)}, f32[8,8,128]{2,1,0:T(8,128)S(1)}, bf16[2,1024,1024]{2,1,0:T(8,128)(2,1)S(1)}) custom-call(s32[512]{0:T(512)S(1)} %reshape.13.lists_ref, s32[64]{0:T(128)S(1)} %reshape.14.counts_ref, ...), custom_call_target="tpu_custom_call" | custom-call | flops 1024 | bytes 1024 | tf_op jit(solution)/shard_map/attend_step/pallas_call | solution.py:521
  23.5 1.2 %collective-permute-start.8 = (bf16[1024,128]{1,0:T(8,128)(2,1)S(1)}, bf16[1024,128]{1,0:T(8,128)(2,1)S(1)}, u32[]{:S(2)}, u32[]{:S(2)}) collective-permute-start(bf16[1024,128]{1,0:T(8,128)(2,1)S(1)} %collective-permute-done.6.mine_values_ref), channel_id=1, source_target_pairs={{0,1},{1,0},{2,3},{3,2},{4,5},{5,4},{6,7},{7,6},{8,9},{9,8},{10,11... | collective-permute-start | bytes 786440 | tf_op jit(solution)/shard_map/ppermute | solution.py:554
  24.7 1.9 %attend_step.4 = (f32[8,128,128]{2,1,0:T(8,128)S(1)}, f32[8,8,128]{2,1,0:T(8,128)S(1)}) custom-call(s32[512]{0:T(512)S(1)} %reshape.13.lists_ref, s32[64]{0:T(128)S(1)} %reshape.14.counts_ref, bf16[8,128,128]{2,1,0:T(8,128)(2,1)S(1)} %get-tuple-element.63.refs_0_.q_ref, bf16[1024,128]{1,0:T(8,128)(2,1)S(1)} %collective-permute-done.3.refs_1_, ...), custom_call_target="tpu_custom_call" | custom-call | flops 1024 | bytes 1024 | tf_op jit(solution)/shard_map/attend_step/pallas_call | solution.py:521
  26.6 2.8 %attend_last.2 = (bf16[128,1024]{1,0:T(8,128)(2,1)S(1)}, bf16[2,128,1024]{2,1,0:T(8,128)(2,1)S(1)}, bf16[2,1024,1024]{2,1,0:T(8,128)(2,1)S(1)}) custom-call(s32[512]{0:T(512)S(1)} %reshape.13.lists_ref, s32[64]{0:T(128)S(1)} %reshape.14.counts_ref, bf16[8,128,128]{2,1,0:T(8,128)(2,1)S(1)} %get-tuple-element.63.refs_0_.q_ref, ...), custom_call_target="tpu_custom_call" | custom-call | flops 1024 | bytes 1024 | tf_op jit(solution)/shard_map/attend_last/pallas_call | solution.py:568
  30.0 1.9 %attend_step.5 = (f32[8,128,128]{2,1,0:T(8,128)S(1)}, f32[8,8,128]{2,1,0:T(8,128)S(1)}) custom-call(s32[512]{0:T(512)S(1)} %reshape.13.lists_ref, s32[64]{0:T(128)S(1)} %reshape.14.counts_ref, bf16[8,128,128]{2,1,0:T(8,128)(2,1)S(1)} %get-tuple-element.69.refs_1_.refs_0_.q_ref, bf16[1024,128]{1,0:T(8,128)(2,1)S(1)} %collective-permute-done.3.refs_1_, ...), custom_call_target="tpu_custom_call" | custom-call | flops 1024 | bytes 1024 | tf_op jit(solution)/shard_map/attend_step/pallas_call | solution.py:521
  32.4 1.5 %collective-permute-start.10 = (bf16[128,1024]{1,0:T(8,128)(2,1)S(1)}, bf16[128,1024]{1,0:T(8,128)(2,1)S(1)}, u32[]{:S(2)}, u32[]{:S(2)}) collective-permute-start(bf16[128,1024]{1,0:T(8,128)(2,1)S(1)} %project_onward.2), channel_id=1, source_target_pairs={{0,2},{1,3},{2,0},{3,1},{4,6},{5,7},{6,4},{7,5},{8,10},{9,11},{10,... | collective-permute-start | bytes 786440 | tf_op jit(solution)/shard_map/ppermute | solution.py:608
  33.8 2.9 %attend_last.3 = (bf16[128,1024]{1,0:T(8,128)(2,1)S(1)}, bf16[2,32,1024]{2,1,0:T(8,128)(2,1)S(1)}, bf16[2,32,1024]{2,1,0:T(8,128)(2,1)S(1)}, bf16[2,32,1024]{2,1,0:T(8,128)(2,1)S(1)}, bf16[2,32,1024]{2,1,0:T(8,128)(2,1)S(1)}) custom-call(s32[512]{0:T(512)S(1)} %reshape.13.lists_ref, s32[64]{0:T(128)S(1)} %reshape.14.counts_ref, ...), custom_call_target="tpu_custom_call" | custom-call | flops 1024 | bytes 1024 | tf_op jit(solution)/shard_map/attend_last/pallas_call | solution.py:568
  37.8 1.3 %project_near.2.near_ref = f32[128,1024]{1,0:T(8,128)S(1)} custom-call(bf16[128,1024]{1,0:T(8,128)(2,1)S(1)} %get-tuple-element.101.attended_ref, bf16[2,1024,1024]{2,1,0:T(8,128)(2,1)S(1)} %get-tuple-element.102.weight_ref, bf16[2,128,4096]{2,1,0:T(8,128)(2,1)} %residual_ref.3, bf16[2,128,1024]{2,1,0:T(8,128)(2,1)S(1)} %collective-permute-done.9.refs_0_), custom_call_target="tpu_custom_call" | custom-call | flops 1024 | bytes 1024 | tf_op jit(solution)/shard_map/project_near/pallas_call | solution.py:612
  39.6 0.7 %collective-permute-start.15 = (bf16[128,1024]{1,0:T(8,128)(2,1)S(1)}, bf16[128,1024]{1,0:T(8,128)(2,1)S(1)}, u32[]{:S(2)}, u32[]{:S(2)}) collective-permute-start(bf16[128,1024]{1,0:T(8,128)(2,1)S(1)} %project_onward.3), channel_id=1, source_target_pairs={{0,2},{1,3},{2,0},{3,1},{4,6},{5,7},{6,4},{7,5},{8,10},{9,11},{10,... | collective-permute-start | bytes 786440 | tf_op jit(solution)/shard_map/ppermute | solution.py:608
  40.7 1.2 %project_near.3.near_ref = f32[128,1024]{1,0:T(8,128)S(1)} custom-call(bf16[128,1024]{1,0:T(8,128)(2,1)S(1)} %get-tuple-element.116.attended_ref, bf16[2,1024,1024]{2,1,0:T(8,128)(2,1)S(1)} %get-tuple-element.102.weight_ref, bf16[2,128,4096]{2,1,0:T(8,128)(2,1)} %residual_ref.3, bf16[2,32,1024]{2,1,0:T(8,128)(2,1)S(1)} %collective-permute-done.11.refs_0_, ...), custom_call_target="tpu_custom_call" | custom-call | flops 34359738368 | bytes 1024 | tf_op jit(solution)/shard_map/project_near/pallas_call | solution.py:612
  42.1 5.9 %collective-permute-done.15.refs_0_ = bf16[128,1024]{1,0:T(8,128)(2,1)S(1)} collective-permute-done((bf16[128,1024]{1,0:T(8,128)(2,1)S(1)}, bf16[128,1024]{1,0:T(8,128)(2,1)S(1)}, u32[]{:S(2)}, u32[]{:S(2)}) %collective-permute-start.15) | collective-permute-done | bytes 262176 | tf_op jit(solution)/shard_map/ppermute | solution.py:608
  48.2 1.2 %collective-permute-done.16 = f32[16,128]{1,0:T(8,128)S(1)} collective-permute-done((f32[16,128]{1,0:T(8,128)S(1)}, f32[16,128]{1,0:T(8,128)S(1)}, u32[]{:S(2)}, u32[]{:S(2)}) %collective-permute-start.16) | collective-permute-done | bytes 8224 | tf_op jit(solution)/shard_map/ppermute | solution.py:656
  50.0 0.8 %stream.1 = bf16[2,128,1024]{2,1,0:T(8,128)(2,1)} custom-call(f32[128,1024]{1,0:T(8,128)S(1)} %get-tuple-element.115.refs_0_, f32[128,1024]{1,0:T(8,128)S(1)} %get-tuple-element.121.refs_1_), custom_call_target="tpu_custom_call" | custom-call | flops 1024 | bytes 1024 | tf_op jit(solution)/shard_map/stream/pallas_call | solution.py:666
  50.9 2.2 %collective-permute-done.17.refs_3_ = f32[16,128]{1,0:T(8,128)S(1)} collective-permute-done((f32[16,128]{1,0:T(8,128)S(1)}, f32[16,128]{1,0:T(8,128)S(1)}, u32[]{:S(2)}, u32[]{:S(2)}) %collective-permute-start.17) | collective-permute-done | bytes 8224 | tf_op jit(solution)/shard_map/ppermute | solution.py:658
  53.0 1.0 %norm.1 = bf16[2,128,1024]{2,1,0:T(8,128)(2,1)} custom-call(f32[128,1024]{1,0:T(8,128)S(1)} %get-tuple-element.115.refs_0_, f32[128,1024]{1,0:T(8,128)S(1)} %get-tuple-element.121.refs_1_, f32[16,128]{1,0:T(8,128)S(1)} %add.3.refs_2_, f32[16,128]{1,0:T(8,128)S(1)} %collective-permute-done.17.refs_3_, bf16[1,1024]{1,0:T(2,128)(2,1)S(1)} %reshape.15.refs_4_), custom_call_target="tpu_custom_call" | custom-call | flops 1024 | bytes 1024 | tf_op jit(solution)/shard_map/norm/pallas_call | solution.py:675
  (38 shorter events, 5.6 us)
Async XLA Ops:
  1.6 10.4 %collective-permute-start = (bf16[1024,128]{1,0:T(8,128)(2,1)S(1)}, bf16[1024,128]{1,0:T(8,128)(2,1)S(1)}, u32[]{:S(2)}, u32[]{:S(2)}) collective-permute-start(bf16[1024,128]{1,0:T(8,128)(2,1)S(1)} %pack_keys.1.keys_ref), channel_id=1, source_target_pairs={{0,4},{1,9},{2,6},{3,11},{4,0},{5,13},{6,2},{7,15},{8,12},{9,1},{1... | collective-permute-start | bytes 786440 | tf_op jit(solution)/shard_map/ppermute | solution.py:549
  5.8 11.3 %collective-permute-start.2 = (bf16[1024,128]{1,0:T(8,128)(2,1)S(1)}, bf16[1024,128]{1,0:T(8,128)(2,1)S(1)}, u32[]{:S(2)}, u32[]{:S(2)}) collective-permute-start(bf16[1024,128]{1,0:T(8,128)(2,1)S(1)} %pack_values.1.values_ref), channel_id=1, source_target_pairs={{0,4},{1,9},{2,6},{3,11},{4,0},{5,13},{6,2},{7,15},{8,12},{9,1},{1... | collective-permute-start | bytes 786440 | tf_op jit(solution)/shard_map/ppermute | solution.py:549
  12.1 11.4 %collective-permute-start.3 = (bf16[1024,128]{1,0:T(8,128)(2,1)S(1)}, bf16[1024,128]{1,0:T(8,128)(2,1)S(1)}, u32[]{:S(2)}, u32[]{:S(2)}) collective-permute-start(bf16[1024,128]{1,0:T(8,128)(2,1)S(1)} %collective-permute-done.refs_2_), channel_id=1, source_target_pairs={{0,1},{1,0},{2,3},{3,2},{4,5},{5,4},{6,7},{7,6},{8,9},{9,8},{10,11... | collective-permute-start | bytes 786440 | tf_op jit(solution)/shard_map/ppermute | solution.py:551
  12.7 10.8 %collective-permute-start.1 = (bf16[1024,128]{1,0:T(8,128)(2,1)S(1)}, bf16[1024,128]{1,0:T(8,128)(2,1)S(1)}, u32[]{:S(2)}, u32[]{:S(2)}) collective-permute-start(bf16[1024,128]{1,0:T(8,128)(2,1)S(1)} %collective-permute-done.refs_2_), channel_id=1, source_target_pairs={{1,5},{3,7},{5,1},{7,3},{9,13},{11,15},{13,9},{15,11},{17,21},{19,... | collective-permute-start | bytes 786440 | tf_op jit(solution)/shard_map/ppermute | solution.py:549
  17.1 6.4 %collective-permute-start.6 = (bf16[1024,128]{1,0:T(8,128)(2,1)S(1)}, bf16[1024,128]{1,0:T(8,128)(2,1)S(1)}, u32[]{:S(2)}, u32[]{:S(2)}) collective-permute-start(bf16[1024,128]{1,0:T(8,128)(2,1)S(1)} %collective-permute-done.2.refs_3_), channel_id=1, source_target_pairs={{1,5},{3,7},{5,1},{7,3},{9,13},{11,15},{13,9},{15,11},{17,21},{19,... | collective-permute-start | bytes 786440 | tf_op jit(solution)/shard_map/ppermute | solution.py:549
  17.8 5.7 %collective-permute-start.5 = (bf16[512,128]{1,0:T(8,128)(2,1)S(1)}, bf16[512,128]{1,0:T(8,128)(2,1)S(1)}, u32[]{:S(2)}, u32[]{:S(2)}) collective-permute-start(bf16[512,128]{1,0:T(8,128)(2,1)S(1)} %get-tuple-element.124), channel_id=1, source_target_pairs={{0,1},{1,0},{2,3},{3,2},{4,5},{5,4},{6,7},{7,6},{8,9},{9,8},{10,11... | collective-permute-start | bytes 393224 | tf_op jit(solution)/shard_map/ppermute | solution.py:554
  20.2 3.3 %collective-permute-start.4 = (bf16[512,128]{1,0:T(8,128)(2,1)S(1)}, bf16[512,128]{1,0:T(8,128)(2,1)S(1)}, u32[]{:S(2)}, u32[]{:S(2)}) collective-permute-start(bf16[512,128]{1,0:T(8,128)(2,1)S(1)} %get-tuple-element.125), channel_id=1, source_target_pairs={{0,1},{1,0},{2,3},{3,2},{4,5},{5,4},{6,7},{7,6},{8,9},{9,8},{10,11... | collective-permute-start | bytes 393224 | tf_op jit(solution)/shard_map/ppermute | solution.py:554
  23.5 3.1 %collective-permute-start.8 = (bf16[1024,128]{1,0:T(8,128)(2,1)S(1)}, bf16[1024,128]{1,0:T(8,128)(2,1)S(1)}, u32[]{:S(2)}, u32[]{:S(2)}) collective-permute-start(bf16[1024,128]{1,0:T(8,128)(2,1)S(1)} %collective-permute-done.6.mine_values_ref), channel_id=1, source_target_pairs={{0,1},{1,0},{2,3},{3,2},{4,5},{5,4},{6,7},{7,6},{8,9},{9,8},{10,11... | collective-permute-start | bytes 786440 | tf_op jit(solution)/shard_map/ppermute | solution.py:554
  24.7 1.9 %collective-permute-start.7 = (bf16[1024,128]{1,0:T(8,128)(2,1)S(1)}, bf16[1024,128]{1,0:T(8,128)(2,1)S(1)}, u32[]{:S(2)}, u32[]{:S(2)}) collective-permute-start(bf16[1024,128]{1,0:T(8,128)(2,1)S(1)} %collective-permute-done.1.mine_keys_ref), channel_id=1, source_target_pairs={{0,1},{1,0},{2,3},{3,2},{4,5},{5,4},{6,7},{7,6},{8,9},{9,8},{10,11... | collective-permute-start | bytes 786440 | tf_op jit(solution)/shard_map/ppermute | solution.py:551
  29.4 2.4 %collective-permute-start.9 = (bf16[2,128,1024]{2,1,0:T(8,128)(2,1)S(1)}, bf16[2,128,1024]{2,1,0:T(8,128)(2,1)S(1)}, u32[]{:S(2)}, u32[]{:S(2)}) collective-permute-start(bf16[2,128,1024]{2,1,0:T(8,128)(2,1)S(1)} %get-tuple-element.103), channel_id=1, source_target_pairs={{0,1},{1,0},{2,3},{3,2},{4,5},{5,4},{6,7},{7,6},{8,9},{9,8},{10,11... | collective-permute-start | bytes 1572872 | tf_op jit(solution)/shard_map/ppermute | solution.py:630
  32.4 8.3 %collective-permute-start.10 = (bf16[128,1024]{1,0:T(8,128)(2,1)S(1)}, bf16[128,1024]{1,0:T(8,128)(2,1)S(1)}, u32[]{:S(2)}, u32[]{:S(2)}) collective-permute-start(bf16[128,1024]{1,0:T(8,128)(2,1)S(1)} %project_onward.2), channel_id=1, source_target_pairs={{0,2},{1,3},{2,0},{3,1},{4,6},{5,7},{6,4},{7,5},{8,10},{9,11},{10,... | collective-permute-start | bytes 786440 | tf_op jit(solution)/shard_map/ppermute | solution.py:608
  36.7 2.4 %collective-permute-start.11 = (bf16[2,32,1024]{2,1,0:T(8,128)(2,1)S(1)}, bf16[2,32,1024]{2,1,0:T(8,128)(2,1)S(1)}, u32[]{:S(2)}, u32[]{:S(2)}) collective-permute-start(bf16[2,32,1024]{2,1,0:T(8,128)(2,1)S(1)} %get-tuple-element.117), channel_id=1, source_target_pairs={{0,1},{1,0},{2,3},{3,2},{4,5},{5,4},{6,7},{7,6},{8,9},{9,8},{10,11... | collective-permute-start | bytes 393224 | tf_op jit(solution)/shard_map/ppermute | solution.py:630
  36.8 2.3 %collective-permute-start.12 = (bf16[2,32,1024]{2,1,0:T(8,128)(2,1)S(1)}, bf16[2,32,1024]{2,1,0:T(8,128)(2,1)S(1)}, u32[]{:S(2)}, u32[]{:S(2)}) collective-permute-start(bf16[2,32,1024]{2,1,0:T(8,128)(2,1)S(1)} %get-tuple-element.118), channel_id=1, source_target_pairs={{0,1},{1,0},{2,3},{3,2},{4,5},{5,4},{6,7},{7,6},{8,9},{9,8},{10,11... | collective-permute-start | bytes 393224 | tf_op jit(solution)/shard_map/ppermute | solution.py:630
  37.3 1.9 %collective-permute-start.13 = (bf16[2,32,1024]{2,1,0:T(8,128)(2,1)S(1)}, bf16[2,32,1024]{2,1,0:T(8,128)(2,1)S(1)}, u32[]{:S(2)}, u32[]{:S(2)}) collective-permute-start(bf16[2,32,1024]{2,1,0:T(8,128)(2,1)S(1)} %get-tuple-element.119), channel_id=1, source_target_pairs={{0,1},{1,0},{2,3},{3,2},{4,5},{5,4},{6,7},{7,6},{8,9},{9,8},{10,11... | collective-permute-start | bytes 393224 | tf_op jit(solution)/shard_map/ppermute | solution.py:630
  37.4 1.8 %collective-permute-start.14 = (bf16[2,32,1024]{2,1,0:T(8,128)(2,1)S(1)}, bf16[2,32,1024]{2,1,0:T(8,128)(2,1)S(1)}, u32[]{:S(2)}, u32[]{:S(2)}) collective-permute-start(bf16[2,32,1024]{2,1,0:T(8,128)(2,1)S(1)} %get-tuple-element.120), channel_id=1, source_target_pairs={{0,1},{1,0},{2,3},{3,2},{4,5},{5,4},{6,7},{7,6},{8,9},{9,8},{10,11... | collective-permute-start | bytes 393224 | tf_op jit(solution)/shard_map/ppermute | solution.py:630
  39.6 10.4 %copy-start = (bf16[1024]{0:T(1024)(128)(2,1)S(1)}, bf16[1024]{0:T(1024)(128)(2,1)}, u32[]{:S(2)}) copy-start(bf16[1024]{0:T(1024)(128)(2,1)} %param.19) | copy-start | bytes 6148
  39.6 8.4 %collective-permute-start.15 = (bf16[128,1024]{1,0:T(8,128)(2,1)S(1)}, bf16[128,1024]{1,0:T(8,128)(2,1)S(1)}, u32[]{:S(2)}, u32[]{:S(2)}) collective-permute-start(bf16[128,1024]{1,0:T(8,128)(2,1)S(1)} %project_onward.3), channel_id=1, source_target_pairs={{0,2},{1,3},{2,0},{3,1},{4,6},{5,7},{6,4},{7,5},{8,10},{9,11},{10,... | collective-permute-start | bytes 786440 | tf_op jit(solution)/shard_map/ppermute | solution.py:608
  48.2 1.2 %collective-permute-start.16 = (f32[16,128]{1,0:T(8,128)S(1)}, f32[16,128]{1,0:T(8,128)S(1)}, u32[]{:S(2)}, u32[]{:S(2)}) collective-permute-start(f32[16,128]{1,0:T(8,128)S(1)} %constant_dynamic-update-slice_fusion), channel_id=1, source_target_pairs={{0,1},{1,0},{2,3},{3,2},{4,5},{5,4},{6,7},{7,6},{8,9},{9,8},{10,11... | collective-permute-start | bytes 24584 | tf_op jit(solution)/shard_map/ppermute | solution.py:656
  49.4 3.7 %collective-permute-start.17 = (f32[16,128]{1,0:T(8,128)S(1)}, f32[16,128]{1,0:T(8,128)S(1)}, u32[]{:S(2)}, u32[]{:S(2)}) collective-permute-start(f32[16,128]{1,0:T(8,128)S(1)} %add.3.refs_2_), channel_id=1, source_target_pairs={{0,2},{1,3},{2,0},{3,1},{4,6},{5,7},{6,4},{7,5},{8,10},{9,11},{10,... | collective-permute-start | bytes 24584 | tf_op jit(solution)/shard_map/ppermute | solution.py:658

commit v14 on v13

--- a/solution.py
+++ b/solution.py
@@ -294,12 +294,12 @@
             jnp.bfloat16
         )
     rows = give_refs[0].shape[1]
-    for k in range(weight_ref.shape[0]):
+    for k in range(1, weight_ref.shape[0]):
         made = jnp.dot(
             attended_ref[...], weight_ref[k], preferred_element_type=jnp.float32
         ).astype(jnp.bfloat16)
         for i, give_ref in enumerate(give_refs):
-            give_ref[k] = made[i * rows : (i + 1) * rows]
+            give_ref[k - 1] = made[i * rows : (i + 1) * rows]
 
 
 def last_kernel(
@@ -360,23 +360,42 @@
     for k, onward_ref in enumerate(onward_refs, 1):
         onward_ref[...] = (
             jnp.dot(attended_ref[...], weight_ref[k], preferred_element_type=jnp.float32)
-            + from_sibling(got_refs, k)
+            + from_sibling(got_refs, k - 1)
         ).astype(jnp.bfloat16)
 
 
-def near_kernel(cont, pieces, attended_ref, weight_ref, residual_ref, *refs):
-    got_refs, (near_ref, own_ref, sem) = refs[:pieces], refs[pieces:]
-    share = near_ref.shape[1]
+def attended_rows(refs):
+    return jnp.concatenate([ref[...] for ref in refs], axis=0)
+
+
+def give_near_kernel(conts, *refs):
+    attended_refs, weight_ref, give_refs = refs[:conts], refs[conts], refs[conts + 1 :]
+    made = jnp.dot(
+        attended_rows(attended_refs), weight_ref[0], preferred_element_type=jnp.float32
+    ).astype(jnp.bfloat16)
+    rows = give_refs[0].shape[0]
+    for i, give_ref in enumerate(give_refs):
+        give_ref[...] = made[i * rows : (i + 1) * rows]
+
+
+def near_kernel(conts, pieces, *refs):
+    attended_refs, weight_ref, residual_ref = refs[:conts], refs[conts], refs[conts + 1]
+    got_refs, refs = refs[conts + 2 : conts + 2 + pieces], refs[conts + 2 + pieces :]
+    near_refs, (own_ref, sem) = refs[:conts], refs[conts:]
+    length, share = near_refs[0].shape
     start = pl.multiple_of(lax.axis_index("tp") * share, HD)
     copy = pltpu.make_async_copy(
-        residual_ref.at[cont, :, pl.ds(start, share)], own_ref, sem.at[0]
+        residual_ref.at[:, :, pl.ds(start, share)], own_ref, sem.at[0]
     )
     copy.start()
-    near_ref[...] = jnp.dot(
-        attended_ref[...], weight_ref[0], preferred_element_type=jnp.float32
-    ) + from_sibling(got_refs, 0)
+    made = jnp.dot(
+        attended_rows(attended_refs), weight_ref[0], preferred_element_type=jnp.float32
+    ) + attended_rows(got_refs).astype(jnp.float32)
+    for cont, near_ref in enumerate(near_refs):
+        near_ref[...] = made[cont * length : (cont + 1) * length]
     copy.wait()
-    near_ref[...] += own_ref[...].astype(jnp.float32)
+    for cont, near_ref in enumerate(near_refs):
+        near_ref[...] += own_ref[cont].astype(jnp.float32)
 
 
 def sum_kernel(near_ref, *refs):
@@ -568,7 +587,7 @@
         made = pl.pallas_call(
             functools.partial(last_kernel, steps, sources, conts, cont, pieces),
             out_shape=(array((length, width), jnp.bfloat16),)
-            + (array((chips, length // pieces, share), jnp.bfloat16),) * pieces
+            + (array((chips - 1, length // pieces, share), jnp.bfloat16),) * pieces
             + (weight_shape,) * fetch,
             in_specs=[smem, smem] + [vmem] * 8 + [hbm] * fetch,
             out_specs=(vmem,) * (1 + pieces + fetch),
@@ -608,36 +627,48 @@
             far.append(lax.ppermute(parts[k - 1], "tp", to_chip))
         return parts, far
 
-    def near(cont, attended, got):
+    def give_near(attended, pieces):
         return pl.pallas_call(
-            functools.partial(near_kernel, cont, len(got)),
-            out_shape=array((length, share), jnp.float32),
-            in_specs=[vmem] * 2 + [hbm] + [vmem] * len(got),
-            out_specs=vmem,
+            functools.partial(give_near_kernel, conts),
+            out_shape=(array((conts * length // pieces, share), jnp.bfloat16),) * pieces,
+            in_specs=[vmem] * (conts + 1),
+            out_specs=(vmem,) * pieces,
+            compiler_params=params,
+            cost_estimate=cost(2**35),
+            name="give_near",
+        )(*attended, give_weight)
+
+    def near(attended, got):
+        return pl.pallas_call(
+            functools.partial(near_kernel, conts, len(got)),
+            out_shape=(array((length, share), jnp.float32),) * conts,
+            in_specs=[vmem] * (conts + 1) + [hbm] + [vmem] * len(got),
+            out_specs=(vmem,) * conts,
             scratch_shapes=[
-                pltpu.VMEM((length, share), jnp.bfloat16),
+                pltpu.VMEM((conts, length, share), jnp.bfloat16),
                 pltpu.SemaphoreType.DMA((1,)),
             ],
             compiler_params=params,
-            cost_estimate=cost(2**35 if cont > 0 else 1024),
+            cost_estimate=cost(),
             name="project_near",
-        )(attended, keep_weight, in_hbm(residual), *got)
-
-    swap_pieces = [1] + [4] * (conts - 1)
+        )(*attended, keep_weight, in_hbm(residual), *got)
+
+    swap_pieces = [1] + [2] * (conts - 1)
     attended, give, (keep_weight,) = attend_last(0, states[0])
-    nears, fars = [], []
+    all_attended, fars = [], []
     for cont in range(conts):
         got = [lax.ppermute(x, "tp", sibling) for x in give]
         if cont + 1 < conts:
             got, state = lax.optimization_barrier((got, states[cont + 1]))
         parts, far = onward(attended, got)
-        if cont > 0:
-            attended, fars[-1] = lax.optimization_barrier((attended, fars[-1]))
-        nears.append(near(cont, attended, got))
+        all_attended.append(attended)
         fars.append(far)
         if cont + 1 < conts:
             state, parts = lax.optimization_barrier((state, parts))
             attended, give, _ = attend_last(cont + 1, state)
+    all_attended, fars[:-1], _ = lax.optimization_barrier((all_attended, fars[:-1], parts))
+    got = [lax.ppermute(x, "tp", sibling) for x in give_near(all_attended, 2 * conts)]
+    nears = near(all_attended, got)
 
     totals, squares = [], []
     for cont in range(conts):

time: 54.4 us -> 53.6 us (0.985)
  waiting for transfers between devices: 13.4 us -> 9.95 us
  starting transfers between devices: 13.3 us -> 16.4 us
    ppermute x2, waiting for transfers between devices: 6.29 us -> 3.34 us  [onward(): far.append(lax.ppermute(parts[k - 1], 'tp', to_chip))]
    ppermute x4, waiting for transfers between devices: 3.74 us -> 1.17 us  [shards(): lax.ppermute(x, ('ctx', 'tp'), across(step))]
    ppermute x2, starting transfers between devices: 0.64 us -> 3.19 us  [shards(): their_keys = lax.ppermute(mine_keys, 'tp', sibling)]
    ppermute x3 -> x7, starting transfers between devices: 3.65 us -> 4.73 us  [shards(): lax.ppermute(x, 'tp', sibling)]
    ppermute x3 -> x7, waiting for transfers between devices: 0.01 us -> 1.03 us  [shards(): lax.ppermute(x, 'tp', sibling)]
    ppermute x5 -> x3, waiting for transfers between devices: 0.01 us -> 1.03 us  [shards(): got = [lax.ppermute(x, 'tp', sibling) for x in give]]
    ppermute x5 -> x3, starting transfers between devices: 1.65 us -> 1.14 us  [shards(): got = [lax.ppermute(x, 'tp', sibling) for x in give]]
  transfers between devices with their start and end apart: 18 -> 20, of which waited for: 5 -> 11; matrix products, arithmetic and copies ran while one was open for 3% -> 3% of each run, Pallas kernels for 36% -> 35%
where the time goes in v14:
time: 53.6 us; the launch traced here: 53.3 us
  Pallas kernels  24.3 us (45%)
  starting transfers between devices  16.4 us (31%)
  waiting for transfers between devices  9.95 us (19%)
  local copies, waits for them, and re-layouts  1.76 us (3%)
  between operations  0.86 us (2%)
    pallas_call x3, Pallas kernels, attend_step(): pl.pallas_call(functools.partial(middle_kernel, step, part, sources, cont...  6.92 us
    pallas_call x2, Pallas kernels, attend_last(): pl.pallas_call(functools.partial(last_kernel, steps, sources, conts, cont...  5.45 us
    ppermute x7, starting transfers between devices, shards(): lax.ppermute(x, 'tp', sibling)  4.73 us
    ppermute x4, starting transfers between devices, shards(): lax.ppermute(x, ('ctx', 'tp'), across(step))  4.53 us
    pallas_call x1, Pallas kernels, shards(): pl.pallas_call(functools.partial(first_kernel, sources, conts), out_shape...  4.44 us
    ppermute x2, waiting for transfers between devices, onward(): far.append(lax.ppermute(parts[k - 1], 'tp', to_chip))  3.34 us
    ppermute x2, starting transfers between devices, shards(): their_keys = lax.ppermute(mine_keys, 'tp', sibling)  3.19 us
    ppermute x1, waiting for transfers between devices, shards(): lax.ppermute(squares, 'tp', [(t, (t // CORES + k) % chips * CORES + t % C...  2.22 us
  transfers between devices with their start and end apart: 20, of which 11 were waited for; matrix products, arithmetic and copies ran while one was open for 3% of the time, Pallas kernels for 35%

profile of v14, /device:TPU:0, one launch (start us, length us, event | category | flops | bytes accessed | tf_op | source)
XLA Modules:
  0.0 53.3 jit_solution(10604251946153771963)
XLA Ops:
  0.6 1.0 %pack_keys.1.keys_ref = bf16[1024,128]{1,0:T(8,128)(2,1)S(1)} custom-call(bf16[1024,256]{1,0:T(8,128)(2,1)} %keys_ref.1), custom_call_target="tpu_custom_call" | custom-call | flops 1024 | bytes 1024 | tf_op jit(solution)/shard_map/pack_keys/pallas_call | solution.py:465
  1.6 3.1 %collective-permute-start = (bf16[1024,128]{1,0:T(8,128)(2,1)S(1)}, bf16[1024,128]{1,0:T(8,128)(2,1)S(1)}, u32[]{:S(2)}, u32[]{:S(2)}) collective-permute-start(bf16[1024,128]{1,0:T(8,128)(2,1)S(1)} %pack_keys.1.keys_ref), channel_id=1, source_target_pairs={{0,4},{1,9},{2,6},{3,11},{4,0},{5,13},{6,2},{7,15},{8,12},{9,1},{1... | collective-permute-start | bytes 786440 | tf_op jit(solution)/shard_map/ppermute | solution.py:568
  4.7 1.1 %pack_values.1.values_ref = bf16[1024,128]{1,0:T(8,128)(2,1)S(1)} custom-call(bf16[1024,256]{1,0:T(8,128)(2,1)} %values_ref.1), custom_call_target="tpu_custom_call" | custom-call | flops 1024 | bytes 1024 | tf_op jit(solution)/shard_map/pack_values/pallas_call | solution.py:475
  5.9 0.8 %copy.13 = s32[8,2,4]{2,1,0:T(2,128)S(1)} copy(s32[8,2,4]{0,2,1:T(4,128)} %param.16) | data formatting | bytes 512 | tf_op args[6]
  6.7 0.9 %reshape.13.lists_ref = s32[512]{0:T(512)S(1)} reshape(s32[8,2,4,8]{3,2,1,0:T(4,128)} %param.15) | data formatting | bytes 4096 | tf_op jit(solution)/shard_map/reshape | solution.py:508
  7.6 4.4 %attend_own.1 = (f32[8,128,128]{2,1,0:T(8,128)S(1)}, f32[8,8,128]{2,1,0:T(8,128)S(1)}, f32[8,128,128]{2,1,0:T(8,128)S(1)}, f32[8,8,128]{2,1,0:T(8,128)S(1)}, bf1...) custom-call(s32[512]{0:T(512)S(1)} %reshape.13.lists_ref, s32[64]{0:T(128)S(1)} %reshape.14.counts_ref, ...), custom_call_target="tpu_custom_call" | custom-call | flops 1024 | bytes 1024 | tf_op jit(solution)/shard_map/attend_own/pallas_call | solution.py:517
  12.8 3.2 %collective-permute-start.3 = (bf16[1024,128]{1,0:T(8,128)(2,1)S(1)}, bf16[1024,128]{1,0:T(8,128)(2,1)S(1)}, u32[]{:S(2)}, u32[]{:S(2)}) collective-permute-start(bf16[1024,128]{1,0:T(8,128)(2,1)S(1)} %collective-permute-done.refs_2_), channel_id=1, source_target_pairs={{0,1},{1,0},{2,3},{3,2},{4,5},{5,4},{6,7},{7,6},{8,9},{9,8},{10,11... | collective-permute-start | bytes 786440 | tf_op jit(solution)/shard_map/ppermute | solution.py:570
  15.9 1.2 %collective-permute-done.2.refs_3_ = bf16[1024,128]{1,0:T(8,128)(2,1)S(1)} collective-permute-done((bf16[1024,128]{1,0:T(8,128)(2,1)S(1)}, bf16[1024,128]{1,0:T(8,128)(2,1)S(1)}, u32[]{:S(2)}, u32[]{:S(2)}) %collective-permute-start.2) | collective-permute-done | bytes 262176 | tf_op jit(solution)/shard_map/ppermute | solution.py:568
  17.8 2.4 %collective-permute-start.4 = (bf16[512,128]{1,0:T(8,128)(2,1)S(1)}, bf16[512,128]{1,0:T(8,128)(2,1)S(1)}, u32[]{:S(2)}, u32[]{:S(2)}) collective-permute-start(bf16[512,128]{1,0:T(8,128)(2,1)S(1)} %get-tuple-element.135), channel_id=1, source_target_pairs={{0,1},{1,0},{2,3},{3,2},{4,5},{5,4},{6,7},{7,6},{8,9},{9,8},{10,11... | collective-permute-start | bytes 393224 | tf_op jit(solution)/shard_map/ppermute | solution.py:573
  20.2 3.2 %attend_step.3 = (f32[8,128,128]{2,1,0:T(8,128)S(1)}, f32[8,8,128]{2,1,0:T(8,128)S(1)}, f32[8,128,128]{2,1,0:T(8,128)S(1)}, f32[8,8,128]{2,1,0:T(8,128)S(1)}, bf16[2,1024,1024]{2,1,0:T(8,128)(2,1)S(1)}) custom-call(s32[512]{0:T(512)S(1)} %reshape.13.lists_ref, s32[64]{0:T(128)S(1)} %reshape.14.counts_ref, ...), custom_call_target="tpu_custom_call" | custom-call | flops 1024 | bytes 1024 | tf_op jit(solution)/shard_map/attend_step/pallas_call | solution.py:540
  23.5 1.2 %collective-permute-start.8 = (bf16[1024,128]{1,0:T(8,128)(2,1)S(1)}, bf16[1024,128]{1,0:T(8,128)(2,1)S(1)}, u32[]{:S(2)}, u32[]{:S(2)}) collective-permute-start(bf16[1024,128]{1,0:T(8,128)(2,1)S(1)} %collective-permute-done.6.mine_values_ref), channel_id=1, source_target_pairs={{0,1},{1,0},{2,3},{3,2},{4,5},{5,4},{6,7},{7,6},{8,9},{9,8},{10,11... | collective-permute-start | bytes 786440 | tf_op jit(solution)/shard_map/ppermute | solution.py:573
  24.7 1.9 %attend_step.4 = (f32[8,128,128]{2,1,0:T(8,128)S(1)}, f32[8,8,128]{2,1,0:T(8,128)S(1)}) custom-call(s32[512]{0:T(512)S(1)} %reshape.13.lists_ref, s32[64]{0:T(128)S(1)} %reshape.14.counts_ref, bf16[8,128,128]{2,1,0:T(8,128)(2,1)S(1)} %get-tuple-element.68.refs_0_.q_ref, bf16[1024,128]{1,0:T(8,128)(2,1)S(1)} %collective-permute-done.3.refs_1_, ...), custom_call_target="tpu_custom_call" | custom-call | flops 1024 | bytes 1024 | tf_op jit(solution)/shard_map/attend_step/pallas_call | solution.py:540
  26.6 2.8 %attend_last.2 = (bf16[128,1024]{1,0:T(8,128)(2,1)S(1)}, bf16[1,128,1024]{2,1,0:T(8,128)(2,1)S(1)}, bf16[2,1024,1024]{2,1,0:T(8,128)(2,1)S(1)}) custom-call(s32[512]{0:T(512)S(1)} %reshape.13.lists_ref, s32[64]{0:T(128)S(1)} %reshape.14.counts_ref, bf16[8,128,128]{2,1,0:T(8,128)(2,1)S(1)} %get-tuple-element.68.refs_0_.q_ref, ...), custom_call_target="tpu_custom_call" | custom-call | flops 1024 | bytes 1024 | tf_op jit(solution)/shard_map/attend_last/pallas_call | solution.py:587
  30.0 1.9 %attend_step.5 = (f32[8,128,128]{2,1,0:T(8,128)S(1)}, f32[8,8,128]{2,1,0:T(8,128)S(1)}) custom-call(s32[512]{0:T(512)S(1)} %reshape.13.lists_ref, s32[64]{0:T(128)S(1)} %reshape.14.counts_ref, bf16[8,128,128]{2,1,0:T(8,128)(2,1)S(1)} %get-tuple-element.74.refs_1_.refs_0_.q_ref, bf16[1024,128]{1,0:T(8,128)(2,1)S(1)} %collective-permute-done.3.refs_1_, ...), custom_call_target="tpu_custom_call" | custom-call | flops 1024 | bytes 1024 | tf_op jit(solution)/shard_map/attend_step/pallas_call | solution.py:540
  32.4 1.6 %collective-permute-start.10 = (bf16[128,1024]{1,0:T(8,128)(2,1)S(1)}, bf16[128,1024]{1,0:T(8,128)(2,1)S(1)}, u32[]{:S(2)}, u32[]{:S(2)}) collective-permute-start(bf16[128,1024]{1,0:T(8,128)(2,1)S(1)} %project_onward.2), channel_id=1, source_target_pairs={{0,2},{1,3},{2,0},{3,1},{4,6},{5,7},{6,4},{7,5},{8,10},{9,11},{10,... | collective-permute-start | bytes 786440 | tf_op jit(solution)/shard_map/ppermute | solution.py:627
  33.9 2.6 %attend_last.3 = (bf16[128,1024]{1,0:T(8,128)(2,1)S(1)}, bf16[1,64,1024]{2,1,0:T(8,128)(2,1)S(1)}, bf16[1,64,1024]{2,1,0:T(8,128)(2,1)S(1)}) custom-call(s32[512]{0:T(512)S(1)} %reshape.13.lists_ref, s32[64]{0:T(128)S(1)} %reshape.14.counts_ref, bf16[8,128,128]{2,1,0:T(8,128)(2,1)S(1)} %get-tuple-element.74.refs_1_.refs_0_.q_ref, ...), custom_call_target="tpu_custom_call" | custom-call | flops 1024 | bytes 1024 | tf_op jit(solution)/shard_map/attend_last/pallas_call | solution.py:587
  37.1 0.8 %collective-permute-done.11.refs_0_ = bf16[1,64,1024]{2,1,0:T(8,128)(2,1)S(1)} collective-permute-done((bf16[1,64,1024]{2,1,0:T(8,128)(2,1)S(1)}, bf16[1,64,1024]{2,1,0:T(8,128)(2,1)S(1)}, u32[]{:S(2)}, u32[]{:S(2)}) %collective-permute-start.11) | collective-permute-done | bytes 131104 | tf_op jit(solution)/shard_map/ppermute | solution.py:660
  39.2 1.5 %collective-permute-done.10.refs_0_ = bf16[128,1024]{1,0:T(8,128)(2,1)S(1)} collective-permute-done((bf16[128,1024]{1,0:T(8,128)(2,1)S(1)}, bf16[128,1024]{1,0:T(8,128)(2,1)S(1)}, u32[]{:S(2)}, u32[]{:S(2)}) %collective-permute-start.10) | collective-permute-done | bytes 262176 | tf_op jit(solution)/shard_map/ppermute | solution.py:627
  43.5 1.6 %project_near.1 = (f32[128,1024]{1,0:T(8,128)S(1)}, f32[128,1024]{1,0:T(8,128)S(1)}) custom-call(bf16[128,1024]{1,0:T(8,128)(2,1)S(1)} %get-tuple-element.121.attended_ref.refs_0_, bf16[128,1024]{1,0:T(8,128)(2,1)S(1)} %get-tuple-element.122.attended_ref.refs_1_, bf16[2,1024,1024]{2,1,0:T(8,128)(2,1)S(1)} %get-tuple-element.114.weight_ref.refs_2_, ...), custom_call_target="tpu_custom_call" | custom-call | flops 1024 | bytes 1024 | tf_op jit(solution)/shard_map/project_near/pallas_call | solution.py:642
  45.3 1.9 %collective-permute-done.17.refs_0_ = bf16[128,1024]{1,0:T(8,128)(2,1)S(1)} collective-permute-done((bf16[128,1024]{1,0:T(8,128)(2,1)S(1)}, bf16[128,1024]{1,0:T(8,128)(2,1)S(1)}, u32[]{:S(2)}, u32[]{:S(2)}) %collective-permute-start.17) | collective-permute-done | bytes 262176 | tf_op jit(solution)/shard_map/ppermute | solution.py:627
  47.4 1.2 %collective-permute-done.18 = f32[16,128]{1,0:T(8,128)S(1)} collective-permute-done((f32[16,128]{1,0:T(8,128)S(1)}, f32[16,128]{1,0:T(8,128)S(1)}, u32[]{:S(2)}, u32[]{:S(2)}) %collective-permute-start.18) | collective-permute-done | bytes 8224 | tf_op jit(solution)/shard_map/ppermute | solution.py:687
  49.2 0.8 %stream.1 = bf16[2,128,1024]{2,1,0:T(8,128)(2,1)} custom-call(f32[128,1024]{1,0:T(8,128)S(1)} %get-tuple-element.129.refs_0_, f32[128,1024]{1,0:T(8,128)S(1)} %get-tuple-element.131.refs_1_), custom_call_target="tpu_custom_call" | custom-call | flops 1024 | bytes 1024 | tf_op jit(solution)/shard_map/stream/pallas_call | solution.py:697
  50.0 2.2 %collective-permute-done.19.refs_3_ = f32[16,128]{1,0:T(8,128)S(1)} collective-permute-done((f32[16,128]{1,0:T(8,128)S(1)}, f32[16,128]{1,0:T(8,128)S(1)}, u32[]{:S(2)}, u32[]{:S(2)}) %collective-permute-start.19) | collective-permute-done | bytes 8224 | tf_op jit(solution)/shard_map/ppermute | solution.py:689
  52.2 1.0 %norm.1 = bf16[2,128,1024]{2,1,0:T(8,128)(2,1)} custom-call(f32[128,1024]{1,0:T(8,128)S(1)} %get-tuple-element.129.refs_0_, f32[128,1024]{1,0:T(8,128)S(1)} %get-tuple-element.131.refs_1_, f32[16,128]{1,0:T(8,128)S(1)} %add.3.refs_2_, f32[16,128]{1,0:T(8,128)S(1)} %collective-permute-done.19.refs_3_, bf16[1,1024]{1,0:T(2,128)(2,1)S(1)} %reshape.15.refs_4_), custom_call_target="tpu_custom_call" | custom-call | flops 1024 | bytes 1024 | tf_op jit(solution)/shard_map/norm/pallas_call | solution.py:706
  (42 shorter events, 8.3 us)
Async XLA Ops:
  1.6 10.4 %collective-permute-start = (bf16[1024,128]{1,0:T(8,128)(2,1)S(1)}, bf16[1024,128]{1,0:T(8,128)(2,1)S(1)}, u32[]{:S(2)}, u32[]{:S(2)}) collective-permute-start(bf16[1024,128]{1,0:T(8,128)(2,1)S(1)} %pack_keys.1.keys_ref), channel_id=1, source_target_pairs={{0,4},{1,9},{2,6},{3,11},{4,0},{5,13},{6,2},{7,15},{8,12},{9,1},{1... | collective-permute-start | bytes 786440 | tf_op jit(solution)/shard_map/ppermute | solution.py:568
  5.8 11.3 %collective-permute-start.2 = (bf16[1024,128]{1,0:T(8,128)(2,1)S(1)}, bf16[1024,128]{1,0:T(8,128)(2,1)S(1)}, u32[]{:S(2)}, u32[]{:S(2)}) collective-permute-start(bf16[1024,128]{1,0:T(8,128)(2,1)S(1)} %pack_values.1.values_ref), channel_id=1, source_target_pairs={{0,4},{1,9},{2,6},{3,11},{4,0},{5,13},{6,2},{7,15},{8,12},{9,1},{1... | collective-permute-start | bytes 786440 | tf_op jit(solution)/shard_map/ppermute | solution.py:568
  12.1 11.4 %collective-permute-start.1 = (bf16[1024,128]{1,0:T(8,128)(2,1)S(1)}, bf16[1024,128]{1,0:T(8,128)(2,1)S(1)}, u32[]{:S(2)}, u32[]{:S(2)}) collective-permute-start(bf16[1024,128]{1,0:T(8,128)(2,1)S(1)} %collective-permute-done.refs_2_), channel_id=1, source_target_pairs={{1,5},{3,7},{5,1},{7,3},{9,13},{11,15},{13,9},{15,11},{17,21},{19,... | collective-permute-start | bytes 786440 | tf_op jit(solution)/shard_map/ppermute | solution.py:568
  12.8 10.7 %collective-permute-start.3 = (bf16[1024,128]{1,0:T(8,128)(2,1)S(1)}, bf16[1024,128]{1,0:T(8,128)(2,1)S(1)}, u32[]{:S(2)}, u32[]{:S(2)}) collective-permute-start(bf16[1024,128]{1,0:T(8,128)(2,1)S(1)} %collective-permute-done.refs_2_), channel_id=1, source_target_pairs={{0,1},{1,0},{2,3},{3,2},{4,5},{5,4},{6,7},{7,6},{8,9},{9,8},{10,11... | collective-permute-start | bytes 786440 | tf_op jit(solution)/shard_map/ppermute | solution.py:570
  17.1 6.4 %collective-permute-start.6 = (bf16[1024,128]{1,0:T(8,128)(2,1)S(1)}, bf16[1024,128]{1,0:T(8,128)(2,1)S(1)}, u32[]{:S(2)}, u32[]{:S(2)}) collective-permute-start(bf16[1024,128]{1,0:T(8,128)(2,1)S(1)} %collective-permute-done.2.refs_3_), channel_id=1, source_target_pairs={{1,5},{3,7},{5,1},{7,3},{9,13},{11,15},{13,9},{15,11},{17,21},{19,... | collective-permute-start | bytes 786440 | tf_op jit(solution)/shard_map/ppermute | solution.py:568
  17.8 5.7 %collective-permute-start.4 = (bf16[512,128]{1,0:T(8,128)(2,1)S(1)}, bf16[512,128]{1,0:T(8,128)(2,1)S(1)}, u32[]{:S(2)}, u32[]{:S(2)}) collective-permute-start(bf16[512,128]{1,0:T(8,128)(2,1)S(1)} %get-tuple-element.135), channel_id=1, source_target_pairs={{0,1},{1,0},{2,3},{3,2},{4,5},{5,4},{6,7},{7,6},{8,9},{9,8},{10,11... | collective-permute-start | bytes 393224 | tf_op jit(solution)/shard_map/ppermute | solution.py:573
  20.2 3.3 %collective-permute-start.5 = (bf16[512,128]{1,0:T(8,128)(2,1)S(1)}, bf16[512,128]{1,0:T(8,128)(2,1)S(1)}, u32[]{:S(2)}, u32[]{:S(2)}) collective-permute-start(bf16[512,128]{1,0:T(8,128)(2,1)S(1)} %get-tuple-element.134), channel_id=1, source_target_pairs={{0,1},{1,0},{2,3},{3,2},{4,5},{5,4},{6,7},{7,6},{8,9},{9,8},{10,11... | collective-permute-start | bytes 393224 | tf_op jit(solution)/shard_map/ppermute | solution.py:573
  23.5 3.1 %collective-permute-start.8 = (bf16[1024,128]{1,0:T(8,128)(2,1)S(1)}, bf16[1024,128]{1,0:T(8,128)(2,1)S(1)}, u32[]{:S(2)}, u32[]{:S(2)}) collective-permute-start(bf16[1024,128]{1,0:T(8,128)(2,1)S(1)} %collective-permute-done.6.mine_values_ref), channel_id=1, source_target_pairs={{0,1},{1,0},{2,3},{3,2},{4,5},{5,4},{6,7},{7,6},{8,9},{9,8},{10,11... | collective-permute-start | bytes 786440 | tf_op jit(solution)/shard_map/ppermute | solution.py:573
  24.7 1.9 %collective-permute-start.7 = (bf16[1024,128]{1,0:T(8,128)(2,1)S(1)}, bf16[1024,128]{1,0:T(8,128)(2,1)S(1)}, u32[]{:S(2)}, u32[]{:S(2)}) collective-permute-start(bf16[1024,128]{1,0:T(8,128)(2,1)S(1)} %collective-permute-done.1.mine_keys_ref), channel_id=1, source_target_pairs={{0,1},{1,0},{2,3},{3,2},{4,5},{5,4},{6,7},{7,6},{8,9},{9,8},{10,11... | collective-permute-start | bytes 786440 | tf_op jit(solution)/shard_map/ppermute | solution.py:570
  29.5 2.4 %collective-permute-start.9 = (bf16[1,128,1024]{2,1,0:T(8,128)(2,1)S(1)}, bf16[1,128,1024]{2,1,0:T(8,128)(2,1)S(1)}, u32[]{:S(2)}, u32[]{:S(2)}) collective-permute-start(bf16[1,128,1024]{2,1,0:T(8,128)(2,1)S(1)} %get-tuple-element.107), channel_id=1, source_target_pairs={{0,1},{1,0},{2,3},{3,2},{4,5},{5,4},{6,7},{7,6},{8,9},{9,8},{10,11... | collective-permute-start | bytes 786440 | tf_op jit(solution)/shard_map/ppermute | solution.py:660
  32.4 8.3 %collective-permute-start.10 = (bf16[128,1024]{1,0:T(8,128)(2,1)S(1)}, bf16[128,1024]{1,0:T(8,128)(2,1)S(1)}, u32[]{:S(2)}, u32[]{:S(2)}) collective-permute-start(bf16[128,1024]{1,0:T(8,128)(2,1)S(1)} %project_onward.2), channel_id=1, source_target_pairs={{0,2},{1,3},{2,0},{3,1},{4,6},{5,7},{6,4},{7,5},{8,10},{9,11},{10,... | collective-permute-start | bytes 786440 | tf_op jit(solution)/shard_map/ppermute | solution.py:627
  36.5 1.4 %collective-permute-start.11 = (bf16[1,64,1024]{2,1,0:T(8,128)(2,1)S(1)}, bf16[1,64,1024]{2,1,0:T(8,128)(2,1)S(1)}, u32[]{:S(2)}, u32[]{:S(2)}) collective-permute-start(bf16[1,64,1024]{2,1,0:T(8,128)(2,1)S(1)} %get-tuple-element.119), channel_id=1, source_target_pairs={{0,1},{1,0},{2,3},{3,2},{4,5},{5,4},{6,7},{7,6},{8,9},{9,8},{10,11... | collective-permute-start | bytes 393224 | tf_op jit(solution)/shard_map/ppermute | solution.py:660
  36.6 1.5 %collective-permute-start.12 = (bf16[1,64,1024]{2,1,0:T(8,128)(2,1)S(1)}, bf16[1,64,1024]{2,1,0:T(8,128)(2,1)S(1)}, u32[]{:S(2)}, u32[]{:S(2)}) collective-permute-start(bf16[1,64,1024]{2,1,0:T(8,128)(2,1)S(1)} %get-tuple-element.120), channel_id=1, source_target_pairs={{0,1},{1,0},{2,3},{3,2},{4,5},{5,4},{6,7},{7,6},{8,9},{9,8},{10,11... | collective-permute-start | bytes 393224 | tf_op jit(solution)/shard_map/ppermute | solution.py:660
  38.6 8.6 %collective-permute-start.17 = (bf16[128,1024]{1,0:T(8,128)(2,1)S(1)}, bf16[128,1024]{1,0:T(8,128)(2,1)S(1)}, u32[]{:S(2)}, u32[]{:S(2)}) collective-permute-start(bf16[128,1024]{1,0:T(8,128)(2,1)S(1)} %project_onward.3), channel_id=1, source_target_pairs={{0,2},{1,3},{2,0},{3,1},{4,6},{5,7},{6,4},{7,5},{8,10},{9,11},{10,... | collective-permute-start | bytes 786440 | tf_op jit(solution)/shard_map/ppermute | solution.py:627
  41.4 1.4 %collective-permute-start.13 = (bf16[64,1024]{1,0:T(8,128)(2,1)S(1)}, bf16[64,1024]{1,0:T(8,128)(2,1)S(1)}, u32[]{:S(2)}, u32[]{:S(2)}) collective-permute-start(bf16[64,1024]{1,0:T(8,128)(2,1)S(1)} %get-tuple-element.123), channel_id=1, source_target_pairs={{0,1},{1,0},{2,3},{3,2},{4,5},{5,4},{6,7},{7,6},{8,9},{9,8},{10,11... | collective-permute-start | bytes 393224 | tf_op jit(solution)/shard_map/ppermute | solution.py:670
  41.5 1.5 %collective-permute-start.14 = (bf16[64,1024]{1,0:T(8,128)(2,1)S(1)}, bf16[64,1024]{1,0:T(8,128)(2,1)S(1)}, u32[]{:S(2)}, u32[]{:S(2)}) collective-permute-start(bf16[64,1024]{1,0:T(8,128)(2,1)S(1)} %get-tuple-element.124), channel_id=1, source_target_pairs={{0,1},{1,0},{2,3},{3,2},{4,5},{5,4},{6,7},{7,6},{8,9},{9,8},{10,11... | collective-permute-start | bytes 393224 | tf_op jit(solution)/shard_map/ppermute | solution.py:670
  42.0 1.3 %collective-permute-start.15 = (bf16[64,1024]{1,0:T(8,128)(2,1)S(1)}, bf16[64,1024]{1,0:T(8,128)(2,1)S(1)}, u32[]{:S(2)}, u32[]{:S(2)}) collective-permute-start(bf16[64,1024]{1,0:T(8,128)(2,1)S(1)} %get-tuple-element.125), channel_id=1, source_target_pairs={{0,1},{1,0},{2,3},{3,2},{4,5},{5,4},{6,7},{7,6},{8,9},{9,8},{10,11... | collective-permute-start | bytes 393224 | tf_op jit(solution)/shard_map/ppermute | solution.py:670
  42.0 7.1 %copy-start = (bf16[1024]{0:T(1024)(128)(2,1)S(1)}, bf16[1024]{0:T(1024)(128)(2,1)}, u32[]{:S(2)}) copy-start(bf16[1024]{0:T(1024)(128)(2,1)} %param.19) | copy-start | bytes 6148
  42.0 1.5 %collective-permute-start.16 = (bf16[64,1024]{1,0:T(8,128)(2,1)S(1)}, bf16[64,1024]{1,0:T(8,128)(2,1)S(1)}, u32[]{:S(2)}, u32[]{:S(2)}) collective-permute-start(bf16[64,1024]{1,0:T(8,128)(2,1)S(1)} %get-tuple-element.126), channel_id=1, source_target_pairs={{0,1},{1,0},{2,3},{3,2},{4,5},{5,4},{6,7},{7,6},{8,9},{9,8},{10,11... | collective-permute-start | bytes 393224 | tf_op jit(solution)/shard_map/ppermute | solution.py:670
  47.4 1.2 %collective-permute-start.18 = (f32[16,128]{1,0:T(8,128)S(1)}, f32[16,128]{1,0:T(8,128)S(1)}, u32[]{:S(2)}, u32[]{:S(2)}) collective-permute-start(f32[16,128]{1,0:T(8,128)S(1)} %constant_dynamic-update-slice_fusion), channel_id=1, source_target_pairs={{0,1},{1,0},{2,3},{3,2},{4,5},{5,4},{6,7},{7,6},{8,9},{9,8},{10,11... | collective-permute-start | bytes 24584 | tf_op jit(solution)/shard_map/ppermute | solution.py:687
  48.6 3.7 %collective-permute-start.19 = (f32[16,128]{1,0:T(8,128)S(1)}, f32[16,128]{1,0:T(8,128)S(1)}, u32[]{:S(2)}, u32[]{:S(2)}) collective-permute-start(f32[16,128]{1,0:T(8,128)S(1)} %add.3.refs_2_), channel_id=1, source_target_pairs={{0,2},{1,3},{2,0},{3,1},{4,6},{5,7},{6,4},{7,5},{8,10},{9,11},{10,... | collective-permute-start | bytes 24584 | tf_op jit(solution)/shard_map/ppermute | solution.py:689

commit v15 on v14

--- a/solution.py
+++ b/solution.py
@@ -121,14 +121,15 @@
     return copies
 
 
-def weight_copies(weight_ref, target, sems, sibling):
-    chips, _, share = target.shape
+def weight_copies(weight_ref, target, sems, sibling, first=0):
+    count, _, share = target.shape
+    chips = weight_ref.shape[1] // (CORES * share)
     place = lax.axis_index("tp")
     chip, core = place // CORES, place % CORES
     held = 1 - core if sibling else core
     copies = []
-    for k in range(chips):
-        start = (lax.rem(chip + k, chips) * CORES + held) * share
+    for k in range(count):
+        start = (lax.rem(chip + first + k, chips) * CORES + held) * share
         copies.append(
             pltpu.make_async_copy(
                 weight_ref.at[:, pl.ds(pl.multiple_of(start, HD), share)],
@@ -149,10 +150,12 @@
     queries_ref,
     cont_keys_ref,
     cont_values_ref,
+    weight_ref,
     *refs,
 ):
     states, refs = by_cont(refs[: 2 * conts]), refs[2 * conts :]
     q_refs, refs = refs[:conts], refs[conts:]
+    give_ref, weight_sems, *refs = refs[0], refs[-1], *refs[1:-1]
     flipped_ref, rows_ref, ck_ref, cv_ref, own_ref, sems = refs
     heads, _, length = q_refs[0].shape
     lanes = group_lanes(heads)
@@ -163,6 +166,7 @@
             pltpu.make_async_copy(cont_keys_ref.at[:, :, lanes], ck_ref, sems.at[2]),
         ]
     )
+    fetched = start_all(weight_copies(weight_ref, give_ref, weight_sems, True))
     place = conts, sources, lax.axis_index("ctx")
     both_ways([values_ref], flipped_ref)
     copies[0].wait()
@@ -205,6 +209,8 @@
         return carry
 
     lax.fori_loop(0, heads // together, some_heads, 0)
+    for copy in fetched:
+        copy.wait()
 
 
 def arrivals(step, sources):
@@ -267,8 +273,9 @@
         weight_ref, *refs = refs
     after, refs = refs[: 2 * count], refs[2 * count :]
     if with_weight:
-        give_ref, flipped_ref, sems = refs
-        copies = start_all(weight_copies(weight_ref, give_ref, sems, True))
+        keep_ref, flipped_ref, sems = refs
+        first = 1 if part == 0 else 0
+        copies = start_all(weight_copies(weight_ref, keep_ref, sems, False, first))
     else:
         (flipped_ref,) = refs
     source, valid = arrivals(step, sources)[part]
@@ -320,12 +327,7 @@
     give_weight_ref,
     *refs,
 ):
-    if cont == 0:
-        weight_ref, *refs, sems = refs
     attended_ref, give_refs, refs = refs[0], refs[1 : 1 + pieces], refs[1 + pieces :]
-    if cont == 0:
-        keep_weight_ref, *refs = refs
-        copies = start_all(weight_copies(weight_ref, keep_weight_ref, sems, False))
     acc_ref, stat_ref, flipped_ref = refs
     before, after = (acc_in, stat_in), (acc_ref, stat_ref)
     one_of_two = sources == 4
@@ -346,9 +348,6 @@
         if part == 0 and not one_of_two:
             pl.when(jnp.logical_not(valid))(lambda: hand_on(before, after))
     finish_and_give(acc_ref, stat_ref, give_weight_ref, attended_ref, give_refs)
-    if cont == 0:
-        for copy in copies:
-            copy.wait()
 
 
 def from_sibling(got_refs, k):
@@ -359,7 +358,7 @@
     got_refs, onward_refs = refs[:pieces], refs[pieces:]
     for k, onward_ref in enumerate(onward_refs, 1):
         onward_ref[...] = (
-            jnp.dot(attended_ref[...], weight_ref[k], preferred_element_type=jnp.float32)
+            jnp.dot(attended_ref[...], weight_ref[k - 1], preferred_element_type=jnp.float32)
             + from_sibling(got_refs, k - 1)
         ).astype(jnp.bfloat16)
 
@@ -516,9 +515,11 @@
 
     made = pl.pallas_call(
         functools.partial(first_kernel, sources, conts),
-        out_shape=state_shape * conts + (array((heads, HD, length), jnp.bfloat16),) * conts,
-        in_specs=[smem, smem, vmem, vmem] + [hbm] * 3,
-        out_specs=(vmem,) * (3 * conts),
+        out_shape=state_shape * conts
+        + (array((heads, HD, length), jnp.bfloat16),) * conts
+        + (weight_shape,),
+        in_specs=[smem, smem, vmem, vmem] + [hbm] * 4,
+        out_specs=(vmem,) * (3 * conts + 1),
         scratch_shapes=[
             flipped,
             pltpu.VMEM(queries.shape, jnp.bfloat16),
@@ -526,25 +527,36 @@
             pltpu.VMEM((conts, length, HD), jnp.bfloat16),
             pltpu.VMEM((conts, HD, length), jnp.bfloat16),
             pltpu.SemaphoreType.DMA((3,)),
+            pltpu.SemaphoreType.DMA((chips,)),
         ],
         compiler_params=params,
         cost_estimate=cost(),
         name="attend_own",
-    )(lists, counts, keys, values, in_hbm(queries), in_hbm(cont_keys), in_hbm(cont_values))
+    )(
+        lists,
+        counts,
+        keys,
+        values,
+        in_hbm(queries),
+        in_hbm(cont_keys),
+        in_hbm(cont_values),
+        in_hbm(out_weight),
+    )
     states = tuple(made[2 * c : 2 * c + 2] for c in range(conts))
-    qs = made[2 * conts :]
+    *qs, give_weight = made[2 * conts :]
 
     def attend_step(step, part, chosen, with_weight, states, held):
         flat = [x for cont in chosen for x in states[cont]]
         count = len(chosen)
+        kept = array((chips - 1 if part == 0 else 1, width, share), jnp.bfloat16)
         made = pl.pallas_call(
             functools.partial(
                 middle_kernel, step, part, sources, conts, chosen, len(held), with_weight
             ),
-            out_shape=state_shape * count + ((weight_shape,) if with_weight else ()),
+            out_shape=state_shape * count + (kept,) * with_weight,
             in_specs=[smem, smem] + [vmem] * (3 * count + len(held)) + [hbm] * with_weight,
             out_specs=(vmem,) * (2 * count + with_weight),
-            scratch_shapes=[flipped] + [pltpu.SemaphoreType.DMA((chips,))] * with_weight,
+            scratch_shapes=[flipped] + [pltpu.SemaphoreType.DMA(kept.shape[:1])] * with_weight,
             compiler_params=params,
             cost_estimate=cost(),
             name="attend_step",
@@ -573,27 +585,28 @@
             lax.ppermute(x, "tp", sibling)
             for x in jnp.split(mine_values, 2 if step < steps else 1)
         ]
-        mine, rest, theirs = (mine_keys, mine_values), theirs, (their_keys, *their_values)
-        if rest is not None:
-            states, _ = attend_step(step - 1, 1, everyone[:1], False, states, rest)
-            theirs, first = lax.optimization_barrier((theirs, states[0]))
-            states = (first, *states[1:])
-            states, _ = attend_step(step - 1, 1, everyone[1:], False, states, rest)
+        before, mine = mine, (mine_keys, mine_values)
+        rest, theirs = theirs, (their_keys, *their_values)
+        if step > 1:
+            states, _ = attend_step(step - 1, 0, everyone[1:], False, states, before)
+            theirs, states = lax.optimization_barrier((theirs, states))
+            states, made = attend_step(step - 1, 1, everyone[1:], step == 2, states, rest)
+            keep_own = made[0] if step == 2 else keep_own
         if step < steps:
-            states, (give_weight,) = attend_step(step, 0, everyone, True, states, mine)
+            states, made = attend_step(step, 0, everyone[:1], step == 1, states, mine)
+            states, _ = attend_step(step, 1, everyone[:1], False, states, theirs)
+            keep_far = made[0] if step == 1 else keep_far
 
     def attend_last(cont, state):
-        fetch, pieces = cont == 0, swap_pieces[cont]
+        pieces = swap_pieces[cont]
         made = pl.pallas_call(
             functools.partial(last_kernel, steps, sources, conts, cont, pieces),
             out_shape=(array((length, width), jnp.bfloat16),)
-            + (array((chips - 1, length // pieces, share), jnp.bfloat16),) * pieces
-            + (weight_shape,) * fetch,
-            in_specs=[smem, smem] + [vmem] * 8 + [hbm] * fetch,
-            out_specs=(vmem,) * (1 + pieces + fetch),
+            + (array((chips - 1, length // pieces, share), jnp.bfloat16),) * pieces,
+            in_specs=[smem, smem] + [vmem] * 8,
+            out_specs=(vmem,) * (1 + pieces),
             scratch_shapes=[pltpu.VMEM(a.shape, a.dtype) for a in state_shape]
-            + [flipped]
-            + [pltpu.SemaphoreType.DMA((chips,))] * fetch,
+            + [flipped],
             compiler_params=params,
             cost_estimate=cost(),
             name="attend_last",
@@ -605,9 +618,8 @@
             *theirs,
             *state,
             give_weight,
-            *([in_hbm(out_weight)] * fetch),
         )
-        return made[0], made[1 : 1 + pieces], made[1 + pieces :]
+        return made[0], made[1:]
 
     def onward(attended, got):
         parts = pl.pallas_call(
@@ -618,7 +630,7 @@
             compiler_params=params,
             cost_estimate=cost(),
             name="project_onward",
-        )(attended, keep_weight, *got)
+        )(attended, keep_far, *got)
         far = []
         for k in range(1, chips):
             to_chip = [
@@ -651,10 +663,10 @@
             compiler_params=params,
             cost_estimate=cost(),
             name="project_near",
-        )(*attended, keep_weight, in_hbm(residual), *got)
+        )(*attended, keep_own, in_hbm(residual), *got)
 
     swap_pieces = [1] + [2] * (conts - 1)
-    attended, give, (keep_weight,) = attend_last(0, states[0])
+    attended, give = attend_last(0, states[0])
     all_attended, fars = [], []
     for cont in range(conts):
         got = [lax.ppermute(x, "tp", sibling) for x in give]
@@ -665,7 +677,7 @@
         fars.append(far)
         if cont + 1 < conts:
             state, parts = lax.optimization_barrier((state, parts))
-            attended, give, _ = attend_last(cont + 1, state)
+            attended, give = attend_last(cont + 1, state)
     all_attended, fars[:-1], _ = lax.optimization_barrier((all_attended, fars[:-1], parts))
     got = [lax.ppermute(x, "tp", sibling) for x in give_near(all_attended, 2 * conts)]
     nears = near(all_attended, got)

time: 53.6 us -> 56 us (1.045)
  Pallas kernels: 24.3 us -> 27.9 us
  starting transfers between devices: 16.4 us -> 15.7 us
    pallas_call x3 -> x4, Pallas kernels: 6.92 us -> 10.4 us  [attend_step(): pl.pallas_call(functools.partial(middle_kernel, step, part, sources, cont...]
    ppermute x7, starting transfers between devices: 4.73 us -> 3.6 us  [shards(): lax.ppermute(x, 'tp', sibling)]
  transfers between devices with their start and end apart: 20 -> 20, of which waited for: 11 -> 11; matrix products, arithmetic and copies ran while one was open for 3% -> 3% of each run, Pallas kernels for 35% -> 41%
where the time goes in v15:
time: 56 us; the launch traced here: 55.6 us
  Pallas kernels  27.9 us (50%)
  starting transfers between devices  15.7 us (28%)
  waiting for transfers between devices  9.44 us (17%)
  local copies, waits for them, and re-layouts  1.76 us (3%)
  between operations  0.87 us (2%)
    pallas_call x4, Pallas kernels, attend_step(): pl.pallas_call(functools.partial(middle_kernel, step, part, sources, cont...  10.4 us
    pallas_call x2, Pallas kernels, attend_last(): pl.pallas_call(functools.partial(last_kernel, steps, sources, conts, cont...  5.03 us
    pallas_call x1, Pallas kernels, shards(): pl.pallas_call(functools.partial(first_kernel, sources, conts), out_shape...  4.86 us
    ppermute x4, starting transfers between devices, shards(): lax.ppermute(x, ('ctx', 'tp'), across(step))  4.53 us
    ppermute x2, starting transfers between devices, shards(): their_keys = lax.ppermute(mine_keys, 'tp', sibling)  3.69 us
    ppermute x7, starting transfers between devices, shards(): lax.ppermute(x, 'tp', sibling)  3.6 us
    ppermute x2, waiting for transfers between devices, onward(): far.append(lax.ppermute(parts[k - 1], 'tp', to_chip))  3.33 us
    ppermute x2, starting transfers between devices, onward(): far.append(lax.ppermute(parts[k - 1], 'tp', to_chip))  2.15 us
  transfers between devices with their start and end apart: 20, of which 11 were waited for; matrix products, arithmetic and copies ran while one was open for 3% of the time, Pallas kernels for 41%

profile of v15, /device:TPU:0, one launch (start us, length us, event | category | flops | bytes accessed | tf_op | source)
XLA Modules:
  0.0 55.6 jit_solution(7780890006872188402)
XLA Ops:
  0.6 1.0 %pack_keys.1.keys_ref = bf16[1024,128]{1,0:T(8,128)(2,1)S(1)} custom-call(bf16[1024,256]{1,0:T(8,128)(2,1)} %keys_ref.1), custom_call_target="tpu_custom_call" | custom-call | flops 1024 | bytes 1024 | tf_op jit(solution)/shard_map/pack_keys/pallas_call | solution.py:464
  1.6 3.1 %collective-permute-start = (bf16[1024,128]{1,0:T(8,128)(2,1)S(1)}, bf16[1024,128]{1,0:T(8,128)(2,1)S(1)}, u32[]{:S(2)}, u32[]{:S(2)}) collective-permute-start(bf16[1024,128]{1,0:T(8,128)(2,1)S(1)} %pack_keys.1.keys_ref), channel_id=1, source_target_pairs={{0,4},{1,9},{2,6},{3,11},{4,0},{5,13},{6,2},{7,15},{8,12},{9,1},{1... | collective-permute-start | bytes 786440 | tf_op jit(solution)/shard_map/ppermute | solution.py:580
  4.7 1.1 %pack_values.1.values_ref = bf16[1024,128]{1,0:T(8,128)(2,1)S(1)} custom-call(bf16[1024,256]{1,0:T(8,128)(2,1)} %values_ref.1), custom_call_target="tpu_custom_call" | custom-call | flops 1024 | bytes 1024 | tf_op jit(solution)/shard_map/pack_values/pallas_call | solution.py:474
  5.9 0.9 %reshape.13.lists_ref = s32[512]{0:T(512)S(1)} reshape(s32[8,2,4,8]{3,2,1,0:T(4,128)} %param.15) | data formatting | bytes 4096 | tf_op jit(solution)/shard_map/reshape | solution.py:507
  6.7 0.8 %copy.13 = s32[8,2,4]{2,1,0:T(2,128)S(1)} copy(s32[8,2,4]{0,2,1:T(4,128)} %param.16) | data formatting | bytes 512 | tf_op args[6]
  7.6 4.9 %attend_own.1 = (f32[8,128,128]{2,1,0:T(8,128)S(1)}, f32[8,8,128]{2,1,0:T(8,128)S(1)}, f32[8,128,128]{2,1,0:T(8,128)S(1)}, f32[8,8,128]{2,1,0:T(8,128)S(1)}, bf1...) custom-call(s32[512]{0:T(512)S(1)} %reshape.13.lists_ref, ...), custom_call_target="tpu_custom_call" | custom-call | flops 1024 | bytes 1024 | tf_op jit(solution)/shard_map/attend_own/pallas_call | solution.py:516
  13.2 3.2 %collective-permute-start.2 = (bf16[1024,128]{1,0:T(8,128)(2,1)S(1)}, bf16[1024,128]{1,0:T(8,128)(2,1)S(1)}, u32[]{:S(2)}, u32[]{:S(2)}) collective-permute-start(bf16[1024,128]{1,0:T(8,128)(2,1)S(1)} %collective-permute-done.refs_1_), channel_id=1, source_target_pairs={{0,1},{1,0},{2,3},{3,2},{4,5},{5,4},{6,7},{7,6},{8,9},{9,8},{10,11... | collective-permute-start | bytes 786440 | tf_op jit(solution)/shard_map/ppermute | solution.py:582
  16.4 0.7 %collective-permute-done.3.refs_2_ = bf16[1024,128]{1,0:T(8,128)(2,1)S(1)} collective-permute-done((bf16[1024,128]{1,0:T(8,128)(2,1)S(1)}, bf16[1024,128]{1,0:T(8,128)(2,1)S(1)}, u32[]{:S(2)}, u32[]{:S(2)}) %collective-permute-start.3) | collective-permute-done | bytes 262176 | tf_op jit(solution)/shard_map/ppermute | solution.py:580
  17.8 2.4 %collective-permute-start.4 = (bf16[512,128]{1,0:T(8,128)(2,1)S(1)}, bf16[512,128]{1,0:T(8,128)(2,1)S(1)}, u32[]{:S(2)}, u32[]{:S(2)}) collective-permute-start(bf16[512,128]{1,0:T(8,128)(2,1)S(1)} %get-tuple-element.141), channel_id=1, source_target_pairs={{0,1},{1,0},{2,3},{3,2},{4,5},{5,4},{6,7},{7,6},{8,9},{9,8},{10,11... | collective-permute-start | bytes 393224 | tf_op jit(solution)/shard_map/ppermute | solution.py:585
  20.2 3.3 %attend_step.4 = (f32[8,128,128]{2,1,0:T(8,128)S(1)}, f32[8,8,128]{2,1,0:T(8,128)S(1)}, bf16[1,1024,1024]{2,1,0:T(8,128)(2,1)S(1)}) custom-call(s32[512]{0:T(512)S(1)} %reshape.13.lists_ref, s32[64]{0:T(128)S(1)} %reshape.14.counts_ref, bf16[8,128,128]{2,1,0:T(8,128)(2,1)S(1)} %get-tuple-element.71.refs_0_.q_ref, ...), custom_call_target="tpu_custom_call" | custom-call | flops 1024 | bytes 1024 | tf_op jit(solution)/shard_map/attend_step/pallas_call | solution.py:552
  23.6 1.9 %attend_step.5 = (f32[8,128,128]{2,1,0:T(8,128)S(1)}, f32[8,8,128]{2,1,0:T(8,128)S(1)}) custom-call(s32[512]{0:T(512)S(1)} %reshape.13.lists_ref, s32[64]{0:T(128)S(1)} %reshape.14.counts_ref, bf16[8,128,128]{2,1,0:T(8,128)(2,1)S(1)} %get-tuple-element.71.refs_0_.q_ref, bf16[1024,128]{1,0:T(8,128)(2,1)S(1)} %collective-permute-done.2.refs_1_, ...), custom_call_target="tpu_custom_call" | custom-call | flops 1024 | bytes 1024 | tf_op jit(solution)/shard_map/attend_step/pallas_call | solution.py:552
  26.1 1.9 %attend_step.6 = (f32[8,128,128]{2,1,0:T(8,128)S(1)}, f32[8,8,128]{2,1,0:T(8,128)S(1)}) custom-call(s32[512]{0:T(512)S(1)} %reshape.13.lists_ref, s32[64]{0:T(128)S(1)} %reshape.14.counts_ref, bf16[8,128,128]{2,1,0:T(8,128)(2,1)S(1)} %get-tuple-element.98.refs_0_.q_ref, bf16[1024,128]{1,0:T(8,128)(2,1)S(1)} %collective-permute-done.refs_1_, ...), custom_call_target="tpu_custom_call" | custom-call | flops 1024 | bytes 1024 | tf_op jit(solution)/shard_map/attend_step/pallas_call | solution.py:552
  28.0 2.4 %attend_last.2 = (bf16[128,1024]{1,0:T(8,128)(2,1)S(1)}, bf16[1,128,1024]{2,1,0:T(8,128)(2,1)S(1)}) custom-call(s32[512]{0:T(512)S(1)} %reshape.13.lists_ref, s32[64]{0:T(128)S(1)} %reshape.14.counts_ref, bf16[8,128,128]{2,1,0:T(8,128)(2,1)S(1)} %get-tuple-element.71.refs_0_.q_ref, bf16[1024,128]{1,0:T(8,128)(2,1)S(1)} %collective-permute-done.1.mine_keys_ref, ...), custom_call_target="tpu_custom_call" | custom-call | flops 1024 | bytes 1024 | tf_op jit(solution)/shard_map/attend_last/pallas_call | solution.py:602
  30.9 3.4 %attend_step.7 = (f32[8,128,128]{2,1,0:T(8,128)S(1)}, f32[8,8,128]{2,1,0:T(8,128)S(1)}, bf16[1,1024,1024]{2,1,0:T(8,128)(2,1)S(1)}) custom-call(s32[512]{0:T(512)S(1)} %reshape.13.lists_ref, s32[64]{0:T(128)S(1)} %reshape.14.counts_ref, bf16[8,128,128]{2,1,0:T(8,128)(2,1)S(1)} %get-tuple-element.98.refs_0_.q_ref, ...), custom_call_target="tpu_custom_call" | custom-call | flops 1024 | bytes 1024 | tf_op jit(solution)/shard_map/attend_step/pallas_call | solution.py:552
  34.7 1.6 %collective-permute-start.10 = (bf16[128,1024]{1,0:T(8,128)(2,1)S(1)}, bf16[128,1024]{1,0:T(8,128)(2,1)S(1)}, u32[]{:S(2)}, u32[]{:S(2)}) collective-permute-start(bf16[128,1024]{1,0:T(8,128)(2,1)S(1)} %project_onward.2), channel_id=1, source_target_pairs={{0,2},{1,3},{2,0},{3,1},{4,6},{5,7},{6,4},{7,5},{8,10},{9,11},{10,... | collective-permute-start | bytes 786440 | tf_op jit(solution)/shard_map/ppermute | solution.py:639
  36.3 2.6 %attend_last.3 = (bf16[128,1024]{1,0:T(8,128)(2,1)S(1)}, bf16[1,64,1024]{2,1,0:T(8,128)(2,1)S(1)}, bf16[1,64,1024]{2,1,0:T(8,128)(2,1)S(1)}) custom-call(s32[512]{0:T(512)S(1)} %reshape.13.lists_ref, s32[64]{0:T(128)S(1)} %reshape.14.counts_ref, bf16[8,128,128]{2,1,0:T(8,128)(2,1)S(1)} %get-tuple-element.98.refs_0_.q_ref, ...), custom_call_target="tpu_custom_call" | custom-call | flops 1024 | bytes 1024 | tf_op jit(solution)/shard_map/attend_last/pallas_call | solution.py:602
  39.5 0.8 %collective-permute-done.11.refs_0_ = bf16[1,64,1024]{2,1,0:T(8,128)(2,1)S(1)} collective-permute-done((bf16[1,64,1024]{2,1,0:T(8,128)(2,1)S(1)}, bf16[1,64,1024]{2,1,0:T(8,128)(2,1)S(1)}, u32[]{:S(2)}, u32[]{:S(2)}) %collective-permute-start.11) | collective-permute-done | bytes 131104 | tf_op jit(solution)/shard_map/ppermute | solution.py:672
  41.6 1.5 %collective-permute-done.10.refs_0_ = bf16[128,1024]{1,0:T(8,128)(2,1)S(1)} collective-permute-done((bf16[128,1024]{1,0:T(8,128)(2,1)S(1)}, bf16[128,1024]{1,0:T(8,128)(2,1)S(1)}, u32[]{:S(2)}, u32[]{:S(2)}) %collective-permute-start.10) | collective-permute-done | bytes 262176 | tf_op jit(solution)/shard_map/ppermute | solution.py:639
  45.9 1.7 %project_near.1 = (f32[128,1024]{1,0:T(8,128)S(1)}, f32[128,1024]{1,0:T(8,128)S(1)}) custom-call(bf16[128,1024]{1,0:T(8,128)(2,1)S(1)} %get-tuple-element.126.attended_ref.refs_0_, bf16[128,1024]{1,0:T(8,128)(2,1)S(1)} %get-tuple-element.127.attended_ref.refs_1_, bf16[1,1024,1024]{2,1,0:T(8,128)(2,1)S(1)} %get-tuple-element.128.refs_2_, ...), custom_call_target="tpu_custom_call" | custom-call | flops 1024 | bytes 1024 | tf_op jit(solution)/shard_map/project_near/pallas_call | solution.py:654
  47.8 1.8 %collective-permute-done.17.refs_0_ = bf16[128,1024]{1,0:T(8,128)(2,1)S(1)} collective-permute-done((bf16[128,1024]{1,0:T(8,128)(2,1)S(1)}, bf16[128,1024]{1,0:T(8,128)(2,1)S(1)}, u32[]{:S(2)}, u32[]{:S(2)}) %collective-permute-start.17) | collective-permute-done | bytes 262176 | tf_op jit(solution)/shard_map/ppermute | solution.py:639
  49.8 1.2 %collective-permute-done.18 = f32[16,128]{1,0:T(8,128)S(1)} collective-permute-done((f32[16,128]{1,0:T(8,128)S(1)}, f32[16,128]{1,0:T(8,128)S(1)}, u32[]{:S(2)}, u32[]{:S(2)}) %collective-permute-start.18) | collective-permute-done | bytes 8224 | tf_op jit(solution)/shard_map/ppermute | solution.py:699
  51.6 0.8 %stream.1 = bf16[2,128,1024]{2,1,0:T(8,128)(2,1)} custom-call(f32[128,1024]{1,0:T(8,128)S(1)} %get-tuple-element.135.refs_0_, f32[128,1024]{1,0:T(8,128)S(1)} %get-tuple-element.137.refs_1_), custom_call_target="tpu_custom_call" | custom-call | flops 1024 | bytes 1024 | tf_op jit(solution)/shard_map/stream/pallas_call | solution.py:709
  52.5 2.1 %collective-permute-done.19.refs_3_ = f32[16,128]{1,0:T(8,128)S(1)} collective-permute-done((f32[16,128]{1,0:T(8,128)S(1)}, f32[16,128]{1,0:T(8,128)S(1)}, u32[]{:S(2)}, u32[]{:S(2)}) %collective-permute-start.19) | collective-permute-done | bytes 8224 | tf_op jit(solution)/shard_map/ppermute | solution.py:701
  54.6 1.0 %norm.1 = bf16[2,128,1024]{2,1,0:T(8,128)(2,1)} custom-call(f32[128,1024]{1,0:T(8,128)S(1)} %get-tuple-element.135.refs_0_, f32[128,1024]{1,0:T(8,128)S(1)} %get-tuple-element.137.refs_1_, f32[16,128]{1,0:T(8,128)S(1)} %add.3.refs_2_, f32[16,128]{1,0:T(8,128)S(1)} %collective-permute-done.19.refs_3_, bf16[1,1024]{1,0:T(2,128)(2,1)S(1)} %reshape.15.refs_4_), custom_call_target="tpu_custom_call" | custom-call | flops 1024 | bytes 1024 | tf_op jit(solution)/shard_map/norm/pallas_call | solution.py:718
  (43 shorter events, 8.8 us)
Async XLA Ops:
  1.6 10.9 %collective-permute-start = (bf16[1024,128]{1,0:T(8,128)(2,1)S(1)}, bf16[1024,128]{1,0:T(8,128)(2,1)S(1)}, u32[]{:S(2)}, u32[]{:S(2)}) collective-permute-start(bf16[1024,128]{1,0:T(8,128)(2,1)S(1)} %pack_keys.1.keys_ref), channel_id=1, source_target_pairs={{0,4},{1,9},{2,6},{3,11},{4,0},{5,13},{6,2},{7,15},{8,12},{9,1},{1... | collective-permute-start | bytes 786440 | tf_op jit(solution)/shard_map/ppermute | solution.py:580
  5.8 11.3 %collective-permute-start.3 = (bf16[1024,128]{1,0:T(8,128)(2,1)S(1)}, bf16[1024,128]{1,0:T(8,128)(2,1)S(1)}, u32[]{:S(2)}, u32[]{:S(2)}) collective-permute-start(bf16[1024,128]{1,0:T(8,128)(2,1)S(1)} %pack_values.1.values_ref), channel_id=1, source_target_pairs={{0,4},{1,9},{2,6},{3,11},{4,0},{5,13},{6,2},{7,15},{8,12},{9,1},{1... | collective-permute-start | bytes 786440 | tf_op jit(solution)/shard_map/ppermute | solution.py:580
  12.5 13.0 %collective-permute-start.1 = (bf16[1024,128]{1,0:T(8,128)(2,1)S(1)}, bf16[1024,128]{1,0:T(8,128)(2,1)S(1)}, u32[]{:S(2)}, u32[]{:S(2)}) collective-permute-start(bf16[1024,128]{1,0:T(8,128)(2,1)S(1)} %collective-permute-done.refs_1_), channel_id=1, source_target_pairs={{1,5},{3,7},{5,1},{7,3},{9,13},{11,15},{13,9},{15,11},{17,21},{19,... | collective-permute-start | bytes 786440 | tf_op jit(solution)/shard_map/ppermute | solution.py:580
  13.2 10.4 %collective-permute-start.2 = (bf16[1024,128]{1,0:T(8,128)(2,1)S(1)}, bf16[1024,128]{1,0:T(8,128)(2,1)S(1)}, u32[]{:S(2)}, u32[]{:S(2)}) collective-permute-start(bf16[1024,128]{1,0:T(8,128)(2,1)S(1)} %collective-permute-done.refs_1_), channel_id=1, source_target_pairs={{0,1},{1,0},{2,3},{3,2},{4,5},{5,4},{6,7},{7,6},{8,9},{9,8},{10,11... | collective-permute-start | bytes 786440 | tf_op jit(solution)/shard_map/ppermute | solution.py:582
  17.1 8.4 %collective-permute-start.6 = (bf16[1024,128]{1,0:T(8,128)(2,1)S(1)}, bf16[1024,128]{1,0:T(8,128)(2,1)S(1)}, u32[]{:S(2)}, u32[]{:S(2)}) collective-permute-start(bf16[1024,128]{1,0:T(8,128)(2,1)S(1)} %collective-permute-done.3.refs_2_), channel_id=1, source_target_pairs={{1,5},{3,7},{5,1},{7,3},{9,13},{11,15},{13,9},{15,11},{17,21},{19,... | collective-permute-start | bytes 786440 | tf_op jit(solution)/shard_map/ppermute | solution.py:580
  17.8 5.8 %collective-permute-start.4 = (bf16[512,128]{1,0:T(8,128)(2,1)S(1)}, bf16[512,128]{1,0:T(8,128)(2,1)S(1)}, u32[]{:S(2)}, u32[]{:S(2)}) collective-permute-start(bf16[512,128]{1,0:T(8,128)(2,1)S(1)} %get-tuple-element.141), channel_id=1, source_target_pairs={{0,1},{1,0},{2,3},{3,2},{4,5},{5,4},{6,7},{7,6},{8,9},{9,8},{10,11... | collective-permute-start | bytes 393224 | tf_op jit(solution)/shard_map/ppermute | solution.py:585
  20.2 3.4 %collective-permute-start.5 = (bf16[512,128]{1,0:T(8,128)(2,1)S(1)}, bf16[512,128]{1,0:T(8,128)(2,1)S(1)}, u32[]{:S(2)}, u32[]{:S(2)}) collective-permute-start(bf16[512,128]{1,0:T(8,128)(2,1)S(1)} %get-tuple-element.140), channel_id=1, source_target_pairs={{0,1},{1,0},{2,3},{3,2},{4,5},{5,4},{6,7},{7,6},{8,9},{9,8},{10,11... | collective-permute-start | bytes 393224 | tf_op jit(solution)/shard_map/ppermute | solution.py:585
  25.5 2.5 %collective-permute-start.7 = (bf16[1024,128]{1,0:T(8,128)(2,1)S(1)}, bf16[1024,128]{1,0:T(8,128)(2,1)S(1)}, u32[]{:S(2)}, u32[]{:S(2)}) collective-permute-start(bf16[1024,128]{1,0:T(8,128)(2,1)S(1)} %collective-permute-done.1.mine_keys_ref), channel_id=1, source_target_pairs={{0,1},{1,0},{2,3},{3,2},{4,5},{5,4},{6,7},{7,6},{8,9},{9,8},{10,11... | collective-permute-start | bytes 786440 | tf_op jit(solution)/shard_map/ppermute | solution.py:582
  26.0 2.0 %collective-permute-start.8 = (bf16[1024,128]{1,0:T(8,128)(2,1)S(1)}, bf16[1024,128]{1,0:T(8,128)(2,1)S(1)}, u32[]{:S(2)}, u32[]{:S(2)}) collective-permute-start(bf16[1024,128]{1,0:T(8,128)(2,1)S(1)} %collective-permute-done.6.mine_values_ref), channel_id=1, source_target_pairs={{0,1},{1,0},{2,3},{3,2},{4,5},{5,4},{6,7},{7,6},{8,9},{9,8},{10,11... | collective-permute-start | bytes 786440 | tf_op jit(solution)/shard_map/ppermute | solution.py:585
  30.4 3.8 %collective-permute-start.9 = (bf16[1,128,1024]{2,1,0:T(8,128)(2,1)S(1)}, bf16[1,128,1024]{2,1,0:T(8,128)(2,1)S(1)}, u32[]{:S(2)}, u32[]{:S(2)}) collective-permute-start(bf16[1,128,1024]{2,1,0:T(8,128)(2,1)S(1)} %get-tuple-element.109), channel_id=1, source_target_pairs={{0,1},{1,0},{2,3},{3,2},{4,5},{5,4},{6,7},{7,6},{8,9},{9,8},{10,11... | collective-permute-start | bytes 786440 | tf_op jit(solution)/shard_map/ppermute | solution.py:672
  34.7 8.4 %collective-permute-start.10 = (bf16[128,1024]{1,0:T(8,128)(2,1)S(1)}, bf16[128,1024]{1,0:T(8,128)(2,1)S(1)}, u32[]{:S(2)}, u32[]{:S(2)}) collective-permute-start(bf16[128,1024]{1,0:T(8,128)(2,1)S(1)} %project_onward.2), channel_id=1, source_target_pairs={{0,2},{1,3},{2,0},{3,1},{4,6},{5,7},{6,4},{7,5},{8,10},{9,11},{10,... | collective-permute-start | bytes 786440 | tf_op jit(solution)/shard_map/ppermute | solution.py:639
  38.9 1.4 %collective-permute-start.11 = (bf16[1,64,1024]{2,1,0:T(8,128)(2,1)S(1)}, bf16[1,64,1024]{2,1,0:T(8,128)(2,1)S(1)}, u32[]{:S(2)}, u32[]{:S(2)}) collective-permute-start(bf16[1,64,1024]{2,1,0:T(8,128)(2,1)S(1)} %get-tuple-element.124), channel_id=1, source_target_pairs={{0,1},{1,0},{2,3},{3,2},{4,5},{5,4},{6,7},{7,6},{8,9},{9,8},{10,11... | collective-permute-start | bytes 393224 | tf_op jit(solution)/shard_map/ppermute | solution.py:672
  39.0 1.5 %collective-permute-start.12 = (bf16[1,64,1024]{2,1,0:T(8,128)(2,1)S(1)}, bf16[1,64,1024]{2,1,0:T(8,128)(2,1)S(1)}, u32[]{:S(2)}, u32[]{:S(2)}) collective-permute-start(bf16[1,64,1024]{2,1,0:T(8,128)(2,1)S(1)} %get-tuple-element.125), channel_id=1, source_target_pairs={{0,1},{1,0},{2,3},{3,2},{4,5},{5,4},{6,7},{7,6},{8,9},{9,8},{10,11... | collective-permute-start | bytes 393224 | tf_op jit(solution)/shard_map/ppermute | solution.py:672
  41.0 8.6 %collective-permute-start.17 = (bf16[128,1024]{1,0:T(8,128)(2,1)S(1)}, bf16[128,1024]{1,0:T(8,128)(2,1)S(1)}, u32[]{:S(2)}, u32[]{:S(2)}) collective-permute-start(bf16[128,1024]{1,0:T(8,128)(2,1)S(1)} %project_onward.3), channel_id=1, source_target_pairs={{0,2},{1,3},{2,0},{3,1},{4,6},{5,7},{6,4},{7,5},{8,10},{9,11},{10,... | collective-permute-start | bytes 786440 | tf_op jit(solution)/shard_map/ppermute | solution.py:639
  43.8 1.4 %collective-permute-start.13 = (bf16[64,1024]{1,0:T(8,128)(2,1)S(1)}, bf16[64,1024]{1,0:T(8,128)(2,1)S(1)}, u32[]{:S(2)}, u32[]{:S(2)}) collective-permute-start(bf16[64,1024]{1,0:T(8,128)(2,1)S(1)} %get-tuple-element.129), channel_id=1, source_target_pairs={{0,1},{1,0},{2,3},{3,2},{4,5},{5,4},{6,7},{7,6},{8,9},{9,8},{10,11... | collective-permute-start | bytes 393224 | tf_op jit(solution)/shard_map/ppermute | solution.py:682
  43.9 1.5 %collective-permute-start.14 = (bf16[64,1024]{1,0:T(8,128)(2,1)S(1)}, bf16[64,1024]{1,0:T(8,128)(2,1)S(1)}, u32[]{:S(2)}, u32[]{:S(2)}) collective-permute-start(bf16[64,1024]{1,0:T(8,128)(2,1)S(1)} %get-tuple-element.130), channel_id=1, source_target_pairs={{0,1},{1,0},{2,3},{3,2},{4,5},{5,4},{6,7},{7,6},{8,9},{9,8},{10,11... | collective-permute-start | bytes 393224 | tf_op jit(solution)/shard_map/ppermute | solution.py:682
  44.4 1.3 %collective-permute-start.15 = (bf16[64,1024]{1,0:T(8,128)(2,1)S(1)}, bf16[64,1024]{1,0:T(8,128)(2,1)S(1)}, u32[]{:S(2)}, u32[]{:S(2)}) collective-permute-start(bf16[64,1024]{1,0:T(8,128)(2,1)S(1)} %get-tuple-element.131), channel_id=1, source_target_pairs={{0,1},{1,0},{2,3},{3,2},{4,5},{5,4},{6,7},{7,6},{8,9},{9,8},{10,11... | collective-permute-start | bytes 393224 | tf_op jit(solution)/shard_map/ppermute | solution.py:682
  44.5 1.5 %collective-permute-start.16 = (bf16[64,1024]{1,0:T(8,128)(2,1)S(1)}, bf16[64,1024]{1,0:T(8,128)(2,1)S(1)}, u32[]{:S(2)}, u32[]{:S(2)}) collective-permute-start(bf16[64,1024]{1,0:T(8,128)(2,1)S(1)} %get-tuple-element.132), channel_id=1, source_target_pairs={{0,1},{1,0},{2,3},{3,2},{4,5},{5,4},{6,7},{7,6},{8,9},{9,8},{10,11... | collective-permute-start | bytes 393224 | tf_op jit(solution)/shard_map/ppermute | solution.py:682
  45.9 5.7 %copy-start = (bf16[1024]{0:T(1024)(128)(2,1)S(1)}, bf16[1024]{0:T(1024)(128)(2,1)}, u32[]{:S(2)}) copy-start(bf16[1024]{0:T(1024)(128)(2,1)} %param.19) | copy-start | bytes 6148
  49.7 1.2 %collective-permute-start.18 = (f32[16,128]{1,0:T(8,128)S(1)}, f32[16,128]{1,0:T(8,128)S(1)}, u32[]{:S(2)}, u32[]{:S(2)}) collective-permute-start(f32[16,128]{1,0:T(8,128)S(1)} %constant_dynamic-update-slice_fusion), channel_id=1, source_target_pairs={{0,1},{1,0},{2,3},{3,2},{4,5},{5,4},{6,7},{7,6},{8,9},{9,8},{10,11... | collective-permute-start | bytes 24584 | tf_op jit(solution)/shard_map/ppermute | solution.py:699
  50.9 3.7 %collective-permute-start.19 = (f32[16,128]{1,0:T(8,128)S(1)}, f32[16,128]{1,0:T(8,128)S(1)}, u32[]{:S(2)}, u32[]{:S(2)}) collective-permute-start(f32[16,128]{1,0:T(8,128)S(1)} %add.3.refs_2_), channel_id=1, source_target_pairs={{0,2},{1,3},{2,0},{3,1},{4,6},{5,7},{6,4},{7,5},{8,10},{9,11},{10,... | collective-permute-start | bytes 24584 | tf_op jit(solution)/shard_map/ppermute | solution.py:701

commit v16 on v15

--- a/solution.py
+++ b/solution.py
@@ -121,7 +121,7 @@
     return copies
 
 
-def weight_copies(weight_ref, target, sems, sibling, first=0):
+def weight_copies(weight_ref, target, sems, sibling):
     count, _, share = target.shape
     chips = weight_ref.shape[1] // (CORES * share)
     place = lax.axis_index("tp")
@@ -129,7 +129,7 @@
     held = 1 - core if sibling else core
     copies = []
     for k in range(count):
-        start = (lax.rem(chip + first + k, chips) * CORES + held) * share
+        start = (lax.rem(chip + k, chips) * CORES + held) * share
         copies.append(
             pltpu.make_async_copy(
                 weight_ref.at[:, pl.ds(pl.multiple_of(start, HD), share)],
@@ -274,8 +274,7 @@
     after, refs = refs[: 2 * count], refs[2 * count :]
     if with_weight:
         keep_ref, flipped_ref, sems = refs
-        first = 1 if part == 0 else 0
-        copies = start_all(weight_copies(weight_ref, keep_ref, sems, False, first))
+        copies = start_all(weight_copies(weight_ref, keep_ref, sems, False))
     else:
         (flipped_ref,) = refs
     source, valid = arrivals(step, sources)[part]
@@ -358,7 +357,7 @@
     got_refs, onward_refs = refs[:pieces], refs[pieces:]
     for k, onward_ref in enumerate(onward_refs, 1):
         onward_ref[...] = (
-            jnp.dot(attended_ref[...], weight_ref[k - 1], preferred_element_type=jnp.float32)
+            jnp.dot(attended_ref[...], weight_ref[k], preferred_element_type=jnp.float32)
             + from_sibling(got_refs, k - 1)
         ).astype(jnp.bfloat16)
 
@@ -548,15 +547,14 @@
     def attend_step(step, part, chosen, with_weight, states, held):
         flat = [x for cont in chosen for x in states[cont]]
         count = len(chosen)
-        kept = array((chips - 1 if part == 0 else 1, width, share), jnp.bfloat16)
         made = pl.pallas_call(
             functools.partial(
                 middle_kernel, step, part, sources, conts, chosen, len(held), with_weight
             ),
-            out_shape=state_shape * count + (kept,) * with_weight,
+            out_shape=state_shape * count + (weight_shape,) * with_weight,
             in_specs=[smem, smem] + [vmem] * (3 * count + len(held)) + [hbm] * with_weight,
             out_specs=(vmem,) * (2 * count + with_weight),
-            scratch_shapes=[flipped] + [pltpu.SemaphoreType.DMA(kept.shape[:1])] * with_weight,
+            scratch_shapes=[flipped] + [pltpu.SemaphoreType.DMA((chips,))] * with_weight,
             compiler_params=params,
             cost_estimate=cost(),
             name="attend_step",
@@ -585,17 +583,16 @@
             lax.ppermute(x, "tp", sibling)
             for x in jnp.split(mine_values, 2 if step < steps else 1)
         ]
-        before, mine = mine, (mine_keys, mine_values)
+        mine = (mine_keys, mine_values)
         rest, theirs = theirs, (their_keys, *their_values)
         if step > 1:
-            states, _ = attend_step(step - 1, 0, everyone[1:], False, states, before)
-            theirs, states = lax.optimization_barrier((theirs, states))
-            states, made = attend_step(step - 1, 1, everyone[1:], step == 2, states, rest)
-            keep_own = made[0] if step == 2 else keep_own
+            states, _ = attend_step(step - 1, 1, everyone[:1], False, states, rest)
+            theirs, first = lax.optimization_barrier((theirs, states[0]))
+            states = (first, *states[1:])
+            states, _ = attend_step(step - 1, 1, everyone[1:], False, states, rest)
         if step < steps:
-            states, made = attend_step(step, 0, everyone[:1], step == 1, states, mine)
-            states, _ = attend_step(step, 1, everyone[:1], False, states, theirs)
-            keep_far = made[0] if step == 1 else keep_far
+            states, made = attend_step(step, 0, everyone, step == 1, states, mine)
+            keep_weight = made[0] if step == 1 else keep_weight
 
     def attend_last(cont, state):
         pieces = swap_pieces[cont]
@@ -630,7 +627,7 @@
             compiler_params=params,
             cost_estimate=cost(),
             name="project_onward",
-        )(attended, keep_far, *got)
+        )(attended, keep_weight, *got)
         far = []
         for k in range(1, chips):
             to_chip = [
@@ -663,7 +660,7 @@
             compiler_params=params,
             cost_estimate=cost(),
             name="project_near",
-        )(*attended, keep_own, in_hbm(residual), *got)
+        )(*attended, keep_weight, in_hbm(residual), *got)
 
     swap_pieces = [1] + [2] * (conts - 1)
     attended, give = attend_last(0, states[0])

time: 56 us -> 53.1 us (0.948)
  Pallas kernels: 27.9 us -> 24.4 us
    pallas_call x4 -> x3, Pallas kernels: 10.4 us -> 6.92 us  [attend_step(): pl.pallas_call(functools.partial(middle_kernel, step, part, sources, cont...]
    ppermute x7, starting transfers between devices: 3.6 us -> 4.63 us  [shards(): lax.ppermute(x, 'tp', sibling)]
  transfers between devices with their start and end apart: 20 -> 20, of which waited for: 11 -> 11; matrix products, arithmetic and copies ran while one was open for 3% -> 3% of each run, Pallas kernels for 41% -> 37%
where the time goes in v16:
time: 53.1 us; the launch traced here: 52.7 us
  Pallas kernels  24.4 us (46%)
  starting transfers between devices  16.2 us (31%)
  waiting for transfers between devices  9.53 us (18%)
  local copies, waits for them, and re-layouts  1.76 us (3%)
  between operations  0.86 us (2%)
    pallas_call x3, Pallas kernels, attend_step(): pl.pallas_call(functools.partial(middle_kernel, step, part, sources, cont...  6.92 us
    pallas_call x2, Pallas kernels, attend_last(): pl.pallas_call(functools.partial(last_kernel, steps, sources, conts, cont...  5.03 us
    pallas_call x1, Pallas kernels, shards(): pl.pallas_call(functools.partial(first_kernel, sources, conts), out_shape...  4.86 us
    ppermute x7, starting transfers between devices, shards(): lax.ppermute(x, 'tp', sibling)  4.63 us
    ppermute x4, starting transfers between devices, shards(): lax.ppermute(x, ('ctx', 'tp'), across(step))  4.53 us
    ppermute x2, waiting for transfers between devices, onward(): far.append(lax.ppermute(parts[k - 1], 'tp', to_chip))  3.35 us
    ppermute x2, starting transfers between devices, shards(): their_keys = lax.ppermute(mine_keys, 'tp', sibling)  3.19 us
    ppermute x1, waiting for transfers between devices, shards(): lax.ppermute(squares, 'tp', [(t, (t // CORES + k) % chips * CORES + t % C...  2.22 us
  transfers between devices with their start and end apart: 20, of which 11 were waited for; matrix products, arithmetic and copies ran while one was open for 3% of the time, Pallas kernels for 37%

profile of v16, /device:TPU:0, one launch (start us, length us, event | category | flops | bytes accessed | tf_op | source)
XLA Modules:
  0.0 52.7 jit_solution(14957596432576710294)
XLA Ops:
  0.6 1.0 %pack_keys.1.keys_ref = bf16[1024,128]{1,0:T(8,128)(2,1)S(1)} custom-call(bf16[1024,256]{1,0:T(8,128)(2,1)} %keys_ref.1), custom_call_target="tpu_custom_call" | custom-call | flops 1024 | bytes 1024 | tf_op jit(solution)/shard_map/pack_keys/pallas_call | solution.py:463
  1.6 3.1 %collective-permute-start = (bf16[1024,128]{1,0:T(8,128)(2,1)S(1)}, bf16[1024,128]{1,0:T(8,128)(2,1)S(1)}, u32[]{:S(2)}, u32[]{:S(2)}) collective-permute-start(bf16[1024,128]{1,0:T(8,128)(2,1)S(1)} %pack_keys.1.keys_ref), channel_id=1, source_target_pairs={{0,4},{1,9},{2,6},{3,11},{4,0},{5,13},{6,2},{7,15},{8,12},{9,1},{1... | collective-permute-start | bytes 786440 | tf_op jit(solution)/shard_map/ppermute | solution.py:578
  4.7 1.1 %pack_values.1.values_ref = bf16[1024,128]{1,0:T(8,128)(2,1)S(1)} custom-call(bf16[1024,256]{1,0:T(8,128)(2,1)} %values_ref.1), custom_call_target="tpu_custom_call" | custom-call | flops 1024 | bytes 1024 | tf_op jit(solution)/shard_map/pack_values/pallas_call | solution.py:473
  5.9 0.8 %copy.13 = s32[8,2,4]{2,1,0:T(2,128)S(1)} copy(s32[8,2,4]{0,2,1:T(4,128)} %param.16) | data formatting | bytes 512 | tf_op args[6]
  6.7 0.9 %reshape.13.lists_ref = s32[512]{0:T(512)S(1)} reshape(s32[8,2,4,8]{3,2,1,0:T(4,128)} %param.15) | data formatting | bytes 4096 | tf_op jit(solution)/shard_map/reshape | solution.py:506
  7.6 4.9 %attend_own.1 = (f32[8,128,128]{2,1,0:T(8,128)S(1)}, f32[8,8,128]{2,1,0:T(8,128)S(1)}, f32[8,128,128]{2,1,0:T(8,128)S(1)}, f32[8,8,128]{2,1,0:T(8,128)S(1)}, bf1...) custom-call(s32[512]{0:T(512)S(1)} %reshape.13.lists_ref, ...), custom_call_target="tpu_custom_call" | custom-call | flops 1024 | bytes 1024 | tf_op jit(solution)/shard_map/attend_own/pallas_call | solution.py:515
  13.2 3.2 %collective-permute-start.3 = (bf16[1024,128]{1,0:T(8,128)(2,1)S(1)}, bf16[1024,128]{1,0:T(8,128)(2,1)S(1)}, u32[]{:S(2)}, u32[]{:S(2)}) collective-permute-start(bf16[1024,128]{1,0:T(8,128)(2,1)S(1)} %collective-permute-done.refs_2_), channel_id=1, source_target_pairs={{0,1},{1,0},{2,3},{3,2},{4,5},{5,4},{6,7},{7,6},{8,9},{9,8},{10,11... | collective-permute-start | bytes 786440 | tf_op jit(solution)/shard_map/ppermute | solution.py:580
  16.4 0.7 %collective-permute-done.2.refs_3_ = bf16[1024,128]{1,0:T(8,128)(2,1)S(1)} collective-permute-done((bf16[1024,128]{1,0:T(8,128)(2,1)S(1)}, bf16[1024,128]{1,0:T(8,128)(2,1)S(1)}, u32[]{:S(2)}, u32[]{:S(2)}) %collective-permute-start.2) | collective-permute-done | bytes 262176 | tf_op jit(solution)/shard_map/ppermute | solution.py:578
  17.8 2.4 %collective-permute-start.4 = (bf16[512,128]{1,0:T(8,128)(2,1)S(1)}, bf16[512,128]{1,0:T(8,128)(2,1)S(1)}, u32[]{:S(2)}, u32[]{:S(2)}) collective-permute-start(bf16[512,128]{1,0:T(8,128)(2,1)S(1)} %get-tuple-element.135), channel_id=1, source_target_pairs={{0,1},{1,0},{2,3},{3,2},{4,5},{5,4},{6,7},{7,6},{8,9},{9,8},{10,11... | collective-permute-start | bytes 393224 | tf_op jit(solution)/shard_map/ppermute | solution.py:583
  20.2 3.2 %attend_step.3 = (f32[8,128,128]{2,1,0:T(8,128)S(1)}, f32[8,8,128]{2,1,0:T(8,128)S(1)}, f32[8,128,128]{2,1,0:T(8,128)S(1)}, f32[8,8,128]{2,1,0:T(8,128)S(1)}, bf16[2,1024,1024]{2,1,0:T(8,128)(2,1)S(1)}) custom-call(s32[512]{0:T(512)S(1)} %reshape.13.lists_ref, s32[64]{0:T(128)S(1)} %reshape.14.counts_ref, ...), custom_call_target="tpu_custom_call" | custom-call | flops 1024 | bytes 1024 | tf_op jit(solution)/shard_map/attend_step/pallas_call | solution.py:550
  23.5 1.1 %collective-permute-start.8 = (bf16[1024,128]{1,0:T(8,128)(2,1)S(1)}, bf16[1024,128]{1,0:T(8,128)(2,1)S(1)}, u32[]{:S(2)}, u32[]{:S(2)}) collective-permute-start(bf16[1024,128]{1,0:T(8,128)(2,1)S(1)} %collective-permute-done.6.mine_values_ref), channel_id=1, source_target_pairs={{0,1},{1,0},{2,3},{3,2},{4,5},{5,4},{6,7},{7,6},{8,9},{9,8},{10,11... | collective-permute-start | bytes 786440 | tf_op jit(solution)/shard_map/ppermute | solution.py:583
  24.6 1.9 %attend_step.4 = (f32[8,128,128]{2,1,0:T(8,128)S(1)}, f32[8,8,128]{2,1,0:T(8,128)S(1)}) custom-call(s32[512]{0:T(512)S(1)} %reshape.13.lists_ref, s32[64]{0:T(128)S(1)} %reshape.14.counts_ref, bf16[8,128,128]{2,1,0:T(8,128)(2,1)S(1)} %get-tuple-element.68.refs_0_.q_ref, bf16[1024,128]{1,0:T(8,128)(2,1)S(1)} %collective-permute-done.3.refs_1_, ...), custom_call_target="tpu_custom_call" | custom-call | flops 1024 | bytes 1024 | tf_op jit(solution)/shard_map/attend_step/pallas_call | solution.py:550
  26.5 2.4 %attend_last.2 = (bf16[128,1024]{1,0:T(8,128)(2,1)S(1)}, bf16[1,128,1024]{2,1,0:T(8,128)(2,1)S(1)}) custom-call(s32[512]{0:T(512)S(1)} %reshape.13.lists_ref, s32[64]{0:T(128)S(1)} %reshape.14.counts_ref, bf16[8,128,128]{2,1,0:T(8,128)(2,1)S(1)} %get-tuple-element.68.refs_0_.q_ref, bf16[1024,128]{1,0:T(8,128)(2,1)S(1)} %collective-permute-done.1.mine_keys_ref, ...), custom_call_target="tpu_custom_call" | custom-call | flops 1024 | bytes 1024 | tf_op jit(solution)/shard_map/attend_last/pallas_call | solution.py:599
  29.5 1.9 %attend_step.5 = (f32[8,128,128]{2,1,0:T(8,128)S(1)}, f32[8,8,128]{2,1,0:T(8,128)S(1)}) custom-call(s32[512]{0:T(512)S(1)} %reshape.13.lists_ref, s32[64]{0:T(128)S(1)} %reshape.14.counts_ref, bf16[8,128,128]{2,1,0:T(8,128)(2,1)S(1)} %get-tuple-element.74.refs_1_.refs_0_.q_ref, bf16[1024,128]{1,0:T(8,128)(2,1)S(1)} %collective-permute-done.3.refs_1_, ...), custom_call_target="tpu_custom_call" | custom-call | flops 1024 | bytes 1024 | tf_op jit(solution)/shard_map/attend_step/pallas_call | solution.py:550
  31.8 1.6 %collective-permute-start.10 = (bf16[128,1024]{1,0:T(8,128)(2,1)S(1)}, bf16[128,1024]{1,0:T(8,128)(2,1)S(1)}, u32[]{:S(2)}, u32[]{:S(2)}) collective-permute-start(bf16[128,1024]{1,0:T(8,128)(2,1)S(1)} %project_onward.2), channel_id=1, source_target_pairs={{0,2},{1,3},{2,0},{3,1},{4,6},{5,7},{6,4},{7,5},{8,10},{9,11},{10,... | collective-permute-start | bytes 786440 | tf_op jit(solution)/shard_map/ppermute | solution.py:636
  33.4 2.6 %attend_last.3 = (bf16[128,1024]{1,0:T(8,128)(2,1)S(1)}, bf16[1,64,1024]{2,1,0:T(8,128)(2,1)S(1)}, bf16[1,64,1024]{2,1,0:T(8,128)(2,1)S(1)}) custom-call(s32[512]{0:T(512)S(1)} %reshape.13.lists_ref, s32[64]{0:T(128)S(1)} %reshape.14.counts_ref, bf16[8,128,128]{2,1,0:T(8,128)(2,1)S(1)} %get-tuple-element.74.refs_1_.refs_0_.q_ref, ...), custom_call_target="tpu_custom_call" | custom-call | flops 1024 | bytes 1024 | tf_op jit(solution)/shard_map/attend_last/pallas_call | solution.py:599
  36.6 0.8 %collective-permute-done.11.refs_0_ = bf16[1,64,1024]{2,1,0:T(8,128)(2,1)S(1)} collective-permute-done((bf16[1,64,1024]{2,1,0:T(8,128)(2,1)S(1)}, bf16[1,64,1024]{2,1,0:T(8,128)(2,1)S(1)}, u32[]{:S(2)}, u32[]{:S(2)}) %collective-permute-start.11) | collective-permute-done | bytes 131104 | tf_op jit(solution)/shard_map/ppermute | solution.py:669
  38.7 1.5 %collective-permute-done.10.refs_0_ = bf16[128,1024]{1,0:T(8,128)(2,1)S(1)} collective-permute-done((bf16[128,1024]{1,0:T(8,128)(2,1)S(1)}, bf16[128,1024]{1,0:T(8,128)(2,1)S(1)}, u32[]{:S(2)}, u32[]{:S(2)}) %collective-permute-start.10) | collective-permute-done | bytes 262176 | tf_op jit(solution)/shard_map/ppermute | solution.py:636
  43.0 1.6 %project_near.1 = (f32[128,1024]{1,0:T(8,128)S(1)}, f32[128,1024]{1,0:T(8,128)S(1)}) custom-call(bf16[128,1024]{1,0:T(8,128)(2,1)S(1)} %get-tuple-element.121.attended_ref.refs_0_, bf16[128,1024]{1,0:T(8,128)(2,1)S(1)} %get-tuple-element.122.attended_ref.refs_1_, bf16[2,1024,1024]{2,1,0:T(8,128)(2,1)S(1)} %get-tuple-element.114.weight_ref.refs_2_, ...), custom_call_target="tpu_custom_call" | custom-call | flops 1024 | bytes 1024 | tf_op jit(solution)/shard_map/project_near/pallas_call | solution.py:651
  44.8 1.9 %collective-permute-done.17.refs_0_ = bf16[128,1024]{1,0:T(8,128)(2,1)S(1)} collective-permute-done((bf16[128,1024]{1,0:T(8,128)(2,1)S(1)}, bf16[128,1024]{1,0:T(8,128)(2,1)S(1)}, u32[]{:S(2)}, u32[]{:S(2)}) %collective-permute-start.17) | collective-permute-done | bytes 262176 | tf_op jit(solution)/shard_map/ppermute | solution.py:636
  46.9 1.2 %collective-permute-done.18 = f32[16,128]{1,0:T(8,128)S(1)} collective-permute-done((f32[16,128]{1,0:T(8,128)S(1)}, f32[16,128]{1,0:T(8,128)S(1)}, u32[]{:S(2)}, u32[]{:S(2)}) %collective-permute-start.18) | collective-permute-done | bytes 8224 | tf_op jit(solution)/shard_map/ppermute | solution.py:696
  48.6 0.8 %stream.1 = bf16[2,128,1024]{2,1,0:T(8,128)(2,1)} custom-call(f32[128,1024]{1,0:T(8,128)S(1)} %get-tuple-element.129.refs_0_, f32[128,1024]{1,0:T(8,128)S(1)} %get-tuple-element.131.refs_1_), custom_call_target="tpu_custom_call" | custom-call | flops 1024 | bytes 1024 | tf_op jit(solution)/shard_map/stream/pallas_call | solution.py:706
  49.5 2.2 %collective-permute-done.19.refs_3_ = f32[16,128]{1,0:T(8,128)S(1)} collective-permute-done((f32[16,128]{1,0:T(8,128)S(1)}, f32[16,128]{1,0:T(8,128)S(1)}, u32[]{:S(2)}, u32[]{:S(2)}) %collective-permute-start.19) | collective-permute-done | bytes 8224 | tf_op jit(solution)/shard_map/ppermute | solution.py:698
  51.7 1.0 %norm.1 = bf16[2,128,1024]{2,1,0:T(8,128)(2,1)} custom-call(f32[128,1024]{1,0:T(8,128)S(1)} %get-tuple-element.129.refs_0_, f32[128,1024]{1,0:T(8,128)S(1)} %get-tuple-element.131.refs_1_, f32[16,128]{1,0:T(8,128)S(1)} %add.3.refs_2_, f32[16,128]{1,0:T(8,128)S(1)} %collective-permute-done.19.refs_3_, bf16[1,1024]{1,0:T(2,128)(2,1)S(1)} %reshape.15.refs_4_), custom_call_target="tpu_custom_call" | custom-call | flops 1024 | bytes 1024 | tf_op jit(solution)/shard_map/norm/pallas_call | solution.py:715
  (42 shorter events, 8.3 us)
Async XLA Ops:
  1.6 10.9 %collective-permute-start = (bf16[1024,128]{1,0:T(8,128)(2,1)S(1)}, bf16[1024,128]{1,0:T(8,128)(2,1)S(1)}, u32[]{:S(2)}, u32[]{:S(2)}) collective-permute-start(bf16[1024,128]{1,0:T(8,128)(2,1)S(1)} %pack_keys.1.keys_ref), channel_id=1, source_target_pairs={{0,4},{1,9},{2,6},{3,11},{4,0},{5,13},{6,2},{7,15},{8,12},{9,1},{1... | collective-permute-start | bytes 786440 | tf_op jit(solution)/shard_map/ppermute | solution.py:578
  5.8 11.3 %collective-permute-start.2 = (bf16[1024,128]{1,0:T(8,128)(2,1)S(1)}, bf16[1024,128]{1,0:T(8,128)(2,1)S(1)}, u32[]{:S(2)}, u32[]{:S(2)}) collective-permute-start(bf16[1024,128]{1,0:T(8,128)(2,1)S(1)} %pack_values.1.values_ref), channel_id=1, source_target_pairs={{0,4},{1,9},{2,6},{3,11},{4,0},{5,13},{6,2},{7,15},{8,12},{9,1},{1... | collective-permute-start | bytes 786440 | tf_op jit(solution)/shard_map/ppermute | solution.py:578
  12.5 11.0 %collective-permute-start.1 = (bf16[1024,128]{1,0:T(8,128)(2,1)S(1)}, bf16[1024,128]{1,0:T(8,128)(2,1)S(1)}, u32[]{:S(2)}, u32[]{:S(2)}) collective-permute-start(bf16[1024,128]{1,0:T(8,128)(2,1)S(1)} %collective-permute-done.refs_2_), channel_id=1, source_target_pairs={{1,5},{3,7},{5,1},{7,3},{9,13},{11,15},{13,9},{15,11},{17,21},{19,... | collective-permute-start | bytes 786440 | tf_op jit(solution)/shard_map/ppermute | solution.py:578
  13.2 10.3 %collective-permute-start.3 = (bf16[1024,128]{1,0:T(8,128)(2,1)S(1)}, bf16[1024,128]{1,0:T(8,128)(2,1)S(1)}, u32[]{:S(2)}, u32[]{:S(2)}) collective-permute-start(bf16[1024,128]{1,0:T(8,128)(2,1)S(1)} %collective-permute-done.refs_2_), channel_id=1, source_target_pairs={{0,1},{1,0},{2,3},{3,2},{4,5},{5,4},{6,7},{7,6},{8,9},{9,8},{10,11... | collective-permute-start | bytes 786440 | tf_op jit(solution)/shard_map/ppermute | solution.py:580
  17.1 6.4 %collective-permute-start.6 = (bf16[1024,128]{1,0:T(8,128)(2,1)S(1)}, bf16[1024,128]{1,0:T(8,128)(2,1)S(1)}, u32[]{:S(2)}, u32[]{:S(2)}) collective-permute-start(bf16[1024,128]{1,0:T(8,128)(2,1)S(1)} %collective-permute-done.2.refs_3_), channel_id=1, source_target_pairs={{1,5},{3,7},{5,1},{7,3},{9,13},{11,15},{13,9},{15,11},{17,21},{19,... | collective-permute-start | bytes 786440 | tf_op jit(solution)/shard_map/ppermute | solution.py:578
  17.8 5.7 %collective-permute-start.4 = (bf16[512,128]{1,0:T(8,128)(2,1)S(1)}, bf16[512,128]{1,0:T(8,128)(2,1)S(1)}, u32[]{:S(2)}, u32[]{:S(2)}) collective-permute-start(bf16[512,128]{1,0:T(8,128)(2,1)S(1)} %get-tuple-element.135), channel_id=1, source_target_pairs={{0,1},{1,0},{2,3},{3,2},{4,5},{5,4},{6,7},{7,6},{8,9},{9,8},{10,11... | collective-permute-start | bytes 393224 | tf_op jit(solution)/shard_map/ppermute | solution.py:583
  20.2 3.3 %collective-permute-start.5 = (bf16[512,128]{1,0:T(8,128)(2,1)S(1)}, bf16[512,128]{1,0:T(8,128)(2,1)S(1)}, u32[]{:S(2)}, u32[]{:S(2)}) collective-permute-start(bf16[512,128]{1,0:T(8,128)(2,1)S(1)} %get-tuple-element.134), channel_id=1, source_target_pairs={{0,1},{1,0},{2,3},{3,2},{4,5},{5,4},{6,7},{7,6},{8,9},{9,8},{10,11... | collective-permute-start | bytes 393224 | tf_op jit(solution)/shard_map/ppermute | solution.py:583
  23.5 3.0 %collective-permute-start.8 = (bf16[1024,128]{1,0:T(8,128)(2,1)S(1)}, bf16[1024,128]{1,0:T(8,128)(2,1)S(1)}, u32[]{:S(2)}, u32[]{:S(2)}) collective-permute-start(bf16[1024,128]{1,0:T(8,128)(2,1)S(1)} %collective-permute-done.6.mine_values_ref), channel_id=1, source_target_pairs={{0,1},{1,0},{2,3},{3,2},{4,5},{5,4},{6,7},{7,6},{8,9},{9,8},{10,11... | collective-permute-start | bytes 786440 | tf_op jit(solution)/shard_map/ppermute | solution.py:583
  24.6 1.9 %collective-permute-start.7 = (bf16[1024,128]{1,0:T(8,128)(2,1)S(1)}, bf16[1024,128]{1,0:T(8,128)(2,1)S(1)}, u32[]{:S(2)}, u32[]{:S(2)}) collective-permute-start(bf16[1024,128]{1,0:T(8,128)(2,1)S(1)} %collective-permute-done.1.mine_keys_ref), channel_id=1, source_target_pairs={{0,1},{1,0},{2,3},{3,2},{4,5},{5,4},{6,7},{7,6},{8,9},{9,8},{10,11... | collective-permute-start | bytes 786440 | tf_op jit(solution)/shard_map/ppermute | solution.py:580
  28.9 2.4 %collective-permute-start.9 = (bf16[1,128,1024]{2,1,0:T(8,128)(2,1)S(1)}, bf16[1,128,1024]{2,1,0:T(8,128)(2,1)S(1)}, u32[]{:S(2)}, u32[]{:S(2)}) collective-permute-start(bf16[1,128,1024]{2,1,0:T(8,128)(2,1)S(1)} %get-tuple-element.107), channel_id=1, source_target_pairs={{0,1},{1,0},{2,3},{3,2},{4,5},{5,4},{6,7},{7,6},{8,9},{9,8},{10,11... | collective-permute-start | bytes 786440 | tf_op jit(solution)/shard_map/ppermute | solution.py:669
  31.8 8.3 %collective-permute-start.10 = (bf16[128,1024]{1,0:T(8,128)(2,1)S(1)}, bf16[128,1024]{1,0:T(8,128)(2,1)S(1)}, u32[]{:S(2)}, u32[]{:S(2)}) collective-permute-start(bf16[128,1024]{1,0:T(8,128)(2,1)S(1)} %project_onward.2), channel_id=1, source_target_pairs={{0,2},{1,3},{2,0},{3,1},{4,6},{5,7},{6,4},{7,5},{8,10},{9,11},{10,... | collective-permute-start | bytes 786440 | tf_op jit(solution)/shard_map/ppermute | solution.py:636
  36.0 1.4 %collective-permute-start.11 = (bf16[1,64,1024]{2,1,0:T(8,128)(2,1)S(1)}, bf16[1,64,1024]{2,1,0:T(8,128)(2,1)S(1)}, u32[]{:S(2)}, u32[]{:S(2)}) collective-permute-start(bf16[1,64,1024]{2,1,0:T(8,128)(2,1)S(1)} %get-tuple-element.119), channel_id=1, source_target_pairs={{0,1},{1,0},{2,3},{3,2},{4,5},{5,4},{6,7},{7,6},{8,9},{9,8},{10,11... | collective-permute-start | bytes 393224 | tf_op jit(solution)/shard_map/ppermute | solution.py:669
  36.1 1.5 %collective-permute-start.12 = (bf16[1,64,1024]{2,1,0:T(8,128)(2,1)S(1)}, bf16[1,64,1024]{2,1,0:T(8,128)(2,1)S(1)}, u32[]{:S(2)}, u32[]{:S(2)}) collective-permute-start(bf16[1,64,1024]{2,1,0:T(8,128)(2,1)S(1)} %get-tuple-element.120), channel_id=1, source_target_pairs={{0,1},{1,0},{2,3},{3,2},{4,5},{5,4},{6,7},{7,6},{8,9},{9,8},{10,11... | collective-permute-start | bytes 393224 | tf_op jit(solution)/shard_map/ppermute | solution.py:669
  38.1 8.6 %collective-permute-start.17 = (bf16[128,1024]{1,0:T(8,128)(2,1)S(1)}, bf16[128,1024]{1,0:T(8,128)(2,1)S(1)}, u32[]{:S(2)}, u32[]{:S(2)}) collective-permute-start(bf16[128,1024]{1,0:T(8,128)(2,1)S(1)} %project_onward.3), channel_id=1, source_target_pairs={{0,2},{1,3},{2,0},{3,1},{4,6},{5,7},{6,4},{7,5},{8,10},{9,11},{10,... | collective-permute-start | bytes 786440 | tf_op jit(solution)/shard_map/ppermute | solution.py:636
  40.8 1.4 %collective-permute-start.13 = (bf16[64,1024]{1,0:T(8,128)(2,1)S(1)}, bf16[64,1024]{1,0:T(8,128)(2,1)S(1)}, u32[]{:S(2)}, u32[]{:S(2)}) collective-permute-start(bf16[64,1024]{1,0:T(8,128)(2,1)S(1)} %get-tuple-element.123), channel_id=1, source_target_pairs={{0,1},{1,0},{2,3},{3,2},{4,5},{5,4},{6,7},{7,6},{8,9},{9,8},{10,11... | collective-permute-start | bytes 393224 | tf_op jit(solution)/shard_map/ppermute | solution.py:679
  40.9 1.5 %collective-permute-start.14 = (bf16[64,1024]{1,0:T(8,128)(2,1)S(1)}, bf16[64,1024]{1,0:T(8,128)(2,1)S(1)}, u32[]{:S(2)}, u32[]{:S(2)}) collective-permute-start(bf16[64,1024]{1,0:T(8,128)(2,1)S(1)} %get-tuple-element.124), channel_id=1, source_target_pairs={{0,1},{1,0},{2,3},{3,2},{4,5},{5,4},{6,7},{7,6},{8,9},{9,8},{10,11... | collective-permute-start | bytes 393224 | tf_op jit(solution)/shard_map/ppermute | solution.py:679
  41.4 1.3 %collective-permute-start.15 = (bf16[64,1024]{1,0:T(8,128)(2,1)S(1)}, bf16[64,1024]{1,0:T(8,128)(2,1)S(1)}, u32[]{:S(2)}, u32[]{:S(2)}) collective-permute-start(bf16[64,1024]{1,0:T(8,128)(2,1)S(1)} %get-tuple-element.125), channel_id=1, source_target_pairs={{0,1},{1,0},{2,3},{3,2},{4,5},{5,4},{6,7},{7,6},{8,9},{9,8},{10,11... | collective-permute-start | bytes 393224 | tf_op jit(solution)/shard_map/ppermute | solution.py:679
  41.5 7.1 %copy-start = (bf16[1024]{0:T(1024)(128)(2,1)S(1)}, bf16[1024]{0:T(1024)(128)(2,1)}, u32[]{:S(2)}) copy-start(bf16[1024]{0:T(1024)(128)(2,1)} %param.19) | copy-start | bytes 6148
  41.5 1.5 %collective-permute-start.16 = (bf16[64,1024]{1,0:T(8,128)(2,1)S(1)}, bf16[64,1024]{1,0:T(8,128)(2,1)S(1)}, u32[]{:S(2)}, u32[]{:S(2)}) collective-permute-start(bf16[64,1024]{1,0:T(8,128)(2,1)S(1)} %get-tuple-element.126), channel_id=1, source_target_pairs={{0,1},{1,0},{2,3},{3,2},{4,5},{5,4},{6,7},{7,6},{8,9},{9,8},{10,11... | collective-permute-start | bytes 393224 | tf_op jit(solution)/shard_map/ppermute | solution.py:679
  46.8 1.2 %collective-permute-start.18 = (f32[16,128]{1,0:T(8,128)S(1)}, f32[16,128]{1,0:T(8,128)S(1)}, u32[]{:S(2)}, u32[]{:S(2)}) collective-permute-start(f32[16,128]{1,0:T(8,128)S(1)} %constant_dynamic-update-slice_fusion), channel_id=1, source_target_pairs={{0,1},{1,0},{2,3},{3,2},{4,5},{5,4},{6,7},{7,6},{8,9},{9,8},{10,11... | collective-permute-start | bytes 24584 | tf_op jit(solution)/shard_map/ppermute | solution.py:696
  48.1 3.7 %collective-permute-start.19 = (f32[16,128]{1,0:T(8,128)S(1)}, f32[16,128]{1,0:T(8,128)S(1)}, u32[]{:S(2)}, u32[]{:S(2)}) collective-permute-start(f32[16,128]{1,0:T(8,128)S(1)} %add.3.refs_2_), channel_id=1, source_target_pairs={{0,2},{1,3},{2,0},{3,1},{4,6},{5,7},{6,4},{7,5},{8,10},{9,11},{10,... | collective-permute-start | bytes 24584 | tf_op jit(solution)/shard_map/ppermute | solution.py:698

commit v17 on v16

--- a/solution.py
+++ b/solution.py
@@ -155,7 +155,7 @@
 ):
     states, refs = by_cont(refs[: 2 * conts]), refs[2 * conts :]
     q_refs, refs = refs[:conts], refs[conts:]
-    give_ref, weight_sems, *refs = refs[0], refs[-1], *refs[1:-1]
+    (give_ref, keep_ref), weight_sems, refs = refs[:2], refs[-1], refs[2:-1]
     flipped_ref, rows_ref, ck_ref, cv_ref, own_ref, sems = refs
     heads, _, length = q_refs[0].shape
     lanes = group_lanes(heads)
@@ -166,7 +166,10 @@
             pltpu.make_async_copy(cont_keys_ref.at[:, :, lanes], ck_ref, sems.at[2]),
         ]
     )
-    fetched = start_all(weight_copies(weight_ref, give_ref, weight_sems, True))
+    fetched = start_all(
+        weight_copies(weight_ref, give_ref, weight_sems.at[0], True)
+        + weight_copies(weight_ref, keep_ref, weight_sems.at[1], False)
+    )
     place = conts, sources, lax.axis_index("ctx")
     both_ways([values_ref], flipped_ref)
     copies[0].wait()
@@ -516,9 +519,9 @@
         functools.partial(first_kernel, sources, conts),
         out_shape=state_shape * conts
         + (array((heads, HD, length), jnp.bfloat16),) * conts
-        + (weight_shape,),
+        + (weight_shape,) * 2,
         in_specs=[smem, smem, vmem, vmem] + [hbm] * 4,
-        out_specs=(vmem,) * (3 * conts + 1),
+        out_specs=(vmem,) * (3 * conts + 2),
         scratch_shapes=[
             flipped,
             pltpu.VMEM(queries.shape, jnp.bfloat16),
@@ -526,7 +529,7 @@
             pltpu.VMEM((conts, length, HD), jnp.bfloat16),
             pltpu.VMEM((conts, HD, length), jnp.bfloat16),
             pltpu.SemaphoreType.DMA((3,)),
-            pltpu.SemaphoreType.DMA((chips,)),
+            pltpu.SemaphoreType.DMA((2, chips)),
         ],
         compiler_params=params,
         cost_estimate=cost(),
@@ -542,7 +545,7 @@
         in_hbm(out_weight),
     )
     states = tuple(made[2 * c : 2 * c + 2] for c in range(conts))
-    *qs, give_weight = made[2 * conts :]
+    *qs, give_weight, keep_weight = made[2 * conts :]
 
     def attend_step(step, part, chosen, with_weight, states, held):
         flat = [x for cont in chosen for x in states[cont]]
@@ -583,16 +586,15 @@
             lax.ppermute(x, "tp", sibling)
             for x in jnp.split(mine_values, 2 if step < steps else 1)
         ]
-        mine = (mine_keys, mine_values)
+        before, mine = mine, (mine_keys, mine_values)
         rest, theirs = theirs, (their_keys, *their_values)
         if step > 1:
-            states, _ = attend_step(step - 1, 1, everyone[:1], False, states, rest)
-            theirs, first = lax.optimization_barrier((theirs, states[0]))
-            states = (first, *states[1:])
+            states, _ = attend_step(step - 1, 0, everyone[1:], False, states, before)
+            theirs, states = lax.optimization_barrier((theirs, states))
             states, _ = attend_step(step - 1, 1, everyone[1:], False, states, rest)
         if step < steps:
-            states, made = attend_step(step, 0, everyone, step == 1, states, mine)
-            keep_weight = made[0] if step == 1 else keep_weight
+            states, _ = attend_step(step, 0, everyone[:1], False, states, mine)
+            states, _ = attend_step(step, 1, everyone[:1], False, states, theirs)
 
     def attend_last(cont, state):
         pieces = swap_pieces[cont]

time: 53.1 us -> 53.6 us (level)
  starting transfers between devices: 16.2 us -> 13.6 us
  Pallas kernels: 24.4 us -> 26.1 us
  waiting for transfers between devices: 9.53 us -> 10.8 us
    ppermute x2, starting transfers between devices: 3.19 us -> 0.64 us  [shards(): their_keys = lax.ppermute(mine_keys, 'tp', sibling)]
    ppermute x4, waiting for transfers between devices: 0.75 us -> 2.04 us  [shards(): lax.ppermute(x, ('ctx', 'tp'), across(step))]
    pallas_call x1, Pallas kernels: 4.86 us -> 6.13 us  [shards(): pl.pallas_call(functools.partial(first_kernel, sources, conts), out_shape...]
    pallas_call x3 -> x4, Pallas kernels: 6.92 us -> 7.44 us  [attend_step(): pl.pallas_call(functools.partial(middle_kernel, step, part, sources, cont...]
  transfers between devices with their start and end apart: 20 -> 20, of which waited for: 11 -> 11; matrix products, arithmetic and copies ran while one was open for 3% -> 3% of each run, Pallas kernels for 37% -> 40%
where the time goes in v17:
time: 53.6 us; the launch traced here: 53.2 us
  Pallas kernels  26.1 us (49%)
  starting transfers between devices  13.6 us (25%)
  waiting for transfers between devices  10.8 us (20%)
  local copies, waits for them, and re-layouts  1.76 us (3%)
  between operations  0.86 us (2%)
    pallas_call x4, Pallas kernels, attend_step(): pl.pallas_call(functools.partial(middle_kernel, step, part, sources, cont...  7.44 us
    pallas_call x1, Pallas kernels, shards(): pl.pallas_call(functools.partial(first_kernel, sources, conts), out_shape...  6.13 us
    pallas_call x2, Pallas kernels, attend_last(): pl.pallas_call(functools.partial(last_kernel, steps, sources, conts, cont...  5.04 us
    ppermute x7, starting transfers between devices, shards(): lax.ppermute(x, 'tp', sibling)  4.58 us
    ppermute x4, starting transfers between devices, shards(): lax.ppermute(x, ('ctx', 'tp'), across(step))  4.51 us
    ppermute x2, waiting for transfers between devices, onward(): far.append(lax.ppermute(parts[k - 1], 'tp', to_chip))  3.35 us
    ppermute x1, waiting for transfers between devices, shards(): lax.ppermute(squares, 'tp', [(t, (t // CORES + k) % chips * CORES + t % C...  2.23 us
    ppermute x2, starting transfers between devices, onward(): far.append(lax.ppermute(parts[k - 1], 'tp', to_chip))  2.16 us
  transfers between devices with their start and end apart: 20, of which 11 were waited for; matrix products, arithmetic and copies ran while one was open for 3% of the time, Pallas kernels for 40%

profile of v17, /device:TPU:0, one launch (start us, length us, event | category | flops | bytes accessed | tf_op | source)
XLA Modules:
  0.0 53.2 jit_solution(13261852249154561371)
XLA Ops:
  0.6 1.0 %pack_keys.1.keys_ref = bf16[1024,128]{1,0:T(8,128)(2,1)S(1)} custom-call(bf16[1024,256]{1,0:T(8,128)(2,1)} %keys_ref.1), custom_call_target="tpu_custom_call" | custom-call | flops 1024 | bytes 1024 | tf_op jit(solution)/shard_map/pack_keys/pallas_call | solution.py:466
  1.6 3.1 %collective-permute-start = (bf16[1024,128]{1,0:T(8,128)(2,1)S(1)}, bf16[1024,128]{1,0:T(8,128)(2,1)S(1)}, u32[]{:S(2)}, u32[]{:S(2)}) collective-permute-start(bf16[1024,128]{1,0:T(8,128)(2,1)S(1)} %pack_keys.1.keys_ref), channel_id=1, source_target_pairs={{0,4},{1,9},{2,6},{3,11},{4,0},{5,13},{6,2},{7,15},{8,12},{9,1},{1... | collective-permute-start | bytes 786440 | tf_op jit(solution)/shard_map/ppermute | solution.py:581
  4.7 1.1 %pack_values.1.values_ref = bf16[1024,128]{1,0:T(8,128)(2,1)S(1)} custom-call(bf16[1024,256]{1,0:T(8,128)(2,1)} %values_ref.1), custom_call_target="tpu_custom_call" | custom-call | flops 1024 | bytes 1024 | tf_op jit(solution)/shard_map/pack_values/pallas_call | solution.py:476
  5.9 0.8 %copy.13 = s32[8,2,4]{2,1,0:T(2,128)S(1)} copy(s32[8,2,4]{0,2,1:T(4,128)} %param.16) | data formatting | bytes 512 | tf_op args[6]
  6.7 0.9 %reshape.13.lists_ref = s32[512]{0:T(512)S(1)} reshape(s32[8,2,4,8]{3,2,1,0:T(4,128)} %param.15) | data formatting | bytes 4096 | tf_op jit(solution)/shard_map/reshape | solution.py:509
  7.6 6.1 %attend_own.1 = (f32[8,128,128]{2,1,0:T(8,128)S(1)}, f32[8,8,128]{2,1,0:T(8,128)S(1)}, f32[8,128,128]{2,1,0:T(8,128)S(1)}, f32[8,8,128]{2,1,0:T(8,128)S(1)}, bf1...) custom-call(s32[512]{0:T(512)S(1)} %reshape.13.lists_ref, ...), custom_call_target="tpu_custom_call" | custom-call | flops 1024 | bytes 1024 | tf_op jit(solution)/shard_map/attend_own/pallas_call | solution.py:518
  15.1 2.0 %collective-permute-done.3.refs_2_ = bf16[1024,128]{1,0:T(8,128)(2,1)S(1)} collective-permute-done((bf16[1024,128]{1,0:T(8,128)(2,1)S(1)}, bf16[1024,128]{1,0:T(8,128)(2,1)S(1)}, u32[]{:S(2)}, u32[]{:S(2)}) %collective-permute-start.3) | collective-permute-done | bytes 262176 | tf_op jit(solution)/shard_map/ppermute | solution.py:581
  17.8 2.4 %collective-permute-start.4 = (bf16[512,128]{1,0:T(8,128)(2,1)S(1)}, bf16[512,128]{1,0:T(8,128)(2,1)S(1)}, u32[]{:S(2)}, u32[]{:S(2)}) collective-permute-start(bf16[512,128]{1,0:T(8,128)(2,1)S(1)} %get-tuple-element.139), channel_id=1, source_target_pairs={{0,1},{1,0},{2,3},{3,2},{4,5},{5,4},{6,7},{7,6},{8,9},{9,8},{10,11... | collective-permute-start | bytes 393224 | tf_op jit(solution)/shard_map/ppermute | solution.py:586
  20.2 1.9 %attend_step.4 = (f32[8,128,128]{2,1,0:T(8,128)S(1)}, f32[8,8,128]{2,1,0:T(8,128)S(1)}) custom-call(s32[512]{0:T(512)S(1)} %reshape.13.lists_ref, s32[64]{0:T(128)S(1)} %reshape.14.counts_ref, bf16[8,128,128]{2,1,0:T(8,128)(2,1)S(1)} %get-tuple-element.70.refs_0_.q_ref, bf16[1024,128]{1,0:T(8,128)(2,1)S(1)} %collective-permute-done.refs_1_, ...), custom_call_target="tpu_custom_call" | custom-call | flops 1024 | bytes 1024 | tf_op jit(solution)/shard_map/attend_step/pallas_call | solution.py:553
  22.1 1.9 %attend_step.5 = (f32[8,128,128]{2,1,0:T(8,128)S(1)}, f32[8,8,128]{2,1,0:T(8,128)S(1)}) custom-call(s32[512]{0:T(512)S(1)} %reshape.13.lists_ref, s32[64]{0:T(128)S(1)} %reshape.14.counts_ref, bf16[8,128,128]{2,1,0:T(8,128)(2,1)S(1)} %get-tuple-element.70.refs_0_.q_ref, bf16[1024,128]{1,0:T(8,128)(2,1)S(1)} %collective-permute-done.2.refs_1_, ...), custom_call_target="tpu_custom_call" | custom-call | flops 1024 | bytes 1024 | tf_op jit(solution)/shard_map/attend_step/pallas_call | solution.py:553
  24.0 1.1 %collective-permute-start.8 = (bf16[1024,128]{1,0:T(8,128)(2,1)S(1)}, bf16[1024,128]{1,0:T(8,128)(2,1)S(1)}, u32[]{:S(2)}, u32[]{:S(2)}) collective-permute-start(bf16[1024,128]{1,0:T(8,128)(2,1)S(1)} %collective-permute-done.6.mine_values_ref), channel_id=1, source_target_pairs={{0,1},{1,0},{2,3},{3,2},{4,5},{5,4},{6,7},{7,6},{8,9},{9,8},{10,11... | collective-permute-start | bytes 786440 | tf_op jit(solution)/shard_map/ppermute | solution.py:586
  25.1 1.9 %attend_step.6 = (f32[8,128,128]{2,1,0:T(8,128)S(1)}, f32[8,8,128]{2,1,0:T(8,128)S(1)}) custom-call(s32[512]{0:T(512)S(1)} %reshape.13.lists_ref, s32[64]{0:T(128)S(1)} %reshape.14.counts_ref, bf16[8,128,128]{2,1,0:T(8,128)(2,1)S(1)} %get-tuple-element.97.refs_0_.q_ref, bf16[1024,128]{1,0:T(8,128)(2,1)S(1)} %collective-permute-done.refs_1_, ...), custom_call_target="tpu_custom_call" | custom-call | flops 1024 | bytes 1024 | tf_op jit(solution)/shard_map/attend_step/pallas_call | solution.py:553
  27.0 2.4 %attend_last.2 = (bf16[128,1024]{1,0:T(8,128)(2,1)S(1)}, bf16[1,128,1024]{2,1,0:T(8,128)(2,1)S(1)}) custom-call(s32[512]{0:T(512)S(1)} %reshape.13.lists_ref, s32[64]{0:T(128)S(1)} %reshape.14.counts_ref, bf16[8,128,128]{2,1,0:T(8,128)(2,1)S(1)} %get-tuple-element.70.refs_0_.q_ref, bf16[1024,128]{1,0:T(8,128)(2,1)S(1)} %collective-permute-done.1.mine_keys_ref, ...), custom_call_target="tpu_custom_call" | custom-call | flops 1024 | bytes 1024 | tf_op jit(solution)/shard_map/attend_last/pallas_call | solution.py:601
  30.0 1.9 %attend_step.7 = (f32[8,128,128]{2,1,0:T(8,128)S(1)}, f32[8,8,128]{2,1,0:T(8,128)S(1)}) custom-call(s32[512]{0:T(512)S(1)} %reshape.13.lists_ref, s32[64]{0:T(128)S(1)} %reshape.14.counts_ref, bf16[8,128,128]{2,1,0:T(8,128)(2,1)S(1)} %get-tuple-element.97.refs_0_.q_ref, bf16[1024,128]{1,0:T(8,128)(2,1)S(1)} %collective-permute-done.2.refs_1_, ...), custom_call_target="tpu_custom_call" | custom-call | flops 1024 | bytes 1024 | tf_op jit(solution)/shard_map/attend_step/pallas_call | solution.py:553
  32.3 1.6 %collective-permute-start.10 = (bf16[128,1024]{1,0:T(8,128)(2,1)S(1)}, bf16[128,1024]{1,0:T(8,128)(2,1)S(1)}, u32[]{:S(2)}, u32[]{:S(2)}) collective-permute-start(bf16[128,1024]{1,0:T(8,128)(2,1)S(1)} %project_onward.2), channel_id=1, source_target_pairs={{0,2},{1,3},{2,0},{3,1},{4,6},{5,7},{6,4},{7,5},{8,10},{9,11},{10,... | collective-permute-start | bytes 786440 | tf_op jit(solution)/shard_map/ppermute | solution.py:638
  33.9 2.6 %attend_last.3 = (bf16[128,1024]{1,0:T(8,128)(2,1)S(1)}, bf16[1,64,1024]{2,1,0:T(8,128)(2,1)S(1)}, bf16[1,64,1024]{2,1,0:T(8,128)(2,1)S(1)}) custom-call(s32[512]{0:T(512)S(1)} %reshape.13.lists_ref, s32[64]{0:T(128)S(1)} %reshape.14.counts_ref, bf16[8,128,128]{2,1,0:T(8,128)(2,1)S(1)} %get-tuple-element.97.refs_0_.q_ref, ...), custom_call_target="tpu_custom_call" | custom-call | flops 1024 | bytes 1024 | tf_op jit(solution)/shard_map/attend_last/pallas_call | solution.py:601
  37.1 0.8 %collective-permute-done.11.refs_0_ = bf16[1,64,1024]{2,1,0:T(8,128)(2,1)S(1)} collective-permute-done((bf16[1,64,1024]{2,1,0:T(8,128)(2,1)S(1)}, bf16[1,64,1024]{2,1,0:T(8,128)(2,1)S(1)}, u32[]{:S(2)}, u32[]{:S(2)}) %collective-permute-start.11) | collective-permute-done | bytes 131104 | tf_op jit(solution)/shard_map/ppermute | solution.py:671
  39.1 1.5 %collective-permute-done.10.refs_0_ = bf16[128,1024]{1,0:T(8,128)(2,1)S(1)} collective-permute-done((bf16[128,1024]{1,0:T(8,128)(2,1)S(1)}, bf16[128,1024]{1,0:T(8,128)(2,1)S(1)}, u32[]{:S(2)}, u32[]{:S(2)}) %collective-permute-start.10) | collective-permute-done | bytes 262176 | tf_op jit(solution)/shard_map/ppermute | solution.py:638
  43.4 1.6 %project_near.1 = (f32[128,1024]{1,0:T(8,128)S(1)}, f32[128,1024]{1,0:T(8,128)S(1)}) custom-call(bf16[128,1024]{1,0:T(8,128)(2,1)S(1)} %get-tuple-element.125.attended_ref.refs_0_, bf16[128,1024]{1,0:T(8,128)(2,1)S(1)} %get-tuple-element.126.attended_ref.refs_1_, bf16[2,1024,1024]{2,1,0:T(8,128)(2,1)S(1)} %get-tuple-element.118.weight_ref.refs_2_, ...), custom_call_target="tpu_custom_call" | custom-call | flops 1024 | bytes 1024 | tf_op jit(solution)/shard_map/project_near/pallas_call | solution.py:653
  45.3 1.9 %collective-permute-done.17.refs_0_ = bf16[128,1024]{1,0:T(8,128)(2,1)S(1)} collective-permute-done((bf16[128,1024]{1,0:T(8,128)(2,1)S(1)}, bf16[128,1024]{1,0:T(8,128)(2,1)S(1)}, u32[]{:S(2)}, u32[]{:S(2)}) %collective-permute-start.17) | collective-permute-done | bytes 262176 | tf_op jit(solution)/shard_map/ppermute | solution.py:638
  47.4 1.2 %collective-permute-done.18 = f32[16,128]{1,0:T(8,128)S(1)} collective-permute-done((f32[16,128]{1,0:T(8,128)S(1)}, f32[16,128]{1,0:T(8,128)S(1)}, u32[]{:S(2)}, u32[]{:S(2)}) %collective-permute-start.18) | collective-permute-done | bytes 8224 | tf_op jit(solution)/shard_map/ppermute | solution.py:698
  49.1 0.8 %stream.1 = bf16[2,128,1024]{2,1,0:T(8,128)(2,1)} custom-call(f32[128,1024]{1,0:T(8,128)S(1)} %get-tuple-element.133.refs_0_, f32[128,1024]{1,0:T(8,128)S(1)} %get-tuple-element.135.refs_1_), custom_call_target="tpu_custom_call" | custom-call | flops 1024 | bytes 1024 | tf_op jit(solution)/shard_map/stream/pallas_call | solution.py:708
  50.0 2.2 %collective-permute-done.19.refs_3_ = f32[16,128]{1,0:T(8,128)S(1)} collective-permute-done((f32[16,128]{1,0:T(8,128)S(1)}, f32[16,128]{1,0:T(8,128)S(1)}, u32[]{:S(2)}, u32[]{:S(2)}) %collective-permute-start.19) | collective-permute-done | bytes 8224 | tf_op jit(solution)/shard_map/ppermute | solution.py:700
  52.2 1.0 %norm.1 = bf16[2,128,1024]{2,1,0:T(8,128)(2,1)} custom-call(f32[128,1024]{1,0:T(8,128)S(1)} %get-tuple-element.133.refs_0_, f32[128,1024]{1,0:T(8,128)S(1)} %get-tuple-element.135.refs_1_, f32[16,128]{1,0:T(8,128)S(1)} %add.3.refs_2_, f32[16,128]{1,0:T(8,128)S(1)} %collective-permute-done.19.refs_3_, bf16[1,1024]{1,0:T(2,128)(2,1)S(1)} %reshape.15.refs_4_), custom_call_target="tpu_custom_call" | custom-call | flops 1024 | bytes 1024 | tf_op jit(solution)/shard_map/norm/pallas_call | solution.py:717
  (43 shorter events, 8.9 us)
Async XLA Ops:
  1.6 12.1 %collective-permute-start = (bf16[1024,128]{1,0:T(8,128)(2,1)S(1)}, bf16[1024,128]{1,0:T(8,128)(2,1)S(1)}, u32[]{:S(2)}, u32[]{:S(2)}) collective-permute-start(bf16[1024,128]{1,0:T(8,128)(2,1)S(1)} %pack_keys.1.keys_ref), channel_id=1, source_target_pairs={{0,4},{1,9},{2,6},{3,11},{4,0},{5,13},{6,2},{7,15},{8,12},{9,1},{1... | collective-permute-start | bytes 786440 | tf_op jit(solution)/shard_map/ppermute | solution.py:581
  5.8 11.3 %collective-permute-start.3 = (bf16[1024,128]{1,0:T(8,128)(2,1)S(1)}, bf16[1024,128]{1,0:T(8,128)(2,1)S(1)}, u32[]{:S(2)}, u32[]{:S(2)}) collective-permute-start(bf16[1024,128]{1,0:T(8,128)(2,1)S(1)} %pack_values.1.values_ref), channel_id=1, source_target_pairs={{0,4},{1,9},{2,6},{3,11},{4,0},{5,13},{6,2},{7,15},{8,12},{9,1},{1... | collective-permute-start | bytes 786440 | tf_op jit(solution)/shard_map/ppermute | solution.py:581
  13.8 8.4 %collective-permute-start.2 = (bf16[1024,128]{1,0:T(8,128)(2,1)S(1)}, bf16[1024,128]{1,0:T(8,128)(2,1)S(1)}, u32[]{:S(2)}, u32[]{:S(2)}) collective-permute-start(bf16[1024,128]{1,0:T(8,128)(2,1)S(1)} %collective-permute-done.refs_1_), channel_id=1, source_target_pairs={{0,1},{1,0},{2,3},{3,2},{4,5},{5,4},{6,7},{7,6},{8,9},{9,8},{10,11... | collective-permute-start | bytes 786440 | tf_op jit(solution)/shard_map/ppermute | solution.py:583
  14.4 9.6 %collective-permute-start.1 = (bf16[1024,128]{1,0:T(8,128)(2,1)S(1)}, bf16[1024,128]{1,0:T(8,128)(2,1)S(1)}, u32[]{:S(2)}, u32[]{:S(2)}) collective-permute-start(bf16[1024,128]{1,0:T(8,128)(2,1)S(1)} %collective-permute-done.refs_1_), channel_id=1, source_target_pairs={{1,5},{3,7},{5,1},{7,3},{9,13},{11,15},{13,9},{15,11},{17,21},{19,... | collective-permute-start | bytes 786440 | tf_op jit(solution)/shard_map/ppermute | solution.py:581
  17.1 6.9 %collective-permute-start.6 = (bf16[1024,128]{1,0:T(8,128)(2,1)S(1)}, bf16[1024,128]{1,0:T(8,128)(2,1)S(1)}, u32[]{:S(2)}, u32[]{:S(2)}) collective-permute-start(bf16[1024,128]{1,0:T(8,128)(2,1)S(1)} %collective-permute-done.3.refs_2_), channel_id=1, source_target_pairs={{1,5},{3,7},{5,1},{7,3},{9,13},{11,15},{13,9},{15,11},{17,21},{19,... | collective-permute-start | bytes 786440 | tf_op jit(solution)/shard_map/ppermute | solution.py:581
  17.8 4.3 %collective-permute-start.4 = (bf16[512,128]{1,0:T(8,128)(2,1)S(1)}, bf16[512,128]{1,0:T(8,128)(2,1)S(1)}, u32[]{:S(2)}, u32[]{:S(2)}) collective-permute-start(bf16[512,128]{1,0:T(8,128)(2,1)S(1)} %get-tuple-element.139), channel_id=1, source_target_pairs={{0,1},{1,0},{2,3},{3,2},{4,5},{5,4},{6,7},{7,6},{8,9},{9,8},{10,11... | collective-permute-start | bytes 393224 | tf_op jit(solution)/shard_map/ppermute | solution.py:586
  20.2 2.0 %collective-permute-start.5 = (bf16[512,128]{1,0:T(8,128)(2,1)S(1)}, bf16[512,128]{1,0:T(8,128)(2,1)S(1)}, u32[]{:S(2)}, u32[]{:S(2)}) collective-permute-start(bf16[512,128]{1,0:T(8,128)(2,1)S(1)} %get-tuple-element.138), channel_id=1, source_target_pairs={{0,1},{1,0},{2,3},{3,2},{4,5},{5,4},{6,7},{7,6},{8,9},{9,8},{10,11... | collective-permute-start | bytes 393224 | tf_op jit(solution)/shard_map/ppermute | solution.py:586
  24.0 2.9 %collective-permute-start.8 = (bf16[1024,128]{1,0:T(8,128)(2,1)S(1)}, bf16[1024,128]{1,0:T(8,128)(2,1)S(1)}, u32[]{:S(2)}, u32[]{:S(2)}) collective-permute-start(bf16[1024,128]{1,0:T(8,128)(2,1)S(1)} %collective-permute-done.6.mine_values_ref), channel_id=1, source_target_pairs={{0,1},{1,0},{2,3},{3,2},{4,5},{5,4},{6,7},{7,6},{8,9},{9,8},{10,11... | collective-permute-start | bytes 786440 | tf_op jit(solution)/shard_map/ppermute | solution.py:586
  25.1 1.9 %collective-permute-start.7 = (bf16[1024,128]{1,0:T(8,128)(2,1)S(1)}, bf16[1024,128]{1,0:T(8,128)(2,1)S(1)}, u32[]{:S(2)}, u32[]{:S(2)}) collective-permute-start(bf16[1024,128]{1,0:T(8,128)(2,1)S(1)} %collective-permute-done.1.mine_keys_ref), channel_id=1, source_target_pairs={{0,1},{1,0},{2,3},{3,2},{4,5},{5,4},{6,7},{7,6},{8,9},{9,8},{10,11... | collective-permute-start | bytes 786440 | tf_op jit(solution)/shard_map/ppermute | solution.py:583
  29.4 2.4 %collective-permute-start.9 = (bf16[1,128,1024]{2,1,0:T(8,128)(2,1)S(1)}, bf16[1,128,1024]{2,1,0:T(8,128)(2,1)S(1)}, u32[]{:S(2)}, u32[]{:S(2)}) collective-permute-start(bf16[1,128,1024]{2,1,0:T(8,128)(2,1)S(1)} %get-tuple-element.108), channel_id=1, source_target_pairs={{0,1},{1,0},{2,3},{3,2},{4,5},{5,4},{6,7},{7,6},{8,9},{9,8},{10,11... | collective-permute-start | bytes 786440 | tf_op jit(solution)/shard_map/ppermute | solution.py:671
  32.3 8.3 %collective-permute-start.10 = (bf16[128,1024]{1,0:T(8,128)(2,1)S(1)}, bf16[128,1024]{1,0:T(8,128)(2,1)S(1)}, u32[]{:S(2)}, u32[]{:S(2)}) collective-permute-start(bf16[128,1024]{1,0:T(8,128)(2,1)S(1)} %project_onward.2), channel_id=1, source_target_pairs={{0,2},{1,3},{2,0},{3,1},{4,6},{5,7},{6,4},{7,5},{8,10},{9,11},{10,... | collective-permute-start | bytes 786440 | tf_op jit(solution)/shard_map/ppermute | solution.py:638
  36.5 1.4 %collective-permute-start.11 = (bf16[1,64,1024]{2,1,0:T(8,128)(2,1)S(1)}, bf16[1,64,1024]{2,1,0:T(8,128)(2,1)S(1)}, u32[]{:S(2)}, u32[]{:S(2)}) collective-permute-start(bf16[1,64,1024]{2,1,0:T(8,128)(2,1)S(1)} %get-tuple-element.123), channel_id=1, source_target_pairs={{0,1},{1,0},{2,3},{3,2},{4,5},{5,4},{6,7},{7,6},{8,9},{9,8},{10,11... | collective-permute-start | bytes 393224 | tf_op jit(solution)/shard_map/ppermute | solution.py:671
  36.6 1.5 %collective-permute-start.12 = (bf16[1,64,1024]{2,1,0:T(8,128)(2,1)S(1)}, bf16[1,64,1024]{2,1,0:T(8,128)(2,1)S(1)}, u32[]{:S(2)}, u32[]{:S(2)}) collective-permute-start(bf16[1,64,1024]{2,1,0:T(8,128)(2,1)S(1)} %get-tuple-element.124), channel_id=1, source_target_pairs={{0,1},{1,0},{2,3},{3,2},{4,5},{5,4},{6,7},{7,6},{8,9},{9,8},{10,11... | collective-permute-start | bytes 393224 | tf_op jit(solution)/shard_map/ppermute | solution.py:671
  38.5 8.6 %collective-permute-start.17 = (bf16[128,1024]{1,0:T(8,128)(2,1)S(1)}, bf16[128,1024]{1,0:T(8,128)(2,1)S(1)}, u32[]{:S(2)}, u32[]{:S(2)}) collective-permute-start(bf16[128,1024]{1,0:T(8,128)(2,1)S(1)} %project_onward.3), channel_id=1, source_target_pairs={{0,2},{1,3},{2,0},{3,1},{4,6},{5,7},{6,4},{7,5},{8,10},{9,11},{10,... | collective-permute-start | bytes 786440 | tf_op jit(solution)/shard_map/ppermute | solution.py:638
  41.3 1.4 %collective-permute-start.13 = (bf16[64,1024]{1,0:T(8,128)(2,1)S(1)}, bf16[64,1024]{1,0:T(8,128)(2,1)S(1)}, u32[]{:S(2)}, u32[]{:S(2)}) collective-permute-start(bf16[64,1024]{1,0:T(8,128)(2,1)S(1)} %get-tuple-element.127), channel_id=1, source_target_pairs={{0,1},{1,0},{2,3},{3,2},{4,5},{5,4},{6,7},{7,6},{8,9},{9,8},{10,11... | collective-permute-start | bytes 393224 | tf_op jit(solution)/shard_map/ppermute | solution.py:681
  41.4 1.5 %collective-permute-start.14 = (bf16[64,1024]{1,0:T(8,128)(2,1)S(1)}, bf16[64,1024]{1,0:T(8,128)(2,1)S(1)}, u32[]{:S(2)}, u32[]{:S(2)}) collective-permute-start(bf16[64,1024]{1,0:T(8,128)(2,1)S(1)} %get-tuple-element.128), channel_id=1, source_target_pairs={{0,1},{1,0},{2,3},{3,2},{4,5},{5,4},{6,7},{7,6},{8,9},{9,8},{10,11... | collective-permute-start | bytes 393224 | tf_op jit(solution)/shard_map/ppermute | solution.py:681
  41.9 1.3 %collective-permute-start.15 = (bf16[64,1024]{1,0:T(8,128)(2,1)S(1)}, bf16[64,1024]{1,0:T(8,128)(2,1)S(1)}, u32[]{:S(2)}, u32[]{:S(2)}) collective-permute-start(bf16[64,1024]{1,0:T(8,128)(2,1)S(1)} %get-tuple-element.129), channel_id=1, source_target_pairs={{0,1},{1,0},{2,3},{3,2},{4,5},{5,4},{6,7},{7,6},{8,9},{9,8},{10,11... | collective-permute-start | bytes 393224 | tf_op jit(solution)/shard_map/ppermute | solution.py:681
  42.0 7.1 %copy-start = (bf16[1024]{0:T(1024)(128)(2,1)S(1)}, bf16[1024]{0:T(1024)(128)(2,1)}, u32[]{:S(2)}) copy-start(bf16[1024]{0:T(1024)(128)(2,1)} %param.19) | copy-start | bytes 6148
  42.0 1.5 %collective-permute-start.16 = (bf16[64,1024]{1,0:T(8,128)(2,1)S(1)}, bf16[64,1024]{1,0:T(8,128)(2,1)S(1)}, u32[]{:S(2)}, u32[]{:S(2)}) collective-permute-start(bf16[64,1024]{1,0:T(8,128)(2,1)S(1)} %get-tuple-element.130), channel_id=1, source_target_pairs={{0,1},{1,0},{2,3},{3,2},{4,5},{5,4},{6,7},{7,6},{8,9},{9,8},{10,11... | collective-permute-start | bytes 393224 | tf_op jit(solution)/shard_map/ppermute | solution.py:681
  47.3 1.2 %collective-permute-start.18 = (f32[16,128]{1,0:T(8,128)S(1)}, f32[16,128]{1,0:T(8,128)S(1)}, u32[]{:S(2)}, u32[]{:S(2)}) collective-permute-start(f32[16,128]{1,0:T(8,128)S(1)} %constant_dynamic-update-slice_fusion), channel_id=1, source_target_pairs={{0,1},{1,0},{2,3},{3,2},{4,5},{5,4},{6,7},{7,6},{8,9},{9,8},{10,11... | collective-permute-start | bytes 24584 | tf_op jit(solution)/shard_map/ppermute | solution.py:698
  48.5 3.7 %collective-permute-start.19 = (f32[16,128]{1,0:T(8,128)S(1)}, f32[16,128]{1,0:T(8,128)S(1)}, u32[]{:S(2)}, u32[]{:S(2)}) collective-permute-start(f32[16,128]{1,0:T(8,128)S(1)} %add.3.refs_2_), channel_id=1, source_target_pairs={{0,2},{1,3},{2,0},{3,1},{4,6},{5,7},{6,4},{7,5},{8,10},{9,11},{10,... | collective-permute-start | bytes 24584 | tf_op jit(solution)/shard_map/ppermute | solution.py:700
